TPU v7x, 32 devices: a whole 2x2x4 slice. The times are simulated.
32 devices in a mesh: seq: 8 (over z, y), head: 4 (over x, core).
Axes of the slice: x: 2, y: 2, z: 4, core: 2. Of those that a mesh axis runs over, the one named last changes fastest.
Arguments:
- queries: float32 [1024, 32, 128], P('seq', 'head'), may hold values from -0.6 to 0.6
- keys: float32 [1024, 32, 128], P('seq', 'head'), may hold values from -0.6 to 0.6
- values: float32 [1024, 32, 128], P('seq', 'head'), may hold values from -6 to 6
- level_weights: float32 [5, 32, 1024], P(None, 'head', 'seq'), may hold values from 0.02 to 0.2
- out_proj: bfloat16 [4096, 4096], P('head'), may hold values from -0.125 to 0.125
- out_grad: bfloat16 [1024, 4096], P('seq', 'head'), may hold values from -6 to 6
Outputs:
- mixed: bfloat16 [1024, 4096], P('seq', 'head')
- query_grad: float32 [1024, 32, 128], P('seq', 'head')
- key_grad: float32 [1024, 32, 128], P('seq', 'head')
- value_grad: float32 [1024, 32, 128], P('seq', 'head')
- proj_grad: float32 [4096, 4096], P('head', 'seq')
All inputs are finite; a program needn't handle non-finite values.
Results may differ from a plain program's by a relative error of at most 0.015.
Values may be sent and summed in bfloat16 or wider, within the bound.
No kernel may reach another device: no remote copies, remote signals or barrier semaphores. Data moves between devices by JAX's collectives and lax.ppermute only.
A program may use at most 128 MiB of HBM per device.

v0:
```python
import functools

import jax
import jax.numpy as jnp
from jax import lax
from jax.experimental import pallas as pl
from jax.experimental.pallas import tpu as pltpu
from jax.sharding import PartitionSpec as P

CH = 64
BF = jnp.bfloat16
F32 = jnp.float32
NN = (((1,), (0,)), ((), ()))
NT = (((1,), (1,)), ((), ()))
TN = (((0,), (0,)), ((), ()))
TT = (((0,), (1,)), ((), ()))
VMEM = pl.BlockSpec(memory_space=pltpu.VMEM)
ANY = pl.BlockSpec(memory_space=pl.ANY)
SMEM = pl.BlockSpec(memory_space=pltpu.SMEM)
PARAMS = pltpu.CompilerParams(vmem_limit_bytes=14 * 2**20)


def mm(a, b, dims):
    return lax.dot_general(a, b, dims, preferred_element_type=F32)


def cost(flops, moved):
    return pl.CostEstimate(flops=flops, bytes_accessed=moved, transcendentals=0)


def like(shape, dtype):
    return jax.ShapeDtypeStruct(shape, dtype)


def across(block, axis, stride, up_only=False, down_only=False):
    count = lax.axis_size(axis)
    route = []
    for low in range(count):
        high = low | 1 << stride
        if high != low and high < count:
            if not down_only:
                route.append((low, high))
            if not up_only:
                route.append((high, low))
    return lax.ppermute(block, axis, route)


def hbm(array):
    return pltpu.with_memory_space_constraint(array, pltpu.HBM)


def state_kernel(k_hbm, v_hbm, s_ref, kh_ref, vh_ref, k_ref, v_ref, sems):
    copies = [
        pltpu.make_async_copy(k_hbm, k_ref, sems.at[0]),
        pltpu.make_async_copy(v_hbm, v_ref, sems.at[1]),
    ]
    for copy in copies:
        copy.start()
    for copy in copies:
        copy.wait()
    for h in range(k_ref.shape[1]):
        k = k_ref[:, h, :].astype(BF)
        v = v_ref[:, h, :].astype(BF)
        kh_ref[h] = k
        vh_ref[h] = v
        s_ref[h] = mm(k, v, TN).astype(BF)


def weight_of(lam_ref, h, rows):
    local_bits = (rows // CH).bit_length() - 1
    s = lax.broadcasted_iota(jnp.int32, (rows, rows), 0)
    t = lax.broadcasted_iota(jnp.int32, (rows, rows), 1)
    differ = (s // CH) ^ (t // CH)
    weight = jnp.broadcast_to(lam_ref[0, h : h + 1, :], (rows, rows))
    for digit in range(local_bits):
        weight = jnp.where(differ >= 1 << digit, lam_ref[1 + digit, h : h + 1, :], weight)
    return jnp.where(s <= t, weight, 0.0)


def upper_weight(place_ref, lam_ref, b, h, rows):
    local_bits = (rows // CH).bit_length() - 1
    upper = (place_ref[0] >> b & 1).astype(F32)
    return lam_ref[1 + local_bits + b, h : h + 1, :] * upper


def local_kernel(place_ref, q_hbm, kh_ref, vh_ref, lam_hbm, w_hbm, *refs):
    pt_ref, att_ref, qh_ref, qw_ref, lam_ref, w_ref, q_ref, lam_rows, sems = refs
    pieces = sems.shape[0] - 2
    share = w_hbm.shape[0] // pieces
    copies = [
        pltpu.make_async_copy(q_hbm, q_ref, sems.at[0]),
        pltpu.make_async_copy(lam_hbm, lam_ref, sems.at[1]),
    ]
    for i in range(pieces):
        piece = pl.ds(i * share, share)
        copies.append(pltpu.make_async_copy(w_hbm.at[piece], w_ref.at[piece], sems.at[2 + i]))
    for copy in copies:
        copy.start()
    for copy in copies[:2]:
        copy.wait()
    rows, heads_dev, _ = q_ref.shape
    bits = qw_ref.shape[0]
    lam_rows[...] = jnp.zeros_like(lam_rows)
    for b in range(bits):
        for h in range(heads_dev):
            at = b * heads_dev + h
            lam_rows[at : at + 1, :] = upper_weight(place_ref, lam_ref, b, h, rows)
    lam_columns = lam_rows[...].T
    for h in range(heads_dev):
        q32 = q_ref[:, h, :]
        q = q32.astype(BF)
        qh_ref[h] = q
        for b in range(bits):
            at = b * heads_dev + h
            qw_ref[b, h] = (q32 * lam_columns[:, at : at + 1]).astype(BF)
        pt = (mm(kh_ref[h], q, NT) * weight_of(lam_ref, h, rows)).astype(BF)
        pt_ref[h] = pt
        att_ref[h] = mm(pt, vh_ref[h], TN)
    for copy in copies[2:]:
        copy.wait()


def attended_kernel(bits, att_ref, qw_ref, after_ref, *refs):
    del after_ref
    states, out_ref = refs[:bits], refs[bits]
    heads_dev, _, head_dim = att_ref.shape
    for h in range(heads_dev):
        total = att_ref[h]
        for b in range(bits):
            total = total + mm(qw_ref[b, h], states[b][h], NN)
        out_ref[:, h * head_dim : (h + 1) * head_dim] = total.astype(BF)


def cotangent_kernel(blocks, bits, head_ref, *refs):
    parts, (w_ref, qw_ref, _, gt_ref), sums = (
        refs[:blocks],
        refs[blocks : blocks + 4],
        refs[blocks + 4 :],
    )
    deep = parts[0].shape[1]
    _, heads_dev, _, head_dim = qw_ref.shape
    total = None
    for i in range(blocks):
        column = pl.multiple_of((head_ref[0] ^ i) * deep, deep)
        product = mm(w_ref[:, pl.ds(column, deep)], parts[i][...], NT)
        total = product if total is None else total + product
    for h in range(heads_dev):
        gt = total[h * head_dim : (h + 1) * head_dim].astype(BF)
        gt_ref[h * head_dim : (h + 1) * head_dim, :] = gt
        for b in range(bits):
            sums[b][h] = mm(gt, qw_ref[b, h], NN).astype(BF)


def running_kernel(running_ref, arrived_ref, *refs):
    refs[-1][...] = (running_ref[...].astype(F32) + arrived_ref[...].astype(F32)).astype(BF)


def meet_kernel(top, place_ref, after_ref, grad_ref, running_ref, arrived_ref, out_ref):
    del after_ref
    upper = (place_ref[0] >> top & 1) == 1
    running = running_ref[...].astype(F32)
    if arrived_ref is not None:
        running = running + arrived_ref[...].astype(F32)
    out_ref[...] = jnp.where(upper, grad_ref[...], running.astype(BF))


def landed_sum(top, place_ref, landed):
    upper = (place_ref[0] >> top & 1) == 1
    total = jnp.where(upper, 0.0, landed[0].astype(F32))
    for block in landed[1:]:
        total = total + block.astype(F32)
    return total


def pending_kernel(top, place_ref, own_ref, after_ref, *refs):
    del after_ref
    landed, out_ref = [ref[...] for ref in refs[:-1]], refs[-1]
    out_ref[...] = (own_ref[...].astype(F32) + landed_sum(top, place_ref, landed)).astype(BF)


def chunk_kernel(place_ref, block_ref, after_ref, *outs):
    del after_ref
    columns = outs[0].shape[1]
    low = place_ref[0] % len(outs)
    for r, out in enumerate(outs):
        out[...] = block_ref[:, pl.ds(pl.multiple_of((low ^ r) * columns, columns), columns)]


def stack_kernel(after_ref, *refs):
    del after_ref
    for r, ref in enumerate(refs[:-1]):
        refs[-1][r] = ref[...]


def columns_kernel(blocks, place_ref, head_ref, *refs):
    parts, out_ref = refs[:blocks], refs[blocks]
    per = parts[0].shape[0]
    low = place_ref[0] % per
    for i in range(blocks):
        for r in range(per):
            out_ref[(head_ref[0] ^ i) * per + (low ^ r)] = parts[i][r]


def local_grad_kernel(
    bits, place_ref, gt_ref, qh_ref, kh_ref, vh_ref, pt_ref, lam_ref, after_ref, *refs
):
    del after_ref
    states, (dq_ref, dk_ref, dv_ref) = refs[:bits], refs[bits:]
    heads_dev, rows, head_dim = qh_ref.shape
    for h in range(heads_dev):
        gt = gt_ref[h * head_dim : (h + 1) * head_dim, :]
        g32 = gt.astype(F32)
        dpt = (mm(vh_ref[h], gt, NN) * weight_of(lam_ref, h, rows)).astype(BF)
        dk_ref[h] = mm(dpt, qh_ref[h], NN)
        dv_ref[h] = mm(pt_ref[h], gt, NT)
        dq = mm(dpt, kh_ref[h], TN)
        for b in range(bits):
            gw = (g32 * upper_weight(place_ref, lam_ref, b, h, rows)).astype(BF)
            dq = dq + mm(gw, states[b][h], TT)
        dq_ref[:, h, :] = dq


def later_grad_kernel(top, place_ref, kh_ref, vh_ref, dkl_ref, dvl_ref, after_ref, *refs):
    del after_ref
    landed, (dk_ref, dv_ref) = refs[:-2], refs[-2:]
    for h in range(kh_ref.shape[0]):
        late = landed_sum(top, place_ref, [ref[h] for ref in landed]).astype(BF)
        dk_ref[:, h, :] = dkl_ref[h] + mm(vh_ref[h], late, NN)
        dv_ref[:, h, :] = dvl_ref[h] + mm(kh_ref[h], late, NT)


def share_kernel(blocks, head_ref, att_ref, w_ref, send_ref, kept_ref):
    width = send_ref.shape[2]
    for i in range(blocks):
        out = send_ref if i % 2 else kept_ref
        column = pl.multiple_of((head_ref[0] ^ i) * width, width)
        out[i // 2] = mm(att_ref[...], w_ref[:, pl.ds(column, width)], NN).astype(out.dtype)


def ring_owner(place, offset, devices):
    at = jnp.where(place % 2 == 0, place // 2, devices - 1 - place // 2)
    at = (at + offset + devices) % devices
    return jnp.where(at < devices // 2, 2 * at, 2 * (devices - 1 - at) + 1)


def proj_kernel(offsets, devices, first, place_ref, cols_ref, *refs):
    total = None if first else refs[len(offsets)][...]
    for i, (offset, low, high) in enumerate(offsets):
        owner = ring_owner(place_ref[0], offset, devices)
        product = mm(refs[i][...], cols_ref[owner, low:high, :], TN)
        total = product if total is None else total + product
    refs[-1][...] = total


def last_kernel(
    offset, devices, place_ref, cols_ref, low_ref, high_ref, total_ref, after_ref, out_ref, held
):
    del after_ref
    half = low_ref.shape[0]
    held[:half] = low_ref[...]
    held[half:] = high_ref[...]
    owner = ring_owner(place_ref[0], offset, devices)
    out_ref[...] = total_ref[...] + mm(held[...], cols_ref[owner], TN)


def body(queries, keys, values, level_weights, out_proj, out_grad):
    rows, heads_dev, head_dim = queries.shape
    width = heads_dev * head_dim
    devices = lax.axis_size("seq")
    seq_bits = devices.bit_length() - 1
    heads = lax.axis_size("head")
    head_bits = heads.bit_length() - 1
    seq_place = lax.axis_index("seq")
    head_place = lax.axis_index("head")
    columns_dev = out_proj.shape[1] // devices

    head_state = like((heads_dev, head_dim, head_dim), BF)
    pinned_state = pltpu.VMEM((heads_dev, head_dim, head_dim), BF)
    per_head = pltpu.VMEM((heads_dev, rows, head_dim), BF)
    per_head_f32 = pltpu.VMEM((heads_dev, rows, head_dim), F32)
    flops_head = 2 * heads_dev * rows * rows * head_dim
    moved_head = 2 * rows * width
    top = seq_bits - 1
    place = seq_place.reshape(1).astype(jnp.int32)
    group = head_place.reshape(1).astype(jnp.int32)

    own_state, kh, vh = pl.pallas_call(
        state_kernel,
        out_shape=(head_state, per_head, per_head),
        in_specs=[ANY] * 2,
        out_specs=(VMEM,) * 3,
        scratch_shapes=[
            pltpu.VMEM(keys.shape, F32),
            pltpu.VMEM(keys.shape, F32),
            pltpu.SemaphoreType.DMA((2,)),
        ],
        compiler_params=PARAMS,
        cost_estimate=cost(flops_head, 7 * moved_head),
    )(hbm(keys), hbm(values))

    def to_group(block, i):
        return lax.ppermute(block, "head", [(at, at ^ i) for at in range(heads)])

    def every_group(block):
        blocks = {0: block}
        for digit in reversed(range(head_bits)):
            for i in sorted(blocks):
                blocks[i ^ 1 << digit] = to_group(blocks[i], 1 << digit)
        return [blocks[i] for i in range(heads)]

    grad_blocks = every_group(out_grad)

    per = devices // heads
    route = [
        ((high * per + low) * heads + group_at, (group_at * per + low) * heads + high)
        for high in range(heads)
        for low in range(per)
        for group_at in range(heads)
    ]
    turned = lax.ppermute(out_grad, ("seq", "head"), route)
    probs_t, att_local, qh, qw, lam, w = pl.pallas_call(
        local_kernel,
        out_shape=(
            pltpu.VMEM((heads_dev, rows, rows), BF),
            per_head_f32,
            per_head,
            pltpu.VMEM((seq_bits, heads_dev, rows, head_dim), BF),
            pltpu.VMEM(level_weights.shape, F32),
            pltpu.VMEM(out_proj.shape, BF),
        ),
        in_specs=[SMEM, ANY, VMEM, VMEM, ANY, ANY],
        out_specs=(VMEM,) * 6,
        scratch_shapes=[
            pltpu.VMEM(queries.shape, F32),
            pltpu.VMEM((rows, rows), F32),
            pltpu.SemaphoreType.DMA((10,)),
        ],
        compiler_params=PARAMS,
        cost_estimate=cost(2 * flops_head, 12 * moved_head),
    )(place, hbm(queries), kh, vh, hbm(level_weights), hbm(out_proj))

    partner_states = []
    running, arrived = own_state, None
    for digit in range(top):
        if arrived is not None:
            running = pl.pallas_call(
                running_kernel,
                out_shape=head_state,
                in_specs=[VMEM] * 2 + [ANY] * 2,
                out_specs=VMEM,
                compiler_params=PARAMS,
                cost_estimate=cost(0, 3 * moved_head),
            )(running, arrived, turned, qw)
        arrived = across(running, "seq", digit)
        partner_states.append(arrived)

    chunks = pl.pallas_call(
        chunk_kernel,
        out_shape=(like((rows, columns_dev), BF),) * per,
        in_specs=[SMEM, VMEM, ANY],
        out_specs=(VMEM,) * per,
        compiler_params=PARAMS,
        cost_estimate=cost(0, 2 * moved_head),
    )(place, turned, running)
    own_chunks = chunks
    chunks = [chunks[0]] + [
        lax.ppermute(chunks[r], "seq", [(at, at ^ r) for at in range(devices)])
        for r in range(1, per)
    ]
    gt, *grad_sums = pl.pallas_call(
        functools.partial(cotangent_kernel, heads, seq_bits),
        out_shape=(pltpu.VMEM((width, rows), BF),) + (pinned_state,) * seq_bits,
        in_specs=[SMEM] + [VMEM] * (heads + 2) + [ANY],
        out_specs=(VMEM,) * (1 + seq_bits),
        compiler_params=PARAMS,
        cost_estimate=cost(2 * rows * width * out_proj.shape[1], 2 * width * out_proj.shape[1]),
    )(group, *grad_blocks, w, qw, own_chunks[-1])

    stacked = pl.pallas_call(
        stack_kernel,
        out_shape=like((per, rows, columns_dev), BF),
        in_specs=[ANY] + [VMEM] * per,
        out_specs=VMEM,
        compiler_params=PARAMS,
        cost_estimate=cost(0, 2 * moved_head),
    )(gt, *chunks)
    column_blocks = every_group(stacked)

    meeting = pl.pallas_call(
        functools.partial(meet_kernel, top)
        if arrived is not None
        else lambda place_ref, after_ref, grad_ref, running_ref, out_ref: meet_kernel(
            top, place_ref, after_ref, grad_ref, running_ref, None, out_ref
        ),
        out_shape=head_state,
        in_specs=[SMEM, ANY] + [VMEM] * (2 if arrived is None else 3),
        out_specs=VMEM,
        compiler_params=PARAMS,
        cost_estimate=cost(0, 4 * moved_head),
    )(place, stacked, grad_sums[top], running, *([] if arrived is None else [arrived]))
    landed = [across(meeting, "seq", top)]
    partner_states.append(landed[0])

    grad_columns = pl.pallas_call(
        functools.partial(columns_kernel, heads),
        out_shape=pltpu.VMEM((devices, rows, columns_dev), BF),
        in_specs=[SMEM] * 2 + [VMEM] * heads,
        out_specs=VMEM,
        compiler_params=PARAMS,
        cost_estimate=cost(0, 8 * moved_head),
    )(place, group, *column_blocks)

    attended = pl.pallas_call(
        functools.partial(attended_kernel, seq_bits),
        out_shape=like((rows, width), BF),
        in_specs=[VMEM] * 2 + [ANY] + [VMEM] * seq_bits,
        out_specs=VMEM,
        compiler_params=PARAMS,
        cost_estimate=cost(seq_bits * flops_head, 8 * moved_head),
    )(att_local, qw, column_blocks[-1], *partner_states)

    for digit in reversed(range(top)):
        outgoing = pl.pallas_call(
            functools.partial(pending_kernel, top),
            out_shape=head_state,
            in_specs=[SMEM, VMEM, ANY] + [VMEM] * len(landed),
            out_specs=VMEM,
            compiler_params=PARAMS,
            cost_estimate=cost(0, 4 * moved_head),
        )(place, grad_sums[digit], attended, *landed)
        landed.append(across(outgoing, "seq", digit))

    send, kept = pl.pallas_call(
        functools.partial(share_kernel, heads),
        out_shape=(like((heads // 2, rows, width), BF), like((heads // 2, rows, width), F32)),
        in_specs=[SMEM, VMEM, VMEM],
        out_specs=(VMEM,) * 2,
        compiler_params=PARAMS,
        cost_estimate=cost(2 * rows * width * out_proj.shape[1], 2 * width * out_proj.shape[1]),
    )(group, attended, w)
    for digit in range(head_bits):
        kept = kept + to_group(send, 1 << digit).astype(F32)
        if digit < head_bits - 1:
            send, kept = kept[1::2].astype(BF), kept[0::2]
    mixed = kept[0].astype(BF)

    query_grad, key_local, value_local = pl.pallas_call(
        functools.partial(local_grad_kernel, seq_bits),
        out_shape=(like((rows, heads_dev, head_dim), F32), per_head_f32, per_head_f32),
        in_specs=[SMEM] + [VMEM] * 6 + [ANY] + [VMEM] * seq_bits,
        out_specs=(VMEM,) * 3,
        compiler_params=PARAMS,
        cost_estimate=cost((4 + seq_bits) * flops_head, 14 * moved_head),
    )(place, gt, qh, kh, vh, probs_t, lam, send, *partner_states)

    ring = list(range(0, devices, 2)) + list(range(devices - 1, 0, -2))
    forward = [(ring[i], ring[(i + 1) % devices]) for i in range(devices)]
    backward = [(b, a) for a, b in forward]

    def accumulate(total, blocks, offsets):
        operands = blocks if total is None else blocks + [total]
        return pl.pallas_call(
            functools.partial(proj_kernel, offsets, devices, total is None),
            out_shape=like((width, columns_dev), F32),
            in_specs=[SMEM] + [VMEM] * (1 + len(operands)),
            out_specs=VMEM,
            compiler_params=PARAMS,
            cost_estimate=cost(
                2 * len(blocks) * rows * width * columns_dev, 4 * width * columns_dev
            ),
        )(place, grad_columns, *operands)

    blocks, offsets = [attended], [(0, 0, rows)]
    ahead = behind = attended
    half, steps, total = rows // 2, devices // 2, None
    for step in range(1, steps):
        ahead = lax.ppermute(ahead, "seq", forward)
        behind = lax.ppermute(behind, "seq", backward)
        blocks += [ahead, behind]
        offsets += [(-step, 0, rows), (step, 0, rows)]
        if step == steps - 2:
            total = accumulate(None, blocks, offsets)
            blocks, offsets = [], []
    if blocks:
        total = accumulate(total, blocks, offsets)
    last = [
        lax.ppermute(ahead[:half], "seq", forward),
        lax.ppermute(behind[half:], "seq", backward),
    ]
    key_grad, value_grad = pl.pallas_call(
        functools.partial(later_grad_kernel, top),
        out_shape=(like((rows, heads_dev, head_dim), F32),) * 2,
        in_specs=[SMEM] + [VMEM] * 4 + [ANY] + [VMEM] * seq_bits,
        out_specs=(VMEM,) * 2,
        compiler_params=PARAMS,
        cost_estimate=cost(2 * flops_head, 11 * moved_head),
    )(place, kh, vh, key_local, value_local, total, *landed)
    quarter_rows = width // 4
    proj_grad = pl.pallas_call(
        functools.partial(last_kernel, steps, devices),
        out_shape=like((width, columns_dev), F32),
        grid=(4,),
        in_specs=[
            SMEM,
            VMEM,
            pl.BlockSpec((half, quarter_rows), lambda i: (0, i)),
            pl.BlockSpec((half, quarter_rows), lambda i: (0, i)),
            pl.BlockSpec((quarter_rows, columns_dev), lambda i: (i, 0)),
            ANY,
        ],
        out_specs=pl.BlockSpec((quarter_rows, columns_dev), lambda i: (i, 0)),
        scratch_shapes=[pltpu.VMEM((rows, quarter_rows), BF)],
        compiler_params=PARAMS,
        cost_estimate=cost(2 * rows * width * columns_dev, 8 * width * columns_dev),
    )(place, grad_columns, *last, total, hbm(key_grad))
    return (mixed, query_grad, key_grad, value_grad, proj_grad)


def solution(mesh):
    placed = (
        P("seq", "head", None),
        P("seq", "head", None),
        P("seq", "head", None),
        P(None, "head", "seq"),
        P("head", None),
        P("seq", "head"),
    )
    return jax.shard_map(
        body,
        mesh=mesh,
        in_specs=placed,
        out_specs=(
            P("seq", "head"),
            P("seq", "head", None),
            P("seq", "head", None),
            P("seq", "head", None),
            P("head", "seq"),
        ),
        check_vma=False,
    )
```

profile of v0, /device:TPU:0, one launch (start us, length us, event | category | flops | bytes accessed | tf_op | source)
XLA Modules:
  0.0 86.4 jit_solution(16002497548314703958)
XLA Ops:
  0.6 3.0 %collective-permute-start.1 = (bf16[128,1024]{1,0:T(8,128)(2,1)}, bf16[128,1024]{1,0:T(8,128)(2,1)}, u32[]{:S(2)}, u32[]{:S(2)}) collective-permute-start(bf16[128,1024]{1,0:T(8,128)(2,1)} %refs_0_.1), channel_id=1, source_target_pairs={{0,2},{1,3},{2,0},{3,1},{4,6},{5,7},{6,4},{7,5},{8,10},{9,11},{10,... | collective-permute-start | bytes 786440 | tf_op jit(solution)/shard_map/ppermute | solution.py:302
  3.6 1.6 %collective-permute-start.3 = (bf16[128,1024]{1,0:T(8,128)(2,1)}, bf16[128,1024]{1,0:T(8,128)(2,1)S(1)}, u32[]{:S(2)}, u32[]{:S(2)}) collective-permute-start(bf16[128,1024]{1,0:T(8,128)(2,1)} %refs_0_.1), channel_id=1, source_target_pairs={{0,0},{1,8},{2,16},{3,24},{4,4},{5,12},{6,20},{7,28},{8,1},{9,9},{... | collective-permute-start | bytes 786440 | tf_op jit(solution)/shard_map/ppermute | solution.py:320
  5.2 2.4 %shard_map.101 = (bf16[8,128,128]{2,1,0:T(8,128)(2,1)S(1)}, bf16[8,128,128]{2,1,0:T(8,128)(2,1)S(1)}, bf16[8,128,128]{2,1,0:T(8,128)(2,1)S(1)}) custom-call(f32[128,8,128]{2,1,0:T(8,128)} %k_hbm.1, f32[128,8,128]{2,1,0:T(8,128)} %v_hbm.1), custom_call_target="tpu_custom_call" | custom-call | flops 33554432 | bytes 1835008 | tf_op jit(solution)/shard_map/pallas_call | solution.py:287
  7.7 1.6 %collective-permute-start.4 = (bf16[8,128,128]{2,1,0:T(8,128)(2,1)S(1)}, bf16[8,128,128]{2,1,0:T(8,128)(2,1)S(1)}, u32[]{:S(2)}, u32[]{:S(2)}) collective-permute-start(bf16[8,128,128]{2,1,0:T(8,128)(2,1)S(1)} %get-tuple-element.32.running_ref), channel_id=1, source_target_pairs={{0,4},{4,0},{8,12},{12,8},{16,20},{20,16},{24,28},{28,24},{1,5},{5... | collective-permute-start | bytes 786440 | tf_op jit(solution)/shard_map/ppermute | solution.py:45
  9.3 1.7 %collective-permute-start = (bf16[128,1024]{1,0:T(8,128)(2,1)}, bf16[128,1024]{1,0:T(8,128)(2,1)}, u32[]{:S(2)}, u32[]{:S(2)}) collective-permute-start(bf16[128,1024]{1,0:T(8,128)(2,1)} %refs_0_.1), channel_id=1, source_target_pairs={{0,1},{1,0},{2,3},{3,2},{4,5},{5,4},{6,7},{7,6},{8,9},{9,8},{10,11... | collective-permute-start | bytes 786440 | tf_op jit(solution)/shard_map/ppermute | solution.py:302
  11.0 0.0 collective-permute-done.1.refs_2_
  11.0 0.0 collective-permute-start.2
  11.0 3.7 %shard_map.102 = (bf16[8,128,128]{2,1,0:T(8,128)(2,1)S(1)}, f32[8,128,128]{2,1,0:T(8,128)S(1)}, bf16[8,128,128]{2,1,0:T(8,128)(2,1)S(1)}, bf16[3,8,128,128]{3,2,...) custom-call(s32[1]{0:T(128)} %bitcast.1.place_ref, f32[128,8,128]{2,1,0:T(8,128)} %q_hbm.1, ...), custom_call_target="tpu_custom_call" | custom-call | flops 67108864 | bytes 3145728 | tf_op jit(solution)/shard_map/pallas_call | solution.py:321
  14.7 3.3 %copy-done = bf16[1024,4096]{1,0:T(8,128)(2,1)} copy-done((bf16[1024,4096]{1,0:T(8,128)(2,1)}, bf16[1024,4096]{1,0:T(8,128)(2,1)S(1)}, u32[]{:S(2)}) %copy-start) | copy-done | bytes 8388632
  17.9 0.6 copy-done.4
  18.5 0.0 collective-permute-done.3.refs_0_.block_ref
  18.5 0.0 collective-permute-done.4.arrived_ref.refs_0_
  18.5 0.1 shard_map.103.after_ref.running_ref
  18.6 1.1 %collective-permute-start.5 = (bf16[128,512]{1,0:T(8,128)(2,1)S(1)}, bf16[128,512]{1,0:T(8,128)(2,1)S(1)}, u32[]{:S(2)}, u32[]{:S(2)}) collective-permute-start(bf16[128,512]{1,0:T(8,128)(2,1)S(1)} %get-tuple-element.33.refs_6_), channel_id=1, source_target_pairs={{0,4},{4,0},{8,12},{12,8},{16,20},{20,16},{24,28},{28,24},{1,5},{5... | collective-permute-start | bytes 393224 | tf_op jit(solution)/shard_map/ppermute | solution.py:367
  19.7 3.4 %collective-permute-start.8 = (bf16[8,128,128]{2,1,0:T(8,128)(2,1)S(1)}, bf16[8,128,128]{2,1,0:T(8,128)(2,1)S(1)}, u32[]{:S(2)}, u32[]{:S(2)}) collective-permute-start(bf16[8,128,128]{2,1,0:T(8,128)(2,1)S(1)} %shard_map.103.after_ref.running_ref), channel_id=1, source_target_pairs={{0,8},{8,0},{4,12},{12,4},{16,24},{24,16},{20,28},{28,20},{1,9},{9... | collective-permute-start | bytes 786440 | tf_op jit(solution)/shard_map/ppermute | solution.py:45
  23.1 0.0 collective-permute-done.refs_1_
  23.1 0.0 collective-permute-done.2.refs_3_
  23.1 3.4 %copy-done.1 = bf16[1024,4096]{1,0:T(8,128)(2,1)S(1)} copy-done((bf16[1024,4096]{1,0:T(8,128)(2,1)S(1)}, bf16[1024,4096]{1,0:T(8,128)(2,1)}, u32[]{:S(2)}) %copy-start.1) | copy-done | bytes 8388632
  26.5 0.9 %copy-done.3 = bf16[128,1024]{1,0:T(8,128)(2,1)S(1)} copy-done((bf16[128,1024]{1,0:T(8,128)(2,1)S(1)}, bf16[128,1024]{1,0:T(8,128)(2,1)}, u32[]{:S(2)}) %copy-start.3) | copy-done | bytes 262168
  27.5 4.1 %shard_map.105 = (bf16[1024,128]{1,0:T(8,128)(2,1)S(1)}, bf16[8,128,128]{2,1,0:T(8,128)(2,1)S(1)}, bf16[8,128,128]{2,1,0:T(8,128)(2,1)S(1)}, bf16[8,128,128]{2,1,0:T(8,128)(2,1)S(1)}) custom-call(s32[1]{0:T(128)} %bitcast.head_ref, bf16[128,1024]{1,0:T(8,128)(2,1)S(1)} %copy-done.3, bf16[128,1024]{1,0:T(8,128)(2,1)} %collective-permute-done.refs_1_, ...), custom_call_target="tpu_custom_call" | custom-call | flops 1073741824 | bytes 8388608 | tf_op jit(solution)/shard_map/pallas_call | solution.py:370
  31.5 0.0 collective-permute-done.5.refs_1_
  31.6 2.7 %collective-permute-start.6 = (bf16[2,128,512]{2,1,0:T(8,128)(2,1)S(1)}, bf16[2,128,512]{2,1,0:T(8,128)(2,1)S(1)}, u32[]{:S(2)}, u32[]{:S(2)}) collective-permute-start(bf16[2,128,512]{2,1,0:T(8,128)(2,1)S(1)} %shard_map.106.after_ref.refs_0_), channel_id=1, source_target_pairs={{0,2},{1,3},{2,0},{3,1},{4,6},{5,7},{6,4},{7,5},{8,10},{9,11},{10,... | collective-permute-start | bytes 786440 | tf_op jit(solution)/shard_map/ppermute | solution.py:302
  34.3 0.0 collective-permute-done.8.arrived_ref.refs_1_
  34.3 0.1 shard_map.107
  34.4 0.1 collective-permute-start.9
  34.5 6.2 %collective-permute-done.6.refs_2_ = bf16[2,128,512]{2,1,0:T(8,128)(2,1)S(1)} collective-permute-done((bf16[2,128,512]{2,1,0:T(8,128)(2,1)S(1)}, bf16[2,128,512]{2,1,0:T(8,128)(2,1)S(1)}, u32[]{:S(2)}, u32[]{:S(2)}) %collective-permute-start.6) | collective-permute-done | bytes 262176 | tf_op jit(solution)/shard_map/ppermute | solution.py:302
  40.7 0.0 collective-permute-start.7
  40.7 7.9 %collective-permute-done.9.refs_2_.refs_0_ = bf16[8,128,128]{2,1,0:T(8,128)(2,1)S(1)} collective-permute-done((bf16[8,128,128]{2,1,0:T(8,128)(2,1)S(1)}, bf16[8,128,128]{2,1,0:T(8,128)(2,1)S(1)}, u32[]{:S(2)}, u32[]{:S(2)}) %collective-permute-start.9) | collective-permute-done | bytes 262176 | tf_op jit(solution)/shard_map/ppermute | solution.py:45
  48.6 0.0 collective-permute-done.7.after_ref.refs_3_
  48.6 0.4 shard_map.108.att_ref.refs_0_.after_ref
  49.0 0.1 collective-permute-start.13
  49.1 2.0 %collective-permute-start.16 = (bf16[128,1024]{1,0:T(8,128)(2,1)S(1)}, bf16[128,1024]{1,0:T(8,128)(2,1)S(1)}, u32[]{:S(2)}, u32[]{:S(2)}) collective-permute-start(bf16[128,1024]{1,0:T(8,128)(2,1)S(1)} %shard_map.108.att_ref.refs_0_.after_ref), channel_id=1, source_target_pairs={{8,0},{16,8},{24,16},{28,24},{20,28},{12,20},{4,12},{0,4},{9,1},{1... | collective-permute-start | bytes 786440 | tf_op jit(solution)/shard_map/ppermute | solution.py:478
  51.1 1.3 %shard_map.109 = (bf16[2,128,1024]{2,1,0:T(8,128)(2,1)S(1)}, f32[2,128,1024]{2,1,0:T(8,128)S(1)}) custom-call(s32[1]{0:T(128)} %bitcast.head_ref, bf16[128,1024]{1,0:T(8,128)(2,1)S(1)} %shard_map.108.att_ref.refs_0_.after_ref, bf16[1024,4096]{1,0:T(8,128)(2,1)S(1)} %copy-done.2), custom_call_target="tpu_custom_call" | custom-call | flops 1073741824 | bytes 8388608 | tf_op jit(solution)/shard_map/pallas_call | solution.py:433
  52.4 0.1 collective-permute-start.10
  52.4 4.8 %collective-permute-done.13.refs_1_ = bf16[128,1024]{1,0:T(8,128)(2,1)S(1)} collective-permute-done((bf16[128,1024]{1,0:T(8,128)(2,1)S(1)}, bf16[128,1024]{1,0:T(8,128)(2,1)S(1)}, u32[]{:S(2)}, u32[]{:S(2)}) %collective-permute-start.13) | collective-permute-done | bytes 262176 | tf_op jit(solution)/shard_map/ppermute | solution.py:477
  57.3 0.3 collective-permute-start.14
  57.5 0.0 collective-permute-done.16.refs_2_
  57.6 1.7 %collective-permute-start.17 = (bf16[128,1024]{1,0:T(8,128)(2,1)S(1)}, bf16[128,1024]{1,0:T(8,128)(2,1)S(1)}, u32[]{:S(2)}, u32[]{:S(2)}) collective-permute-start(bf16[128,1024]{1,0:T(8,128)(2,1)S(1)} %collective-permute-done.16.refs_2_), channel_id=1, source_target_pairs={{8,0},{16,8},{24,16},{28,24},{20,28},{12,20},{4,12},{0,4},{9,1},{1... | collective-permute-start | bytes 786440 | tf_op jit(solution)/shard_map/ppermute | solution.py:478
  59.3 0.0 collective-permute-start.12
  59.3 0.1 shard_map.114
  59.4 0.4 collective-permute-start.19
  59.7 4.9 %collective-permute-done.14.refs_3_ = bf16[128,1024]{1,0:T(8,128)(2,1)S(1)} collective-permute-done((bf16[128,1024]{1,0:T(8,128)(2,1)S(1)}, bf16[128,1024]{1,0:T(8,128)(2,1)S(1)}, u32[]{:S(2)}, u32[]{:S(2)}) %collective-permute-start.14) | collective-permute-done | bytes 262176 | tf_op jit(solution)/shard_map/ppermute | solution.py:477
  64.6 2.2 %collective-permute-start.15 = (bf16[128,1024]{1,0:T(8,128)(2,1)S(1)}, bf16[128,1024]{1,0:T(8,128)(2,1)S(1)}, u32[]{:S(2)}, u32[]{:S(2)}) collective-permute-start(bf16[128,1024]{1,0:T(8,128)(2,1)S(1)} %collective-permute-done.14.refs_3_), channel_id=1, source_target_pairs={{0,8},{8,16},{16,24},{24,28},{28,20},{20,12},{12,4},{4,0},{1,9},{9... | collective-permute-start | bytes 786440 | tf_op jit(solution)/shard_map/ppermute | solution.py:477
  66.8 0.2 collective-permute-start.18
  67.0 0.0 collective-permute-done.10
  67.0 0.1 convert_add_fusion
  67.2 0.0 copy-start.5
  67.2 0.4 collective-permute-start.11
  67.6 0.1 shard_map.111.cols_ref
  67.7 4.7 %collective-permute-done.19.refs_1_ = bf16[8,128,128]{2,1,0:T(8,128)(2,1)S(1)} collective-permute-done((bf16[8,128,128]{2,1,0:T(8,128)(2,1)S(1)}, bf16[8,128,128]{2,1,0:T(8,128)(2,1)S(1)}, u32[]{:S(2)}, u32[]{:S(2)}) %collective-permute-start.19) | collective-permute-done | bytes 262176 | tf_op jit(solution)/shard_map/ppermute | solution.py:45
  72.4 0.1 shard_map.115
  72.5 0.3 collective-permute-start.20
  72.8 2.5 %shard_map.110 = (f32[128,8,128]{2,1,0:T(8,128)}, f32[8,128,128]{2,1,0:T(8,128)S(1)}, f32[8,128,128]{2,1,0:T(8,128)S(1)}) custom-call(s32[1]{0:T(128)} %bitcast.1.place_ref, bf16[1024,128]{1,0:T(8,128)(2,1)S(1)} %get-tuple-element.34.after_ref.gt_ref, bf16[8,128,128]{2,1,0:T(8,128)(2,1)S(1)} %get-tuple-element.39.qh_ref, ...), custom_call_target="tpu_custom_call" | custom-call | flops 234881024 | bytes 3670016 | tf_op jit(solution)/shard_map/pallas_call | solution.py:447
  75.3 1.5 %shard_map.112.refs_2_ = f32[1024,512]{1,0:T(8,128)S(1)} custom-call(s32[1]{0:T(128)} %bitcast.1.place_ref, bf16[8,128,512]{2,1,0:T(8,128)(2,1)S(1)} %shard_map.111.cols_ref, bf16[128,1024]{1,0:T(8,128)(2,1)S(1)} %shard_map.108.att_ref.refs_0_.after_ref, bf16[128,1024]{1,0:T(8,128)(2,1)S(1)} %collective-permute-done.13.refs_1_, ...), custom_call_target="tpu_custom_call" | custom-call | flops 671088640 | bytes 2097152 | tf_op jit(solution)/shard_map/pallas_call | solution.py:462
  76.9 0.0 collective-permute-done.15.refs_0_
  76.9 2.1 %collective-permute-start.21 = (bf16[64,1024]{1,0:T(8,128)(2,1)S(1)}, bf16[64,1024]{1,0:T(8,128)(2,1)S(1)}, u32[]{:S(2)}, u32[]{:S(2)}) collective-permute-start(bf16[64,1024]{1,0:T(8,128)(2,1)S(1)} %slice.21), channel_id=1, source_target_pairs={{0,8},{8,16},{16,24},{24,28},{28,20},{20,12},{12,4},{4,0},{1,9},{9... | collective-permute-start | bytes 393224 | tf_op jit(solution)/shard_map/ppermute | solution.py:487
  79.0 0.0 collective-permute-done.18.refs_1_
  79.0 0.1 collective-permute-start.22
  79.1 0.8 fusion.1
  79.9 0.7 shard_map.113.after_ref.total_ref
  80.6 1.7 %shard_map.116 = (f32[128,8,128]{2,1,0:T(8,128)}, f32[128,8,128]{2,1,0:T(8,128)}) custom-call(s32[1]{0:T(128)} %bitcast.1.place_ref, bf16[8,128,128]{2,1,0:T(8,128)(2,1)S(1)} %get-tuple-element.27.kh_ref, bf16[8,128,128]{2,1,0:T(8,128)(2,1)S(1)} %get-tuple-element.28.vh_ref, f32[8,128,128]{2,1,0:T(8,128)S(1)} %get-tuple-element.43.dkl_ref, ...), custom_call_target="tpu_custom_call" | custom-call | flops 67108864 | bytes 2883584 | tf_op jit(solution)/shard_map/pallas_call | solution.py:490
  82.3 0.0 collective-permute-done.21.low_ref
  82.3 1.7 %collective-permute-done.22.high_ref = bf16[64,1024]{1,0:T(8,128)(2,1)S(1)} collective-permute-done((bf16[64,1024]{1,0:T(8,128)(2,1)S(1)}, bf16[64,1024]{1,0:T(8,128)(2,1)S(1)}, u32[]{:S(2)}, u32[]{:S(2)}) %collective-permute-start.22) | collective-permute-done | bytes 131104 | tf_op jit(solution)/shard_map/ppermute | solution.py:488
  84.0 2.4 %shard_map.117 = f32[1024,512]{1,0:T(8,128)} custom-call(s32[1]{0:T(128)} %bitcast.1.place_ref, bf16[8,128,512]{2,1,0:T(8,128)(2,1)S(1)} %shard_map.111.cols_ref, bf16[64,1024]{1,0:T(8,128)(2,1)S(1)} %collective-permute-done.21.low_ref, bf16[64,1024]{1,0:T(8,128)(2,1)S(1)} %collective-permute-done.22.high_ref, ...), custom_call_target="tpu_custom_call" | custom-call | flops 134217728 | bytes 4194304 | tf_op jit(solution)/shard_map/pallas_call | solution.py:499
  (16 shorter events, 0.1 us)
Async XLA Ops:
  0.6 10.4 %collective-permute-start.1 = (bf16[128,1024]{1,0:T(8,128)(2,1)}, bf16[128,1024]{1,0:T(8,128)(2,1)}, u32[]{:S(2)}, u32[]{:S(2)}) collective-permute-start(bf16[128,1024]{1,0:T(8,128)(2,1)} %refs_0_.1), channel_id=1, source_target_pairs={{0,2},{1,3},{2,0},{3,1},{4,6},{5,7},{6,4},{7,5},{8,10},{9,11},{10,... | collective-permute-start | bytes 786440 | tf_op jit(solution)/shard_map/ppermute | solution.py:302
  3.6 14.9 %collective-permute-start.3 = (bf16[128,1024]{1,0:T(8,128)(2,1)}, bf16[128,1024]{1,0:T(8,128)(2,1)S(1)}, u32[]{:S(2)}, u32[]{:S(2)}) collective-permute-start(bf16[128,1024]{1,0:T(8,128)(2,1)} %refs_0_.1), channel_id=1, source_target_pairs={{0,0},{1,8},{2,16},{3,24},{4,4},{5,12},{6,20},{7,28},{8,1},{9,9},{... | collective-permute-start | bytes 786440 | tf_op jit(solution)/shard_map/ppermute | solution.py:320
  7.7 10.9 %collective-permute-start.4 = (bf16[8,128,128]{2,1,0:T(8,128)(2,1)S(1)}, bf16[8,128,128]{2,1,0:T(8,128)(2,1)S(1)}, u32[]{:S(2)}, u32[]{:S(2)}) collective-permute-start(bf16[8,128,128]{2,1,0:T(8,128)(2,1)S(1)} %get-tuple-element.32.running_ref), channel_id=1, source_target_pairs={{0,4},{4,0},{8,12},{12,8},{16,20},{20,16},{24,28},{28,24},{1,5},{5... | collective-permute-start | bytes 786440 | tf_op jit(solution)/shard_map/ppermute | solution.py:45
  9.3 13.9 %collective-permute-start = (bf16[128,1024]{1,0:T(8,128)(2,1)}, bf16[128,1024]{1,0:T(8,128)(2,1)}, u32[]{:S(2)}, u32[]{:S(2)}) collective-permute-start(bf16[128,1024]{1,0:T(8,128)(2,1)} %refs_0_.1), channel_id=1, source_target_pairs={{0,1},{1,0},{2,3},{3,2},{4,5},{5,4},{6,7},{7,6},{8,9},{9,8},{10,11... | collective-permute-start | bytes 786440 | tf_op jit(solution)/shard_map/ppermute | solution.py:302
  11.0 12.2 %collective-permute-start.2 = (bf16[128,1024]{1,0:T(8,128)(2,1)}, bf16[128,1024]{1,0:T(8,128)(2,1)}, u32[]{:S(2)}, u32[]{:S(2)}) collective-permute-start(bf16[128,1024]{1,0:T(8,128)(2,1)} %collective-permute-done.1.refs_2_), channel_id=1, source_target_pairs={{0,1},{1,0},{2,3},{3,2},{4,5},{5,4},{6,7},{7,6},{8,9},{9,8},{10,11... | collective-permute-start | bytes 786440 | tf_op jit(solution)/shard_map/ppermute | solution.py:302
  14.7 3.3 %copy-start = (bf16[1024,4096]{1,0:T(8,128)(2,1)}, bf16[1024,4096]{1,0:T(8,128)(2,1)S(1)}, u32[]{:S(2)}) copy-start(bf16[1024,4096]{1,0:T(8,128)(2,1)S(1)} %get-tuple-element.31.refs_4_.w_ref) | copy-start | bytes 25165828
  17.9 0.6 copy-start.4
  18.6 12.9 %collective-permute-start.5 = (bf16[128,512]{1,0:T(8,128)(2,1)S(1)}, bf16[128,512]{1,0:T(8,128)(2,1)S(1)}, u32[]{:S(2)}, u32[]{:S(2)}) collective-permute-start(bf16[128,512]{1,0:T(8,128)(2,1)S(1)} %get-tuple-element.33.refs_6_), channel_id=1, source_target_pairs={{0,4},{4,0},{8,12},{12,8},{16,20},{20,16},{24,28},{28,24},{1,5},{5... | collective-permute-start | bytes 393224 | tf_op jit(solution)/shard_map/ppermute | solution.py:367
  19.7 14.5 %collective-permute-start.8 = (bf16[8,128,128]{2,1,0:T(8,128)(2,1)S(1)}, bf16[8,128,128]{2,1,0:T(8,128)(2,1)S(1)}, u32[]{:S(2)}, u32[]{:S(2)}) collective-permute-start(bf16[8,128,128]{2,1,0:T(8,128)(2,1)S(1)} %shard_map.103.after_ref.running_ref), channel_id=1, source_target_pairs={{0,8},{8,0},{4,12},{12,4},{16,24},{24,16},{20,28},{28,20},{1,9},{9... | collective-permute-start | bytes 786440 | tf_op jit(solution)/shard_map/ppermute | solution.py:45
  23.1 3.4 %copy-start.1 = (bf16[1024,4096]{1,0:T(8,128)(2,1)S(1)}, bf16[1024,4096]{1,0:T(8,128)(2,1)}, u32[]{:S(2)}) copy-start(bf16[1024,4096]{1,0:T(8,128)(2,1)} %copy-done) | copy-start | bytes 25165828
  26.5 0.9 %copy-start.3 = (bf16[128,1024]{1,0:T(8,128)(2,1)S(1)}, bf16[128,1024]{1,0:T(8,128)(2,1)}, u32[]{:S(2)}) copy-start(bf16[128,1024]{1,0:T(8,128)(2,1)} %refs_0_.1) | copy-start | bytes 786436
  27.5 23.6 %copy-start.2 = (bf16[1024,4096]{1,0:T(8,128)(2,1)S(1)}, bf16[1024,4096]{1,0:T(8,128)(2,1)}, u32[]{:S(2)}) copy-start(bf16[1024,4096]{1,0:T(8,128)(2,1)} %copy-done) | copy-start | bytes 25165828
  31.6 9.1 %collective-permute-start.6 = (bf16[2,128,512]{2,1,0:T(8,128)(2,1)S(1)}, bf16[2,128,512]{2,1,0:T(8,128)(2,1)S(1)}, u32[]{:S(2)}, u32[]{:S(2)}) collective-permute-start(bf16[2,128,512]{2,1,0:T(8,128)(2,1)S(1)} %shard_map.106.after_ref.refs_0_), channel_id=1, source_target_pairs={{0,2},{1,3},{2,0},{3,1},{4,6},{5,7},{6,4},{7,5},{8,10},{9,11},{10,... | collective-permute-start | bytes 786440 | tf_op jit(solution)/shard_map/ppermute | solution.py:302
  34.4 14.2 %collective-permute-start.9 = (bf16[8,128,128]{2,1,0:T(8,128)(2,1)S(1)}, bf16[8,128,128]{2,1,0:T(8,128)(2,1)S(1)}, u32[]{:S(2)}, u32[]{:S(2)}) collective-permute-start(bf16[8,128,128]{2,1,0:T(8,128)(2,1)S(1)} %shard_map.107), channel_id=1, source_target_pairs={{0,16},{16,0},{4,20},{20,4},{8,24},{24,8},{12,28},{28,12},{1,17},{... | collective-permute-start | bytes 786440 | tf_op jit(solution)/shard_map/ppermute | solution.py:45
  40.7 7.9 %collective-permute-start.7 = (bf16[2,128,512]{2,1,0:T(8,128)(2,1)S(1)}, bf16[2,128,512]{2,1,0:T(8,128)(2,1)S(1)}, u32[]{:S(2)}, u32[]{:S(2)}) collective-permute-start(bf16[2,128,512]{2,1,0:T(8,128)(2,1)S(1)} %collective-permute-done.6.refs_2_), channel_id=1, source_target_pairs={{0,1},{1,0},{2,3},{3,2},{4,5},{5,4},{6,7},{7,6},{8,9},{9,8},{10,11... | collective-permute-start | bytes 786440 | tf_op jit(solution)/shard_map/ppermute | solution.py:302
  49.0 8.3 %collective-permute-start.13 = (bf16[128,1024]{1,0:T(8,128)(2,1)S(1)}, bf16[128,1024]{1,0:T(8,128)(2,1)S(1)}, u32[]{:S(2)}, u32[]{:S(2)}) collective-permute-start(bf16[128,1024]{1,0:T(8,128)(2,1)S(1)} %shard_map.108.att_ref.refs_0_.after_ref), channel_id=1, source_target_pairs={{0,8},{8,16},{16,24},{24,28},{28,20},{20,12},{12,4},{4,0},{1,9},{9... | collective-permute-start | bytes 786440 | tf_op jit(solution)/shard_map/ppermute | solution.py:477
  49.1 8.5 %collective-permute-start.16 = (bf16[128,1024]{1,0:T(8,128)(2,1)S(1)}, bf16[128,1024]{1,0:T(8,128)(2,1)S(1)}, u32[]{:S(2)}, u32[]{:S(2)}) collective-permute-start(bf16[128,1024]{1,0:T(8,128)(2,1)S(1)} %shard_map.108.att_ref.refs_0_.after_ref), channel_id=1, source_target_pairs={{8,0},{16,8},{24,16},{28,24},{20,28},{12,20},{4,12},{0,4},{9,1},{1... | collective-permute-start | bytes 786440 | tf_op jit(solution)/shard_map/ppermute | solution.py:478
  52.4 14.6 %collective-permute-start.10 = (bf16[2,128,1024]{2,1,0:T(8,128)(2,1)S(1)}, bf16[2,128,1024]{2,1,0:T(8,128)(2,1)S(1)}, u32[]{:S(2)}, u32[]{:S(2)}) collective-permute-start(bf16[2,128,1024]{2,1,0:T(8,128)(2,1)S(1)} %get-tuple-element.38), channel_id=1, source_target_pairs={{0,1},{1,0},{2,3},{3,2},{4,5},{5,4},{6,7},{7,6},{8,9},{9,8},{10,11... | collective-permute-start | bytes 1572872 | tf_op jit(solution)/shard_map/ppermute | solution.py:302
  57.3 7.4 %collective-permute-start.14 = (bf16[128,1024]{1,0:T(8,128)(2,1)S(1)}, bf16[128,1024]{1,0:T(8,128)(2,1)S(1)}, u32[]{:S(2)}, u32[]{:S(2)}) collective-permute-start(bf16[128,1024]{1,0:T(8,128)(2,1)S(1)} %collective-permute-done.13.refs_1_), channel_id=1, source_target_pairs={{0,8},{8,16},{16,24},{24,28},{28,20},{20,12},{12,4},{4,0},{1,9},{9... | collective-permute-start | bytes 786440 | tf_op jit(solution)/shard_map/ppermute | solution.py:477
  57.6 9.2 %collective-permute-start.17 = (bf16[128,1024]{1,0:T(8,128)(2,1)S(1)}, bf16[128,1024]{1,0:T(8,128)(2,1)S(1)}, u32[]{:S(2)}, u32[]{:S(2)}) collective-permute-start(bf16[128,1024]{1,0:T(8,128)(2,1)S(1)} %collective-permute-done.16.refs_2_), channel_id=1, source_target_pairs={{8,0},{16,8},{24,16},{28,24},{20,28},{12,20},{4,12},{0,4},{9,1},{1... | collective-permute-start | bytes 786440 | tf_op jit(solution)/shard_map/ppermute | solution.py:478
  59.3 8.3 %collective-permute-start.12 = (bf16[2,128,512]{2,1,0:T(8,128)(2,1)S(1)}, bf16[2,128,512]{2,1,0:T(8,128)(2,1)S(1)}, u32[]{:S(2)}, u32[]{:S(2)}) collective-permute-start(bf16[2,128,512]{2,1,0:T(8,128)(2,1)S(1)} %shard_map.106.after_ref.refs_0_), channel_id=1, source_target_pairs={{0,1},{1,0},{2,3},{3,2},{4,5},{5,4},{6,7},{7,6},{8,9},{9,8},{10,11... | collective-permute-start | bytes 786440 | tf_op jit(solution)/shard_map/ppermute | solution.py:302
  59.4 13.0 %collective-permute-start.19 = (bf16[8,128,128]{2,1,0:T(8,128)(2,1)S(1)}, bf16[8,128,128]{2,1,0:T(8,128)(2,1)S(1)}, u32[]{:S(2)}, u32[]{:S(2)}) collective-permute-start(bf16[8,128,128]{2,1,0:T(8,128)(2,1)S(1)} %shard_map.114), channel_id=1, source_target_pairs={{0,8},{8,0},{4,12},{12,4},{16,24},{24,16},{20,28},{28,20},{1,9},{9... | collective-permute-start | bytes 786440 | tf_op jit(solution)/shard_map/ppermute | solution.py:45
  64.6 12.2 %collective-permute-start.15 = (bf16[128,1024]{1,0:T(8,128)(2,1)S(1)}, bf16[128,1024]{1,0:T(8,128)(2,1)S(1)}, u32[]{:S(2)}, u32[]{:S(2)}) collective-permute-start(bf16[128,1024]{1,0:T(8,128)(2,1)S(1)} %collective-permute-done.14.refs_3_), channel_id=1, source_target_pairs={{0,8},{8,16},{16,24},{24,28},{28,20},{20,12},{12,4},{4,0},{1,9},{9... | collective-permute-start | bytes 786440 | tf_op jit(solution)/shard_map/ppermute | solution.py:477
  66.8 12.2 %collective-permute-start.18 = (bf16[128,1024]{1,0:T(8,128)(2,1)S(1)}, bf16[128,1024]{1,0:T(8,128)(2,1)S(1)}, u32[]{:S(2)}, u32[]{:S(2)}) collective-permute-start(bf16[128,1024]{1,0:T(8,128)(2,1)S(1)} %collective-permute-done.17.refs_4_), channel_id=1, source_target_pairs={{8,0},{16,8},{24,16},{28,24},{20,28},{12,20},{4,12},{0,4},{9,1},{1... | collective-permute-start | bytes 786440 | tf_op jit(solution)/shard_map/ppermute | solution.py:478
  67.2 5.6 %copy-start.5 = (f32[5,8,128]{2,1,0:T(8,128)S(1)}, f32[5,8,128]{2,1,0:T(8,128)}, u32[]{:S(2)}) copy-start(f32[5,8,128]{2,1,0:T(8,128)} %copy-done.4) | copy-start | bytes 61444
  67.2 11.9 %collective-permute-start.11 = (bf16[1,128,1024]{2,1,0:T(8,128)(2,1)S(1)}, bf16[1,128,1024]{2,1,0:T(8,128)(2,1)S(1)}, u32[]{:S(2)}, u32[]{:S(2)}) collective-permute-start(bf16[1,128,1024]{2,1,0:T(8,128)(2,1)S(1)} %slice.29.after_ref), channel_id=1, source_target_pairs={{0,2},{1,3},{2,0},{3,1},{4,6},{5,7},{6,4},{7,5},{8,10},{9,11},{10,... | collective-permute-start | bytes 786440 | tf_op jit(solution)/shard_map/ppermute | solution.py:302
  72.5 8.1 %collective-permute-start.20 = (bf16[8,128,128]{2,1,0:T(8,128)(2,1)S(1)}, bf16[8,128,128]{2,1,0:T(8,128)(2,1)S(1)}, u32[]{:S(2)}, u32[]{:S(2)}) collective-permute-start(bf16[8,128,128]{2,1,0:T(8,128)(2,1)S(1)} %shard_map.115), channel_id=1, source_target_pairs={{0,4},{4,0},{8,12},{12,8},{16,20},{20,16},{24,28},{28,24},{1,5},{5... | collective-permute-start | bytes 786440 | tf_op jit(solution)/shard_map/ppermute | solution.py:45
  76.9 5.4 %collective-permute-start.21 = (bf16[64,1024]{1,0:T(8,128)(2,1)S(1)}, bf16[64,1024]{1,0:T(8,128)(2,1)S(1)}, u32[]{:S(2)}, u32[]{:S(2)}) collective-permute-start(bf16[64,1024]{1,0:T(8,128)(2,1)S(1)} %slice.21), channel_id=1, source_target_pairs={{0,8},{8,16},{16,24},{24,28},{28,20},{20,12},{12,4},{4,0},{1,9},{9... | collective-permute-start | bytes 393224 | tf_op jit(solution)/shard_map/ppermute | solution.py:487
  79.0 5.0 %collective-permute-start.22 = (bf16[64,1024]{1,0:T(8,128)(2,1)S(1)}, bf16[64,1024]{1,0:T(8,128)(2,1)S(1)}, u32[]{:S(2)}, u32[]{:S(2)}) collective-permute-start(bf16[64,1024]{1,0:T(8,128)(2,1)S(1)} %slice.22), channel_id=1, source_target_pairs={{8,0},{16,8},{24,16},{28,24},{20,28},{12,20},{4,12},{0,4},{9,1},{1... | collective-permute-start | bytes 393224 | tf_op jit(solution)/shard_map/ppermute | solution.py:488
where the time goes:
time: 86.7 us; the launch traced here: 86.4 us
  waiting for transfers between devices  30.3 us (35%)
  starting transfers between devices  24.8 us (29%)
  Pallas kernels  21.3 us (25%)
  local copies, waits for them, and re-layouts  8.26 us (10%)
  other arithmetic  0.91 us (1%)
    ppermute x5, waiting for transfers between devices, across(): return lax.ppermute(block, axis, route)  12.6 us
    ppermute x3, waiting for transfers between devices, body(): ahead = lax.ppermute(ahead, 'seq', forward)  9.74 us
    unnamed x12, local copies, waits for them, and re-layouts  8.21 us
    ppermute x8, starting transfers between devices, to_group(): return lax.ppermute(block, 'head', [(at, at ^ i) for at in range(heads)])  7.87 us
    ppermute x8, waiting for transfers between devices, to_group(): return lax.ppermute(block, 'head', [(at, at ^ i) for at in range(heads)])  6.23 us
    ppermute x5, starting transfers between devices, across(): return lax.ppermute(block, axis, route)  5.66 us
    pallas_call x1, Pallas kernels, body(): pl.pallas_call(functools.partial(cotangent_kernel, heads, seq_bits), out_...  4.06 us
    ppermute x3, starting transfers between devices, body(): behind = lax.ppermute(behind, 'seq', backward)  3.96 us
  transfers between devices with their start and end apart: 23, of which 6 were waited for; matrix products, arithmetic and copies ran while one was open for 1% of the time, Pallas kernels for 21%

commit v1 on v0

--- a/solution.py
+++ b/solution.py
@@ -49,7 +49,8 @@
     return pltpu.with_memory_space_constraint(array, pltpu.HBM)
 
 
-def state_kernel(k_hbm, v_hbm, s_ref, kh_ref, vh_ref, k_ref, v_ref, sems):
+def state_kernel(place_ref, k_hbm, v_hbm, s_ref, kh_ref, vh_ref, k_ref, v_ref, sems):
+    del place_ref
     copies = [
         pltpu.make_async_copy(k_hbm, k_ref, sems.at[0]),
         pltpu.make_async_copy(v_hbm, v_ref, sems.at[1]),
@@ -83,9 +84,9 @@
     return lam_ref[1 + local_bits + b, h : h + 1, :] * upper
 
 
-def local_kernel(place_ref, q_hbm, kh_ref, vh_ref, lam_hbm, w_hbm, *refs):
-    pt_ref, att_ref, qh_ref, qw_ref, lam_ref, w_ref, q_ref, lam_rows, sems = refs
-    pieces = sems.shape[0] - 2
+def local_kernel(place_ref, q_hbm, kh_ref, vh_ref, lam_hbm, w_hbm, grad_hbm, *refs):
+    pt_ref, att_ref, qh_ref, qw_ref, lam_ref, w_ref, grad_ref, q_ref, lam_rows, sems = refs
+    pieces = sems.shape[0] - 3
     share = w_hbm.shape[0] // pieces
     copies = [
         pltpu.make_async_copy(q_hbm, q_ref, sems.at[0]),
@@ -93,7 +94,8 @@
     ]
     for i in range(pieces):
         piece = pl.ds(i * share, share)
-        copies.append(pltpu.make_async_copy(w_hbm.at[piece], w_ref.at[piece], sems.at[2 + i]))
+        copies.append(pltpu.make_async_copy(w_hbm.at[piece], w_ref.at[piece], sems.at[3 + i]))
+    copies.append(pltpu.make_async_copy(grad_hbm, grad_ref, sems.at[2]))
     for copy in copies:
         copy.start()
     for copy in copies[:2]:
@@ -120,9 +122,8 @@
         copy.wait()
 
 
-def attended_kernel(bits, att_ref, qw_ref, after_ref, *refs):
-    del after_ref
-    states, out_ref = refs[:bits], refs[bits]
+def attended_kernel(bits, att_ref, qw_ref, *refs):
+    states, out_ref = refs[:bits], refs[-1]
     heads_dev, _, head_dim = att_ref.shape
     for h in range(heads_dev):
         total = att_ref[h]
@@ -131,7 +132,7 @@
         out_ref[:, h * head_dim : (h + 1) * head_dim] = total.astype(BF)
 
 
-def cotangent_kernel(blocks, bits, head_ref, *refs):
+def cotangent_kernel(blocks, bits, place_ref, *refs):
     parts, (w_ref, qw_ref, _, gt_ref), sums = (
         refs[:blocks],
         refs[blocks : blocks + 4],
@@ -141,7 +142,7 @@
     _, heads_dev, _, head_dim = qw_ref.shape
     total = None
     for i in range(blocks):
-        column = pl.multiple_of((head_ref[0] ^ i) * deep, deep)
+        column = pl.multiple_of((place_ref[1] ^ i) * deep, deep)
         product = mm(w_ref[:, pl.ds(column, deep)], parts[i][...], NT)
         total = product if total is None else total + product
     for h in range(heads_dev):
@@ -192,13 +193,13 @@
         refs[-1][r] = ref[...]
 
 
-def columns_kernel(blocks, place_ref, head_ref, *refs):
+def columns_kernel(blocks, place_ref, *refs):
     parts, out_ref = refs[:blocks], refs[blocks]
     per = parts[0].shape[0]
     low = place_ref[0] % per
     for i in range(blocks):
         for r in range(per):
-            out_ref[(head_ref[0] ^ i) * per + (low ^ r)] = parts[i][r]
+            out_ref[(place_ref[1] ^ i) * per + (low ^ r)] = parts[i][r]
 
 
 def local_grad_kernel(
@@ -217,7 +218,15 @@
         for b in range(bits):
             gw = (g32 * upper_weight(place_ref, lam_ref, b, h, rows)).astype(BF)
             dq = dq + mm(gw, states[b][h], TT)
-        dq_ref[:, h, :] = dq
+        dq_ref[h] = dq
+
+
+def query_grad_kernel(top, place_ref, gt_ref, lam_ref, dql_ref, state_ref, dq_ref):
+    heads_dev, rows, head_dim = dql_ref.shape
+    for h in range(heads_dev):
+        g32 = gt_ref[h * head_dim : (h + 1) * head_dim, :].astype(F32)
+        gw = (g32 * upper_weight(place_ref, lam_ref, top, h, rows)).astype(BF)
+        dq_ref[:, h, :] = dql_ref[h] + mm(gw, state_ref[h], TT)
 
 
 def later_grad_kernel(top, place_ref, kh_ref, vh_ref, dkl_ref, dvl_ref, after_ref, *refs):
@@ -229,11 +238,12 @@
         dv_ref[:, h, :] = dvl_ref[h] + mm(kh_ref[h], late, NT)
 
 
-def share_kernel(blocks, head_ref, att_ref, w_ref, send_ref, kept_ref):
+def share_kernel(blocks, place_ref, att_ref, w_ref, after_ref, send_ref, kept_ref):
+    del after_ref
     width = send_ref.shape[2]
     for i in range(blocks):
         out = send_ref if i % 2 else kept_ref
-        column = pl.multiple_of((head_ref[0] ^ i) * width, width)
+        column = pl.multiple_of((place_ref[1] ^ i) * width, width)
         out[i // 2] = mm(att_ref[...], w_ref[:, pl.ds(column, width)], NN).astype(out.dtype)
 
 
@@ -256,11 +266,12 @@
     offset, devices, place_ref, cols_ref, low_ref, high_ref, total_ref, after_ref, out_ref, held
 ):
     del after_ref
-    half = low_ref.shape[0]
-    held[:half] = low_ref[...]
-    held[half:] = high_ref[...]
+    half, block = low_ref.shape[0], out_ref.shape[0]
+    at = pl.ds(pl.multiple_of(pl.program_id(0) * block, block), block)
+    held[:half] = low_ref[:, at]
+    held[half:] = high_ref[:, at]
     owner = ring_owner(place_ref[0], offset, devices)
-    out_ref[...] = total_ref[...] + mm(held[...], cols_ref[owner], TN)
+    out_ref[...] = total_ref[at, :] + mm(held[...], cols_ref[owner], TN)
 
 
 def body(queries, keys, values, level_weights, out_proj, out_grad):
@@ -281,13 +292,12 @@
     flops_head = 2 * heads_dev * rows * rows * head_dim
     moved_head = 2 * rows * width
     top = seq_bits - 1
-    place = seq_place.reshape(1).astype(jnp.int32)
-    group = head_place.reshape(1).astype(jnp.int32)
+    place = jnp.stack([seq_place, head_place]).astype(jnp.int32)
 
     own_state, kh, vh = pl.pallas_call(
         state_kernel,
         out_shape=(head_state, per_head, per_head),
-        in_specs=[ANY] * 2,
+        in_specs=[SMEM] + [ANY] * 2,
         out_specs=(VMEM,) * 3,
         scratch_shapes=[
             pltpu.VMEM(keys.shape, F32),
@@ -296,7 +306,7 @@
         ],
         compiler_params=PARAMS,
         cost_estimate=cost(flops_head, 7 * moved_head),
-    )(hbm(keys), hbm(values))
+    )(place, hbm(keys), hbm(values))
 
     def to_group(block, i):
         return lax.ppermute(block, "head", [(at, at ^ i) for at in range(heads)])
@@ -318,7 +328,7 @@
         for group_at in range(heads)
     ]
     turned = lax.ppermute(out_grad, ("seq", "head"), route)
-    probs_t, att_local, qh, qw, lam, w = pl.pallas_call(
+    probs_t, att_local, qh, qw, lam, w, own_grad = pl.pallas_call(
         local_kernel,
         out_shape=(
             pltpu.VMEM((heads_dev, rows, rows), BF),
@@ -327,18 +337,32 @@
             pltpu.VMEM((seq_bits, heads_dev, rows, head_dim), BF),
             pltpu.VMEM(level_weights.shape, F32),
             pltpu.VMEM(out_proj.shape, BF),
+            pltpu.VMEM(out_grad.shape, BF),
         ),
-        in_specs=[SMEM, ANY, VMEM, VMEM, ANY, ANY],
-        out_specs=(VMEM,) * 6,
+        in_specs=[SMEM, ANY, VMEM, VMEM, ANY, ANY, ANY],
+        out_specs=(VMEM,) * 7,
         scratch_shapes=[
             pltpu.VMEM(queries.shape, F32),
             pltpu.VMEM((rows, rows), F32),
-            pltpu.SemaphoreType.DMA((10,)),
+            pltpu.SemaphoreType.DMA((11,)),
         ],
         compiler_params=PARAMS,
         cost_estimate=cost(2 * flops_head, 12 * moved_head),
-    )(place, hbm(queries), kh, vh, hbm(level_weights), hbm(out_proj))
-
+    )(place, hbm(queries), kh, vh, hbm(level_weights), hbm(out_proj), hbm(out_grad))
+
+    chunks = pl.pallas_call(
+        chunk_kernel,
+        out_shape=(like((rows, columns_dev), BF),) * per,
+        in_specs=[SMEM, VMEM, ANY],
+        out_specs=(VMEM,) * per,
+        compiler_params=PARAMS,
+        cost_estimate=cost(0, 2 * moved_head),
+    )(place, turned, qw)
+    own_chunks = chunks
+    chunks = [chunks[0]] + [
+        lax.ppermute(chunks[r], "seq", [(at, at ^ r) for at in range(devices)])
+        for r in range(1, per)
+    ]
     partner_states = []
     running, arrived = own_state, None
     for digit in range(top):
@@ -346,27 +370,14 @@
             running = pl.pallas_call(
                 running_kernel,
                 out_shape=head_state,
-                in_specs=[VMEM] * 2 + [ANY] * 2,
+                in_specs=[VMEM] * 2 + [ANY],
                 out_specs=VMEM,
                 compiler_params=PARAMS,
                 cost_estimate=cost(0, 3 * moved_head),
-            )(running, arrived, turned, qw)
+            )(running, arrived, own_chunks[-1])
         arrived = across(running, "seq", digit)
         partner_states.append(arrived)
 
-    chunks = pl.pallas_call(
-        chunk_kernel,
-        out_shape=(like((rows, columns_dev), BF),) * per,
-        in_specs=[SMEM, VMEM, ANY],
-        out_specs=(VMEM,) * per,
-        compiler_params=PARAMS,
-        cost_estimate=cost(0, 2 * moved_head),
-    )(place, turned, running)
-    own_chunks = chunks
-    chunks = [chunks[0]] + [
-        lax.ppermute(chunks[r], "seq", [(at, at ^ r) for at in range(devices)])
-        for r in range(1, per)
-    ]
     gt, *grad_sums = pl.pallas_call(
         functools.partial(cotangent_kernel, heads, seq_bits),
         out_shape=(pltpu.VMEM((width, rows), BF),) + (pinned_state,) * seq_bits,
@@ -374,7 +385,7 @@
         out_specs=(VMEM,) * (1 + seq_bits),
         compiler_params=PARAMS,
         cost_estimate=cost(2 * rows * width * out_proj.shape[1], 2 * width * out_proj.shape[1]),
-    )(group, *grad_blocks, w, qw, own_chunks[-1])
+    )(place, own_grad, *grad_blocks[1:], w, qw, own_chunks[-1])
 
     stacked = pl.pallas_call(
         stack_kernel,
@@ -404,21 +415,31 @@
     grad_columns = pl.pallas_call(
         functools.partial(columns_kernel, heads),
         out_shape=pltpu.VMEM((devices, rows, columns_dev), BF),
-        in_specs=[SMEM] * 2 + [VMEM] * heads,
+        in_specs=[SMEM] + [VMEM] * heads,
         out_specs=VMEM,
         compiler_params=PARAMS,
         cost_estimate=cost(0, 8 * moved_head),
-    )(place, group, *column_blocks)
+    )(place, *column_blocks)
+
+    query_local, key_local, value_local = pl.pallas_call(
+        functools.partial(local_grad_kernel, top),
+        out_shape=(per_head_f32,) * 3,
+        in_specs=[SMEM] + [VMEM] * 6 + [ANY] + [VMEM] * top,
+        out_specs=(VMEM,) * 3,
+        compiler_params=PARAMS,
+        cost_estimate=cost((4 + top) * flops_head, 14 * moved_head),
+    )(place, gt, qh, kh, vh, probs_t, lam, meeting, *partner_states[:top])
 
     attended = pl.pallas_call(
         functools.partial(attended_kernel, seq_bits),
         out_shape=like((rows, width), BF),
-        in_specs=[VMEM] * 2 + [ANY] + [VMEM] * seq_bits,
+        in_specs=[VMEM] * (2 + seq_bits) + [ANY] * heads,
         out_specs=VMEM,
         compiler_params=PARAMS,
         cost_estimate=cost(seq_bits * flops_head, 8 * moved_head),
-    )(att_local, qw, column_blocks[-1], *partner_states)
-
+    )(att_local, qw, *partner_states, key_local, *column_blocks[1:])
+
+    first_pending = attended
     for digit in reversed(range(top)):
         outgoing = pl.pallas_call(
             functools.partial(pending_kernel, top),
@@ -428,30 +449,32 @@
             compiler_params=PARAMS,
             cost_estimate=cost(0, 4 * moved_head),
         )(place, grad_sums[digit], attended, *landed)
+        if len(landed) == 1:
+            first_pending = outgoing
         landed.append(across(outgoing, "seq", digit))
 
     send, kept = pl.pallas_call(
         functools.partial(share_kernel, heads),
         out_shape=(like((heads // 2, rows, width), BF), like((heads // 2, rows, width), F32)),
-        in_specs=[SMEM, VMEM, VMEM],
+        in_specs=[SMEM, VMEM, VMEM, ANY],
         out_specs=(VMEM,) * 2,
         compiler_params=PARAMS,
         cost_estimate=cost(2 * rows * width * out_proj.shape[1], 2 * width * out_proj.shape[1]),
-    )(group, attended, w)
+    )(place, attended, w, first_pending)
     for digit in range(head_bits):
         kept = kept + to_group(send, 1 << digit).astype(F32)
         if digit < head_bits - 1:
             send, kept = kept[1::2].astype(BF), kept[0::2]
     mixed = kept[0].astype(BF)
 
-    query_grad, key_local, value_local = pl.pallas_call(
-        functools.partial(local_grad_kernel, seq_bits),
-        out_shape=(like((rows, heads_dev, head_dim), F32), per_head_f32, per_head_f32),
-        in_specs=[SMEM] + [VMEM] * 6 + [ANY] + [VMEM] * seq_bits,
-        out_specs=(VMEM,) * 3,
-        compiler_params=PARAMS,
-        cost_estimate=cost((4 + seq_bits) * flops_head, 14 * moved_head),
-    )(place, gt, qh, kh, vh, probs_t, lam, send, *partner_states)
+    query_grad = pl.pallas_call(
+        functools.partial(query_grad_kernel, top),
+        out_shape=like((rows, heads_dev, head_dim), F32),
+        in_specs=[SMEM] + [VMEM] * 4,
+        out_specs=VMEM,
+        compiler_params=PARAMS,
+        cost_estimate=cost(flops_head, 6 * moved_head),
+    )(place, gt, lam, query_local, partner_states[top])
 
     ring = list(range(0, devices, 2)) + list(range(devices - 1, 0, -2))
     forward = [(ring[i], ring[(i + 1) % devices]) for i in range(devices)]
@@ -503,9 +526,9 @@
         in_specs=[
             SMEM,
             VMEM,
-            pl.BlockSpec((half, quarter_rows), lambda i: (0, i)),
-            pl.BlockSpec((half, quarter_rows), lambda i: (0, i)),
-            pl.BlockSpec((quarter_rows, columns_dev), lambda i: (i, 0)),
+            VMEM,
+            VMEM,
+            VMEM,
             ANY,
         ],
         out_specs=pl.BlockSpec((quarter_rows, columns_dev), lambda i: (i, 0)),

time: 86.7 us -> 82 us (0.946)
  local copies, waits for them, and re-layouts: 8.26 us -> 0.05 us
  Pallas kernels: 21.3 us -> 28.2 us
  waiting for transfers between devices: 30.3 us -> 23.6 us
  starting transfers between devices: 24.8 us -> 28.1 us
    unnamed x12 -> x0, local copies, waits for them, and re-layouts: 8.21 us -> none
    ppermute x8, waiting for transfers between devices: 6.23 us -> 1.78 us  [to_group(): return lax.ppermute(block, 'head', [(at, at ^ i) for at in range(heads)])]
    ppermute x5, starting transfers between devices: 5.66 us -> 8.01 us  [across(): return lax.ppermute(block, axis, route)]
    ppermute x8, starting transfers between devices: 7.87 us -> 9.63 us  [to_group(): return lax.ppermute(block, 'head', [(at, at ^ i) for at in range(heads)])]
    ppermute x1, waiting for transfers between devices: 1.69 us -> 0.45 us  [body(): lax.ppermute(behind[half:], 'seq', backward)]
    pallas_call x1 -> x2, Pallas kernels: 2.55 us -> 3.69 us  [the longest x1 1.86 us: body(): pl.pallas_call(functools.partial(query_grad_kernel, top), out_shape=like(...]
    pallas_call x2, Pallas kernels: 2.27 us -> 3.35 us  [accumulate(): pl.pallas_call(functools.partial(proj_kernel, offsets, devices, total is...]
    pallas_call x2, Pallas kernels: 0.19 us -> 1.27 us  [body(): pl.pallas_call(functools.partial(pending_kernel, top), out_shape=head_sta...]
  transfers between devices with their start and end apart: 23 -> 23, of which waited for: 6 -> 7; matrix products, arithmetic and copies ran while one was open for 1% -> 1% of each run, Pallas kernels for 21% -> 30%
where the time goes in v1:
time: 82 us; the launch traced here: 81.8 us
  Pallas kernels  28.2 us (34%)
  starting transfers between devices  28.1 us (34%)
  waiting for transfers between devices  23.6 us (29%)
  other arithmetic  1 us (1%)
  between operations  0.84 us (1%)
    ppermute x5, waiting for transfers between devices, across(): return lax.ppermute(block, axis, route)  12.5 us
    ppermute x8, starting transfers between devices, to_group(): return lax.ppermute(block, 'head', [(at, at ^ i) for at in range(heads)])  9.63 us
    ppermute x3, waiting for transfers between devices, body(): ahead = lax.ppermute(ahead, 'seq', forward)  8.91 us
    ppermute x5, starting transfers between devices, across(): return lax.ppermute(block, axis, route)  8.01 us
    pallas_call x1, Pallas kernels, body(): pl.pallas_call(local_kernel, out_shape=(pltpu.VMEM((heads_dev, rows, rows...  4.22 us
    ppermute x3, starting transfers between devices, body(): behind = lax.ppermute(behind, 'seq', backward)  3.79 us
    pallas_call x1, Pallas kernels, body(): pl.pallas_call(functools.partial(cotangent_kernel, heads, seq_bits), out_...  3.36 us
    pallas_call x2, Pallas kernels, accumulate(): pl.pallas_call(functools.partial(proj_kernel, offsets, devices, total is...  3.35 us
  transfers between devices with their start and end apart: 23, of which 7 were waited for; matrix products, arithmetic and copies ran while one was open for 1% of the time, Pallas kernels for 30%

profile of v1, /device:TPU:0, one launch (start us, length us, event | category | flops | bytes accessed | tf_op | source)
XLA Modules:
  0.0 81.8 jit_solution(1399289267179979990)
XLA Ops:
  0.6 3.0 %collective-permute-start.4 = (bf16[128,1024]{1,0:T(8,128)(2,1)}, bf16[128,1024]{1,0:T(8,128)(2,1)S(1)}, u32[]{:S(2)}, u32[]{:S(2)}) collective-permute-start(bf16[128,1024]{1,0:T(8,128)(2,1)} %grad_hbm.1), channel_id=1, source_target_pairs={{0,2},{1,3},{2,0},{3,1},{4,6},{5,7},{6,4},{7,5},{8,10},{9,11},{10,... | collective-permute-start | bytes 786440 | tf_op jit(solution)/shard_map/ppermute | solution.py:312
  3.6 1.6 %collective-permute-start.1 = (bf16[128,1024]{1,0:T(8,128)(2,1)}, bf16[128,1024]{1,0:T(8,128)(2,1)S(1)}, u32[]{:S(2)}, u32[]{:S(2)}) collective-permute-start(bf16[128,1024]{1,0:T(8,128)(2,1)} %grad_hbm.1), channel_id=1, source_target_pairs={{0,0},{1,8},{2,16},{3,24},{4,4},{5,12},{6,20},{7,28},{8,1},{9,9},{... | collective-permute-start | bytes 786440 | tf_op jit(solution)/shard_map/ppermute | solution.py:330
  5.2 0.1 pad_add_fusion.place_ref
  5.3 3.0 %shard_map.101 = (bf16[8,128,128]{2,1,0:T(8,128)(2,1)S(1)}, bf16[8,128,128]{2,1,0:T(8,128)(2,1)S(1)}, bf16[8,128,128]{2,1,0:T(8,128)(2,1)S(1)}) custom-call(s32[2]{0:T(128)S(1)} %pad_add_fusion.place_ref, f32[128,8,128]{2,1,0:T(8,128)} %k_hbm.1, f32[128,8,128]{2,1,0:T(8,128)} %v_hbm.1), custom_call_target="tpu_custom_call" | custom-call | flops 33554432 | bytes 1835008 | tf_op jit(solution)/shard_map/pallas_call | solution.py:297
  8.3 1.6 %collective-permute-start = (bf16[8,128,128]{2,1,0:T(8,128)(2,1)S(1)}, bf16[8,128,128]{2,1,0:T(8,128)(2,1)S(1)}, u32[]{:S(2)}, u32[]{:S(2)}) collective-permute-start(bf16[8,128,128]{2,1,0:T(8,128)(2,1)S(1)} %get-tuple-element.32.running_ref), channel_id=1, source_target_pairs={{0,4},{4,0},{8,12},{12,8},{16,20},{20,16},{24,28},{28,24},{1,5},{5... | collective-permute-start | bytes 786440 | tf_op jit(solution)/shard_map/ppermute | solution.py:45
  9.9 1.7 %collective-permute-start.3 = (bf16[128,1024]{1,0:T(8,128)(2,1)}, bf16[128,1024]{1,0:T(8,128)(2,1)S(1)}, u32[]{:S(2)}, u32[]{:S(2)}) collective-permute-start(bf16[128,1024]{1,0:T(8,128)(2,1)} %grad_hbm.1), channel_id=1, source_target_pairs={{0,1},{1,0},{2,3},{3,2},{4,5},{5,4},{6,7},{7,6},{8,9},{9,8},{10,11... | collective-permute-start | bytes 786440 | tf_op jit(solution)/shard_map/ppermute | solution.py:312
  11.6 0.0 collective-permute-done.4.refs_2_
  11.6 0.0 collective-permute-start.5
  11.6 4.2 %shard_map.102 = (bf16[8,128,128]{2,1,0:T(8,128)(2,1)S(1)}, f32[8,128,128]{2,1,0:T(8,128)S(1)}, bf16[8,128,128]{2,1,0:T(8,128)(2,1)S(1)}, bf16[3,8,128,128]{3,2,...) custom-call(s32[2]{0:T(128)S(1)} %pad_add_fusion.place_ref, ...), custom_call_target="tpu_custom_call" | custom-call | flops 67108864 | bytes 3145728 | tf_op jit(solution)/shard_map/pallas_call | solution.py:331
  15.8 0.0 collective-permute-done.1.block_ref
  15.9 0.6 shard_map.103
  16.4 0.6 collective-permute-start.6
  17.0 0.0 collective-permute-done.arrived_ref.refs_0_
  17.0 0.1 shard_map.104.running_ref
  17.1 3.4 %collective-permute-start.2 = (bf16[8,128,128]{2,1,0:T(8,128)(2,1)S(1)}, bf16[8,128,128]{2,1,0:T(8,128)(2,1)S(1)}, u32[]{:S(2)}, u32[]{:S(2)}) collective-permute-start(bf16[8,128,128]{2,1,0:T(8,128)(2,1)S(1)} %shard_map.104.running_ref), channel_id=1, source_target_pairs={{0,8},{8,0},{4,12},{12,4},{16,24},{24,16},{20,28},{28,20},{1,9},{9... | collective-permute-start | bytes 786440 | tf_op jit(solution)/shard_map/ppermute | solution.py:45
  20.4 0.0 collective-permute-done.3.refs_1_
  20.4 0.0 collective-permute-done.5.refs_3_
  20.4 3.4 %shard_map.105 = (bf16[1024,128]{1,0:T(8,128)(2,1)S(1)}, bf16[8,128,128]{2,1,0:T(8,128)(2,1)S(1)}, bf16[8,128,128]{2,1,0:T(8,128)(2,1)S(1)}, bf16[8,128,128]{2,1,0:T(8,128)(2,1)S(1)}) custom-call(s32[2]{0:T(128)S(1)} %pad_add_fusion.place_ref, bf16[128,1024]{1,0:T(8,128)(2,1)S(1)} %get-tuple-element.34.refs_0_, ...), custom_call_target="tpu_custom_call" | custom-call | flops 1073741824 | bytes 8388608 | tf_op jit(solution)/shard_map/pallas_call | solution.py:381
  23.8 0.0 collective-permute-done.6.refs_1_
  23.9 4.8 %collective-permute-start.9 = (bf16[2,128,512]{2,1,0:T(8,128)(2,1)S(1)}, bf16[2,128,512]{2,1,0:T(8,128)(2,1)S(1)}, u32[]{:S(2)}, u32[]{:S(2)}) collective-permute-start(bf16[2,128,512]{2,1,0:T(8,128)(2,1)S(1)} %shard_map.106.after_ref.refs_0_), channel_id=1, source_target_pairs={{0,2},{1,3},{2,0},{3,1},{4,6},{5,7},{6,4},{7,5},{8,10},{9,11},{10,... | collective-permute-start | bytes 786440 | tf_op jit(solution)/shard_map/ppermute | solution.py:312
  28.6 0.0 collective-permute-start.8
  28.6 0.0 collective-permute-done.2.arrived_ref.refs_1_
  28.6 0.7 shard_map.107.after_ref
  29.3 2.7 %collective-permute-start.7 = (bf16[8,128,128]{2,1,0:T(8,128)(2,1)S(1)}, bf16[8,128,128]{2,1,0:T(8,128)(2,1)S(1)}, u32[]{:S(2)}, u32[]{:S(2)}) collective-permute-start(bf16[8,128,128]{2,1,0:T(8,128)(2,1)S(1)} %shard_map.107.after_ref), channel_id=1, source_target_pairs={{0,16},{16,0},{4,20},{20,4},{8,24},{24,8},{12,28},{28,12},{1,17},{... | collective-permute-start | bytes 786440 | tf_op jit(solution)/shard_map/ppermute | solution.py:45
  32.0 1.8 %collective-permute-done.9.refs_5_.refs_2_ = bf16[2,128,512]{2,1,0:T(8,128)(2,1)S(1)} collective-permute-done((bf16[2,128,512]{2,1,0:T(8,128)(2,1)S(1)}, bf16[2,128,512]{2,1,0:T(8,128)(2,1)S(1)}, u32[]{:S(2)}, u32[]{:S(2)}) %collective-permute-start.9) | collective-permute-done | bytes 262176 | tf_op jit(solution)/shard_map/ppermute | solution.py:312
  33.7 0.0 collective-permute-start.10
  33.7 1.8 %shard_map.108 = (f32[8,128,128]{2,1,0:T(8,128)S(1)}, f32[8,128,128]{2,1,0:T(8,128)S(1)}, f32[8,128,128]{2,1,0:T(8,128)S(1)}) custom-call(s32[2]{0:T(128)S(1)} %pad_add_fusion.place_ref, bf16[1024,128]{1,0:T(8,128)(2,1)S(1)} %get-tuple-element.36.after_ref.gt_ref, bf16[8,128,128]{2,1,0:T(8,128)(2,1)S(1)} %get-tuple-element.39.qh_ref, ...), custom_call_target="tpu_custom_call" | custom-call | flops 201326592 | bytes 3670016 | tf_op jit(solution)/shard_map/pallas_call | solution.py:424
  35.6 9.5 %collective-permute-done.7.refs_2_.refs_0_.state_ref = bf16[8,128,128]{2,1,0:T(8,128)(2,1)S(1)} collective-permute-done((bf16[8,128,128]{2,1,0:T(8,128)(2,1)S(1)}, bf16[8,128,128]{2,1,0:T(8,128)(2,1)S(1)}, u32[]{:S(2)}, u32[]{:S(2)}) %collective-permute-start.7) | collective-permute-done | bytes 262176 | tf_op jit(solution)/shard_map/ppermute | solution.py:45
  45.0 0.0 collective-permute-done.8.refs_4_.refs_1_
  45.0 0.4 shard_map.109.after_ref.att_ref.refs_0_
  45.4 0.1 collective-permute-start.13
  45.5 2.0 %collective-permute-start.16 = (bf16[128,1024]{1,0:T(8,128)(2,1)S(1)}, bf16[128,1024]{1,0:T(8,128)(2,1)S(1)}, u32[]{:S(2)}, u32[]{:S(2)}) collective-permute-start(bf16[128,1024]{1,0:T(8,128)(2,1)S(1)} %shard_map.109.after_ref.att_ref.refs_0_), channel_id=1, source_target_pairs={{8,0},{16,8},{24,16},{28,24},{20,28},{12,20},{4,12},{0,4},{9,1},{1... | collective-permute-start | bytes 786440 | tf_op jit(solution)/shard_map/ppermute | solution.py:501
  47.5 0.6 shard_map.110.after_ref
  48.1 1.9 %shard_map.111 = (bf16[2,128,1024]{2,1,0:T(8,128)(2,1)S(1)}, f32[2,128,1024]{2,1,0:T(8,128)S(1)}) custom-call(s32[2]{0:T(128)S(1)} %pad_add_fusion.place_ref, bf16[128,1024]{1,0:T(8,128)(2,1)S(1)} %shard_map.109.after_ref.att_ref.refs_0_, bf16[1024,4096]{1,0:T(8,128)(2,1)S(1)} %get-tuple-element.35.refs_4_.w_ref, bf16[8,128,128]{2,1,0:T(8,128)(2,1)S(1)} %shard_map.110.after_ref), custom_call_target="tpu_custom_call" | custom-call | flops 1073741824 | bytes 8388608 | tf_op jit(solution)/shard_map/pallas_call | solution.py:456
  50.0 0.1 collective-permute-start.11
  50.0 3.7 %collective-permute-done.13.refs_1_ = bf16[128,1024]{1,0:T(8,128)(2,1)S(1)} collective-permute-done((bf16[128,1024]{1,0:T(8,128)(2,1)S(1)}, bf16[128,1024]{1,0:T(8,128)(2,1)S(1)}, u32[]{:S(2)}, u32[]{:S(2)}) %collective-permute-start.13) | collective-permute-done | bytes 262176 | tf_op jit(solution)/shard_map/ppermute | solution.py:500
  53.8 0.3 collective-permute-start.14
  54.1 0.0 collective-permute-done.16.refs_2_
  54.1 1.7 %collective-permute-start.17 = (bf16[128,1024]{1,0:T(8,128)(2,1)S(1)}, bf16[128,1024]{1,0:T(8,128)(2,1)S(1)}, u32[]{:S(2)}, u32[]{:S(2)}) collective-permute-start(bf16[128,1024]{1,0:T(8,128)(2,1)S(1)} %collective-permute-done.16.refs_2_), channel_id=1, source_target_pairs={{8,0},{16,8},{24,16},{28,24},{20,28},{12,20},{4,12},{0,4},{9,1},{1... | collective-permute-start | bytes 786440 | tf_op jit(solution)/shard_map/ppermute | solution.py:501
  55.8 0.3 collective-permute-start.19
  56.1 5.2 %collective-permute-done.14.refs_3_ = bf16[128,1024]{1,0:T(8,128)(2,1)S(1)} collective-permute-done((bf16[128,1024]{1,0:T(8,128)(2,1)S(1)}, bf16[128,1024]{1,0:T(8,128)(2,1)S(1)}, u32[]{:S(2)}, u32[]{:S(2)}) %collective-permute-start.14) | collective-permute-done | bytes 262176 | tf_op jit(solution)/shard_map/ppermute | solution.py:500
  61.3 2.0 %collective-permute-start.15 = (bf16[128,1024]{1,0:T(8,128)(2,1)S(1)}, bf16[128,1024]{1,0:T(8,128)(2,1)S(1)}, u32[]{:S(2)}, u32[]{:S(2)}) collective-permute-start(bf16[128,1024]{1,0:T(8,128)(2,1)S(1)} %collective-permute-done.14.refs_3_), channel_id=1, source_target_pairs={{0,8},{8,16},{16,24},{24,28},{28,20},{20,12},{12,4},{4,0},{1,9},{9... | collective-permute-start | bytes 786440 | tf_op jit(solution)/shard_map/ppermute | solution.py:500
  63.3 0.0 collective-permute-done.17.refs_4_
  63.3 0.0 collective-permute-start.18
  63.4 0.0 collective-permute-done.11
  63.4 0.2 convert_add_fusion
  63.6 0.1 collective-permute-start.12
  63.6 1.9 %shard_map.112 = f32[128,8,128]{2,1,0:T(8,128)} custom-call(s32[2]{0:T(128)S(1)} %pad_add_fusion.place_ref, bf16[1024,128]{1,0:T(8,128)(2,1)S(1)} %get-tuple-element.36.after_ref.gt_ref, f32[5,8,128]{2,1,0:T(8,128)S(1)} %get-tuple-element.41.lam_ref, f32[8,128,128]{2,1,0:T(8,128)S(1)} %get-tuple-element.46.dql_ref, ...), custom_call_target="tpu_custom_call" | custom-call | flops 33554432 | bytes 1572864 | tf_op jit(solution)/shard_map/pallas_call | solution.py:470
  65.5 0.6 shard_map.113.cols_ref
  66.1 2.8 %collective-permute-done.19.refs_1_ = bf16[8,128,128]{2,1,0:T(8,128)(2,1)S(1)} collective-permute-done((bf16[8,128,128]{2,1,0:T(8,128)(2,1)S(1)}, bf16[8,128,128]{2,1,0:T(8,128)(2,1)S(1)}, u32[]{:S(2)}, u32[]{:S(2)}) %collective-permute-start.19) | collective-permute-done | bytes 262176 | tf_op jit(solution)/shard_map/ppermute | solution.py:45
  68.9 0.7 shard_map.116
  69.6 0.1 collective-permute-start.20
  69.7 2.1 %shard_map.114.refs_2_ = f32[1024,512]{1,0:T(8,128)S(1)} custom-call(s32[2]{0:T(128)S(1)} %pad_add_fusion.place_ref, bf16[8,128,512]{2,1,0:T(8,128)(2,1)S(1)} %shard_map.113.cols_ref, bf16[128,1024]{1,0:T(8,128)(2,1)S(1)} %shard_map.109.after_ref.att_ref.refs_0_, bf16[128,1024]{1,0:T(8,128)(2,1)S(1)} %collective-permute-done.13.refs_1_, ...), custom_call_target="tpu_custom_call" | custom-call | flops 671088640 | bytes 2097152 | tf_op jit(solution)/shard_map/pallas_call | solution.py:485
  71.8 0.0 collective-permute-done.15.refs_0_
  71.8 2.1 %collective-permute-start.21 = (bf16[64,1024]{1,0:T(8,128)(2,1)S(1)}, bf16[64,1024]{1,0:T(8,128)(2,1)S(1)}, u32[]{:S(2)}, u32[]{:S(2)}) collective-permute-start(bf16[64,1024]{1,0:T(8,128)(2,1)S(1)} %slice.21), channel_id=1, source_target_pairs={{0,8},{8,16},{16,24},{24,28},{28,20},{20,12},{12,4},{4,0},{1,9},{9... | collective-permute-start | bytes 393224 | tf_op jit(solution)/shard_map/ppermute | solution.py:510
  73.9 0.1 collective-permute-start.22
  74.0 0.0 collective-permute-done.12
  74.0 0.8 fusion.1
  74.7 1.3 %shard_map.115.after_ref.total_ref = f32[1024,512]{1,0:T(8,128)S(1)} custom-call(s32[2]{0:T(128)S(1)} %pad_add_fusion.place_ref, bf16[8,128,512]{2,1,0:T(8,128)(2,1)S(1)} %shard_map.113.cols_ref, bf16[128,1024]{1,0:T(8,128)(2,1)S(1)} %collective-permute-done.15.refs_0_, bf16[128,1024]{1,0:T(8,128)(2,1)S(1)} %collective-permute-done.18.refs_1_, ...), custom_call_target="tpu_custom_call" | custom-call | flops 268435456 | bytes 2097152 | tf_op jit(solution)/shard_map/pallas_call | solution.py:485
  76.0 0.2 collective-permute-done.20.refs_2_
  76.2 2.3 %shard_map.117 = (f32[128,8,128]{2,1,0:T(8,128)}, f32[128,8,128]{2,1,0:T(8,128)}) custom-call(s32[2]{0:T(128)S(1)} %pad_add_fusion.place_ref, bf16[8,128,128]{2,1,0:T(8,128)(2,1)S(1)} %get-tuple-element.28.kh_ref, bf16[8,128,128]{2,1,0:T(8,128)(2,1)S(1)} %get-tuple-element.29.vh_ref, f32[8,128,128]{2,1,0:T(8,128)S(1)} %get-tuple-element.42.refs_3_.dkl_ref, ...), custom_call_target="tpu_custom_call" | custom-call | flops 67108864 | bytes 2883584 | tf_op jit(solution)/shard_map/pallas_call | solution.py:513
  78.5 0.0 collective-permute-done.21.low_ref
  78.5 0.4 collective-permute-done.22.high_ref
  78.9 2.9 %shard_map.118 = f32[1024,512]{1,0:T(8,128)} custom-call(s32[2]{0:T(128)S(1)} %pad_add_fusion.place_ref, bf16[8,128,512]{2,1,0:T(8,128)(2,1)S(1)} %shard_map.113.cols_ref, bf16[64,1024]{1,0:T(8,128)(2,1)S(1)} %collective-permute-done.21.low_ref, bf16[64,1024]{1,0:T(8,128)(2,1)S(1)} %collective-permute-done.22.high_ref, ...), custom_call_target="tpu_custom_call" | custom-call | flops 134217728 | bytes 4194304 | tf_op jit(solution)/shard_map/pallas_call | solution.py:522
  (6 shorter events, 0.1 us)
Async XLA Ops:
  0.6 11.0 %collective-permute-start.4 = (bf16[128,1024]{1,0:T(8,128)(2,1)}, bf16[128,1024]{1,0:T(8,128)(2,1)S(1)}, u32[]{:S(2)}, u32[]{:S(2)}) collective-permute-start(bf16[128,1024]{1,0:T(8,128)(2,1)} %grad_hbm.1), channel_id=1, source_target_pairs={{0,2},{1,3},{2,0},{3,1},{4,6},{5,7},{6,4},{7,5},{8,10},{9,11},{10,... | collective-permute-start | bytes 786440 | tf_op jit(solution)/shard_map/ppermute | solution.py:312
  3.6 12.2 %collective-permute-start.1 = (bf16[128,1024]{1,0:T(8,128)(2,1)}, bf16[128,1024]{1,0:T(8,128)(2,1)S(1)}, u32[]{:S(2)}, u32[]{:S(2)}) collective-permute-start(bf16[128,1024]{1,0:T(8,128)(2,1)} %grad_hbm.1), channel_id=1, source_target_pairs={{0,0},{1,8},{2,16},{3,24},{4,4},{5,12},{6,20},{7,28},{8,1},{9,9},{... | collective-permute-start | bytes 786440 | tf_op jit(solution)/shard_map/ppermute | solution.py:330
  8.3 8.7 %collective-permute-start = (bf16[8,128,128]{2,1,0:T(8,128)(2,1)S(1)}, bf16[8,128,128]{2,1,0:T(8,128)(2,1)S(1)}, u32[]{:S(2)}, u32[]{:S(2)}) collective-permute-start(bf16[8,128,128]{2,1,0:T(8,128)(2,1)S(1)} %get-tuple-element.32.running_ref), channel_id=1, source_target_pairs={{0,4},{4,0},{8,12},{12,8},{16,20},{20,16},{24,28},{28,24},{1,5},{5... | collective-permute-start | bytes 786440 | tf_op jit(solution)/shard_map/ppermute | solution.py:45
  9.9 10.6 %collective-permute-start.3 = (bf16[128,1024]{1,0:T(8,128)(2,1)}, bf16[128,1024]{1,0:T(8,128)(2,1)S(1)}, u32[]{:S(2)}, u32[]{:S(2)}) collective-permute-start(bf16[128,1024]{1,0:T(8,128)(2,1)} %grad_hbm.1), channel_id=1, source_target_pairs={{0,1},{1,0},{2,3},{3,2},{4,5},{5,4},{6,7},{7,6},{8,9},{9,8},{10,11... | collective-permute-start | bytes 786440 | tf_op jit(solution)/shard_map/ppermute | solution.py:312
  11.6 8.8 %collective-permute-start.5 = (bf16[128,1024]{1,0:T(8,128)(2,1)S(1)}, bf16[128,1024]{1,0:T(8,128)(2,1)S(1)}, u32[]{:S(2)}, u32[]{:S(2)}) collective-permute-start(bf16[128,1024]{1,0:T(8,128)(2,1)S(1)} %collective-permute-done.4.refs_2_), channel_id=1, source_target_pairs={{0,1},{1,0},{2,3},{3,2},{4,5},{5,4},{6,7},{7,6},{8,9},{9,8},{10,11... | collective-permute-start | bytes 786440 | tf_op jit(solution)/shard_map/ppermute | solution.py:312
  16.4 7.4 %collective-permute-start.6 = (bf16[128,512]{1,0:T(8,128)(2,1)S(1)}, bf16[128,512]{1,0:T(8,128)(2,1)S(1)}, u32[]{:S(2)}, u32[]{:S(2)}) collective-permute-start(bf16[128,512]{1,0:T(8,128)(2,1)S(1)} %get-tuple-element.33.refs_0_.refs_6_), channel_id=1, source_target_pairs={{0,4},{4,0},{8,12},{12,8},{16,20},{20,16},{24,28},{28,24},{1,5},{5... | collective-permute-start | bytes 393224 | tf_op jit(solution)/shard_map/ppermute | solution.py:363
  17.1 11.5 %collective-permute-start.2 = (bf16[8,128,128]{2,1,0:T(8,128)(2,1)S(1)}, bf16[8,128,128]{2,1,0:T(8,128)(2,1)S(1)}, u32[]{:S(2)}, u32[]{:S(2)}) collective-permute-start(bf16[8,128,128]{2,1,0:T(8,128)(2,1)S(1)} %shard_map.104.running_ref), channel_id=1, source_target_pairs={{0,8},{8,0},{4,12},{12,4},{16,24},{24,16},{20,28},{28,20},{1,9},{9... | collective-permute-start | bytes 786440 | tf_op jit(solution)/shard_map/ppermute | solution.py:45
  23.9 9.9 %collective-permute-start.9 = (bf16[2,128,512]{2,1,0:T(8,128)(2,1)S(1)}, bf16[2,128,512]{2,1,0:T(8,128)(2,1)S(1)}, u32[]{:S(2)}, u32[]{:S(2)}) collective-permute-start(bf16[2,128,512]{2,1,0:T(8,128)(2,1)S(1)} %shard_map.106.after_ref.refs_0_), channel_id=1, source_target_pairs={{0,2},{1,3},{2,0},{3,1},{4,6},{5,7},{6,4},{7,5},{8,10},{9,11},{10,... | collective-permute-start | bytes 786440 | tf_op jit(solution)/shard_map/ppermute | solution.py:312
  28.6 16.4 %collective-permute-start.8 = (bf16[2,128,512]{2,1,0:T(8,128)(2,1)S(1)}, bf16[2,128,512]{2,1,0:T(8,128)(2,1)S(1)}, u32[]{:S(2)}, u32[]{:S(2)}) collective-permute-start(bf16[2,128,512]{2,1,0:T(8,128)(2,1)S(1)} %shard_map.106.after_ref.refs_0_), channel_id=1, source_target_pairs={{0,1},{1,0},{2,3},{3,2},{4,5},{5,4},{6,7},{7,6},{8,9},{9,8},{10,11... | collective-permute-start | bytes 786440 | tf_op jit(solution)/shard_map/ppermute | solution.py:312
  29.3 15.8 %collective-permute-start.7 = (bf16[8,128,128]{2,1,0:T(8,128)(2,1)S(1)}, bf16[8,128,128]{2,1,0:T(8,128)(2,1)S(1)}, u32[]{:S(2)}, u32[]{:S(2)}) collective-permute-start(bf16[8,128,128]{2,1,0:T(8,128)(2,1)S(1)} %shard_map.107.after_ref), channel_id=1, source_target_pairs={{0,16},{16,0},{4,20},{20,4},{8,24},{24,8},{12,28},{28,12},{1,17},{... | collective-permute-start | bytes 786440 | tf_op jit(solution)/shard_map/ppermute | solution.py:45
  33.7 11.3 %collective-permute-start.10 = (bf16[2,128,512]{2,1,0:T(8,128)(2,1)S(1)}, bf16[2,128,512]{2,1,0:T(8,128)(2,1)S(1)}, u32[]{:S(2)}, u32[]{:S(2)}) collective-permute-start(bf16[2,128,512]{2,1,0:T(8,128)(2,1)S(1)} %collective-permute-done.9.refs_5_.refs_2_), channel_id=1, source_target_pairs={{0,1},{1,0},{2,3},{3,2},{4,5},{5,4},{6,7},{7,6},{8,9},{9,8},{10,11... | collective-permute-start | bytes 786440 | tf_op jit(solution)/shard_map/ppermute | solution.py:312
  45.4 8.4 %collective-permute-start.13 = (bf16[128,1024]{1,0:T(8,128)(2,1)S(1)}, bf16[128,1024]{1,0:T(8,128)(2,1)S(1)}, u32[]{:S(2)}, u32[]{:S(2)}) collective-permute-start(bf16[128,1024]{1,0:T(8,128)(2,1)S(1)} %shard_map.109.after_ref.att_ref.refs_0_), channel_id=1, source_target_pairs={{0,8},{8,16},{16,24},{24,28},{28,20},{20,12},{12,4},{4,0},{1,9},{9... | collective-permute-start | bytes 786440 | tf_op jit(solution)/shard_map/ppermute | solution.py:500
  45.5 8.6 %collective-permute-start.16 = (bf16[128,1024]{1,0:T(8,128)(2,1)S(1)}, bf16[128,1024]{1,0:T(8,128)(2,1)S(1)}, u32[]{:S(2)}, u32[]{:S(2)}) collective-permute-start(bf16[128,1024]{1,0:T(8,128)(2,1)S(1)} %shard_map.109.after_ref.att_ref.refs_0_), channel_id=1, source_target_pairs={{8,0},{16,8},{24,16},{28,24},{20,28},{12,20},{4,12},{0,4},{9,1},{1... | collective-permute-start | bytes 786440 | tf_op jit(solution)/shard_map/ppermute | solution.py:501
  50.0 13.4 %collective-permute-start.11 = (bf16[2,128,1024]{2,1,0:T(8,128)(2,1)S(1)}, bf16[2,128,1024]{2,1,0:T(8,128)(2,1)S(1)}, u32[]{:S(2)}, u32[]{:S(2)}) collective-permute-start(bf16[2,128,1024]{2,1,0:T(8,128)(2,1)S(1)} %get-tuple-element.45), channel_id=1, source_target_pairs={{0,1},{1,0},{2,3},{3,2},{4,5},{5,4},{6,7},{7,6},{8,9},{9,8},{10,11... | collective-permute-start | bytes 1572872 | tf_op jit(solution)/shard_map/ppermute | solution.py:312
  53.8 7.5 %collective-permute-start.14 = (bf16[128,1024]{1,0:T(8,128)(2,1)S(1)}, bf16[128,1024]{1,0:T(8,128)(2,1)S(1)}, u32[]{:S(2)}, u32[]{:S(2)}) collective-permute-start(bf16[128,1024]{1,0:T(8,128)(2,1)S(1)} %collective-permute-done.13.refs_1_), channel_id=1, source_target_pairs={{0,8},{8,16},{16,24},{24,28},{28,20},{20,12},{12,4},{4,0},{1,9},{9... | collective-permute-start | bytes 786440 | tf_op jit(solution)/shard_map/ppermute | solution.py:500
  54.1 9.2 %collective-permute-start.17 = (bf16[128,1024]{1,0:T(8,128)(2,1)S(1)}, bf16[128,1024]{1,0:T(8,128)(2,1)S(1)}, u32[]{:S(2)}, u32[]{:S(2)}) collective-permute-start(bf16[128,1024]{1,0:T(8,128)(2,1)S(1)} %collective-permute-done.16.refs_2_), channel_id=1, source_target_pairs={{8,0},{16,8},{24,16},{28,24},{20,28},{12,20},{4,12},{0,4},{9,1},{1... | collective-permute-start | bytes 786440 | tf_op jit(solution)/shard_map/ppermute | solution.py:501
  55.8 13.1 %collective-permute-start.19 = (bf16[8,128,128]{2,1,0:T(8,128)(2,1)S(1)}, bf16[8,128,128]{2,1,0:T(8,128)(2,1)S(1)}, u32[]{:S(2)}, u32[]{:S(2)}) collective-permute-start(bf16[8,128,128]{2,1,0:T(8,128)(2,1)S(1)} %shard_map.110.after_ref), channel_id=1, source_target_pairs={{0,8},{8,0},{4,12},{12,4},{16,24},{24,16},{20,28},{28,20},{1,9},{9... | collective-permute-start | bytes 786440 | tf_op jit(solution)/shard_map/ppermute | solution.py:45
  61.3 10.5 %collective-permute-start.15 = (bf16[128,1024]{1,0:T(8,128)(2,1)S(1)}, bf16[128,1024]{1,0:T(8,128)(2,1)S(1)}, u32[]{:S(2)}, u32[]{:S(2)}) collective-permute-start(bf16[128,1024]{1,0:T(8,128)(2,1)S(1)} %collective-permute-done.14.refs_3_), channel_id=1, source_target_pairs={{0,8},{8,16},{16,24},{24,28},{28,20},{20,12},{12,4},{4,0},{1,9},{9... | collective-permute-start | bytes 786440 | tf_op jit(solution)/shard_map/ppermute | solution.py:500
  63.3 10.6 %collective-permute-start.18 = (bf16[128,1024]{1,0:T(8,128)(2,1)S(1)}, bf16[128,1024]{1,0:T(8,128)(2,1)S(1)}, u32[]{:S(2)}, u32[]{:S(2)}) collective-permute-start(bf16[128,1024]{1,0:T(8,128)(2,1)S(1)} %collective-permute-done.17.refs_4_), channel_id=1, source_target_pairs={{8,0},{16,8},{24,16},{28,24},{20,28},{12,20},{4,12},{0,4},{9,1},{1... | collective-permute-start | bytes 786440 | tf_op jit(solution)/shard_map/ppermute | solution.py:501
  63.6 10.4 %collective-permute-start.12 = (bf16[1,128,1024]{2,1,0:T(8,128)(2,1)S(1)}, bf16[1,128,1024]{2,1,0:T(8,128)(2,1)S(1)}, u32[]{:S(2)}, u32[]{:S(2)}) collective-permute-start(bf16[1,128,1024]{2,1,0:T(8,128)(2,1)S(1)} %slice.29), channel_id=1, source_target_pairs={{0,2},{1,3},{2,0},{3,1},{4,6},{5,7},{6,4},{7,5},{8,10},{9,11},{10,... | collective-permute-start | bytes 786440 | tf_op jit(solution)/shard_map/ppermute | solution.py:312
  69.6 6.6 %collective-permute-start.20 = (bf16[8,128,128]{2,1,0:T(8,128)(2,1)S(1)}, bf16[8,128,128]{2,1,0:T(8,128)(2,1)S(1)}, u32[]{:S(2)}, u32[]{:S(2)}) collective-permute-start(bf16[8,128,128]{2,1,0:T(8,128)(2,1)S(1)} %shard_map.116), channel_id=1, source_target_pairs={{0,4},{4,0},{8,12},{12,8},{16,20},{20,16},{24,28},{28,24},{1,5},{5... | collective-permute-start | bytes 786440 | tf_op jit(solution)/shard_map/ppermute | solution.py:45
  71.8 6.7 %collective-permute-start.21 = (bf16[64,1024]{1,0:T(8,128)(2,1)S(1)}, bf16[64,1024]{1,0:T(8,128)(2,1)S(1)}, u32[]{:S(2)}, u32[]{:S(2)}) collective-permute-start(bf16[64,1024]{1,0:T(8,128)(2,1)S(1)} %slice.21), channel_id=1, source_target_pairs={{0,8},{8,16},{16,24},{24,28},{28,20},{20,12},{12,4},{4,0},{1,9},{9... | collective-permute-start | bytes 393224 | tf_op jit(solution)/shard_map/ppermute | solution.py:510
  73.9 5.0 %collective-permute-start.22 = (bf16[64,1024]{1,0:T(8,128)(2,1)S(1)}, bf16[64,1024]{1,0:T(8,128)(2,1)S(1)}, u32[]{:S(2)}, u32[]{:S(2)}) collective-permute-start(bf16[64,1024]{1,0:T(8,128)(2,1)S(1)} %slice.22), channel_id=1, source_target_pairs={{8,0},{16,8},{24,16},{28,24},{20,28},{12,20},{4,12},{0,4},{9,1},{1... | collective-permute-start | bytes 393224 | tf_op jit(solution)/shard_map/ppermute | solution.py:511

commit v2 on v1

--- a/solution.py
+++ b/solution.py
@@ -16,7 +16,6 @@
 TT = (((0,), (1,)), ((), ()))
 VMEM = pl.BlockSpec(memory_space=pltpu.VMEM)
 ANY = pl.BlockSpec(memory_space=pl.ANY)
-SMEM = pl.BlockSpec(memory_space=pltpu.SMEM)
 PARAMS = pltpu.CompilerParams(vmem_limit_bytes=14 * 2**20)
 
 
@@ -49,15 +48,15 @@
     return pltpu.with_memory_space_constraint(array, pltpu.HBM)
 
 
-def state_kernel(place_ref, k_hbm, v_hbm, s_ref, kh_ref, vh_ref, k_ref, v_ref, sems):
-    del place_ref
+def state_kernel(k_hbm, v_hbm, grad_hbm, s_ref, kh_ref, vh_ref, grad_ref, k_ref, v_ref, sems):
     copies = [
         pltpu.make_async_copy(k_hbm, k_ref, sems.at[0]),
         pltpu.make_async_copy(v_hbm, v_ref, sems.at[1]),
+        pltpu.make_async_copy(grad_hbm, grad_ref, sems.at[2]),
     ]
     for copy in copies:
         copy.start()
-    for copy in copies:
+    for copy in copies[:2]:
         copy.wait()
     for h in range(k_ref.shape[1]):
         k = k_ref[:, h, :].astype(BF)
@@ -65,6 +64,7 @@
         kh_ref[h] = k
         vh_ref[h] = v
         s_ref[h] = mm(k, v, TN).astype(BF)
+    copies[2].wait()
 
 
 def weight_of(lam_ref, h, rows):
@@ -78,15 +78,15 @@
     return jnp.where(s <= t, weight, 0.0)
 
 
-def upper_weight(place_ref, lam_ref, b, h, rows):
+def upper_weight(lam_ref, b, h, rows):
     local_bits = (rows // CH).bit_length() - 1
-    upper = (place_ref[0] >> b & 1).astype(F32)
+    upper = (lax.axis_index("seq") >> b & 1).astype(F32)
     return lam_ref[1 + local_bits + b, h : h + 1, :] * upper
 
 
-def local_kernel(place_ref, q_hbm, kh_ref, vh_ref, lam_hbm, w_hbm, grad_hbm, *refs):
-    pt_ref, att_ref, qh_ref, qw_ref, lam_ref, w_ref, grad_ref, q_ref, lam_rows, sems = refs
-    pieces = sems.shape[0] - 3
+def local_kernel(q_hbm, kh_ref, vh_ref, lam_hbm, w_hbm, *refs):
+    pt_ref, att_ref, qh_ref, qw_ref, lam_ref, w_ref, q_ref, lam_rows, sems = refs
+    pieces = sems.shape[0] - 2
     share = w_hbm.shape[0] // pieces
     copies = [
         pltpu.make_async_copy(q_hbm, q_ref, sems.at[0]),
@@ -94,8 +94,7 @@
     ]
     for i in range(pieces):
         piece = pl.ds(i * share, share)
-        copies.append(pltpu.make_async_copy(w_hbm.at[piece], w_ref.at[piece], sems.at[3 + i]))
-    copies.append(pltpu.make_async_copy(grad_hbm, grad_ref, sems.at[2]))
+        copies.append(pltpu.make_async_copy(w_hbm.at[piece], w_ref.at[piece], sems.at[2 + i]))
     for copy in copies:
         copy.start()
     for copy in copies[:2]:
@@ -106,7 +105,7 @@
     for b in range(bits):
         for h in range(heads_dev):
             at = b * heads_dev + h
-            lam_rows[at : at + 1, :] = upper_weight(place_ref, lam_ref, b, h, rows)
+            lam_rows[at : at + 1, :] = upper_weight(lam_ref, b, h, rows)
     lam_columns = lam_rows[...].T
     for h in range(heads_dev):
         q32 = q_ref[:, h, :]
@@ -132,7 +131,7 @@
         out_ref[:, h * head_dim : (h + 1) * head_dim] = total.astype(BF)
 
 
-def cotangent_kernel(blocks, bits, place_ref, *refs):
+def cotangent_kernel(blocks, bits, *refs):
     parts, (w_ref, qw_ref, _, gt_ref), sums = (
         refs[:blocks],
         refs[blocks : blocks + 4],
@@ -142,7 +141,7 @@
     _, heads_dev, _, head_dim = qw_ref.shape
     total = None
     for i in range(blocks):
-        column = pl.multiple_of((place_ref[1] ^ i) * deep, deep)
+        column = pl.multiple_of((lax.axis_index("head") ^ i) * deep, deep)
         product = mm(w_ref[:, pl.ds(column, deep)], parts[i][...], NT)
         total = product if total is None else total + product
     for h in range(heads_dev):
@@ -156,33 +155,33 @@
     refs[-1][...] = (running_ref[...].astype(F32) + arrived_ref[...].astype(F32)).astype(BF)
 
 
-def meet_kernel(top, place_ref, after_ref, grad_ref, running_ref, arrived_ref, out_ref):
-    del after_ref
-    upper = (place_ref[0] >> top & 1) == 1
+def meet_kernel(top, after_ref, grad_ref, running_ref, arrived_ref, out_ref):
+    del after_ref
+    upper = (lax.axis_index("seq") >> top & 1) == 1
     running = running_ref[...].astype(F32)
     if arrived_ref is not None:
         running = running + arrived_ref[...].astype(F32)
     out_ref[...] = jnp.where(upper, grad_ref[...], running.astype(BF))
 
 
-def landed_sum(top, place_ref, landed):
-    upper = (place_ref[0] >> top & 1) == 1
+def landed_sum(top, landed):
+    upper = (lax.axis_index("seq") >> top & 1) == 1
     total = jnp.where(upper, 0.0, landed[0].astype(F32))
     for block in landed[1:]:
         total = total + block.astype(F32)
     return total
 
 
-def pending_kernel(top, place_ref, own_ref, after_ref, *refs):
+def pending_kernel(top, own_ref, after_ref, *refs):
     del after_ref
     landed, out_ref = [ref[...] for ref in refs[:-1]], refs[-1]
-    out_ref[...] = (own_ref[...].astype(F32) + landed_sum(top, place_ref, landed)).astype(BF)
-
-
-def chunk_kernel(place_ref, block_ref, after_ref, *outs):
+    out_ref[...] = (own_ref[...].astype(F32) + landed_sum(top, landed)).astype(BF)
+
+
+def chunk_kernel(block_ref, after_ref, *outs):
     del after_ref
     columns = outs[0].shape[1]
-    low = place_ref[0] % len(outs)
+    low = lax.axis_index("seq") % len(outs)
     for r, out in enumerate(outs):
         out[...] = block_ref[:, pl.ds(pl.multiple_of((low ^ r) * columns, columns), columns)]
 
@@ -193,17 +192,17 @@
         refs[-1][r] = ref[...]
 
 
-def columns_kernel(blocks, place_ref, *refs):
+def columns_kernel(blocks, *refs):
     parts, out_ref = refs[:blocks], refs[blocks]
     per = parts[0].shape[0]
-    low = place_ref[0] % per
+    low = lax.axis_index("seq") % per
     for i in range(blocks):
         for r in range(per):
-            out_ref[(place_ref[1] ^ i) * per + (low ^ r)] = parts[i][r]
+            out_ref[(lax.axis_index("head") ^ i) * per + (low ^ r)] = parts[i][r]
 
 
 def local_grad_kernel(
-    bits, place_ref, gt_ref, qh_ref, kh_ref, vh_ref, pt_ref, lam_ref, after_ref, *refs
+    bits, gt_ref, qh_ref, kh_ref, vh_ref, pt_ref, lam_ref, after_ref, *refs
 ):
     del after_ref
     states, (dq_ref, dk_ref, dv_ref) = refs[:bits], refs[bits:]
@@ -216,34 +215,35 @@
         dv_ref[h] = mm(pt_ref[h], gt, NT)
         dq = mm(dpt, kh_ref[h], TN)
         for b in range(bits):
-            gw = (g32 * upper_weight(place_ref, lam_ref, b, h, rows)).astype(BF)
+            gw = (g32 * upper_weight(lam_ref, b, h, rows)).astype(BF)
             dq = dq + mm(gw, states[b][h], TT)
         dq_ref[h] = dq
 
 
-def query_grad_kernel(top, place_ref, gt_ref, lam_ref, dql_ref, state_ref, dq_ref):
+def query_grad_kernel(top, gt_ref, lam_ref, dql_ref, state_ref, after_ref, dq_ref):
+    del after_ref
     heads_dev, rows, head_dim = dql_ref.shape
     for h in range(heads_dev):
         g32 = gt_ref[h * head_dim : (h + 1) * head_dim, :].astype(F32)
-        gw = (g32 * upper_weight(place_ref, lam_ref, top, h, rows)).astype(BF)
+        gw = (g32 * upper_weight(lam_ref, top, h, rows)).astype(BF)
         dq_ref[:, h, :] = dql_ref[h] + mm(gw, state_ref[h], TT)
 
 
-def later_grad_kernel(top, place_ref, kh_ref, vh_ref, dkl_ref, dvl_ref, after_ref, *refs):
+def later_grad_kernel(top, kh_ref, vh_ref, dkl_ref, dvl_ref, after_ref, *refs):
     del after_ref
     landed, (dk_ref, dv_ref) = refs[:-2], refs[-2:]
     for h in range(kh_ref.shape[0]):
-        late = landed_sum(top, place_ref, [ref[h] for ref in landed]).astype(BF)
+        late = landed_sum(top, [ref[h] for ref in landed]).astype(BF)
         dk_ref[:, h, :] = dkl_ref[h] + mm(vh_ref[h], late, NN)
         dv_ref[:, h, :] = dvl_ref[h] + mm(kh_ref[h], late, NT)
 
 
-def share_kernel(blocks, place_ref, att_ref, w_ref, after_ref, send_ref, kept_ref):
-    del after_ref
+def share_kernel(blocks, att_ref, w_ref, *refs):
+    send_ref, kept_ref = refs[-2:]
     width = send_ref.shape[2]
     for i in range(blocks):
         out = send_ref if i % 2 else kept_ref
-        column = pl.multiple_of((place_ref[1] ^ i) * width, width)
+        column = pl.multiple_of((lax.axis_index("head") ^ i) * width, width)
         out[i // 2] = mm(att_ref[...], w_ref[:, pl.ds(column, width)], NN).astype(out.dtype)
 
 
@@ -253,24 +253,24 @@
     return jnp.where(at < devices // 2, 2 * at, 2 * (devices - 1 - at) + 1)
 
 
-def proj_kernel(offsets, devices, first, place_ref, cols_ref, *refs):
+def proj_kernel(offsets, devices, first, cols_ref, *refs):
     total = None if first else refs[len(offsets)][...]
     for i, (offset, low, high) in enumerate(offsets):
-        owner = ring_owner(place_ref[0], offset, devices)
+        owner = ring_owner(lax.axis_index("seq"), offset, devices)
         product = mm(refs[i][...], cols_ref[owner, low:high, :], TN)
         total = product if total is None else total + product
     refs[-1][...] = total
 
 
 def last_kernel(
-    offset, devices, place_ref, cols_ref, low_ref, high_ref, total_ref, after_ref, out_ref, held
+    offset, devices, cols_ref, low_ref, high_ref, total_ref, after_ref, out_ref, held
 ):
     del after_ref
     half, block = low_ref.shape[0], out_ref.shape[0]
     at = pl.ds(pl.multiple_of(pl.program_id(0) * block, block), block)
     held[:half] = low_ref[:, at]
     held[half:] = high_ref[:, at]
-    owner = ring_owner(place_ref[0], offset, devices)
+    owner = ring_owner(lax.axis_index("seq"), offset, devices)
     out_ref[...] = total_ref[at, :] + mm(held[...], cols_ref[owner], TN)
 
 
@@ -281,8 +281,6 @@
     seq_bits = devices.bit_length() - 1
     heads = lax.axis_size("head")
     head_bits = heads.bit_length() - 1
-    seq_place = lax.axis_index("seq")
-    head_place = lax.axis_index("head")
     columns_dev = out_proj.shape[1] // devices
 
     head_state = like((heads_dev, head_dim, head_dim), BF)
@@ -292,21 +290,20 @@
     flops_head = 2 * heads_dev * rows * rows * head_dim
     moved_head = 2 * rows * width
     top = seq_bits - 1
-    place = jnp.stack([seq_place, head_place]).astype(jnp.int32)
-
-    own_state, kh, vh = pl.pallas_call(
+
+    own_state, kh, vh, own_grad = pl.pallas_call(
         state_kernel,
-        out_shape=(head_state, per_head, per_head),
-        in_specs=[SMEM] + [ANY] * 2,
-        out_specs=(VMEM,) * 3,
+        out_shape=(head_state, per_head, per_head, like(out_grad.shape, BF)),
+        in_specs=[ANY] * 3,
+        out_specs=(VMEM,) * 4,
         scratch_shapes=[
             pltpu.VMEM(keys.shape, F32),
             pltpu.VMEM(keys.shape, F32),
-            pltpu.SemaphoreType.DMA((2,)),
+            pltpu.SemaphoreType.DMA((3,)),
         ],
         compiler_params=PARAMS,
         cost_estimate=cost(flops_head, 7 * moved_head),
-    )(place, hbm(keys), hbm(values))
+    )(hbm(keys), hbm(values), hbm(out_grad))
 
     def to_group(block, i):
         return lax.ppermute(block, "head", [(at, at ^ i) for at in range(heads)])
@@ -318,7 +315,7 @@
                 blocks[i ^ 1 << digit] = to_group(blocks[i], 1 << digit)
         return [blocks[i] for i in range(heads)]
 
-    grad_blocks = every_group(out_grad)
+    grad_blocks = [own_grad] + [to_group(own_grad, i) for i in range(1, heads)]
 
     per = devices // heads
     route = [
@@ -328,7 +325,7 @@
         for group_at in range(heads)
     ]
     turned = lax.ppermute(out_grad, ("seq", "head"), route)
-    probs_t, att_local, qh, qw, lam, w, own_grad = pl.pallas_call(
+    probs_t, att_local, qh, qw, lam, w = pl.pallas_call(
         local_kernel,
         out_shape=(
             pltpu.VMEM((heads_dev, rows, rows), BF),
@@ -337,27 +334,26 @@
             pltpu.VMEM((seq_bits, heads_dev, rows, head_dim), BF),
             pltpu.VMEM(level_weights.shape, F32),
             pltpu.VMEM(out_proj.shape, BF),
-            pltpu.VMEM(out_grad.shape, BF),
         ),
-        in_specs=[SMEM, ANY, VMEM, VMEM, ANY, ANY, ANY],
-        out_specs=(VMEM,) * 7,
+        in_specs=[ANY, VMEM, VMEM, ANY, ANY],
+        out_specs=(VMEM,) * 6,
         scratch_shapes=[
             pltpu.VMEM(queries.shape, F32),
             pltpu.VMEM((rows, rows), F32),
-            pltpu.SemaphoreType.DMA((11,)),
+            pltpu.SemaphoreType.DMA((10,)),
         ],
         compiler_params=PARAMS,
         cost_estimate=cost(2 * flops_head, 12 * moved_head),
-    )(place, hbm(queries), kh, vh, hbm(level_weights), hbm(out_proj), hbm(out_grad))
+    )(hbm(queries), kh, vh, hbm(level_weights), hbm(out_proj))
 
     chunks = pl.pallas_call(
         chunk_kernel,
         out_shape=(like((rows, columns_dev), BF),) * per,
-        in_specs=[SMEM, VMEM, ANY],
+        in_specs=[VMEM, ANY],
         out_specs=(VMEM,) * per,
         compiler_params=PARAMS,
         cost_estimate=cost(0, 2 * moved_head),
-    )(place, turned, qw)
+    )(turned, qw)
     own_chunks = chunks
     chunks = [chunks[0]] + [
         lax.ppermute(chunks[r], "seq", [(at, at ^ r) for at in range(devices)])
@@ -381,11 +377,11 @@
     gt, *grad_sums = pl.pallas_call(
         functools.partial(cotangent_kernel, heads, seq_bits),
         out_shape=(pltpu.VMEM((width, rows), BF),) + (pinned_state,) * seq_bits,
-        in_specs=[SMEM] + [VMEM] * (heads + 2) + [ANY],
+        in_specs=[VMEM] * (heads + 2) + [ANY],
         out_specs=(VMEM,) * (1 + seq_bits),
         compiler_params=PARAMS,
         cost_estimate=cost(2 * rows * width * out_proj.shape[1], 2 * width * out_proj.shape[1]),
-    )(place, own_grad, *grad_blocks[1:], w, qw, own_chunks[-1])
+    )(*grad_blocks, w, qw, own_chunks[-1])
 
     stacked = pl.pallas_call(
         stack_kernel,
@@ -400,35 +396,35 @@
     meeting = pl.pallas_call(
         functools.partial(meet_kernel, top)
         if arrived is not None
-        else lambda place_ref, after_ref, grad_ref, running_ref, out_ref: meet_kernel(
-            top, place_ref, after_ref, grad_ref, running_ref, None, out_ref
+        else lambda after_ref, grad_ref, running_ref, out_ref: meet_kernel(
+            top, after_ref, grad_ref, running_ref, None, out_ref
         ),
         out_shape=head_state,
-        in_specs=[SMEM, ANY] + [VMEM] * (2 if arrived is None else 3),
+        in_specs=[ANY] + [VMEM] * (2 if arrived is None else 3),
         out_specs=VMEM,
         compiler_params=PARAMS,
         cost_estimate=cost(0, 4 * moved_head),
-    )(place, stacked, grad_sums[top], running, *([] if arrived is None else [arrived]))
+    )(stacked, grad_sums[top], running, *([] if arrived is None else [arrived]))
     landed = [across(meeting, "seq", top)]
     partner_states.append(landed[0])
 
     grad_columns = pl.pallas_call(
         functools.partial(columns_kernel, heads),
         out_shape=pltpu.VMEM((devices, rows, columns_dev), BF),
-        in_specs=[SMEM] + [VMEM] * heads,
+        in_specs=[VMEM] * heads,
         out_specs=VMEM,
         compiler_params=PARAMS,
         cost_estimate=cost(0, 8 * moved_head),
-    )(place, *column_blocks)
+    )(*column_blocks)
 
     query_local, key_local, value_local = pl.pallas_call(
         functools.partial(local_grad_kernel, top),
         out_shape=(per_head_f32,) * 3,
-        in_specs=[SMEM] + [VMEM] * 6 + [ANY] + [VMEM] * top,
+        in_specs=[VMEM] * 6 + [ANY] + [VMEM] * top,
         out_specs=(VMEM,) * 3,
         compiler_params=PARAMS,
         cost_estimate=cost((4 + top) * flops_head, 14 * moved_head),
-    )(place, gt, qh, kh, vh, probs_t, lam, meeting, *partner_states[:top])
+    )(gt, qh, kh, vh, probs_t, lam, meeting, *partner_states[:top])
 
     attended = pl.pallas_call(
         functools.partial(attended_kernel, seq_bits),
@@ -444,38 +440,38 @@
         outgoing = pl.pallas_call(
             functools.partial(pending_kernel, top),
             out_shape=head_state,
-            in_specs=[SMEM, VMEM, ANY] + [VMEM] * len(landed),
+            in_specs=[VMEM, ANY] + [VMEM] * len(landed),
             out_specs=VMEM,
             compiler_params=PARAMS,
             cost_estimate=cost(0, 4 * moved_head),
-        )(place, grad_sums[digit], attended, *landed)
+        )(grad_sums[digit], attended, *landed)
         if len(landed) == 1:
             first_pending = outgoing
         landed.append(across(outgoing, "seq", digit))
 
+    query_grad = pl.pallas_call(
+        functools.partial(query_grad_kernel, top),
+        out_shape=like((rows, heads_dev, head_dim), F32),
+        in_specs=[VMEM] * 4 + [ANY],
+        out_specs=VMEM,
+        compiler_params=PARAMS,
+        cost_estimate=cost(flops_head, 6 * moved_head),
+    )(gt, lam, query_local, partner_states[top], attended)
+
     send, kept = pl.pallas_call(
         functools.partial(share_kernel, heads),
         out_shape=(like((heads // 2, rows, width), BF), like((heads // 2, rows, width), F32)),
-        in_specs=[SMEM, VMEM, VMEM, ANY],
+        in_specs=[VMEM, VMEM, ANY, ANY, ANY],
         out_specs=(VMEM,) * 2,
         compiler_params=PARAMS,
         cost_estimate=cost(2 * rows * width * out_proj.shape[1], 2 * width * out_proj.shape[1]),
-    )(place, attended, w, first_pending)
+    )(attended, w, first_pending, hbm(query_grad), grad_columns)
     for digit in range(head_bits):
         kept = kept + to_group(send, 1 << digit).astype(F32)
         if digit < head_bits - 1:
             send, kept = kept[1::2].astype(BF), kept[0::2]
     mixed = kept[0].astype(BF)
 
-    query_grad = pl.pallas_call(
-        functools.partial(query_grad_kernel, top),
-        out_shape=like((rows, heads_dev, head_dim), F32),
-        in_specs=[SMEM] + [VMEM] * 4,
-        out_specs=VMEM,
-        compiler_params=PARAMS,
-        cost_estimate=cost(flops_head, 6 * moved_head),
-    )(place, gt, lam, query_local, partner_states[top])
-
     ring = list(range(0, devices, 2)) + list(range(devices - 1, 0, -2))
     forward = [(ring[i], ring[(i + 1) % devices]) for i in range(devices)]
     backward = [(b, a) for a, b in forward]
@@ -484,14 +480,14 @@
         operands = blocks if total is None else blocks + [total]
         return pl.pallas_call(
             functools.partial(proj_kernel, offsets, devices, total is None),
-            out_shape=like((width, columns_dev), F32),
-            in_specs=[SMEM] + [VMEM] * (1 + len(operands)),
+            out_shape=pltpu.VMEM((width, columns_dev), F32),
+            in_specs=[VMEM] * (1 + len(operands)),
             out_specs=VMEM,
             compiler_params=PARAMS,
             cost_estimate=cost(
                 2 * len(blocks) * rows * width * columns_dev, 4 * width * columns_dev
             ),
-        )(place, grad_columns, *operands)
+        )(grad_columns, *operands)
 
     blocks, offsets = [attended], [(0, 0, rows)]
     ahead = behind = attended
@@ -513,18 +509,17 @@
     key_grad, value_grad = pl.pallas_call(
         functools.partial(later_grad_kernel, top),
         out_shape=(like((rows, heads_dev, head_dim), F32),) * 2,
-        in_specs=[SMEM] + [VMEM] * 4 + [ANY] + [VMEM] * seq_bits,
+        in_specs=[VMEM] * 4 + [ANY] + [VMEM] * seq_bits,
         out_specs=(VMEM,) * 2,
         compiler_params=PARAMS,
         cost_estimate=cost(2 * flops_head, 11 * moved_head),
-    )(place, kh, vh, key_local, value_local, total, *landed)
+    )(kh, vh, key_local, value_local, total, *landed)
     quarter_rows = width // 4
     proj_grad = pl.pallas_call(
         functools.partial(last_kernel, steps, devices),
         out_shape=like((width, columns_dev), F32),
         grid=(4,),
         in_specs=[
-            SMEM,
             VMEM,
             VMEM,
             VMEM,
@@ -535,7 +530,7 @@
         scratch_shapes=[pltpu.VMEM((rows, quarter_rows), BF)],
         compiler_params=PARAMS,
         cost_estimate=cost(2 * rows * width * columns_dev, 8 * width * columns_dev),
-    )(place, grad_columns, *last, total, hbm(key_grad))
+    )(grad_columns, *last, total, hbm(key_grad))
     return (mixed, query_grad, key_grad, value_grad, proj_grad)
 
 

time: 82 us -> 83.3 us (1.016)
  waiting for transfers between devices: 23.6 us -> 36.6 us
  Pallas kernels: 28.2 us -> 20 us
  starting transfers between devices: 28.1 us -> 24.6 us
    ppermute x8, waiting for transfers between devices: 1.78 us -> 17 us  [to_group(): return lax.ppermute(block, 'head', [(at, at ^ i) for at in range(heads)])]
    ppermute x5, starting transfers between devices: 8.01 us -> 4.49 us  [across(): return lax.ppermute(block, axis, route)]
    ppermute x5, waiting for transfers between devices: 12.5 us -> 10.2 us  [across(): return lax.ppermute(block, axis, route)]
    ppermute x1, starting transfers between devices: 2.07 us -> 0.13 us  [body(): lax.ppermute(ahead[:half], 'seq', forward)]
    ppermute x1, starting transfers between devices: 0.06 us -> 2 us  [body(): lax.ppermute(behind[half:], 'seq', backward)]
    ppermute x8, starting transfers between devices: 9.63 us -> 8.52 us  [to_group(): return lax.ppermute(block, 'head', [(at, at ^ i) for at in range(heads)])]
    pallas_call x2, Pallas kernels: 3.35 us -> 2.27 us  [accumulate(): pl.pallas_call(functools.partial(proj_kernel, offsets, devices, total is...]
    pallas_call x2, Pallas kernels: 1.27 us -> 0.21 us  [body(): pl.pallas_call(functools.partial(pending_kernel, top), out_shape=head_sta...]
  transfers between devices with their start and end apart: 23 -> 23, of which waited for: 7 -> 8; matrix products, arithmetic and copies ran while one was open for 1% -> 1% of each run, Pallas kernels for 30% -> 21%
where the time goes in v2:
time: 83.3 us; the launch traced here: 83.1 us
  waiting for transfers between devices  36.6 us (44%)
  starting transfers between devices  24.6 us (30%)
  Pallas kernels  20 us (24%)
  other arithmetic  0.94 us (1%)
  between operations  0.84 us (1%)
    ppermute x8, waiting for transfers between devices, to_group(): return lax.ppermute(block, 'head', [(at, at ^ i) for at in range(heads)])  17 us
    ppermute x5, waiting for transfers between devices, across(): return lax.ppermute(block, axis, route)  10.2 us
    ppermute x3, waiting for transfers between devices, body(): ahead = lax.ppermute(ahead, 'seq', forward)  9.41 us
    ppermute x8, starting transfers between devices, to_group(): return lax.ppermute(block, 'head', [(at, at ^ i) for at in range(heads)])  8.52 us
    ppermute x5, starting transfers between devices, across(): return lax.ppermute(block, axis, route)  4.49 us
    ppermute x3, starting transfers between devices, body(): behind = lax.ppermute(behind, 'seq', backward)  4.24 us
    pallas_call x1, Pallas kernels, body(): pl.pallas_call(local_kernel, out_shape=(pltpu.VMEM((heads_dev, rows, rows...  3.66 us
    ppermute x3, starting transfers between devices, body(): ahead = lax.ppermute(ahead, 'seq', forward)  3.06 us
  transfers between devices with their start and end apart: 23, of which 8 were waited for; matrix products, arithmetic and copies ran while one was open for 1% of the time, Pallas kernels for 21%

profile of v2, /device:TPU:0, one launch (start us, length us, event | category | flops | bytes accessed | tf_op | source)
XLA Modules:
  0.0 83.1 jit_solution(6921839291169866133)
XLA Ops:
  0.6 1.6 %collective-permute-start.1 = (bf16[128,1024]{1,0:T(8,128)(2,1)}, bf16[128,1024]{1,0:T(8,128)(2,1)S(1)}, u32[]{:S(2)}, u32[]{:S(2)}) collective-permute-start(bf16[128,1024]{1,0:T(8,128)(2,1)} %grad_hbm.1), channel_id=1, source_target_pairs={{0,0},{1,8},{2,16},{3,24},{4,4},{5,12},{6,20},{7,28},{8,1},{9,9},{... | collective-permute-start | bytes 786440 | tf_op jit(solution)/shard_map/ppermute | solution.py:327
  2.2 2.4 %shard_map.101 = (bf16[8,128,128]{2,1,0:T(8,128)(2,1)S(1)}, bf16[8,128,128]{2,1,0:T(8,128)(2,1)S(1)}, bf16[8,128,128]{2,1,0:T(8,128)(2,1)S(1)}, bf16[128,1024]{1,0:T(8,128)(2,1)S(1)}) custom-call(f32[128,8,128]{2,1,0:T(8,128)} %k_hbm.1, f32[128,8,128]{2,1,0:T(8,128)} %v_hbm.1, bf16[128,1024]{1,0:T(8,128)(2,1)} %grad_hbm.1), custom_call_target="tpu_custom_call" | custom-call | flops 33554432 | bytes 1835008 | tf_op jit(solution)/shard_map/pallas_call | solution.py:294
  4.7 3.0 %collective-permute-start = (bf16[8,128,128]{2,1,0:T(8,128)(2,1)S(1)}, bf16[8,128,128]{2,1,0:T(8,128)(2,1)S(1)}, u32[]{:S(2)}, u32[]{:S(2)}) collective-permute-start(bf16[8,128,128]{2,1,0:T(8,128)(2,1)S(1)} %get-tuple-element.32.running_ref), channel_id=1, source_target_pairs={{0,4},{4,0},{8,12},{12,8},{16,20},{20,16},{24,28},{28,24},{1,5},{5... | collective-permute-start | bytes 786440 | tf_op jit(solution)/shard_map/ppermute | solution.py:44
  7.7 1.7 %collective-permute-start.3 = (bf16[128,1024]{1,0:T(8,128)(2,1)S(1)}, bf16[128,1024]{1,0:T(8,128)(2,1)S(1)}, u32[]{:S(2)}, u32[]{:S(2)}) collective-permute-start(bf16[128,1024]{1,0:T(8,128)(2,1)S(1)} %get-tuple-element.34.refs_0_), channel_id=1, source_target_pairs={{0,1},{1,0},{2,3},{3,2},{4,5},{5,4},{6,7},{7,6},{8,9},{9,8},{10,11... | collective-permute-start | bytes 786440 | tf_op jit(solution)/shard_map/ppermute | solution.py:309
  9.4 3.5 %collective-permute-start.4 = (bf16[128,1024]{1,0:T(8,128)(2,1)S(1)}, bf16[128,1024]{1,0:T(8,128)(2,1)S(1)}, u32[]{:S(2)}, u32[]{:S(2)}) collective-permute-start(bf16[128,1024]{1,0:T(8,128)(2,1)S(1)} %get-tuple-element.34.refs_0_), channel_id=1, source_target_pairs={{0,2},{1,3},{2,0},{3,1},{4,6},{5,7},{6,4},{7,5},{8,10},{9,11},{10,... | collective-permute-start | bytes 786440 | tf_op jit(solution)/shard_map/ppermute | solution.py:309
  12.9 0.0 collective-permute-start.5
  12.9 3.7 %shard_map.102 = (bf16[8,128,128]{2,1,0:T(8,128)(2,1)S(1)}, f32[8,128,128]{2,1,0:T(8,128)S(1)}, bf16[8,128,128]{2,1,0:T(8,128)(2,1)S(1)}, bf16[3,8,128,128]{3,2,...) custom-call(f32[128,8,128]{2,1,0:T(8,128)} %q_hbm.1, ...), custom_call_target="tpu_custom_call" | custom-call | flops 67108864 | bytes 3145728 | tf_op jit(solution)/shard_map/pallas_call | solution.py:328
  16.6 0.0 collective-permute-done.1.block_ref
  16.7 0.6 collective-permute-start.6
  17.2 0.0 collective-permute-done.arrived_ref.refs_0_
  17.2 0.1 shard_map.104.running_ref
  17.3 0.1 collective-permute-start.2
  17.4 0.0 collective-permute-done.3.refs_1_
  17.4 5.3 %collective-permute-done.4.refs_2_ = bf16[128,1024]{1,0:T(8,128)(2,1)S(1)} collective-permute-done((bf16[128,1024]{1,0:T(8,128)(2,1)S(1)}, bf16[128,1024]{1,0:T(8,128)(2,1)S(1)}, u32[]{:S(2)}, u32[]{:S(2)}) %collective-permute-start.4) | collective-permute-done | bytes 262176 | tf_op jit(solution)/shard_map/ppermute | solution.py:309
  22.7 5.2 %collective-permute-done.5.refs_3_ = bf16[128,1024]{1,0:T(8,128)(2,1)S(1)} collective-permute-done((bf16[128,1024]{1,0:T(8,128)(2,1)S(1)}, bf16[128,1024]{1,0:T(8,128)(2,1)S(1)}, u32[]{:S(2)}, u32[]{:S(2)}) %collective-permute-start.5) | collective-permute-done | bytes 262176 | tf_op jit(solution)/shard_map/ppermute | solution.py:309
  27.8 2.8 %shard_map.105 = (bf16[1024,128]{1,0:T(8,128)(2,1)S(1)}, bf16[8,128,128]{2,1,0:T(8,128)(2,1)S(1)}, bf16[8,128,128]{2,1,0:T(8,128)(2,1)S(1)}, bf16[8,128,128]{2,1,0:T(8,128)(2,1)S(1)}) custom-call(bf16[128,1024]{1,0:T(8,128)(2,1)S(1)} %get-tuple-element.34.refs_0_, bf16[128,1024]{1,0:T(8,128)(2,1)S(1)} %collective-permute-done.3.refs_1_, ...), custom_call_target="tpu_custom_call" | custom-call | flops 1073741824 | bytes 8388608 | tf_op jit(solution)/shard_map/pallas_call | solution.py:377
  30.6 0.0 collective-permute-done.6.refs_1_
  30.7 2.1 %collective-permute-start.9 = (bf16[2,128,512]{2,1,0:T(8,128)(2,1)S(1)}, bf16[2,128,512]{2,1,0:T(8,128)(2,1)S(1)}, u32[]{:S(2)}, u32[]{:S(2)}) collective-permute-start(bf16[2,128,512]{2,1,0:T(8,128)(2,1)S(1)} %shard_map.106.after_ref.refs_0_), channel_id=1, source_target_pairs={{0,2},{1,3},{2,0},{3,1},{4,6},{5,7},{6,4},{7,5},{8,10},{9,11},{10,... | collective-permute-start | bytes 786440 | tf_op jit(solution)/shard_map/ppermute | solution.py:309
  32.8 0.0 collective-permute-start.8
  32.8 0.0 collective-permute-done.2.arrived_ref.refs_1_
  32.8 0.1 shard_map.107.after_ref
  32.9 0.1 collective-permute-start.7
  33.0 6.5 %collective-permute-done.9.refs_5_.refs_2_ = bf16[2,128,512]{2,1,0:T(8,128)(2,1)S(1)} collective-permute-done((bf16[2,128,512]{2,1,0:T(8,128)(2,1)S(1)}, bf16[2,128,512]{2,1,0:T(8,128)(2,1)S(1)}, u32[]{:S(2)}, u32[]{:S(2)}) %collective-permute-start.9) | collective-permute-done | bytes 262176 | tf_op jit(solution)/shard_map/ppermute | solution.py:309
  39.5 0.0 collective-permute-start.10
  39.5 1.3 %shard_map.108 = (f32[8,128,128]{2,1,0:T(8,128)S(1)}, f32[8,128,128]{2,1,0:T(8,128)S(1)}, f32[8,128,128]{2,1,0:T(8,128)S(1)}) custom-call(bf16[1024,128]{1,0:T(8,128)(2,1)S(1)} %get-tuple-element.36.after_ref.gt_ref, bf16[8,128,128]{2,1,0:T(8,128)(2,1)S(1)} %get-tuple-element.39.qh_ref, bf16[8,128,128]{2,1,0:T(8,128)(2,1)S(1)} %get-tuple-element.28.kh_ref, ...), custom_call_target="tpu_custom_call" | custom-call | flops 201326592 | bytes 3670016 | tf_op jit(solution)/shard_map/pallas_call | solution.py:420
  40.8 0.0 collective-permute-done.8.refs_4_.refs_1_
  40.8 6.2 %collective-permute-done.7.refs_2_.refs_0_.state_ref = bf16[8,128,128]{2,1,0:T(8,128)(2,1)S(1)} collective-permute-done((bf16[8,128,128]{2,1,0:T(8,128)(2,1)S(1)}, bf16[8,128,128]{2,1,0:T(8,128)(2,1)S(1)}, u32[]{:S(2)}, u32[]{:S(2)}) %collective-permute-start.7) | collective-permute-done | bytes 262176 | tf_op jit(solution)/shard_map/ppermute | solution.py:44
  47.1 0.0 collective-permute-done.10.refs_6_.refs_3_
  47.1 0.4 shard_map.109.after_ref.att_ref.refs_0_
  47.5 0.1 collective-permute-start.13
  47.5 2.0 %collective-permute-start.16 = (bf16[128,1024]{1,0:T(8,128)(2,1)S(1)}, bf16[128,1024]{1,0:T(8,128)(2,1)S(1)}, u32[]{:S(2)}, u32[]{:S(2)}) collective-permute-start(bf16[128,1024]{1,0:T(8,128)(2,1)S(1)} %shard_map.109.after_ref.att_ref.refs_0_), channel_id=1, source_target_pairs={{8,0},{16,8},{24,16},{28,24},{20,28},{12,20},{4,12},{0,4},{9,1},{1... | collective-permute-start | bytes 786440 | tf_op jit(solution)/shard_map/ppermute | solution.py:497
  49.5 0.1 shard_map.112.refs_2_.cols_ref
  49.6 0.1 shard_map.110.refs_0_
  49.7 1.3 %shard_map.111.refs_1_ = f32[128,8,128]{2,1,0:T(8,128)} custom-call(bf16[1024,128]{1,0:T(8,128)(2,1)S(1)} %get-tuple-element.36.after_ref.gt_ref, f32[5,8,128]{2,1,0:T(8,128)S(1)} %get-tuple-element.41.lam_ref, f32[8,128,128]{2,1,0:T(8,128)S(1)} %get-tuple-element.44.dql_ref, bf16[8,128,128]{2,1,0:T(8,128)(2,1)S(1)} %collective-permute-done.7.refs_2_.refs_0_.state_ref, ...), custom_call_target="tpu_custom_call" | custom-call | flops 33554432 | bytes 1572864 | tf_op jit(solution)/shard_map/pallas_call | solution.py:452
  51.0 1.3 %shard_map.113 = (bf16[2,128,1024]{2,1,0:T(8,128)(2,1)S(1)}, f32[2,128,1024]{2,1,0:T(8,128)S(1)}) custom-call(bf16[128,1024]{1,0:T(8,128)(2,1)S(1)} %shard_map.109.after_ref.att_ref.refs_0_, bf16[1024,4096]{1,0:T(8,128)(2,1)S(1)} %get-tuple-element.35.refs_4_.w_ref, bf16[8,128,128]{2,1,0:T(8,128)(2,1)S(1)} %shard_map.110.refs_0_, ...), custom_call_target="tpu_custom_call" | custom-call | flops 1073741824 | bytes 8388608 | tf_op jit(solution)/shard_map/pallas_call | solution.py:461
  52.3 0.1 collective-permute-start.11
  52.4 0.1 collective-permute-start.19
  52.5 3.3 %collective-permute-done.13.refs_1_ = bf16[128,1024]{1,0:T(8,128)(2,1)S(1)} collective-permute-done((bf16[128,1024]{1,0:T(8,128)(2,1)S(1)}, bf16[128,1024]{1,0:T(8,128)(2,1)S(1)}, u32[]{:S(2)}, u32[]{:S(2)}) %collective-permute-start.13) | collective-permute-done | bytes 262176 | tf_op jit(solution)/shard_map/ppermute | solution.py:496
  55.8 0.5 collective-permute-start.14
  56.3 0.0 collective-permute-done.16.refs_2_
  56.3 1.5 %collective-permute-start.17 = (bf16[128,1024]{1,0:T(8,128)(2,1)S(1)}, bf16[128,1024]{1,0:T(8,128)(2,1)S(1)}, u32[]{:S(2)}, u32[]{:S(2)}) collective-permute-start(bf16[128,1024]{1,0:T(8,128)(2,1)S(1)} %collective-permute-done.16.refs_2_), channel_id=1, source_target_pairs={{8,0},{16,8},{24,16},{28,24},{20,28},{12,20},{4,12},{0,4},{9,1},{1... | collective-permute-start | bytes 786440 | tf_op jit(solution)/shard_map/ppermute | solution.py:497
  57.8 3.9 %collective-permute-done.19.refs_1_ = bf16[8,128,128]{2,1,0:T(8,128)(2,1)S(1)} collective-permute-done((bf16[8,128,128]{2,1,0:T(8,128)(2,1)S(1)}, bf16[8,128,128]{2,1,0:T(8,128)(2,1)S(1)}, u32[]{:S(2)}, u32[]{:S(2)}) %collective-permute-start.19) | collective-permute-done | bytes 262176 | tf_op jit(solution)/shard_map/ppermute | solution.py:44
  61.7 0.1 shard_map.116
  61.9 1.2 %collective-permute-start.20 = (bf16[8,128,128]{2,1,0:T(8,128)(2,1)S(1)}, bf16[8,128,128]{2,1,0:T(8,128)(2,1)S(1)}, u32[]{:S(2)}, u32[]{:S(2)}) collective-permute-start(bf16[8,128,128]{2,1,0:T(8,128)(2,1)S(1)} %shard_map.116), channel_id=1, source_target_pairs={{0,4},{4,0},{8,12},{12,8},{16,20},{20,16},{24,28},{28,24},{1,5},{5... | collective-permute-start | bytes 786440 | tf_op jit(solution)/shard_map/ppermute | solution.py:44
  63.1 1.8 %collective-permute-done.14.refs_3_ = bf16[128,1024]{1,0:T(8,128)(2,1)S(1)} collective-permute-done((bf16[128,1024]{1,0:T(8,128)(2,1)S(1)}, bf16[128,1024]{1,0:T(8,128)(2,1)S(1)}, u32[]{:S(2)}, u32[]{:S(2)}) %collective-permute-start.14) | collective-permute-done | bytes 262176 | tf_op jit(solution)/shard_map/ppermute | solution.py:496
  64.8 2.5 %collective-permute-start.15 = (bf16[128,1024]{1,0:T(8,128)(2,1)S(1)}, bf16[128,1024]{1,0:T(8,128)(2,1)S(1)}, u32[]{:S(2)}, u32[]{:S(2)}) collective-permute-start(bf16[128,1024]{1,0:T(8,128)(2,1)S(1)} %collective-permute-done.14.refs_3_), channel_id=1, source_target_pairs={{0,8},{8,16},{16,24},{24,28},{28,20},{20,12},{12,4},{4,0},{1,9},{9... | collective-permute-start | bytes 786440 | tf_op jit(solution)/shard_map/ppermute | solution.py:496
  67.3 0.0 collective-permute-done.17.refs_4_
  67.3 0.7 collective-permute-start.18
  68.0 0.0 collective-permute-done.11
  68.0 0.2 convert_add_fusion
  68.3 1.1 %collective-permute-start.12 = (bf16[1,128,1024]{2,1,0:T(8,128)(2,1)S(1)}, bf16[1,128,1024]{2,1,0:T(8,128)(2,1)S(1)}, u32[]{:S(2)}, u32[]{:S(2)}) collective-permute-start(bf16[1,128,1024]{2,1,0:T(8,128)(2,1)S(1)} %slice.29), channel_id=1, source_target_pairs={{0,2},{1,3},{2,0},{3,1},{4,6},{5,7},{6,4},{7,5},{8,10},{9,11},{10,... | collective-permute-start | bytes 786440 | tf_op jit(solution)/shard_map/ppermute | solution.py:309
  69.4 1.5 %shard_map.114.refs_2_ = f32[1024,512]{1,0:T(8,128)S(1)} custom-call(bf16[8,128,512]{2,1,0:T(8,128)(2,1)S(1)} %shard_map.112.refs_2_.cols_ref, bf16[128,1024]{1,0:T(8,128)(2,1)S(1)} %shard_map.109.after_ref.att_ref.refs_0_, bf16[128,1024]{1,0:T(8,128)(2,1)S(1)} %collective-permute-done.13.refs_1_, bf16[128,1024]{1,0:T(8,128)(2,1)S(1)} %collective-permute-done.16.refs_2_, ...), custom_call_target="tpu_custom_call" | custom-call | flops 671088640 | bytes 2097152 | tf_op jit(solution)/shard_map/pallas_call | solution.py:481
  70.9 4.4 %collective-permute-done.15.refs_0_ = bf16[128,1024]{1,0:T(8,128)(2,1)S(1)} collective-permute-done((bf16[128,1024]{1,0:T(8,128)(2,1)S(1)}, bf16[128,1024]{1,0:T(8,128)(2,1)S(1)}, u32[]{:S(2)}, u32[]{:S(2)}) %collective-permute-start.15) | collective-permute-done | bytes 262176 | tf_op jit(solution)/shard_map/ppermute | solution.py:496
  75.3 0.1 collective-permute-start.21
  75.5 0.0 collective-permute-done.18.refs_1_
  75.5 2.0 %collective-permute-start.22 = (bf16[64,1024]{1,0:T(8,128)(2,1)S(1)}, bf16[64,1024]{1,0:T(8,128)(2,1)S(1)}, u32[]{:S(2)}, u32[]{:S(2)}) collective-permute-start(bf16[64,1024]{1,0:T(8,128)(2,1)S(1)} %slice.22), channel_id=1, source_target_pairs={{8,0},{16,8},{24,16},{28,24},{20,28},{12,20},{4,12},{0,4},{9,1},{1... | collective-permute-start | bytes 393224 | tf_op jit(solution)/shard_map/ppermute | solution.py:507
  77.5 0.7 shard_map.115.after_ref.total_ref
  78.2 0.0 collective-permute-done.20.refs_2_
  78.2 1.7 %shard_map.117 = (f32[128,8,128]{2,1,0:T(8,128)}, f32[128,8,128]{2,1,0:T(8,128)}) custom-call(bf16[8,128,128]{2,1,0:T(8,128)(2,1)S(1)} %get-tuple-element.28.kh_ref, bf16[8,128,128]{2,1,0:T(8,128)(2,1)S(1)} %get-tuple-element.29.vh_ref, f32[8,128,128]{2,1,0:T(8,128)S(1)} %get-tuple-element.42.refs_3_.dkl_ref, f32[8,128,128]{2,1,0:T(8,128)S(1)} %get-tuple-element.47.dvl_ref, ...), custom_call_target="tpu_custom_call" | custom-call | flops 67108864 | bytes 2883584 | tf_op jit(solution)/shard_map/pallas_call | solution.py:509
  80.0 0.0 collective-permute-done.12
  80.0 0.8 fusion.1
  80.7 0.0 collective-permute-done.21.low_ref
  80.7 0.0 collective-permute-done.22.high_ref
  80.7 2.3 %shard_map.118 = f32[1024,512]{1,0:T(8,128)} custom-call(bf16[8,128,512]{2,1,0:T(8,128)(2,1)S(1)} %shard_map.112.refs_2_.cols_ref, bf16[64,1024]{1,0:T(8,128)(2,1)S(1)} %collective-permute-done.21.low_ref, bf16[64,1024]{1,0:T(8,128)(2,1)S(1)} %collective-permute-done.22.high_ref, f32[1024,512]{1,0:T(8,128)S(1)} %shard_map.115.after_ref.total_ref, ...), custom_call_target="tpu_custom_call" | custom-call | flops 134217728 | bytes 4194304 | tf_op jit(solution)/shard_map/pallas_call | solution.py:518
  (5 shorter events, 0.1 us)
Async XLA Ops:
  0.6 16.0 %collective-permute-start.1 = (bf16[128,1024]{1,0:T(8,128)(2,1)}, bf16[128,1024]{1,0:T(8,128)(2,1)S(1)}, u32[]{:S(2)}, u32[]{:S(2)}) collective-permute-start(bf16[128,1024]{1,0:T(8,128)(2,1)} %grad_hbm.1), channel_id=1, source_target_pairs={{0,0},{1,8},{2,16},{3,24},{4,4},{5,12},{6,20},{7,28},{8,1},{9,9},{... | collective-permute-start | bytes 786440 | tf_op jit(solution)/shard_map/ppermute | solution.py:327
  4.7 12.5 %collective-permute-start = (bf16[8,128,128]{2,1,0:T(8,128)(2,1)S(1)}, bf16[8,128,128]{2,1,0:T(8,128)(2,1)S(1)}, u32[]{:S(2)}, u32[]{:S(2)}) collective-permute-start(bf16[8,128,128]{2,1,0:T(8,128)(2,1)S(1)} %get-tuple-element.32.running_ref), channel_id=1, source_target_pairs={{0,4},{4,0},{8,12},{12,8},{16,20},{20,16},{24,28},{28,24},{1,5},{5... | collective-permute-start | bytes 786440 | tf_op jit(solution)/shard_map/ppermute | solution.py:44
  7.7 9.7 %collective-permute-start.3 = (bf16[128,1024]{1,0:T(8,128)(2,1)S(1)}, bf16[128,1024]{1,0:T(8,128)(2,1)S(1)}, u32[]{:S(2)}, u32[]{:S(2)}) collective-permute-start(bf16[128,1024]{1,0:T(8,128)(2,1)S(1)} %get-tuple-element.34.refs_0_), channel_id=1, source_target_pairs={{0,1},{1,0},{2,3},{3,2},{4,5},{5,4},{6,7},{7,6},{8,9},{9,8},{10,11... | collective-permute-start | bytes 786440 | tf_op jit(solution)/shard_map/ppermute | solution.py:309
  9.4 13.2 %collective-permute-start.4 = (bf16[128,1024]{1,0:T(8,128)(2,1)S(1)}, bf16[128,1024]{1,0:T(8,128)(2,1)S(1)}, u32[]{:S(2)}, u32[]{:S(2)}) collective-permute-start(bf16[128,1024]{1,0:T(8,128)(2,1)S(1)} %get-tuple-element.34.refs_0_), channel_id=1, source_target_pairs={{0,2},{1,3},{2,0},{3,1},{4,6},{5,7},{6,4},{7,5},{8,10},{9,11},{10,... | collective-permute-start | bytes 786440 | tf_op jit(solution)/shard_map/ppermute | solution.py:309
  12.9 14.9 %collective-permute-start.5 = (bf16[128,1024]{1,0:T(8,128)(2,1)S(1)}, bf16[128,1024]{1,0:T(8,128)(2,1)S(1)}, u32[]{:S(2)}, u32[]{:S(2)}) collective-permute-start(bf16[128,1024]{1,0:T(8,128)(2,1)S(1)} %get-tuple-element.34.refs_0_), channel_id=1, source_target_pairs={{0,3},{1,2},{2,1},{3,0},{4,7},{5,6},{6,5},{7,4},{8,11},{9,10},{10,... | collective-permute-start | bytes 786440 | tf_op jit(solution)/shard_map/ppermute | solution.py:309
  16.7 14.0 %collective-permute-start.6 = (bf16[128,512]{1,0:T(8,128)(2,1)S(1)}, bf16[128,512]{1,0:T(8,128)(2,1)S(1)}, u32[]{:S(2)}, u32[]{:S(2)}) collective-permute-start(bf16[128,512]{1,0:T(8,128)(2,1)S(1)} %get-tuple-element.33.refs_0_.refs_6_), channel_id=1, source_target_pairs={{0,4},{4,0},{8,12},{12,8},{16,20},{20,16},{24,28},{28,24},{1,5},{5... | collective-permute-start | bytes 393224 | tf_op jit(solution)/shard_map/ppermute | solution.py:359
  17.3 15.5 %collective-permute-start.2 = (bf16[8,128,128]{2,1,0:T(8,128)(2,1)S(1)}, bf16[8,128,128]{2,1,0:T(8,128)(2,1)S(1)}, u32[]{:S(2)}, u32[]{:S(2)}) collective-permute-start(bf16[8,128,128]{2,1,0:T(8,128)(2,1)S(1)} %shard_map.104.running_ref), channel_id=1, source_target_pairs={{0,8},{8,0},{4,12},{12,4},{16,24},{24,16},{20,28},{28,20},{1,9},{9... | collective-permute-start | bytes 786440 | tf_op jit(solution)/shard_map/ppermute | solution.py:44
  30.7 8.8 %collective-permute-start.9 = (bf16[2,128,512]{2,1,0:T(8,128)(2,1)S(1)}, bf16[2,128,512]{2,1,0:T(8,128)(2,1)S(1)}, u32[]{:S(2)}, u32[]{:S(2)}) collective-permute-start(bf16[2,128,512]{2,1,0:T(8,128)(2,1)S(1)} %shard_map.106.after_ref.refs_0_), channel_id=1, source_target_pairs={{0,2},{1,3},{2,0},{3,1},{4,6},{5,7},{6,4},{7,5},{8,10},{9,11},{10,... | collective-permute-start | bytes 786440 | tf_op jit(solution)/shard_map/ppermute | solution.py:309
  32.8 8.0 %collective-permute-start.8 = (bf16[2,128,512]{2,1,0:T(8,128)(2,1)S(1)}, bf16[2,128,512]{2,1,0:T(8,128)(2,1)S(1)}, u32[]{:S(2)}, u32[]{:S(2)}) collective-permute-start(bf16[2,128,512]{2,1,0:T(8,128)(2,1)S(1)} %shard_map.106.after_ref.refs_0_), channel_id=1, source_target_pairs={{0,1},{1,0},{2,3},{3,2},{4,5},{5,4},{6,7},{7,6},{8,9},{9,8},{10,11... | collective-permute-start | bytes 786440 | tf_op jit(solution)/shard_map/ppermute | solution.py:309
  32.9 14.2 %collective-permute-start.7 = (bf16[8,128,128]{2,1,0:T(8,128)(2,1)S(1)}, bf16[8,128,128]{2,1,0:T(8,128)(2,1)S(1)}, u32[]{:S(2)}, u32[]{:S(2)}) collective-permute-start(bf16[8,128,128]{2,1,0:T(8,128)(2,1)S(1)} %shard_map.107.after_ref), channel_id=1, source_target_pairs={{0,16},{16,0},{4,20},{20,4},{8,24},{24,8},{12,28},{28,12},{1,17},{... | collective-permute-start | bytes 786440 | tf_op jit(solution)/shard_map/ppermute | solution.py:44
  39.5 7.5 %collective-permute-start.10 = (bf16[2,128,512]{2,1,0:T(8,128)(2,1)S(1)}, bf16[2,128,512]{2,1,0:T(8,128)(2,1)S(1)}, u32[]{:S(2)}, u32[]{:S(2)}) collective-permute-start(bf16[2,128,512]{2,1,0:T(8,128)(2,1)S(1)} %collective-permute-done.9.refs_5_.refs_2_), channel_id=1, source_target_pairs={{0,1},{1,0},{2,3},{3,2},{4,5},{5,4},{6,7},{7,6},{8,9},{9,8},{10,11... | collective-permute-start | bytes 786440 | tf_op jit(solution)/shard_map/ppermute | solution.py:309
  47.5 8.3 %collective-permute-start.13 = (bf16[128,1024]{1,0:T(8,128)(2,1)S(1)}, bf16[128,1024]{1,0:T(8,128)(2,1)S(1)}, u32[]{:S(2)}, u32[]{:S(2)}) collective-permute-start(bf16[128,1024]{1,0:T(8,128)(2,1)S(1)} %shard_map.109.after_ref.att_ref.refs_0_), channel_id=1, source_target_pairs={{0,8},{8,16},{16,24},{24,28},{28,20},{20,12},{12,4},{4,0},{1,9},{9... | collective-permute-start | bytes 786440 | tf_op jit(solution)/shard_map/ppermute | solution.py:496
  47.5 8.8 %collective-permute-start.16 = (bf16[128,1024]{1,0:T(8,128)(2,1)S(1)}, bf16[128,1024]{1,0:T(8,128)(2,1)S(1)}, u32[]{:S(2)}, u32[]{:S(2)}) collective-permute-start(bf16[128,1024]{1,0:T(8,128)(2,1)S(1)} %shard_map.109.after_ref.att_ref.refs_0_), channel_id=1, source_target_pairs={{8,0},{16,8},{24,16},{28,24},{20,28},{12,20},{4,12},{0,4},{9,1},{1... | collective-permute-start | bytes 786440 | tf_op jit(solution)/shard_map/ppermute | solution.py:497
  52.3 15.7 %collective-permute-start.11 = (bf16[2,128,1024]{2,1,0:T(8,128)(2,1)S(1)}, bf16[2,128,1024]{2,1,0:T(8,128)(2,1)S(1)}, u32[]{:S(2)}, u32[]{:S(2)}) collective-permute-start(bf16[2,128,1024]{2,1,0:T(8,128)(2,1)S(1)} %get-tuple-element.46), channel_id=1, source_target_pairs={{0,1},{1,0},{2,3},{3,2},{4,5},{5,4},{6,7},{7,6},{8,9},{9,8},{10,11... | collective-permute-start | bytes 1572872 | tf_op jit(solution)/shard_map/ppermute | solution.py:309
  52.4 9.3 %collective-permute-start.19 = (bf16[8,128,128]{2,1,0:T(8,128)(2,1)S(1)}, bf16[8,128,128]{2,1,0:T(8,128)(2,1)S(1)}, u32[]{:S(2)}, u32[]{:S(2)}) collective-permute-start(bf16[8,128,128]{2,1,0:T(8,128)(2,1)S(1)} %shard_map.110.refs_0_), channel_id=1, source_target_pairs={{0,8},{8,0},{4,12},{12,4},{16,24},{24,16},{20,28},{28,20},{1,9},{9... | collective-permute-start | bytes 786440 | tf_op jit(solution)/shard_map/ppermute | solution.py:44
  55.8 9.0 %collective-permute-start.14 = (bf16[128,1024]{1,0:T(8,128)(2,1)S(1)}, bf16[128,1024]{1,0:T(8,128)(2,1)S(1)}, u32[]{:S(2)}, u32[]{:S(2)}) collective-permute-start(bf16[128,1024]{1,0:T(8,128)(2,1)S(1)} %collective-permute-done.13.refs_1_), channel_id=1, source_target_pairs={{0,8},{8,16},{16,24},{24,28},{28,20},{20,12},{12,4},{4,0},{1,9},{9... | collective-permute-start | bytes 786440 | tf_op jit(solution)/shard_map/ppermute | solution.py:496
  56.3 11.0 %collective-permute-start.17 = (bf16[128,1024]{1,0:T(8,128)(2,1)S(1)}, bf16[128,1024]{1,0:T(8,128)(2,1)S(1)}, u32[]{:S(2)}, u32[]{:S(2)}) collective-permute-start(bf16[128,1024]{1,0:T(8,128)(2,1)S(1)} %collective-permute-done.16.refs_2_), channel_id=1, source_target_pairs={{8,0},{16,8},{24,16},{28,24},{20,28},{12,20},{4,12},{0,4},{9,1},{1... | collective-permute-start | bytes 786440 | tf_op jit(solution)/shard_map/ppermute | solution.py:497
  61.9 16.4 %collective-permute-start.20 = (bf16[8,128,128]{2,1,0:T(8,128)(2,1)S(1)}, bf16[8,128,128]{2,1,0:T(8,128)(2,1)S(1)}, u32[]{:S(2)}, u32[]{:S(2)}) collective-permute-start(bf16[8,128,128]{2,1,0:T(8,128)(2,1)S(1)} %shard_map.116), channel_id=1, source_target_pairs={{0,4},{4,0},{8,12},{12,8},{16,20},{20,16},{24,28},{28,24},{1,5},{5... | collective-permute-start | bytes 786440 | tf_op jit(solution)/shard_map/ppermute | solution.py:44
  64.8 10.5 %collective-permute-start.15 = (bf16[128,1024]{1,0:T(8,128)(2,1)S(1)}, bf16[128,1024]{1,0:T(8,128)(2,1)S(1)}, u32[]{:S(2)}, u32[]{:S(2)}) collective-permute-start(bf16[128,1024]{1,0:T(8,128)(2,1)S(1)} %collective-permute-done.14.refs_3_), channel_id=1, source_target_pairs={{0,8},{8,16},{16,24},{24,28},{28,20},{20,12},{12,4},{4,0},{1,9},{9... | collective-permute-start | bytes 786440 | tf_op jit(solution)/shard_map/ppermute | solution.py:496
  67.3 8.2 %collective-permute-start.18 = (bf16[128,1024]{1,0:T(8,128)(2,1)S(1)}, bf16[128,1024]{1,0:T(8,128)(2,1)S(1)}, u32[]{:S(2)}, u32[]{:S(2)}) collective-permute-start(bf16[128,1024]{1,0:T(8,128)(2,1)S(1)} %collective-permute-done.17.refs_4_), channel_id=1, source_target_pairs={{8,0},{16,8},{24,16},{28,24},{20,28},{12,20},{4,12},{0,4},{9,1},{1... | collective-permute-start | bytes 786440 | tf_op jit(solution)/shard_map/ppermute | solution.py:497
  68.3 11.7 %collective-permute-start.12 = (bf16[1,128,1024]{2,1,0:T(8,128)(2,1)S(1)}, bf16[1,128,1024]{2,1,0:T(8,128)(2,1)S(1)}, u32[]{:S(2)}, u32[]{:S(2)}) collective-permute-start(bf16[1,128,1024]{2,1,0:T(8,128)(2,1)S(1)} %slice.29), channel_id=1, source_target_pairs={{0,2},{1,3},{2,0},{3,1},{4,6},{5,7},{6,4},{7,5},{8,10},{9,11},{10,... | collective-permute-start | bytes 786440 | tf_op jit(solution)/shard_map/ppermute | solution.py:309
  75.3 5.4 %collective-permute-start.21 = (bf16[64,1024]{1,0:T(8,128)(2,1)S(1)}, bf16[64,1024]{1,0:T(8,128)(2,1)S(1)}, u32[]{:S(2)}, u32[]{:S(2)}) collective-permute-start(bf16[64,1024]{1,0:T(8,128)(2,1)S(1)} %slice.21), channel_id=1, source_target_pairs={{0,8},{8,16},{16,24},{24,28},{28,20},{20,12},{12,4},{4,0},{1,9},{9... | collective-permute-start | bytes 393224 | tf_op jit(solution)/shard_map/ppermute | solution.py:506
  75.5 5.3 %collective-permute-start.22 = (bf16[64,1024]{1,0:T(8,128)(2,1)S(1)}, bf16[64,1024]{1,0:T(8,128)(2,1)S(1)}, u32[]{:S(2)}, u32[]{:S(2)}) collective-permute-start(bf16[64,1024]{1,0:T(8,128)(2,1)S(1)} %slice.22), channel_id=1, source_target_pairs={{8,0},{16,8},{24,16},{28,24},{20,28},{12,20},{4,12},{0,4},{9,1},{1... | collective-permute-start | bytes 393224 | tf_op jit(solution)/shard_map/ppermute | solution.py:507

commit v3 on v2

--- a/solution.py
+++ b/solution.py
@@ -155,8 +155,7 @@
     refs[-1][...] = (running_ref[...].astype(F32) + arrived_ref[...].astype(F32)).astype(BF)
 
 
-def meet_kernel(top, after_ref, grad_ref, running_ref, arrived_ref, out_ref):
-    del after_ref
+def meet_kernel(top, grad_ref, running_ref, arrived_ref, out_ref):
     upper = (lax.axis_index("seq") >> top & 1) == 1
     running = running_ref[...].astype(F32)
     if arrived_ref is not None:
@@ -178,6 +177,16 @@
     out_ref[...] = (own_ref[...].astype(F32) + landed_sum(top, landed)).astype(BF)
 
 
+def turned_group(high, group, bits):
+    turned = high >> 1 | (high & 1) << bits - 1
+    return turned ^ ((group >> bits - 1 ^ group) & 1) << bits - 1
+
+
+def turned_high(turned, group, bits):
+    turned = turned ^ ((group >> bits - 1 ^ group) & 1) << bits - 1
+    return (turned << 1 & (1 << bits) - 1) | turned >> bits - 1
+
+
 def chunk_kernel(block_ref, after_ref, *outs):
     del after_ref
     columns = outs[0].shape[1]
@@ -195,10 +204,12 @@
 def columns_kernel(blocks, *refs):
     parts, out_ref = refs[:blocks], refs[blocks]
     per = parts[0].shape[0]
+    bits = blocks.bit_length() - 1
     low = lax.axis_index("seq") % per
     for i in range(blocks):
+        high = turned_high(lax.axis_index("head") ^ i, lax.axis_index("seq") // per, bits)
         for r in range(per):
-            out_ref[(lax.axis_index("head") ^ i) * per + (low ^ r)] = parts[i][r]
+            out_ref[high * per + (low ^ r)] = parts[i][r]
 
 
 def local_grad_kernel(
@@ -319,7 +330,10 @@
 
     per = devices // heads
     route = [
-        ((high * per + low) * heads + group_at, (group_at * per + low) * heads + high)
+        (
+            (high * per + low) * heads + group_at,
+            (group_at * per + low) * heads + turned_group(high, group_at, head_bits),
+        )
         for high in range(heads)
         for low in range(per)
         for group_at in range(heads)
@@ -383,6 +397,21 @@
         cost_estimate=cost(2 * rows * width * out_proj.shape[1], 2 * width * out_proj.shape[1]),
     )(*grad_blocks, w, qw, own_chunks[-1])
 
+    meeting = pl.pallas_call(
+        functools.partial(meet_kernel, top)
+        if arrived is not None
+        else lambda grad_ref, running_ref, out_ref: meet_kernel(
+            top, grad_ref, running_ref, None, out_ref
+        ),
+        out_shape=head_state,
+        in_specs=[VMEM] * (2 if arrived is None else 3),
+        out_specs=VMEM,
+        compiler_params=PARAMS,
+        cost_estimate=cost(0, 4 * moved_head),
+    )(grad_sums[top], running, *([] if arrived is None else [arrived]))
+    landed = [across(meeting, "seq", top)]
+    partner_states.append(landed[0])
+
     stacked = pl.pallas_call(
         stack_kernel,
         out_shape=like((per, rows, columns_dev), BF),
@@ -390,23 +419,8 @@
         out_specs=VMEM,
         compiler_params=PARAMS,
         cost_estimate=cost(0, 2 * moved_head),
-    )(gt, *chunks)
-    column_blocks = every_group(stacked)
-
-    meeting = pl.pallas_call(
-        functools.partial(meet_kernel, top)
-        if arrived is not None
-        else lambda after_ref, grad_ref, running_ref, out_ref: meet_kernel(
-            top, after_ref, grad_ref, running_ref, None, out_ref
-        ),
-        out_shape=head_state,
-        in_specs=[ANY] + [VMEM] * (2 if arrived is None else 3),
-        out_specs=VMEM,
-        compiler_params=PARAMS,
-        cost_estimate=cost(0, 4 * moved_head),
-    )(stacked, grad_sums[top], running, *([] if arrived is None else [arrived]))
-    landed = [across(meeting, "seq", top)]
-    partner_states.append(landed[0])
+    )(meeting, *chunks)
+    column_blocks = [stacked] + [to_group(stacked, i) for i in range(1, heads)]
 
     grad_columns = pl.pallas_call(
         functools.partial(columns_kernel, heads),
@@ -429,11 +443,11 @@
     attended = pl.pallas_call(
         functools.partial(attended_kernel, seq_bits),
         out_shape=like((rows, width), BF),
-        in_specs=[VMEM] * (2 + seq_bits) + [ANY] * heads,
+        in_specs=[VMEM] * (2 + seq_bits) + [ANY] * 2,
         out_specs=VMEM,
         compiler_params=PARAMS,
         cost_estimate=cost(seq_bits * flops_head, 8 * moved_head),
-    )(att_local, qw, *partner_states, key_local, *column_blocks[1:])
+    )(att_local, qw, *partner_states, key_local, stacked)
 
     first_pending = attended
     for digit in reversed(range(top)):

time: 83.3 us -> 79.1 us (0.950)
  waiting for transfers between devices: 36.6 us -> 27.3 us
  starting transfers between devices: 24.6 us -> 29.8 us
    ppermute x8, waiting for transfers between devices: 17 us -> 6.05 us  [to_group(): return lax.ppermute(block, 'head', [(at, at ^ i) for at in range(heads)])]
    ppermute x5, starting transfers between devices: 4.49 us -> 8.39 us  [across(): return lax.ppermute(block, axis, route)]
    ppermute x5, waiting for transfers between devices: 10.2 us -> 13.8 us  [across(): return lax.ppermute(block, axis, route)]
    ppermute x3, waiting for transfers between devices: 9.41 us -> 7.34 us  [body(): ahead = lax.ppermute(ahead, 'seq', forward)]
  transfers between devices with their start and end apart: 23 -> 23, of which waited for: 8 -> 7; matrix products, arithmetic and copies ran while one was open for 1% -> 1% of each run, Pallas kernels for 21% -> 22%
where the time goes in v3:
time: 79.1 us; the launch traced here: 78.9 us
  starting transfers between devices  29.8 us (38%)
  waiting for transfers between devices  27.3 us (35%)
  Pallas kernels  20.1 us (25%)
  other arithmetic  0.94 us (1%)
  between operations  0.81 us (1%)
    ppermute x5, waiting for transfers between devices, across(): return lax.ppermute(block, axis, route)  13.8 us
    ppermute x8, starting transfers between devices, to_group(): return lax.ppermute(block, 'head', [(at, at ^ i) for at in range(heads)])  9.21 us
    ppermute x5, starting transfers between devices, across(): return lax.ppermute(block, axis, route)  8.39 us
    ppermute x3, waiting for transfers between devices, body(): ahead = lax.ppermute(ahead, 'seq', forward)  7.34 us
    ppermute x8, waiting for transfers between devices, to_group(): return lax.ppermute(block, 'head', [(at, at ^ i) for at in range(heads)])  6.05 us
    ppermute x3, starting transfers between devices, body(): ahead = lax.ppermute(ahead, 'seq', forward)  3.87 us
    pallas_call x1, Pallas kernels, body(): pl.pallas_call(local_kernel, out_shape=(pltpu.VMEM((heads_dev, rows, rows...  3.66 us
    ppermute x3, starting transfers between devices, body(): behind = lax.ppermute(behind, 'seq', backward)  3.51 us
  transfers between devices with their start and end apart: 23, of which 7 were waited for; matrix products, arithmetic and copies ran while one was open for 1% of the time, Pallas kernels for 22%

profile of v3, /device:TPU:0, one launch (start us, length us, event | category | flops | bytes accessed | tf_op | source)
XLA Modules:
  0.0 78.9 jit_solution(4261131276640662065)
XLA Ops:
  0.6 1.6 %collective-permute-start.1 = (bf16[128,1024]{1,0:T(8,128)(2,1)}, bf16[128,1024]{1,0:T(8,128)(2,1)S(1)}, u32[]{:S(2)}, u32[]{:S(2)}) collective-permute-start(bf16[128,1024]{1,0:T(8,128)(2,1)} %grad_hbm.1), channel_id=1, source_target_pairs={{0,0},{1,10},{2,18},{3,24},{4,4},{5,14},{6,22},{7,28},{8,2},{9,8},... | collective-permute-start | bytes 786440 | tf_op jit(solution)/shard_map/ppermute | solution.py:341
  2.2 2.4 %shard_map.101 = (bf16[8,128,128]{2,1,0:T(8,128)(2,1)S(1)}, bf16[8,128,128]{2,1,0:T(8,128)(2,1)S(1)}, bf16[8,128,128]{2,1,0:T(8,128)(2,1)S(1)}, bf16[128,1024]{1,0:T(8,128)(2,1)S(1)}) custom-call(f32[128,8,128]{2,1,0:T(8,128)} %k_hbm.1, f32[128,8,128]{2,1,0:T(8,128)} %v_hbm.1, bf16[128,1024]{1,0:T(8,128)(2,1)} %grad_hbm.1), custom_call_target="tpu_custom_call" | custom-call | flops 33554432 | bytes 1835008 | tf_op jit(solution)/shard_map/pallas_call | solution.py:305
  4.7 3.0 %collective-permute-start = (bf16[8,128,128]{2,1,0:T(8,128)(2,1)S(1)}, bf16[8,128,128]{2,1,0:T(8,128)(2,1)S(1)}, u32[]{:S(2)}, u32[]{:S(2)}) collective-permute-start(bf16[8,128,128]{2,1,0:T(8,128)(2,1)S(1)} %get-tuple-element.32.running_ref), channel_id=1, source_target_pairs={{0,4},{4,0},{8,12},{12,8},{16,20},{20,16},{24,28},{28,24},{1,5},{5... | collective-permute-start | bytes 786440 | tf_op jit(solution)/shard_map/ppermute | solution.py:44
  7.7 2.6 %collective-permute-start.3 = (bf16[128,1024]{1,0:T(8,128)(2,1)S(1)}, bf16[128,1024]{1,0:T(8,128)(2,1)S(1)}, u32[]{:S(2)}, u32[]{:S(2)}) collective-permute-start(bf16[128,1024]{1,0:T(8,128)(2,1)S(1)} %get-tuple-element.34.refs_0_), channel_id=1, source_target_pairs={{0,1},{1,0},{2,3},{3,2},{4,5},{5,4},{6,7},{7,6},{8,9},{9,8},{10,11... | collective-permute-start | bytes 786440 | tf_op jit(solution)/shard_map/ppermute | solution.py:320
  10.4 2.6 %collective-permute-start.4 = (bf16[128,1024]{1,0:T(8,128)(2,1)S(1)}, bf16[128,1024]{1,0:T(8,128)(2,1)S(1)}, u32[]{:S(2)}, u32[]{:S(2)}) collective-permute-start(bf16[128,1024]{1,0:T(8,128)(2,1)S(1)} %get-tuple-element.34.refs_0_), channel_id=1, source_target_pairs={{0,2},{1,3},{2,0},{3,1},{4,6},{5,7},{6,4},{7,5},{8,10},{9,11},{10,... | collective-permute-start | bytes 786440 | tf_op jit(solution)/shard_map/ppermute | solution.py:320
  12.9 0.0 collective-permute-start.5
  12.9 3.7 %shard_map.102 = (bf16[8,128,128]{2,1,0:T(8,128)(2,1)S(1)}, f32[8,128,128]{2,1,0:T(8,128)S(1)}, bf16[8,128,128]{2,1,0:T(8,128)(2,1)S(1)}, bf16[3,8,128,128]{3,2,...) custom-call(f32[128,8,128]{2,1,0:T(8,128)} %q_hbm.1, ...), custom_call_target="tpu_custom_call" | custom-call | flops 67108864 | bytes 3145728 | tf_op jit(solution)/shard_map/pallas_call | solution.py:342
  16.6 0.0 collective-permute-done.1.block_ref
  16.7 0.0 collective-permute-done.arrived_ref.refs_0_
  16.7 0.1 shard_map.104.running_ref
  16.7 0.7 collective-permute-start.2
  17.4 1.1 %collective-permute-start.7 = (bf16[128,512]{1,0:T(8,128)(2,1)S(1)}, bf16[128,512]{1,0:T(8,128)(2,1)S(1)}, u32[]{:S(2)}, u32[]{:S(2)}) collective-permute-start(bf16[128,512]{1,0:T(8,128)(2,1)S(1)} %get-tuple-element.33.refs_0_.refs_6_), channel_id=1, source_target_pairs={{0,4},{4,0},{8,12},{12,8},{16,20},{20,16},{24,28},{28,24},{1,5},{5... | collective-permute-start | bytes 393224 | tf_op jit(solution)/shard_map/ppermute | solution.py:373
  18.5 0.0 collective-permute-done.3.refs_1_
  18.5 1.6 %collective-permute-done.4.refs_2_ = bf16[128,1024]{1,0:T(8,128)(2,1)S(1)} collective-permute-done((bf16[128,1024]{1,0:T(8,128)(2,1)S(1)}, bf16[128,1024]{1,0:T(8,128)(2,1)S(1)}, u32[]{:S(2)}, u32[]{:S(2)}) %collective-permute-start.4) | collective-permute-done | bytes 262176 | tf_op jit(solution)/shard_map/ppermute | solution.py:320
  20.1 4.5 %collective-permute-done.5.refs_3_ = bf16[128,1024]{1,0:T(8,128)(2,1)S(1)} collective-permute-done((bf16[128,1024]{1,0:T(8,128)(2,1)S(1)}, bf16[128,1024]{1,0:T(8,128)(2,1)S(1)}, u32[]{:S(2)}, u32[]{:S(2)}) %collective-permute-start.5) | collective-permute-done | bytes 262176 | tf_op jit(solution)/shard_map/ppermute | solution.py:320
  24.5 2.8 %shard_map.105 = (bf16[1024,128]{1,0:T(8,128)(2,1)S(1)}, bf16[8,128,128]{2,1,0:T(8,128)(2,1)S(1)}, bf16[8,128,128]{2,1,0:T(8,128)(2,1)S(1)}, bf16[8,128,128]{2,1,0:T(8,128)(2,1)S(1)}) custom-call(bf16[128,1024]{1,0:T(8,128)(2,1)S(1)} %get-tuple-element.34.refs_0_, bf16[128,1024]{1,0:T(8,128)(2,1)S(1)} %collective-permute-done.3.refs_1_, ...), custom_call_target="tpu_custom_call" | custom-call | flops 1073741824 | bytes 8388608 | tf_op jit(solution)/shard_map/pallas_call | solution.py:391
  27.3 0.0 collective-permute-done.2.arrived_ref.refs_1_
  27.3 0.1 shard_map.106.after_ref
  27.4 2.7 %collective-permute-start.6 = (bf16[8,128,128]{2,1,0:T(8,128)(2,1)S(1)}, bf16[8,128,128]{2,1,0:T(8,128)(2,1)S(1)}, u32[]{:S(2)}, u32[]{:S(2)}) collective-permute-start(bf16[8,128,128]{2,1,0:T(8,128)(2,1)S(1)} %shard_map.106.after_ref), channel_id=1, source_target_pairs={{0,16},{16,0},{4,20},{20,4},{8,24},{24,8},{12,28},{28,12},{1,17},{... | collective-permute-start | bytes 786440 | tf_op jit(solution)/shard_map/ppermute | solution.py:44
  30.2 0.0 collective-permute-done.7.refs_1_
  30.2 0.4 collective-permute-start.8
  30.6 0.0 collective-permute-start.9
  30.6 1.5 %collective-permute-start.10 = (bf16[2,128,512]{2,1,0:T(8,128)(2,1)S(1)}, bf16[2,128,512]{2,1,0:T(8,128)(2,1)S(1)}, u32[]{:S(2)}, u32[]{:S(2)}) collective-permute-start(bf16[2,128,512]{2,1,0:T(8,128)(2,1)S(1)} %shard_map.108.refs_4_.refs_0_), channel_id=1, source_target_pairs={{0,3},{1,2},{2,1},{3,0},{4,7},{5,6},{6,5},{7,4},{8,11},{9,10},{10,... | collective-permute-start | bytes 786440 | tf_op jit(solution)/shard_map/ppermute | solution.py:320
  32.1 1.3 %shard_map.107 = (f32[8,128,128]{2,1,0:T(8,128)S(1)}, f32[8,128,128]{2,1,0:T(8,128)S(1)}, f32[8,128,128]{2,1,0:T(8,128)S(1)}) custom-call(bf16[1024,128]{1,0:T(8,128)(2,1)S(1)} %get-tuple-element.37.gt_ref, bf16[8,128,128]{2,1,0:T(8,128)(2,1)S(1)} %get-tuple-element.38.qh_ref, bf16[8,128,128]{2,1,0:T(8,128)(2,1)S(1)} %get-tuple-element.28.kh_ref, ...), custom_call_target="tpu_custom_call" | custom-call | flops 201326592 | bytes 3670016 | tf_op jit(solution)/shard_map/pallas_call | solution.py:434
  33.4 9.5 %collective-permute-done.6.refs_2_.refs_0_.state_ref = bf16[8,128,128]{2,1,0:T(8,128)(2,1)S(1)} collective-permute-done((bf16[8,128,128]{2,1,0:T(8,128)(2,1)S(1)}, bf16[8,128,128]{2,1,0:T(8,128)(2,1)S(1)}, u32[]{:S(2)}, u32[]{:S(2)}) %collective-permute-start.6) | collective-permute-done | bytes 262176 | tf_op jit(solution)/shard_map/ppermute | solution.py:44
  42.9 0.4 shard_map.109.after_ref.att_ref.refs_0_
  43.3 0.7 collective-permute-start.13
  43.9 1.4 %collective-permute-start.16 = (bf16[128,1024]{1,0:T(8,128)(2,1)S(1)}, bf16[128,1024]{1,0:T(8,128)(2,1)S(1)}, u32[]{:S(2)}, u32[]{:S(2)}) collective-permute-start(bf16[128,1024]{1,0:T(8,128)(2,1)S(1)} %shard_map.109.after_ref.att_ref.refs_0_), channel_id=1, source_target_pairs={{8,0},{16,8},{24,16},{28,24},{20,28},{12,20},{4,12},{0,4},{9,1},{1... | collective-permute-start | bytes 786440 | tf_op jit(solution)/shard_map/ppermute | solution.py:511
  45.3 0.1 shard_map.110.refs_0_
  45.4 1.3 %shard_map.111.refs_1_ = f32[128,8,128]{2,1,0:T(8,128)} custom-call(bf16[1024,128]{1,0:T(8,128)(2,1)S(1)} %get-tuple-element.37.gt_ref, f32[5,8,128]{2,1,0:T(8,128)S(1)} %get-tuple-element.40.lam_ref, f32[8,128,128]{2,1,0:T(8,128)S(1)} %get-tuple-element.44.dql_ref, bf16[8,128,128]{2,1,0:T(8,128)(2,1)S(1)} %collective-permute-done.6.refs_2_.refs_0_.state_ref, ...), custom_call_target="tpu_custom_call" | custom-call | flops 33554432 | bytes 1572864 | tf_op jit(solution)/shard_map/pallas_call | solution.py:466
  46.8 0.0 collective-permute-done.8.refs_1_
  46.8 0.0 collective-permute-done.9.refs_2_
  46.8 0.0 collective-permute-done.10.refs_3_
  46.8 0.1 shard_map.112.refs_2_.cols_ref
  46.9 1.3 %shard_map.113 = (bf16[2,128,1024]{2,1,0:T(8,128)(2,1)S(1)}, f32[2,128,1024]{2,1,0:T(8,128)S(1)}) custom-call(bf16[128,1024]{1,0:T(8,128)(2,1)S(1)} %shard_map.109.after_ref.att_ref.refs_0_, bf16[1024,4096]{1,0:T(8,128)(2,1)S(1)} %get-tuple-element.35.refs_4_.w_ref, bf16[8,128,128]{2,1,0:T(8,128)(2,1)S(1)} %shard_map.110.refs_0_, ...), custom_call_target="tpu_custom_call" | custom-call | flops 1073741824 | bytes 8388608 | tf_op jit(solution)/shard_map/pallas_call | solution.py:475
  48.1 0.1 collective-permute-start.11
  48.2 0.7 collective-permute-start.19
  48.9 2.4 %collective-permute-done.13.refs_1_ = bf16[128,1024]{1,0:T(8,128)(2,1)S(1)} collective-permute-done((bf16[128,1024]{1,0:T(8,128)(2,1)S(1)}, bf16[128,1024]{1,0:T(8,128)(2,1)S(1)}, u32[]{:S(2)}, u32[]{:S(2)}) %collective-permute-start.13) | collective-permute-done | bytes 262176 | tf_op jit(solution)/shard_map/ppermute | solution.py:510
  51.3 0.7 collective-permute-start.14
  52.0 0.0 collective-permute-done.16.refs_2_
  52.1 1.3 %collective-permute-start.17 = (bf16[128,1024]{1,0:T(8,128)(2,1)S(1)}, bf16[128,1024]{1,0:T(8,128)(2,1)S(1)}, u32[]{:S(2)}, u32[]{:S(2)}) collective-permute-start(bf16[128,1024]{1,0:T(8,128)(2,1)S(1)} %collective-permute-done.16.refs_2_), channel_id=1, source_target_pairs={{8,0},{16,8},{24,16},{28,24},{20,28},{12,20},{4,12},{0,4},{9,1},{1... | collective-permute-start | bytes 786440 | tf_op jit(solution)/shard_map/ppermute | solution.py:511
  53.3 4.4 %collective-permute-done.19.refs_1_ = bf16[8,128,128]{2,1,0:T(8,128)(2,1)S(1)} collective-permute-done((bf16[8,128,128]{2,1,0:T(8,128)(2,1)S(1)}, bf16[8,128,128]{2,1,0:T(8,128)(2,1)S(1)}, u32[]{:S(2)}, u32[]{:S(2)}) %collective-permute-start.19) | collective-permute-done | bytes 262176 | tf_op jit(solution)/shard_map/ppermute | solution.py:44
  57.7 0.1 shard_map.116
  57.8 1.3 %collective-permute-start.20 = (bf16[8,128,128]{2,1,0:T(8,128)(2,1)S(1)}, bf16[8,128,128]{2,1,0:T(8,128)(2,1)S(1)}, u32[]{:S(2)}, u32[]{:S(2)}) collective-permute-start(bf16[8,128,128]{2,1,0:T(8,128)(2,1)S(1)} %shard_map.116), channel_id=1, source_target_pairs={{0,4},{4,0},{8,12},{12,8},{16,20},{20,16},{24,28},{28,24},{1,5},{5... | collective-permute-start | bytes 786440 | tf_op jit(solution)/shard_map/ppermute | solution.py:44
  59.1 1.7 %collective-permute-done.14.refs_3_ = bf16[128,1024]{1,0:T(8,128)(2,1)S(1)} collective-permute-done((bf16[128,1024]{1,0:T(8,128)(2,1)S(1)}, bf16[128,1024]{1,0:T(8,128)(2,1)S(1)}, u32[]{:S(2)}, u32[]{:S(2)}) %collective-permute-start.14) | collective-permute-done | bytes 262176 | tf_op jit(solution)/shard_map/ppermute | solution.py:510
  60.8 2.5 %collective-permute-start.15 = (bf16[128,1024]{1,0:T(8,128)(2,1)S(1)}, bf16[128,1024]{1,0:T(8,128)(2,1)S(1)}, u32[]{:S(2)}, u32[]{:S(2)}) collective-permute-start(bf16[128,1024]{1,0:T(8,128)(2,1)S(1)} %collective-permute-done.14.refs_3_), channel_id=1, source_target_pairs={{0,8},{8,16},{16,24},{24,28},{28,20},{20,12},{12,4},{4,0},{1,9},{9... | collective-permute-start | bytes 786440 | tf_op jit(solution)/shard_map/ppermute | solution.py:510
  63.3 0.0 collective-permute-done.17.refs_4_
  63.3 0.8 %collective-permute-start.18 = (bf16[128,1024]{1,0:T(8,128)(2,1)S(1)}, bf16[128,1024]{1,0:T(8,128)(2,1)S(1)}, u32[]{:S(2)}, u32[]{:S(2)}) collective-permute-start(bf16[128,1024]{1,0:T(8,128)(2,1)S(1)} %collective-permute-done.17.refs_4_), channel_id=1, source_target_pairs={{8,0},{16,8},{24,16},{28,24},{20,28},{12,20},{4,12},{0,4},{9,1},{1... | collective-permute-start | bytes 786440 | tf_op jit(solution)/shard_map/ppermute | solution.py:511
  64.1 0.0 collective-permute-done.11
  64.1 0.2 convert_add_fusion
  64.3 2.0 %collective-permute-start.12 = (bf16[1,128,1024]{2,1,0:T(8,128)(2,1)S(1)}, bf16[1,128,1024]{2,1,0:T(8,128)(2,1)S(1)}, u32[]{:S(2)}, u32[]{:S(2)}) collective-permute-start(bf16[1,128,1024]{2,1,0:T(8,128)(2,1)S(1)} %slice.29), channel_id=1, source_target_pairs={{0,2},{1,3},{2,0},{3,1},{4,6},{5,7},{6,4},{7,5},{8,10},{9,11},{10,... | collective-permute-start | bytes 786440 | tf_op jit(solution)/shard_map/ppermute | solution.py:320
  66.3 1.5 %shard_map.114.refs_2_ = f32[1024,512]{1,0:T(8,128)S(1)} custom-call(bf16[8,128,512]{2,1,0:T(8,128)(2,1)S(1)} %shard_map.112.refs_2_.cols_ref, bf16[128,1024]{1,0:T(8,128)(2,1)S(1)} %shard_map.109.after_ref.att_ref.refs_0_, bf16[128,1024]{1,0:T(8,128)(2,1)S(1)} %collective-permute-done.13.refs_1_, bf16[128,1024]{1,0:T(8,128)(2,1)S(1)} %collective-permute-done.16.refs_2_, ...), custom_call_target="tpu_custom_call" | custom-call | flops 671088640 | bytes 2097152 | tf_op jit(solution)/shard_map/pallas_call | solution.py:495
  67.9 3.3 %collective-permute-done.15.refs_0_ = bf16[128,1024]{1,0:T(8,128)(2,1)S(1)} collective-permute-done((bf16[128,1024]{1,0:T(8,128)(2,1)S(1)}, bf16[128,1024]{1,0:T(8,128)(2,1)S(1)}, u32[]{:S(2)}, u32[]{:S(2)}) %collective-permute-start.15) | collective-permute-done | bytes 262176 | tf_op jit(solution)/shard_map/ppermute | solution.py:510
  71.2 0.1 collective-permute-start.21
  71.3 0.0 collective-permute-done.18.refs_1_
  71.3 2.0 %collective-permute-start.22 = (bf16[64,1024]{1,0:T(8,128)(2,1)S(1)}, bf16[64,1024]{1,0:T(8,128)(2,1)S(1)}, u32[]{:S(2)}, u32[]{:S(2)}) collective-permute-start(bf16[64,1024]{1,0:T(8,128)(2,1)S(1)} %slice.22), channel_id=1, source_target_pairs={{8,0},{16,8},{24,16},{28,24},{20,28},{12,20},{4,12},{0,4},{9,1},{1... | collective-permute-start | bytes 393224 | tf_op jit(solution)/shard_map/ppermute | solution.py:521
  73.3 0.7 shard_map.115.after_ref.total_ref
  74.0 0.0 collective-permute-done.20.refs_2_
  74.1 1.7 %shard_map.117 = (f32[128,8,128]{2,1,0:T(8,128)}, f32[128,8,128]{2,1,0:T(8,128)}) custom-call(bf16[8,128,128]{2,1,0:T(8,128)(2,1)S(1)} %get-tuple-element.28.kh_ref, bf16[8,128,128]{2,1,0:T(8,128)(2,1)S(1)} %get-tuple-element.29.vh_ref, f32[8,128,128]{2,1,0:T(8,128)S(1)} %get-tuple-element.41.refs_3_.dkl_ref, f32[8,128,128]{2,1,0:T(8,128)S(1)} %get-tuple-element.47.dvl_ref, ...), custom_call_target="tpu_custom_call" | custom-call | flops 67108864 | bytes 2883584 | tf_op jit(solution)/shard_map/pallas_call | solution.py:523
  75.8 0.0 collective-permute-done.12
  75.8 0.8 fusion.1
  76.6 0.0 collective-permute-done.21.low_ref
  76.6 0.0 collective-permute-done.22.high_ref
  76.6 2.4 %shard_map.118 = f32[1024,512]{1,0:T(8,128)} custom-call(bf16[8,128,512]{2,1,0:T(8,128)(2,1)S(1)} %shard_map.112.refs_2_.cols_ref, bf16[64,1024]{1,0:T(8,128)(2,1)S(1)} %collective-permute-done.21.low_ref, bf16[64,1024]{1,0:T(8,128)(2,1)S(1)} %collective-permute-done.22.high_ref, f32[1024,512]{1,0:T(8,128)S(1)} %shard_map.115.after_ref.total_ref, ...), custom_call_target="tpu_custom_call" | custom-call | flops 134217728 | bytes 4194304 | tf_op jit(solution)/shard_map/pallas_call | solution.py:532
  (5 shorter events, 0.1 us)
Async XLA Ops:
  0.6 16.0 %collective-permute-start.1 = (bf16[128,1024]{1,0:T(8,128)(2,1)}, bf16[128,1024]{1,0:T(8,128)(2,1)S(1)}, u32[]{:S(2)}, u32[]{:S(2)}) collective-permute-start(bf16[128,1024]{1,0:T(8,128)(2,1)} %grad_hbm.1), channel_id=1, source_target_pairs={{0,0},{1,10},{2,18},{3,24},{4,4},{5,14},{6,22},{7,28},{8,2},{9,8},... | collective-permute-start | bytes 786440 | tf_op jit(solution)/shard_map/ppermute | solution.py:341
  4.7 12.0 %collective-permute-start = (bf16[8,128,128]{2,1,0:T(8,128)(2,1)S(1)}, bf16[8,128,128]{2,1,0:T(8,128)(2,1)S(1)}, u32[]{:S(2)}, u32[]{:S(2)}) collective-permute-start(bf16[8,128,128]{2,1,0:T(8,128)(2,1)S(1)} %get-tuple-element.32.running_ref), channel_id=1, source_target_pairs={{0,4},{4,0},{8,12},{12,8},{16,20},{20,16},{24,28},{28,24},{1,5},{5... | collective-permute-start | bytes 786440 | tf_op jit(solution)/shard_map/ppermute | solution.py:44
  7.7 10.7 %collective-permute-start.3 = (bf16[128,1024]{1,0:T(8,128)(2,1)S(1)}, bf16[128,1024]{1,0:T(8,128)(2,1)S(1)}, u32[]{:S(2)}, u32[]{:S(2)}) collective-permute-start(bf16[128,1024]{1,0:T(8,128)(2,1)S(1)} %get-tuple-element.34.refs_0_), channel_id=1, source_target_pairs={{0,1},{1,0},{2,3},{3,2},{4,5},{5,4},{6,7},{7,6},{8,9},{9,8},{10,11... | collective-permute-start | bytes 786440 | tf_op jit(solution)/shard_map/ppermute | solution.py:320
  10.4 9.7 %collective-permute-start.4 = (bf16[128,1024]{1,0:T(8,128)(2,1)S(1)}, bf16[128,1024]{1,0:T(8,128)(2,1)S(1)}, u32[]{:S(2)}, u32[]{:S(2)}) collective-permute-start(bf16[128,1024]{1,0:T(8,128)(2,1)S(1)} %get-tuple-element.34.refs_0_), channel_id=1, source_target_pairs={{0,2},{1,3},{2,0},{3,1},{4,6},{5,7},{6,4},{7,5},{8,10},{9,11},{10,... | collective-permute-start | bytes 786440 | tf_op jit(solution)/shard_map/ppermute | solution.py:320
  12.9 11.6 %collective-permute-start.5 = (bf16[128,1024]{1,0:T(8,128)(2,1)S(1)}, bf16[128,1024]{1,0:T(8,128)(2,1)S(1)}, u32[]{:S(2)}, u32[]{:S(2)}) collective-permute-start(bf16[128,1024]{1,0:T(8,128)(2,1)S(1)} %get-tuple-element.34.refs_0_), channel_id=1, source_target_pairs={{0,3},{1,2},{2,1},{3,0},{4,7},{5,6},{6,5},{7,4},{8,11},{9,10},{10,... | collective-permute-start | bytes 786440 | tf_op jit(solution)/shard_map/ppermute | solution.py:320
  16.7 10.6 %collective-permute-start.2 = (bf16[8,128,128]{2,1,0:T(8,128)(2,1)S(1)}, bf16[8,128,128]{2,1,0:T(8,128)(2,1)S(1)}, u32[]{:S(2)}, u32[]{:S(2)}) collective-permute-start(bf16[8,128,128]{2,1,0:T(8,128)(2,1)S(1)} %shard_map.104.running_ref), channel_id=1, source_target_pairs={{0,8},{8,0},{4,12},{12,4},{16,24},{24,16},{20,28},{28,20},{1,9},{9... | collective-permute-start | bytes 786440 | tf_op jit(solution)/shard_map/ppermute | solution.py:44
  17.4 12.8 %collective-permute-start.7 = (bf16[128,512]{1,0:T(8,128)(2,1)S(1)}, bf16[128,512]{1,0:T(8,128)(2,1)S(1)}, u32[]{:S(2)}, u32[]{:S(2)}) collective-permute-start(bf16[128,512]{1,0:T(8,128)(2,1)S(1)} %get-tuple-element.33.refs_0_.refs_6_), channel_id=1, source_target_pairs={{0,4},{4,0},{8,12},{12,8},{16,20},{20,16},{24,28},{28,24},{1,5},{5... | collective-permute-start | bytes 393224 | tf_op jit(solution)/shard_map/ppermute | solution.py:373
  27.4 15.4 %collective-permute-start.6 = (bf16[8,128,128]{2,1,0:T(8,128)(2,1)S(1)}, bf16[8,128,128]{2,1,0:T(8,128)(2,1)S(1)}, u32[]{:S(2)}, u32[]{:S(2)}) collective-permute-start(bf16[8,128,128]{2,1,0:T(8,128)(2,1)S(1)} %shard_map.106.after_ref), channel_id=1, source_target_pairs={{0,16},{16,0},{4,20},{20,4},{8,24},{24,8},{12,28},{28,12},{1,17},{... | collective-permute-start | bytes 786440 | tf_op jit(solution)/shard_map/ppermute | solution.py:44
  30.2 16.6 %collective-permute-start.8 = (bf16[2,128,512]{2,1,0:T(8,128)(2,1)S(1)}, bf16[2,128,512]{2,1,0:T(8,128)(2,1)S(1)}, u32[]{:S(2)}, u32[]{:S(2)}) collective-permute-start(bf16[2,128,512]{2,1,0:T(8,128)(2,1)S(1)} %shard_map.108.refs_4_.refs_0_), channel_id=1, source_target_pairs={{0,1},{1,0},{2,3},{3,2},{4,5},{5,4},{6,7},{7,6},{8,9},{9,8},{10,11... | collective-permute-start | bytes 786440 | tf_op jit(solution)/shard_map/ppermute | solution.py:320
  30.6 16.2 %collective-permute-start.9 = (bf16[2,128,512]{2,1,0:T(8,128)(2,1)S(1)}, bf16[2,128,512]{2,1,0:T(8,128)(2,1)S(1)}, u32[]{:S(2)}, u32[]{:S(2)}) collective-permute-start(bf16[2,128,512]{2,1,0:T(8,128)(2,1)S(1)} %shard_map.108.refs_4_.refs_0_), channel_id=1, source_target_pairs={{0,2},{1,3},{2,0},{3,1},{4,6},{5,7},{6,4},{7,5},{8,10},{9,11},{10,... | collective-permute-start | bytes 786440 | tf_op jit(solution)/shard_map/ppermute | solution.py:320
  30.6 16.2 %collective-permute-start.10 = (bf16[2,128,512]{2,1,0:T(8,128)(2,1)S(1)}, bf16[2,128,512]{2,1,0:T(8,128)(2,1)S(1)}, u32[]{:S(2)}, u32[]{:S(2)}) collective-permute-start(bf16[2,128,512]{2,1,0:T(8,128)(2,1)S(1)} %shard_map.108.refs_4_.refs_0_), channel_id=1, source_target_pairs={{0,3},{1,2},{2,1},{3,0},{4,7},{5,6},{6,5},{7,4},{8,11},{9,10},{10,... | collective-permute-start | bytes 786440 | tf_op jit(solution)/shard_map/ppermute | solution.py:320
  43.3 8.1 %collective-permute-start.13 = (bf16[128,1024]{1,0:T(8,128)(2,1)S(1)}, bf16[128,1024]{1,0:T(8,128)(2,1)S(1)}, u32[]{:S(2)}, u32[]{:S(2)}) collective-permute-start(bf16[128,1024]{1,0:T(8,128)(2,1)S(1)} %shard_map.109.after_ref.att_ref.refs_0_), channel_id=1, source_target_pairs={{0,8},{8,16},{16,24},{24,28},{28,20},{20,12},{12,4},{4,0},{1,9},{9... | collective-permute-start | bytes 786440 | tf_op jit(solution)/shard_map/ppermute | solution.py:510
  43.9 8.2 %collective-permute-start.16 = (bf16[128,1024]{1,0:T(8,128)(2,1)S(1)}, bf16[128,1024]{1,0:T(8,128)(2,1)S(1)}, u32[]{:S(2)}, u32[]{:S(2)}) collective-permute-start(bf16[128,1024]{1,0:T(8,128)(2,1)S(1)} %shard_map.109.after_ref.att_ref.refs_0_), channel_id=1, source_target_pairs={{8,0},{16,8},{24,16},{28,24},{20,28},{12,20},{4,12},{0,4},{9,1},{1... | collective-permute-start | bytes 786440 | tf_op jit(solution)/shard_map/ppermute | solution.py:511
  48.1 16.0 %collective-permute-start.11 = (bf16[2,128,1024]{2,1,0:T(8,128)(2,1)S(1)}, bf16[2,128,1024]{2,1,0:T(8,128)(2,1)S(1)}, u32[]{:S(2)}, u32[]{:S(2)}) collective-permute-start(bf16[2,128,1024]{2,1,0:T(8,128)(2,1)S(1)} %get-tuple-element.46), channel_id=1, source_target_pairs={{0,1},{1,0},{2,3},{3,2},{4,5},{5,4},{6,7},{7,6},{8,9},{9,8},{10,11... | collective-permute-start | bytes 1572872 | tf_op jit(solution)/shard_map/ppermute | solution.py:320
  48.2 9.5 %collective-permute-start.19 = (bf16[8,128,128]{2,1,0:T(8,128)(2,1)S(1)}, bf16[8,128,128]{2,1,0:T(8,128)(2,1)S(1)}, u32[]{:S(2)}, u32[]{:S(2)}) collective-permute-start(bf16[8,128,128]{2,1,0:T(8,128)(2,1)S(1)} %shard_map.110.refs_0_), channel_id=1, source_target_pairs={{0,8},{8,0},{4,12},{12,4},{16,24},{24,16},{20,28},{28,20},{1,9},{9... | collective-permute-start | bytes 786440 | tf_op jit(solution)/shard_map/ppermute | solution.py:44
  51.3 9.5 %collective-permute-start.14 = (bf16[128,1024]{1,0:T(8,128)(2,1)S(1)}, bf16[128,1024]{1,0:T(8,128)(2,1)S(1)}, u32[]{:S(2)}, u32[]{:S(2)}) collective-permute-start(bf16[128,1024]{1,0:T(8,128)(2,1)S(1)} %collective-permute-done.13.refs_1_), channel_id=1, source_target_pairs={{0,8},{8,16},{16,24},{24,28},{28,20},{20,12},{12,4},{4,0},{1,9},{9... | collective-permute-start | bytes 786440 | tf_op jit(solution)/shard_map/ppermute | solution.py:510
  52.1 11.2 %collective-permute-start.17 = (bf16[128,1024]{1,0:T(8,128)(2,1)S(1)}, bf16[128,1024]{1,0:T(8,128)(2,1)S(1)}, u32[]{:S(2)}, u32[]{:S(2)}) collective-permute-start(bf16[128,1024]{1,0:T(8,128)(2,1)S(1)} %collective-permute-done.16.refs_2_), channel_id=1, source_target_pairs={{8,0},{16,8},{24,16},{28,24},{20,28},{12,20},{4,12},{0,4},{9,1},{1... | collective-permute-start | bytes 786440 | tf_op jit(solution)/shard_map/ppermute | solution.py:511
  57.8 16.2 %collective-permute-start.20 = (bf16[8,128,128]{2,1,0:T(8,128)(2,1)S(1)}, bf16[8,128,128]{2,1,0:T(8,128)(2,1)S(1)}, u32[]{:S(2)}, u32[]{:S(2)}) collective-permute-start(bf16[8,128,128]{2,1,0:T(8,128)(2,1)S(1)} %shard_map.116), channel_id=1, source_target_pairs={{0,4},{4,0},{8,12},{12,8},{16,20},{20,16},{24,28},{28,24},{1,5},{5... | collective-permute-start | bytes 786440 | tf_op jit(solution)/shard_map/ppermute | solution.py:44
  60.8 10.4 %collective-permute-start.15 = (bf16[128,1024]{1,0:T(8,128)(2,1)S(1)}, bf16[128,1024]{1,0:T(8,128)(2,1)S(1)}, u32[]{:S(2)}, u32[]{:S(2)}) collective-permute-start(bf16[128,1024]{1,0:T(8,128)(2,1)S(1)} %collective-permute-done.14.refs_3_), channel_id=1, source_target_pairs={{0,8},{8,16},{16,24},{24,28},{28,20},{20,12},{12,4},{4,0},{1,9},{9... | collective-permute-start | bytes 786440 | tf_op jit(solution)/shard_map/ppermute | solution.py:510
  63.3 8.0 %collective-permute-start.18 = (bf16[128,1024]{1,0:T(8,128)(2,1)S(1)}, bf16[128,1024]{1,0:T(8,128)(2,1)S(1)}, u32[]{:S(2)}, u32[]{:S(2)}) collective-permute-start(bf16[128,1024]{1,0:T(8,128)(2,1)S(1)} %collective-permute-done.17.refs_4_), channel_id=1, source_target_pairs={{8,0},{16,8},{24,16},{28,24},{20,28},{12,20},{4,12},{0,4},{9,1},{1... | collective-permute-start | bytes 786440 | tf_op jit(solution)/shard_map/ppermute | solution.py:511
  64.3 11.5 %collective-permute-start.12 = (bf16[1,128,1024]{2,1,0:T(8,128)(2,1)S(1)}, bf16[1,128,1024]{2,1,0:T(8,128)(2,1)S(1)}, u32[]{:S(2)}, u32[]{:S(2)}) collective-permute-start(bf16[1,128,1024]{2,1,0:T(8,128)(2,1)S(1)} %slice.29), channel_id=1, source_target_pairs={{0,2},{1,3},{2,0},{3,1},{4,6},{5,7},{6,4},{7,5},{8,10},{9,11},{10,... | collective-permute-start | bytes 786440 | tf_op jit(solution)/shard_map/ppermute | solution.py:320
  71.2 5.4 %collective-permute-start.21 = (bf16[64,1024]{1,0:T(8,128)(2,1)S(1)}, bf16[64,1024]{1,0:T(8,128)(2,1)S(1)}, u32[]{:S(2)}, u32[]{:S(2)}) collective-permute-start(bf16[64,1024]{1,0:T(8,128)(2,1)S(1)} %slice.21), channel_id=1, source_target_pairs={{0,8},{8,16},{16,24},{24,28},{28,20},{20,12},{12,4},{4,0},{1,9},{9... | collective-permute-start | bytes 393224 | tf_op jit(solution)/shard_map/ppermute | solution.py:520
  71.3 5.3 %collective-permute-start.22 = (bf16[64,1024]{1,0:T(8,128)(2,1)S(1)}, bf16[64,1024]{1,0:T(8,128)(2,1)S(1)}, u32[]{:S(2)}, u32[]{:S(2)}) collective-permute-start(bf16[64,1024]{1,0:T(8,128)(2,1)S(1)} %slice.22), channel_id=1, source_target_pairs={{8,0},{16,8},{24,16},{28,24},{20,28},{12,20},{4,12},{0,4},{9,1},{1... | collective-permute-start | bytes 393224 | tf_op jit(solution)/shard_map/ppermute | solution.py:521

commit v4 on v3

--- a/solution.py
+++ b/solution.py
@@ -84,7 +84,8 @@
     return lam_ref[1 + local_bits + b, h : h + 1, :] * upper
 
 
-def local_kernel(q_hbm, kh_ref, vh_ref, lam_hbm, w_hbm, *refs):
+def local_kernel(q_hbm, kh_ref, vh_ref, lam_hbm, w_hbm, after_ref, *refs):
+    del after_ref
     pt_ref, att_ref, qh_ref, qw_ref, lam_ref, w_ref, q_ref, lam_rows, sems = refs
     pieces = sems.shape[0] - 2
     share = w_hbm.shape[0] // pieces
@@ -326,7 +327,7 @@
                 blocks[i ^ 1 << digit] = to_group(blocks[i], 1 << digit)
         return [blocks[i] for i in range(heads)]
 
-    grad_blocks = [own_grad] + [to_group(own_grad, i) for i in range(1, heads)]
+    grad_blocks = every_group(own_grad)
 
     per = devices // heads
     route = [
@@ -338,7 +339,22 @@
         for low in range(per)
         for group_at in range(heads)
     ]
-    turned = lax.ppermute(out_grad, ("seq", "head"), route)
+    turned = lax.ppermute(own_grad, ("seq", "head"), route)
+    partner_states = []
+    running, arrived = own_state, None
+    for digit in range(top):
+        if arrived is not None:
+            running = pl.pallas_call(
+                running_kernel,
+                out_shape=head_state,
+                in_specs=[VMEM] * 2,
+                out_specs=VMEM,
+                compiler_params=PARAMS,
+                cost_estimate=cost(0, 3 * moved_head),
+            )(running, arrived)
+        arrived = across(running, "seq", digit)
+        partner_states.append(arrived)
+
     probs_t, att_local, qh, qw, lam, w = pl.pallas_call(
         local_kernel,
         out_shape=(
@@ -349,7 +365,7 @@
             pltpu.VMEM(level_weights.shape, F32),
             pltpu.VMEM(out_proj.shape, BF),
         ),
-        in_specs=[ANY, VMEM, VMEM, ANY, ANY],
+        in_specs=[ANY, VMEM, VMEM, ANY, ANY, ANY],
         out_specs=(VMEM,) * 6,
         scratch_shapes=[
             pltpu.VMEM(queries.shape, F32),
@@ -358,7 +374,7 @@
         ],
         compiler_params=PARAMS,
         cost_estimate=cost(2 * flops_head, 12 * moved_head),
-    )(hbm(queries), kh, vh, hbm(level_weights), hbm(out_proj))
+    )(hbm(queries), kh, vh, hbm(level_weights), hbm(out_proj), running)
 
     chunks = pl.pallas_call(
         chunk_kernel,
@@ -373,21 +389,6 @@
         lax.ppermute(chunks[r], "seq", [(at, at ^ r) for at in range(devices)])
         for r in range(1, per)
     ]
-    partner_states = []
-    running, arrived = own_state, None
-    for digit in range(top):
-        if arrived is not None:
-            running = pl.pallas_call(
-                running_kernel,
-                out_shape=head_state,
-                in_specs=[VMEM] * 2 + [ANY],
-                out_specs=VMEM,
-                compiler_params=PARAMS,
-                cost_estimate=cost(0, 3 * moved_head),
-            )(running, arrived, own_chunks[-1])
-        arrived = across(running, "seq", digit)
-        partner_states.append(arrived)
-
     gt, *grad_sums = pl.pallas_call(
         functools.partial(cotangent_kernel, heads, seq_bits),
         out_shape=(pltpu.VMEM((width, rows), BF),) + (pinned_state,) * seq_bits,

time: 79.1 us -> 78 us (0.986)
  waiting for transfers between devices: 27.3 us -> 24.6 us
  starting transfers between devices: 29.8 us -> 31.4 us
    ppermute x8, waiting for transfers between devices: 6.05 us -> 1.17 us  [to_group(): return lax.ppermute(block, 'head', [(at, at ^ i) for at in range(heads)])]
    ppermute x5, starting transfers between devices: 8.39 us -> 9.65 us  [across(): return lax.ppermute(block, axis, route)]
    ppermute x3, waiting for transfers between devices: 7.34 us -> 8.49 us  [body(): ahead = lax.ppermute(ahead, 'seq', forward)]
    ppermute x5, waiting for transfers between devices: 13.8 us -> 14.9 us  [across(): return lax.ppermute(block, axis, route)]
    ppermute x1, starting transfers between devices: 1.61 us -> 0.67 us  [body(): turned = lax.ppermute(own_grad, ('seq', 'head'), route)]
    ppermute x3, starting transfers between devices: 3.51 us -> 4.41 us  [body(): behind = lax.ppermute(behind, 'seq', backward)]
    ppermute x3, starting transfers between devices: 3.87 us -> 2.98 us  [body(): ahead = lax.ppermute(ahead, 'seq', forward)]
  transfers between devices with their start and end apart: 23 -> 23, of which waited for: 7 -> 8; matrix products, arithmetic and copies ran while one was open for 1% -> 1% of each run, Pallas kernels for 22% -> 20%
where the time goes in v4:
time: 78 us; the launch traced here: 77.9 us
  starting transfers between devices  31.4 us (40%)
  waiting for transfers between devices  24.6 us (32%)
  Pallas kernels  20 us (26%)
  other arithmetic  0.94 us (1%)
  between operations  0.83 us (1%)
    ppermute x5, waiting for transfers between devices, across(): return lax.ppermute(block, axis, route)  14.9 us
    ppermute x8, starting transfers between devices, to_group(): return lax.ppermute(block, 'head', [(at, at ^ i) for at in range(heads)])  9.72 us
    ppermute x5, starting transfers between devices, across(): return lax.ppermute(block, axis, route)  9.65 us
    ppermute x3, waiting for transfers between devices, body(): ahead = lax.ppermute(ahead, 'seq', forward)  8.49 us
    ppermute x3, starting transfers between devices, body(): behind = lax.ppermute(behind, 'seq', backward)  4.41 us
    pallas_call x1, Pallas kernels, body(): pl.pallas_call(local_kernel, out_shape=(pltpu.VMEM((heads_dev, rows, rows...  3.66 us
    ppermute x3, starting transfers between devices, body(): ahead = lax.ppermute(ahead, 'seq', forward)  2.98 us
    pallas_call x1, Pallas kernels, body(): pl.pallas_call(functools.partial(cotangent_kernel, heads, seq_bits), out_...  2.79 us
  transfers between devices with their start and end apart: 23, of which 8 were waited for; matrix products, arithmetic and copies ran while one was open for 1% of the time, Pallas kernels for 20%

profile of v4, /device:TPU:0, one launch (start us, length us, event | category | flops | bytes accessed | tf_op | source)
XLA Modules:
  0.0 77.9 jit_solution(15385845405944979546)
XLA Ops:
  0.6 2.4 %shard_map.101 = (bf16[8,128,128]{2,1,0:T(8,128)(2,1)S(1)}, bf16[8,128,128]{2,1,0:T(8,128)(2,1)S(1)}, bf16[8,128,128]{2,1,0:T(8,128)(2,1)S(1)}, bf16[128,1024]{1,0:T(8,128)(2,1)S(1)}) custom-call(f32[128,8,128]{2,1,0:T(8,128)} %k_hbm.1, f32[128,8,128]{2,1,0:T(8,128)} %v_hbm.1, bf16[128,1024]{1,0:T(8,128)(2,1)} %grad_hbm.1), custom_call_target="tpu_custom_call" | custom-call | flops 33554432 | bytes 1835008 | tf_op jit(solution)/shard_map/pallas_call | solution.py:306
  3.1 3.0 %collective-permute-start.3 = (bf16[128,1024]{1,0:T(8,128)(2,1)S(1)}, bf16[128,1024]{1,0:T(8,128)(2,1)S(1)}, u32[]{:S(2)}, u32[]{:S(2)}) collective-permute-start(bf16[128,1024]{1,0:T(8,128)(2,1)S(1)} %get-tuple-element.33.refs_0_), channel_id=1, source_target_pairs={{0,2},{1,3},{2,0},{3,1},{4,6},{5,7},{6,4},{7,5},{8,10},{9,11},{10,... | collective-permute-start | bytes 786440 | tf_op jit(solution)/shard_map/ppermute | solution.py:321
  6.1 1.5 %collective-permute-start = (bf16[8,128,128]{2,1,0:T(8,128)(2,1)S(1)}, bf16[8,128,128]{2,1,0:T(8,128)(2,1)S(1)}, u32[]{:S(2)}, u32[]{:S(2)}) collective-permute-start(bf16[8,128,128]{2,1,0:T(8,128)(2,1)S(1)} %get-tuple-element.30.running_ref), channel_id=1, source_target_pairs={{0,4},{4,0},{8,12},{12,8},{16,20},{20,16},{24,28},{28,24},{1,5},{5... | collective-permute-start | bytes 786440 | tf_op jit(solution)/shard_map/ppermute | solution.py:44
  7.6 0.7 collective-permute-start.5
  8.3 3.0 %collective-permute-start.2 = (bf16[128,1024]{1,0:T(8,128)(2,1)S(1)}, bf16[128,1024]{1,0:T(8,128)(2,1)S(1)}, u32[]{:S(2)}, u32[]{:S(2)}) collective-permute-start(bf16[128,1024]{1,0:T(8,128)(2,1)S(1)} %get-tuple-element.33.refs_0_), channel_id=1, source_target_pairs={{0,1},{1,0},{2,3},{3,2},{4,5},{5,4},{6,7},{7,6},{8,9},{9,8},{10,11... | collective-permute-start | bytes 786440 | tf_op jit(solution)/shard_map/ppermute | solution.py:321
  11.2 1.2 %collective-permute-done.3.refs_2_ = bf16[128,1024]{1,0:T(8,128)(2,1)S(1)} collective-permute-done((bf16[128,1024]{1,0:T(8,128)(2,1)S(1)}, bf16[128,1024]{1,0:T(8,128)(2,1)S(1)}, u32[]{:S(2)}, u32[]{:S(2)}) %collective-permute-start.3) | collective-permute-done | bytes 262176 | tf_op jit(solution)/shard_map/ppermute | solution.py:321
  12.4 0.0 collective-permute-start.4
  12.4 1.5 %collective-permute-done.arrived_ref.refs_0_ = bf16[8,128,128]{2,1,0:T(8,128)(2,1)S(1)} collective-permute-done((bf16[8,128,128]{2,1,0:T(8,128)(2,1)S(1)}, bf16[8,128,128]{2,1,0:T(8,128)(2,1)S(1)}, u32[]{:S(2)}, u32[]{:S(2)}) %collective-permute-start) | collective-permute-done | bytes 262176 | tf_op jit(solution)/shard_map/ppermute | solution.py:44
  13.9 0.1 shard_map.102.after_ref.running_ref
  13.9 3.3 %collective-permute-start.1 = (bf16[8,128,128]{2,1,0:T(8,128)(2,1)S(1)}, bf16[8,128,128]{2,1,0:T(8,128)(2,1)S(1)}, u32[]{:S(2)}, u32[]{:S(2)}) collective-permute-start(bf16[8,128,128]{2,1,0:T(8,128)(2,1)S(1)} %shard_map.102.after_ref.running_ref), channel_id=1, source_target_pairs={{0,8},{8,0},{4,12},{12,4},{16,24},{24,16},{20,28},{28,20},{1,9},{9... | collective-permute-start | bytes 786440 | tf_op jit(solution)/shard_map/ppermute | solution.py:44
  17.2 3.7 %shard_map.103 = (bf16[8,128,128]{2,1,0:T(8,128)(2,1)S(1)}, f32[8,128,128]{2,1,0:T(8,128)S(1)}, bf16[8,128,128]{2,1,0:T(8,128)(2,1)S(1)}, bf16[3,8,128,128]{3,2,...) custom-call(f32[128,8,128]{2,1,0:T(8,128)} %q_hbm.1, ...), custom_call_target="tpu_custom_call" | custom-call | flops 67108864 | bytes 3145728 | tf_op jit(solution)/shard_map/pallas_call | solution.py:358
  20.9 0.0 collective-permute-done.5.block_ref
  20.9 1.8 %collective-permute-start.7 = (bf16[128,512]{1,0:T(8,128)(2,1)S(1)}, bf16[128,512]{1,0:T(8,128)(2,1)S(1)}, u32[]{:S(2)}, u32[]{:S(2)}) collective-permute-start(bf16[128,512]{1,0:T(8,128)(2,1)S(1)} %get-tuple-element.35.refs_6_), channel_id=1, source_target_pairs={{0,4},{4,0},{8,12},{12,8},{16,20},{20,16},{24,28},{28,24},{1,5},{5... | collective-permute-start | bytes 393224 | tf_op jit(solution)/shard_map/ppermute | solution.py:389
  22.8 0.0 collective-permute-done.2.refs_1_
  22.8 0.0 collective-permute-done.4.refs_3_
  22.8 2.8 %shard_map.105 = (bf16[1024,128]{1,0:T(8,128)(2,1)S(1)}, bf16[8,128,128]{2,1,0:T(8,128)(2,1)S(1)}, bf16[8,128,128]{2,1,0:T(8,128)(2,1)S(1)}, bf16[8,128,128]{2,1,0:T(8,128)(2,1)S(1)}) custom-call(bf16[128,1024]{1,0:T(8,128)(2,1)S(1)} %get-tuple-element.33.refs_0_, bf16[128,1024]{1,0:T(8,128)(2,1)S(1)} %collective-permute-done.2.refs_1_, ...), custom_call_target="tpu_custom_call" | custom-call | flops 1073741824 | bytes 8388608 | tf_op jit(solution)/shard_map/pallas_call | solution.py:392
  25.6 1.8 %collective-permute-done.1.arrived_ref.refs_1_ = bf16[8,128,128]{2,1,0:T(8,128)(2,1)S(1)} collective-permute-done((bf16[8,128,128]{2,1,0:T(8,128)(2,1)S(1)}, bf16[8,128,128]{2,1,0:T(8,128)(2,1)S(1)}, u32[]{:S(2)}, u32[]{:S(2)}) %collective-permute-start.1) | collective-permute-done | bytes 262176 | tf_op jit(solution)/shard_map/ppermute | solution.py:44
  27.4 0.1 shard_map.106.after_ref
  27.5 3.4 %collective-permute-start.6 = (bf16[8,128,128]{2,1,0:T(8,128)(2,1)S(1)}, bf16[8,128,128]{2,1,0:T(8,128)(2,1)S(1)}, u32[]{:S(2)}, u32[]{:S(2)}) collective-permute-start(bf16[8,128,128]{2,1,0:T(8,128)(2,1)S(1)} %shard_map.106.after_ref), channel_id=1, source_target_pairs={{0,16},{16,0},{4,20},{20,4},{8,24},{24,8},{12,28},{28,12},{1,17},{... | collective-permute-start | bytes 786440 | tf_op jit(solution)/shard_map/ppermute | solution.py:44
  30.9 0.0 collective-permute-done.7.refs_1_
  30.9 0.1 collective-permute-start.8
  31.0 0.1 collective-permute-start.9
  31.1 1.8 %collective-permute-start.10 = (bf16[2,128,512]{2,1,0:T(8,128)(2,1)S(1)}, bf16[2,128,512]{2,1,0:T(8,128)(2,1)S(1)}, u32[]{:S(2)}, u32[]{:S(2)}) collective-permute-start(bf16[2,128,512]{2,1,0:T(8,128)(2,1)S(1)} %shard_map.108.refs_4_.refs_0_), channel_id=1, source_target_pairs={{0,3},{1,2},{2,1},{3,0},{4,7},{5,6},{6,5},{7,4},{8,11},{9,10},{10,... | collective-permute-start | bytes 786440 | tf_op jit(solution)/shard_map/ppermute | solution.py:321
  32.8 1.3 %shard_map.107 = (f32[8,128,128]{2,1,0:T(8,128)S(1)}, f32[8,128,128]{2,1,0:T(8,128)S(1)}, f32[8,128,128]{2,1,0:T(8,128)S(1)}) custom-call(bf16[1024,128]{1,0:T(8,128)(2,1)S(1)} %get-tuple-element.37.gt_ref, bf16[8,128,128]{2,1,0:T(8,128)(2,1)S(1)} %get-tuple-element.38.qh_ref, bf16[8,128,128]{2,1,0:T(8,128)(2,1)S(1)} %get-tuple-element.28.kh_ref, ...), custom_call_target="tpu_custom_call" | custom-call | flops 201326592 | bytes 3670016 | tf_op jit(solution)/shard_map/pallas_call | solution.py:435
  34.1 7.8 %collective-permute-done.6.refs_2_.refs_0_.state_ref = bf16[8,128,128]{2,1,0:T(8,128)(2,1)S(1)} collective-permute-done((bf16[8,128,128]{2,1,0:T(8,128)(2,1)S(1)}, bf16[8,128,128]{2,1,0:T(8,128)(2,1)S(1)}, u32[]{:S(2)}, u32[]{:S(2)}) %collective-permute-start.6) | collective-permute-done | bytes 262176 | tf_op jit(solution)/shard_map/ppermute | solution.py:44
  41.9 0.4 shard_map.109.after_ref.att_ref.refs_0_
  42.3 0.1 collective-permute-start.13
  42.3 2.0 %collective-permute-start.16 = (bf16[128,1024]{1,0:T(8,128)(2,1)S(1)}, bf16[128,1024]{1,0:T(8,128)(2,1)S(1)}, u32[]{:S(2)}, u32[]{:S(2)}) collective-permute-start(bf16[128,1024]{1,0:T(8,128)(2,1)S(1)} %shard_map.109.after_ref.att_ref.refs_0_), channel_id=1, source_target_pairs={{8,0},{16,8},{24,16},{28,24},{20,28},{12,20},{4,12},{0,4},{9,1},{1... | collective-permute-start | bytes 786440 | tf_op jit(solution)/shard_map/ppermute | solution.py:512
  44.3 0.1 shard_map.110.refs_0_
  44.4 1.3 %shard_map.111.refs_1_ = f32[128,8,128]{2,1,0:T(8,128)} custom-call(bf16[1024,128]{1,0:T(8,128)(2,1)S(1)} %get-tuple-element.37.gt_ref, f32[5,8,128]{2,1,0:T(8,128)S(1)} %get-tuple-element.40.lam_ref, f32[8,128,128]{2,1,0:T(8,128)S(1)} %get-tuple-element.44.dql_ref, bf16[8,128,128]{2,1,0:T(8,128)(2,1)S(1)} %collective-permute-done.6.refs_2_.refs_0_.state_ref, ...), custom_call_target="tpu_custom_call" | custom-call | flops 33554432 | bytes 1572864 | tf_op jit(solution)/shard_map/pallas_call | solution.py:467
  45.8 0.0 collective-permute-done.8.refs_1_
  45.8 0.0 collective-permute-done.9.refs_2_
  45.8 0.0 collective-permute-done.10.refs_3_
  45.8 0.1 shard_map.112.refs_2_.cols_ref
  45.9 1.3 %shard_map.113 = (bf16[2,128,1024]{2,1,0:T(8,128)(2,1)S(1)}, f32[2,128,1024]{2,1,0:T(8,128)S(1)}) custom-call(bf16[128,1024]{1,0:T(8,128)(2,1)S(1)} %shard_map.109.after_ref.att_ref.refs_0_, bf16[1024,4096]{1,0:T(8,128)(2,1)S(1)} %get-tuple-element.34.refs_4_.w_ref, bf16[8,128,128]{2,1,0:T(8,128)(2,1)S(1)} %shard_map.110.refs_0_, ...), custom_call_target="tpu_custom_call" | custom-call | flops 1073741824 | bytes 8388608 | tf_op jit(solution)/shard_map/pallas_call | solution.py:476
  47.2 0.1 collective-permute-start.11
  47.2 0.1 collective-permute-start.19
  47.4 3.2 %collective-permute-done.13.refs_1_ = bf16[128,1024]{1,0:T(8,128)(2,1)S(1)} collective-permute-done((bf16[128,1024]{1,0:T(8,128)(2,1)S(1)}, bf16[128,1024]{1,0:T(8,128)(2,1)S(1)}, u32[]{:S(2)}, u32[]{:S(2)}) %collective-permute-start.13) | collective-permute-done | bytes 262176 | tf_op jit(solution)/shard_map/ppermute | solution.py:511
  50.5 0.4 collective-permute-start.14
  51.0 0.0 collective-permute-done.16.refs_2_
  51.0 1.6 %collective-permute-start.17 = (bf16[128,1024]{1,0:T(8,128)(2,1)S(1)}, bf16[128,1024]{1,0:T(8,128)(2,1)S(1)}, u32[]{:S(2)}, u32[]{:S(2)}) collective-permute-start(bf16[128,1024]{1,0:T(8,128)(2,1)S(1)} %collective-permute-done.16.refs_2_), channel_id=1, source_target_pairs={{8,0},{16,8},{24,16},{28,24},{20,28},{12,20},{4,12},{0,4},{9,1},{1... | collective-permute-start | bytes 786440 | tf_op jit(solution)/shard_map/ppermute | solution.py:512
  52.6 3.9 %collective-permute-done.19.refs_1_ = bf16[8,128,128]{2,1,0:T(8,128)(2,1)S(1)} collective-permute-done((bf16[8,128,128]{2,1,0:T(8,128)(2,1)S(1)}, bf16[8,128,128]{2,1,0:T(8,128)(2,1)S(1)}, u32[]{:S(2)}, u32[]{:S(2)}) %collective-permute-start.19) | collective-permute-done | bytes 262176 | tf_op jit(solution)/shard_map/ppermute | solution.py:44
  56.5 0.1 shard_map.116
  56.6 1.4 %collective-permute-start.20 = (bf16[8,128,128]{2,1,0:T(8,128)(2,1)S(1)}, bf16[8,128,128]{2,1,0:T(8,128)(2,1)S(1)}, u32[]{:S(2)}, u32[]{:S(2)}) collective-permute-start(bf16[8,128,128]{2,1,0:T(8,128)(2,1)S(1)} %shard_map.116), channel_id=1, source_target_pairs={{0,4},{4,0},{8,12},{12,8},{16,20},{20,16},{24,28},{28,24},{1,5},{5... | collective-permute-start | bytes 786440 | tf_op jit(solution)/shard_map/ppermute | solution.py:44
  58.0 1.6 %collective-permute-done.14.refs_3_ = bf16[128,1024]{1,0:T(8,128)(2,1)S(1)} collective-permute-done((bf16[128,1024]{1,0:T(8,128)(2,1)S(1)}, bf16[128,1024]{1,0:T(8,128)(2,1)S(1)}, u32[]{:S(2)}, u32[]{:S(2)}) %collective-permute-start.14) | collective-permute-done | bytes 262176 | tf_op jit(solution)/shard_map/ppermute | solution.py:511
  59.6 2.5 %collective-permute-start.15 = (bf16[128,1024]{1,0:T(8,128)(2,1)S(1)}, bf16[128,1024]{1,0:T(8,128)(2,1)S(1)}, u32[]{:S(2)}, u32[]{:S(2)}) collective-permute-start(bf16[128,1024]{1,0:T(8,128)(2,1)S(1)} %collective-permute-done.14.refs_3_), channel_id=1, source_target_pairs={{0,8},{8,16},{16,24},{24,28},{28,20},{20,12},{12,4},{4,0},{1,9},{9... | collective-permute-start | bytes 786440 | tf_op jit(solution)/shard_map/ppermute | solution.py:511
  62.1 0.0 collective-permute-done.17.refs_4_
  62.1 0.8 %collective-permute-start.18 = (bf16[128,1024]{1,0:T(8,128)(2,1)S(1)}, bf16[128,1024]{1,0:T(8,128)(2,1)S(1)}, u32[]{:S(2)}, u32[]{:S(2)}) collective-permute-start(bf16[128,1024]{1,0:T(8,128)(2,1)S(1)} %collective-permute-done.17.refs_4_), channel_id=1, source_target_pairs={{8,0},{16,8},{24,16},{28,24},{20,28},{12,20},{4,12},{0,4},{9,1},{1... | collective-permute-start | bytes 786440 | tf_op jit(solution)/shard_map/ppermute | solution.py:512
  62.9 0.0 collective-permute-done.11
  62.9 0.2 convert_add_fusion
  63.1 1.8 %collective-permute-start.12 = (bf16[1,128,1024]{2,1,0:T(8,128)(2,1)S(1)}, bf16[1,128,1024]{2,1,0:T(8,128)(2,1)S(1)}, u32[]{:S(2)}, u32[]{:S(2)}) collective-permute-start(bf16[1,128,1024]{2,1,0:T(8,128)(2,1)S(1)} %slice.29), channel_id=1, source_target_pairs={{0,2},{1,3},{2,0},{3,1},{4,6},{5,7},{6,4},{7,5},{8,10},{9,11},{10,... | collective-permute-start | bytes 786440 | tf_op jit(solution)/shard_map/ppermute | solution.py:321
  64.9 1.5 %shard_map.114.refs_2_ = f32[1024,512]{1,0:T(8,128)S(1)} custom-call(bf16[8,128,512]{2,1,0:T(8,128)(2,1)S(1)} %shard_map.112.refs_2_.cols_ref, bf16[128,1024]{1,0:T(8,128)(2,1)S(1)} %shard_map.109.after_ref.att_ref.refs_0_, bf16[128,1024]{1,0:T(8,128)(2,1)S(1)} %collective-permute-done.13.refs_1_, bf16[128,1024]{1,0:T(8,128)(2,1)S(1)} %collective-permute-done.16.refs_2_, ...), custom_call_target="tpu_custom_call" | custom-call | flops 671088640 | bytes 2097152 | tf_op jit(solution)/shard_map/pallas_call | solution.py:496
  66.4 3.7 %collective-permute-done.15.refs_0_ = bf16[128,1024]{1,0:T(8,128)(2,1)S(1)} collective-permute-done((bf16[128,1024]{1,0:T(8,128)(2,1)S(1)}, bf16[128,1024]{1,0:T(8,128)(2,1)S(1)}, u32[]{:S(2)}, u32[]{:S(2)}) %collective-permute-start.15) | collective-permute-done | bytes 262176 | tf_op jit(solution)/shard_map/ppermute | solution.py:511
  70.1 0.2 collective-permute-start.21
  70.3 0.0 collective-permute-done.18.refs_1_
  70.3 2.0 %collective-permute-start.22 = (bf16[64,1024]{1,0:T(8,128)(2,1)S(1)}, bf16[64,1024]{1,0:T(8,128)(2,1)S(1)}, u32[]{:S(2)}, u32[]{:S(2)}) collective-permute-start(bf16[64,1024]{1,0:T(8,128)(2,1)S(1)} %slice.22), channel_id=1, source_target_pairs={{8,0},{16,8},{24,16},{28,24},{20,28},{12,20},{4,12},{0,4},{9,1},{1... | collective-permute-start | bytes 393224 | tf_op jit(solution)/shard_map/ppermute | solution.py:522
  72.3 0.7 shard_map.115.after_ref.total_ref
  73.0 0.0 collective-permute-done.20.refs_2_
  73.0 1.7 %shard_map.117 = (f32[128,8,128]{2,1,0:T(8,128)}, f32[128,8,128]{2,1,0:T(8,128)}) custom-call(bf16[8,128,128]{2,1,0:T(8,128)(2,1)S(1)} %get-tuple-element.28.kh_ref, bf16[8,128,128]{2,1,0:T(8,128)(2,1)S(1)} %get-tuple-element.29.vh_ref, f32[8,128,128]{2,1,0:T(8,128)S(1)} %get-tuple-element.41.refs_3_.dkl_ref, f32[8,128,128]{2,1,0:T(8,128)S(1)} %get-tuple-element.47.dvl_ref, ...), custom_call_target="tpu_custom_call" | custom-call | flops 67108864 | bytes 2883584 | tf_op jit(solution)/shard_map/pallas_call | solution.py:524
  74.8 0.0 collective-permute-done.12
  74.8 0.8 fusion.1
  75.5 0.0 collective-permute-done.21.low_ref
  75.5 0.0 collective-permute-done.22.high_ref
  75.5 2.4 %shard_map.118 = f32[1024,512]{1,0:T(8,128)} custom-call(bf16[8,128,512]{2,1,0:T(8,128)(2,1)S(1)} %shard_map.112.refs_2_.cols_ref, bf16[64,1024]{1,0:T(8,128)(2,1)S(1)} %collective-permute-done.21.low_ref, bf16[64,1024]{1,0:T(8,128)(2,1)S(1)} %collective-permute-done.22.high_ref, f32[1024,512]{1,0:T(8,128)S(1)} %shard_map.115.after_ref.total_ref, ...), custom_call_target="tpu_custom_call" | custom-call | flops 134217728 | bytes 4194304 | tf_op jit(solution)/shard_map/pallas_call | solution.py:533
  (5 shorter events, 0.1 us)
Async XLA Ops:
  3.1 9.3 %collective-permute-start.3 = (bf16[128,1024]{1,0:T(8,128)(2,1)S(1)}, bf16[128,1024]{1,0:T(8,128)(2,1)S(1)}, u32[]{:S(2)}, u32[]{:S(2)}) collective-permute-start(bf16[128,1024]{1,0:T(8,128)(2,1)S(1)} %get-tuple-element.33.refs_0_), channel_id=1, source_target_pairs={{0,2},{1,3},{2,0},{3,1},{4,6},{5,7},{6,4},{7,5},{8,10},{9,11},{10,... | collective-permute-start | bytes 786440 | tf_op jit(solution)/shard_map/ppermute | solution.py:321
  6.1 7.8 %collective-permute-start = (bf16[8,128,128]{2,1,0:T(8,128)(2,1)S(1)}, bf16[8,128,128]{2,1,0:T(8,128)(2,1)S(1)}, u32[]{:S(2)}, u32[]{:S(2)}) collective-permute-start(bf16[8,128,128]{2,1,0:T(8,128)(2,1)S(1)} %get-tuple-element.30.running_ref), channel_id=1, source_target_pairs={{0,4},{4,0},{8,12},{12,8},{16,20},{20,16},{24,28},{28,24},{1,5},{5... | collective-permute-start | bytes 786440 | tf_op jit(solution)/shard_map/ppermute | solution.py:44
  7.6 13.3 %collective-permute-start.5 = (bf16[128,1024]{1,0:T(8,128)(2,1)S(1)}, bf16[128,1024]{1,0:T(8,128)(2,1)S(1)}, u32[]{:S(2)}, u32[]{:S(2)}) collective-permute-start(bf16[128,1024]{1,0:T(8,128)(2,1)S(1)} %get-tuple-element.33.refs_0_), channel_id=1, source_target_pairs={{0,0},{1,10},{2,18},{3,24},{4,4},{5,14},{6,22},{7,28},{8,2},{9,8},... | collective-permute-start | bytes 786440 | tf_op jit(solution)/shard_map/ppermute | solution.py:342
  8.3 14.5 %collective-permute-start.2 = (bf16[128,1024]{1,0:T(8,128)(2,1)S(1)}, bf16[128,1024]{1,0:T(8,128)(2,1)S(1)}, u32[]{:S(2)}, u32[]{:S(2)}) collective-permute-start(bf16[128,1024]{1,0:T(8,128)(2,1)S(1)} %get-tuple-element.33.refs_0_), channel_id=1, source_target_pairs={{0,1},{1,0},{2,3},{3,2},{4,5},{5,4},{6,7},{7,6},{8,9},{9,8},{10,11... | collective-permute-start | bytes 786440 | tf_op jit(solution)/shard_map/ppermute | solution.py:321
  12.4 10.4 %collective-permute-start.4 = (bf16[128,1024]{1,0:T(8,128)(2,1)S(1)}, bf16[128,1024]{1,0:T(8,128)(2,1)S(1)}, u32[]{:S(2)}, u32[]{:S(2)}) collective-permute-start(bf16[128,1024]{1,0:T(8,128)(2,1)S(1)} %collective-permute-done.3.refs_2_), channel_id=1, source_target_pairs={{0,1},{1,0},{2,3},{3,2},{4,5},{5,4},{6,7},{7,6},{8,9},{9,8},{10,11... | collective-permute-start | bytes 786440 | tf_op jit(solution)/shard_map/ppermute | solution.py:321
  13.9 13.5 %collective-permute-start.1 = (bf16[8,128,128]{2,1,0:T(8,128)(2,1)S(1)}, bf16[8,128,128]{2,1,0:T(8,128)(2,1)S(1)}, u32[]{:S(2)}, u32[]{:S(2)}) collective-permute-start(bf16[8,128,128]{2,1,0:T(8,128)(2,1)S(1)} %shard_map.102.after_ref.running_ref), channel_id=1, source_target_pairs={{0,8},{8,0},{4,12},{12,4},{16,24},{24,16},{20,28},{28,20},{1,9},{9... | collective-permute-start | bytes 786440 | tf_op jit(solution)/shard_map/ppermute | solution.py:44
  20.9 9.9 %collective-permute-start.7 = (bf16[128,512]{1,0:T(8,128)(2,1)S(1)}, bf16[128,512]{1,0:T(8,128)(2,1)S(1)}, u32[]{:S(2)}, u32[]{:S(2)}) collective-permute-start(bf16[128,512]{1,0:T(8,128)(2,1)S(1)} %get-tuple-element.35.refs_6_), channel_id=1, source_target_pairs={{0,4},{4,0},{8,12},{12,8},{16,20},{20,16},{24,28},{28,24},{1,5},{5... | collective-permute-start | bytes 393224 | tf_op jit(solution)/shard_map/ppermute | solution.py:389
  27.5 14.4 %collective-permute-start.6 = (bf16[8,128,128]{2,1,0:T(8,128)(2,1)S(1)}, bf16[8,128,128]{2,1,0:T(8,128)(2,1)S(1)}, u32[]{:S(2)}, u32[]{:S(2)}) collective-permute-start(bf16[8,128,128]{2,1,0:T(8,128)(2,1)S(1)} %shard_map.106.after_ref), channel_id=1, source_target_pairs={{0,16},{16,0},{4,20},{20,4},{8,24},{24,8},{12,28},{28,12},{1,17},{... | collective-permute-start | bytes 786440 | tf_op jit(solution)/shard_map/ppermute | solution.py:44
  30.9 14.9 %collective-permute-start.8 = (bf16[2,128,512]{2,1,0:T(8,128)(2,1)S(1)}, bf16[2,128,512]{2,1,0:T(8,128)(2,1)S(1)}, u32[]{:S(2)}, u32[]{:S(2)}) collective-permute-start(bf16[2,128,512]{2,1,0:T(8,128)(2,1)S(1)} %shard_map.108.refs_4_.refs_0_), channel_id=1, source_target_pairs={{0,1},{1,0},{2,3},{3,2},{4,5},{5,4},{6,7},{7,6},{8,9},{9,8},{10,11... | collective-permute-start | bytes 786440 | tf_op jit(solution)/shard_map/ppermute | solution.py:321
  31.0 14.8 %collective-permute-start.9 = (bf16[2,128,512]{2,1,0:T(8,128)(2,1)S(1)}, bf16[2,128,512]{2,1,0:T(8,128)(2,1)S(1)}, u32[]{:S(2)}, u32[]{:S(2)}) collective-permute-start(bf16[2,128,512]{2,1,0:T(8,128)(2,1)S(1)} %shard_map.108.refs_4_.refs_0_), channel_id=1, source_target_pairs={{0,2},{1,3},{2,0},{3,1},{4,6},{5,7},{6,4},{7,5},{8,10},{9,11},{10,... | collective-permute-start | bytes 786440 | tf_op jit(solution)/shard_map/ppermute | solution.py:321
  31.1 14.7 %collective-permute-start.10 = (bf16[2,128,512]{2,1,0:T(8,128)(2,1)S(1)}, bf16[2,128,512]{2,1,0:T(8,128)(2,1)S(1)}, u32[]{:S(2)}, u32[]{:S(2)}) collective-permute-start(bf16[2,128,512]{2,1,0:T(8,128)(2,1)S(1)} %shard_map.108.refs_4_.refs_0_), channel_id=1, source_target_pairs={{0,3},{1,2},{2,1},{3,0},{4,7},{5,6},{6,5},{7,4},{8,11},{9,10},{10,... | collective-permute-start | bytes 786440 | tf_op jit(solution)/shard_map/ppermute | solution.py:321
  42.3 8.3 %collective-permute-start.13 = (bf16[128,1024]{1,0:T(8,128)(2,1)S(1)}, bf16[128,1024]{1,0:T(8,128)(2,1)S(1)}, u32[]{:S(2)}, u32[]{:S(2)}) collective-permute-start(bf16[128,1024]{1,0:T(8,128)(2,1)S(1)} %shard_map.109.after_ref.att_ref.refs_0_), channel_id=1, source_target_pairs={{0,8},{8,16},{16,24},{24,28},{28,20},{20,12},{12,4},{4,0},{1,9},{9... | collective-permute-start | bytes 786440 | tf_op jit(solution)/shard_map/ppermute | solution.py:511
  42.3 8.7 %collective-permute-start.16 = (bf16[128,1024]{1,0:T(8,128)(2,1)S(1)}, bf16[128,1024]{1,0:T(8,128)(2,1)S(1)}, u32[]{:S(2)}, u32[]{:S(2)}) collective-permute-start(bf16[128,1024]{1,0:T(8,128)(2,1)S(1)} %shard_map.109.after_ref.att_ref.refs_0_), channel_id=1, source_target_pairs={{8,0},{16,8},{24,16},{28,24},{20,28},{12,20},{4,12},{0,4},{9,1},{1... | collective-permute-start | bytes 786440 | tf_op jit(solution)/shard_map/ppermute | solution.py:512
  47.2 15.7 %collective-permute-start.11 = (bf16[2,128,1024]{2,1,0:T(8,128)(2,1)S(1)}, bf16[2,128,1024]{2,1,0:T(8,128)(2,1)S(1)}, u32[]{:S(2)}, u32[]{:S(2)}) collective-permute-start(bf16[2,128,1024]{2,1,0:T(8,128)(2,1)S(1)} %get-tuple-element.46), channel_id=1, source_target_pairs={{0,1},{1,0},{2,3},{3,2},{4,5},{5,4},{6,7},{7,6},{8,9},{9,8},{10,11... | collective-permute-start | bytes 1572872 | tf_op jit(solution)/shard_map/ppermute | solution.py:321
  47.2 9.2 %collective-permute-start.19 = (bf16[8,128,128]{2,1,0:T(8,128)(2,1)S(1)}, bf16[8,128,128]{2,1,0:T(8,128)(2,1)S(1)}, u32[]{:S(2)}, u32[]{:S(2)}) collective-permute-start(bf16[8,128,128]{2,1,0:T(8,128)(2,1)S(1)} %shard_map.110.refs_0_), channel_id=1, source_target_pairs={{0,8},{8,0},{4,12},{12,4},{16,24},{24,16},{20,28},{28,20},{1,9},{9... | collective-permute-start | bytes 786440 | tf_op jit(solution)/shard_map/ppermute | solution.py:44
  50.5 9.0 %collective-permute-start.14 = (bf16[128,1024]{1,0:T(8,128)(2,1)S(1)}, bf16[128,1024]{1,0:T(8,128)(2,1)S(1)}, u32[]{:S(2)}, u32[]{:S(2)}) collective-permute-start(bf16[128,1024]{1,0:T(8,128)(2,1)S(1)} %collective-permute-done.13.refs_1_), channel_id=1, source_target_pairs={{0,8},{8,16},{16,24},{24,28},{28,20},{20,12},{12,4},{4,0},{1,9},{9... | collective-permute-start | bytes 786440 | tf_op jit(solution)/shard_map/ppermute | solution.py:511
  51.0 11.1 %collective-permute-start.17 = (bf16[128,1024]{1,0:T(8,128)(2,1)S(1)}, bf16[128,1024]{1,0:T(8,128)(2,1)S(1)}, u32[]{:S(2)}, u32[]{:S(2)}) collective-permute-start(bf16[128,1024]{1,0:T(8,128)(2,1)S(1)} %collective-permute-done.16.refs_2_), channel_id=1, source_target_pairs={{8,0},{16,8},{24,16},{28,24},{20,28},{12,20},{4,12},{0,4},{9,1},{1... | collective-permute-start | bytes 786440 | tf_op jit(solution)/shard_map/ppermute | solution.py:512
  56.6 16.4 %collective-permute-start.20 = (bf16[8,128,128]{2,1,0:T(8,128)(2,1)S(1)}, bf16[8,128,128]{2,1,0:T(8,128)(2,1)S(1)}, u32[]{:S(2)}, u32[]{:S(2)}) collective-permute-start(bf16[8,128,128]{2,1,0:T(8,128)(2,1)S(1)} %shard_map.116), channel_id=1, source_target_pairs={{0,4},{4,0},{8,12},{12,8},{16,20},{20,16},{24,28},{28,24},{1,5},{5... | collective-permute-start | bytes 786440 | tf_op jit(solution)/shard_map/ppermute | solution.py:44
  59.6 10.5 %collective-permute-start.15 = (bf16[128,1024]{1,0:T(8,128)(2,1)S(1)}, bf16[128,1024]{1,0:T(8,128)(2,1)S(1)}, u32[]{:S(2)}, u32[]{:S(2)}) collective-permute-start(bf16[128,1024]{1,0:T(8,128)(2,1)S(1)} %collective-permute-done.14.refs_3_), channel_id=1, source_target_pairs={{0,8},{8,16},{16,24},{24,28},{28,20},{20,12},{12,4},{4,0},{1,9},{9... | collective-permute-start | bytes 786440 | tf_op jit(solution)/shard_map/ppermute | solution.py:511
  62.1 8.2 %collective-permute-start.18 = (bf16[128,1024]{1,0:T(8,128)(2,1)S(1)}, bf16[128,1024]{1,0:T(8,128)(2,1)S(1)}, u32[]{:S(2)}, u32[]{:S(2)}) collective-permute-start(bf16[128,1024]{1,0:T(8,128)(2,1)S(1)} %collective-permute-done.17.refs_4_), channel_id=1, source_target_pairs={{8,0},{16,8},{24,16},{28,24},{20,28},{12,20},{4,12},{0,4},{9,1},{1... | collective-permute-start | bytes 786440 | tf_op jit(solution)/shard_map/ppermute | solution.py:512
  63.1 11.6 %collective-permute-start.12 = (bf16[1,128,1024]{2,1,0:T(8,128)(2,1)S(1)}, bf16[1,128,1024]{2,1,0:T(8,128)(2,1)S(1)}, u32[]{:S(2)}, u32[]{:S(2)}) collective-permute-start(bf16[1,128,1024]{2,1,0:T(8,128)(2,1)S(1)} %slice.29), channel_id=1, source_target_pairs={{0,2},{1,3},{2,0},{3,1},{4,6},{5,7},{6,4},{7,5},{8,10},{9,11},{10,... | collective-permute-start | bytes 786440 | tf_op jit(solution)/shard_map/ppermute | solution.py:321
  70.1 5.4 %collective-permute-start.21 = (bf16[64,1024]{1,0:T(8,128)(2,1)S(1)}, bf16[64,1024]{1,0:T(8,128)(2,1)S(1)}, u32[]{:S(2)}, u32[]{:S(2)}) collective-permute-start(bf16[64,1024]{1,0:T(8,128)(2,1)S(1)} %slice.21), channel_id=1, source_target_pairs={{0,8},{8,16},{16,24},{24,28},{28,20},{20,12},{12,4},{4,0},{1,9},{9... | collective-permute-start | bytes 393224 | tf_op jit(solution)/shard_map/ppermute | solution.py:521
  70.3 5.2 %collective-permute-start.22 = (bf16[64,1024]{1,0:T(8,128)(2,1)S(1)}, bf16[64,1024]{1,0:T(8,128)(2,1)S(1)}, u32[]{:S(2)}, u32[]{:S(2)}) collective-permute-start(bf16[64,1024]{1,0:T(8,128)(2,1)S(1)} %slice.22), channel_id=1, source_target_pairs={{8,0},{16,8},{24,16},{28,24},{20,28},{12,20},{4,12},{0,4},{9,1},{1... | collective-permute-start | bytes 393224 | tf_op jit(solution)/shard_map/ppermute | solution.py:522

commit v5 on v4

--- a/solution.py
+++ b/solution.py
@@ -188,8 +188,12 @@
     return (turned << 1 & (1 << bits) - 1) | turned >> bits - 1
 
 
-def chunk_kernel(block_ref, after_ref, *outs):
-    del after_ref
+def relay_kernel(block_ref, after_ref, out_ref):
+    del after_ref
+    out_ref[...] = block_ref[...]
+
+
+def chunk_kernel(block_ref, *outs):
     columns = outs[0].shape[1]
     low = lax.axis_index("seq") % len(outs)
     for r, out in enumerate(outs):
@@ -327,8 +331,6 @@
                 blocks[i ^ 1 << digit] = to_group(blocks[i], 1 << digit)
         return [blocks[i] for i in range(heads)]
 
-    grad_blocks = every_group(own_grad)
-
     per = devices // heads
     route = [
         (
@@ -340,6 +342,32 @@
         for group_at in range(heads)
     ]
     turned = lax.ppermute(own_grad, ("seq", "head"), route)
+    chunks = pl.pallas_call(
+        chunk_kernel,
+        out_shape=(like((rows, columns_dev), BF),) * per,
+        in_specs=[VMEM],
+        out_specs=(VMEM,) * per,
+        compiler_params=PARAMS,
+        cost_estimate=cost(0, 2 * moved_head),
+    )(turned)
+
+    def relayed(block):
+        return pl.pallas_call(
+            relay_kernel,
+            out_shape=like(block.shape, block.dtype),
+            in_specs=[VMEM, ANY],
+            out_specs=VMEM,
+            compiler_params=PARAMS,
+            cost_estimate=cost(0, 2 * moved_head),
+        )(block, chunks[-1])
+
+    grad_blocks = {0: own_grad}
+    for digit in reversed(range(head_bits)):
+        for i in sorted(grad_blocks):
+            block = relayed(grad_blocks[i]) if i else own_grad
+            grad_blocks[i ^ 1 << digit] = to_group(block, 1 << digit)
+    grad_blocks = [grad_blocks[i] for i in range(heads)]
+
     partner_states = []
     running, arrived = own_state, None
     for digit in range(top):
@@ -376,15 +404,6 @@
         cost_estimate=cost(2 * flops_head, 12 * moved_head),
     )(hbm(queries), kh, vh, hbm(level_weights), hbm(out_proj), running)
 
-    chunks = pl.pallas_call(
-        chunk_kernel,
-        out_shape=(like((rows, columns_dev), BF),) * per,
-        in_specs=[VMEM, ANY],
-        out_specs=(VMEM,) * per,
-        compiler_params=PARAMS,
-        cost_estimate=cost(0, 2 * moved_head),
-    )(turned, qw)
-    own_chunks = chunks
     chunks = [chunks[0]] + [
         lax.ppermute(chunks[r], "seq", [(at, at ^ r) for at in range(devices)])
         for r in range(1, per)
@@ -396,7 +415,7 @@
         out_specs=(VMEM,) * (1 + seq_bits),
         compiler_params=PARAMS,
         cost_estimate=cost(2 * rows * width * out_proj.shape[1], 2 * width * out_proj.shape[1]),
-    )(*grad_blocks, w, qw, own_chunks[-1])
+    )(*grad_blocks, w, qw, running)
 
     meeting = pl.pallas_call(
         functools.partial(meet_kernel, top)

time: 78 us -> 81.5 us (1.045)
  waiting for transfers between devices: 24.6 us -> 29.2 us
  starting transfers between devices: 31.4 us -> 30.3 us
    ppermute x8, waiting for transfers between devices: 1.17 us -> 8.46 us  [to_group(): return lax.ppermute(block, 'head', [(at, at ^ i) for at in range(heads)])]
    ppermute x5, starting transfers between devices: 9.65 us -> 7.12 us  [across(): return lax.ppermute(block, axis, route)]
    ppermute x5, waiting for transfers between devices: 14.9 us -> 13.1 us  [across(): return lax.ppermute(block, axis, route)]
    ppermute x8, starting transfers between devices: 9.72 us -> 11.4 us  [to_group(): return lax.ppermute(block, 'head', [(at, at ^ i) for at in range(heads)])]
    ppermute x3, starting transfers between devices: 2.98 us -> 4.34 us  [body(): ahead = lax.ppermute(ahead, 'seq', forward)]
    ppermute x3, starting transfers between devices: 4.41 us -> 3.13 us  [body(): behind = lax.ppermute(behind, 'seq', backward)]
    ppermute x3, waiting for transfers between devices: 8.49 us -> 7.42 us  [body(): ahead = lax.ppermute(ahead, 'seq', forward)]
  transfers between devices with their start and end apart: 23 -> 23, of which waited for: 8 -> 8; matrix products, arithmetic and copies ran while one was open for 1% -> 1% of each run, Pallas kernels for 20% -> 19%
where the time goes in v5:
time: 81.5 us; the launch traced here: 81.4 us
  starting transfers between devices  30.3 us (37%)
  waiting for transfers between devices  29.2 us (36%)
  Pallas kernels  20.1 us (25%)
  other arithmetic  0.94 us (1%)
  between operations  0.83 us (1%)
    ppermute x5, waiting for transfers between devices, across(): return lax.ppermute(block, axis, route)  13.1 us
    ppermute x8, starting transfers between devices, to_group(): return lax.ppermute(block, 'head', [(at, at ^ i) for at in range(heads)])  11.4 us
    ppermute x8, waiting for transfers between devices, to_group(): return lax.ppermute(block, 'head', [(at, at ^ i) for at in range(heads)])  8.46 us
    ppermute x3, waiting for transfers between devices, body(): ahead = lax.ppermute(ahead, 'seq', forward)  7.42 us
    ppermute x5, starting transfers between devices, across(): return lax.ppermute(block, axis, route)  7.12 us
    ppermute x3, starting transfers between devices, body(): ahead = lax.ppermute(ahead, 'seq', forward)  4.34 us
    pallas_call x1, Pallas kernels, body(): pl.pallas_call(local_kernel, out_shape=(pltpu.VMEM((heads_dev, rows, rows...  3.66 us
    ppermute x3, starting transfers between devices, body(): behind = lax.ppermute(behind, 'seq', backward)  3.13 us
  transfers between devices with their start and end apart: 23, of which 8 were waited for; matrix products, arithmetic and copies ran while one was open for 1% of the time, Pallas kernels for 19%

profile of v5, /device:TPU:0, one launch (start us, length us, event | category | flops | bytes accessed | tf_op | source)
XLA Modules:
  0.0 81.4 jit_solution(3490305054825575198)
XLA Ops:
  0.6 2.4 %shard_map.101 = (bf16[8,128,128]{2,1,0:T(8,128)(2,1)S(1)}, bf16[8,128,128]{2,1,0:T(8,128)(2,1)S(1)}, bf16[8,128,128]{2,1,0:T(8,128)(2,1)S(1)}, bf16[128,1024]{1,0:T(8,128)(2,1)S(1)}) custom-call(f32[128,8,128]{2,1,0:T(8,128)} %k_hbm.1, f32[128,8,128]{2,1,0:T(8,128)} %v_hbm.1, bf16[128,1024]{1,0:T(8,128)(2,1)} %grad_hbm.1), custom_call_target="tpu_custom_call" | custom-call | flops 33554432 | bytes 1835008 | tf_op jit(solution)/shard_map/pallas_call | solution.py:310
  3.1 0.7 collective-permute-start.4
  3.8 6.8 %collective-permute-start.3 = (bf16[128,1024]{1,0:T(8,128)(2,1)S(1)}, bf16[128,1024]{1,0:T(8,128)(2,1)S(1)}, u32[]{:S(2)}, u32[]{:S(2)}) collective-permute-start(bf16[128,1024]{1,0:T(8,128)(2,1)S(1)} %get-tuple-element.33.refs_0_), channel_id=1, source_target_pairs={{0,2},{1,3},{2,0},{3,1},{4,6},{5,7},{6,4},{7,5},{8,10},{9,11},{10,... | collective-permute-start | bytes 786440 | tf_op jit(solution)/shard_map/ppermute | solution.py:325
  10.6 1.5 %collective-permute-start = (bf16[8,128,128]{2,1,0:T(8,128)(2,1)S(1)}, bf16[8,128,128]{2,1,0:T(8,128)(2,1)S(1)}, u32[]{:S(2)}, u32[]{:S(2)}) collective-permute-start(bf16[8,128,128]{2,1,0:T(8,128)(2,1)S(1)} %get-tuple-element.30.running_ref), channel_id=1, source_target_pairs={{0,4},{4,0},{8,12},{12,8},{16,20},{20,16},{24,28},{28,24},{1,5},{5... | collective-permute-start | bytes 786440 | tf_op jit(solution)/shard_map/ppermute | solution.py:44
  12.1 0.5 collective-permute-start.2
  12.7 0.0 collective-permute-done.4.block_ref
  12.7 8.4 %collective-permute-done.3.block_ref.refs_2_ = bf16[128,1024]{1,0:T(8,128)(2,1)S(1)} collective-permute-done((bf16[128,1024]{1,0:T(8,128)(2,1)S(1)}, bf16[128,1024]{1,0:T(8,128)(2,1)S(1)}, u32[]{:S(2)}, u32[]{:S(2)}) %collective-permute-start.3) | collective-permute-done | bytes 262176 | tf_op jit(solution)/shard_map/ppermute | solution.py:325
  21.1 0.4 collective-permute-start.5
  21.5 0.0 collective-permute-done.arrived_ref.refs_0_
  21.5 0.1 shard_map.102.after_ref.refs_6_.running_ref
  21.6 0.8 %collective-permute-start.1 = (bf16[8,128,128]{2,1,0:T(8,128)(2,1)S(1)}, bf16[8,128,128]{2,1,0:T(8,128)(2,1)S(1)}, u32[]{:S(2)}, u32[]{:S(2)}) collective-permute-start(bf16[8,128,128]{2,1,0:T(8,128)(2,1)S(1)} %shard_map.102.after_ref.refs_6_.running_ref), channel_id=1, source_target_pairs={{0,8},{8,0},{4,12},{12,4},{16,24},{24,16},{20,28},{28,20},{1,9},{9... | collective-permute-start | bytes 786440 | tf_op jit(solution)/shard_map/ppermute | solution.py:44
  22.5 1.5 %collective-permute-start.7 = (bf16[128,512]{1,0:T(8,128)(2,1)S(1)}, bf16[128,512]{1,0:T(8,128)(2,1)S(1)}, u32[]{:S(2)}, u32[]{:S(2)}) collective-permute-start(bf16[128,512]{1,0:T(8,128)(2,1)S(1)} %get-tuple-element.34.after_ref), channel_id=1, source_target_pairs={{0,4},{4,0},{8,12},{12,8},{16,20},{20,16},{24,28},{28,24},{1,5},{5... | collective-permute-start | bytes 393224 | tf_op jit(solution)/shard_map/ppermute | solution.py:408
  24.0 3.7 %shard_map.103 = (bf16[8,128,128]{2,1,0:T(8,128)(2,1)S(1)}, f32[8,128,128]{2,1,0:T(8,128)S(1)}, bf16[8,128,128]{2,1,0:T(8,128)(2,1)S(1)}, bf16[3,8,128,128]{3,2,...) custom-call(f32[128,8,128]{2,1,0:T(8,128)} %q_hbm.1, ...), custom_call_target="tpu_custom_call" | custom-call | flops 67108864 | bytes 3145728 | tf_op jit(solution)/shard_map/pallas_call | solution.py:386
  27.6 0.0 collective-permute-done.2.refs_1_
  27.7 0.0 collective-permute-done.5.refs_3_
  27.7 2.8 %shard_map.106 = (bf16[1024,128]{1,0:T(8,128)(2,1)S(1)}, bf16[8,128,128]{2,1,0:T(8,128)(2,1)S(1)}, bf16[8,128,128]{2,1,0:T(8,128)(2,1)S(1)}, bf16[8,128,128]{2,1,0:T(8,128)(2,1)S(1)}) custom-call(bf16[128,1024]{1,0:T(8,128)(2,1)S(1)} %get-tuple-element.33.refs_0_, bf16[128,1024]{1,0:T(8,128)(2,1)S(1)} %collective-permute-done.2.refs_1_, ...), custom_call_target="tpu_custom_call" | custom-call | flops 1073741824 | bytes 8388608 | tf_op jit(solution)/shard_map/pallas_call | solution.py:411
  30.5 0.0 collective-permute-done.1.arrived_ref.refs_1_
  30.5 0.1 shard_map.107.after_ref
  30.6 2.9 %collective-permute-start.6 = (bf16[8,128,128]{2,1,0:T(8,128)(2,1)S(1)}, bf16[8,128,128]{2,1,0:T(8,128)(2,1)S(1)}, u32[]{:S(2)}, u32[]{:S(2)}) collective-permute-start(bf16[8,128,128]{2,1,0:T(8,128)(2,1)S(1)} %shard_map.107.after_ref), channel_id=1, source_target_pairs={{0,16},{16,0},{4,20},{20,4},{8,24},{24,8},{12,28},{28,12},{1,17},{... | collective-permute-start | bytes 786440 | tf_op jit(solution)/shard_map/ppermute | solution.py:44
  33.5 0.0 collective-permute-done.7.refs_1_
  33.5 0.1 collective-permute-start.8
  33.6 1.8 %collective-permute-start.9 = (bf16[2,128,512]{2,1,0:T(8,128)(2,1)S(1)}, bf16[2,128,512]{2,1,0:T(8,128)(2,1)S(1)}, u32[]{:S(2)}, u32[]{:S(2)}) collective-permute-start(bf16[2,128,512]{2,1,0:T(8,128)(2,1)S(1)} %shard_map.109.refs_4_.refs_0_), channel_id=1, source_target_pairs={{0,2},{1,3},{2,0},{3,1},{4,6},{5,7},{6,4},{7,5},{8,10},{9,11},{10,... | collective-permute-start | bytes 786440 | tf_op jit(solution)/shard_map/ppermute | solution.py:325
  35.4 0.1 collective-permute-start.10
  35.5 1.3 %shard_map.108 = (f32[8,128,128]{2,1,0:T(8,128)S(1)}, f32[8,128,128]{2,1,0:T(8,128)S(1)}, f32[8,128,128]{2,1,0:T(8,128)S(1)}) custom-call(bf16[1024,128]{1,0:T(8,128)(2,1)S(1)} %get-tuple-element.37.gt_ref, bf16[8,128,128]{2,1,0:T(8,128)(2,1)S(1)} %get-tuple-element.38.qh_ref, bf16[8,128,128]{2,1,0:T(8,128)(2,1)S(1)} %get-tuple-element.28.kh_ref, ...), custom_call_target="tpu_custom_call" | custom-call | flops 201326592 | bytes 3670016 | tf_op jit(solution)/shard_map/pallas_call | solution.py:454
  36.8 8.5 %collective-permute-done.6.refs_2_.refs_0_.state_ref = bf16[8,128,128]{2,1,0:T(8,128)(2,1)S(1)} collective-permute-done((bf16[8,128,128]{2,1,0:T(8,128)(2,1)S(1)}, bf16[8,128,128]{2,1,0:T(8,128)(2,1)S(1)}, u32[]{:S(2)}, u32[]{:S(2)}) %collective-permute-start.6) | collective-permute-done | bytes 262176 | tf_op jit(solution)/shard_map/ppermute | solution.py:44
  45.3 0.4 shard_map.110.after_ref.att_ref.refs_0_
  45.7 0.8 collective-permute-start.13
  46.4 1.3 %collective-permute-start.16 = (bf16[128,1024]{1,0:T(8,128)(2,1)S(1)}, bf16[128,1024]{1,0:T(8,128)(2,1)S(1)}, u32[]{:S(2)}, u32[]{:S(2)}) collective-permute-start(bf16[128,1024]{1,0:T(8,128)(2,1)S(1)} %shard_map.110.after_ref.att_ref.refs_0_), channel_id=1, source_target_pairs={{8,0},{16,8},{24,16},{28,24},{20,28},{12,20},{4,12},{0,4},{9,1},{1... | collective-permute-start | bytes 786440 | tf_op jit(solution)/shard_map/ppermute | solution.py:531
  47.7 0.1 shard_map.111.refs_0_
  47.8 1.3 %shard_map.112.refs_1_ = f32[128,8,128]{2,1,0:T(8,128)} custom-call(bf16[1024,128]{1,0:T(8,128)(2,1)S(1)} %get-tuple-element.37.gt_ref, f32[5,8,128]{2,1,0:T(8,128)S(1)} %get-tuple-element.40.lam_ref, f32[8,128,128]{2,1,0:T(8,128)S(1)} %get-tuple-element.44.dql_ref, bf16[8,128,128]{2,1,0:T(8,128)(2,1)S(1)} %collective-permute-done.6.refs_2_.refs_0_.state_ref, ...), custom_call_target="tpu_custom_call" | custom-call | flops 33554432 | bytes 1572864 | tf_op jit(solution)/shard_map/pallas_call | solution.py:486
  49.2 0.0 collective-permute-done.8.refs_1_
  49.2 0.0 collective-permute-done.9.refs_2_
  49.2 0.0 collective-permute-done.10.refs_3_
  49.2 0.1 shard_map.113.refs_2_.cols_ref
  49.3 1.3 %shard_map.114 = (bf16[2,128,1024]{2,1,0:T(8,128)(2,1)S(1)}, f32[2,128,1024]{2,1,0:T(8,128)S(1)}) custom-call(bf16[128,1024]{1,0:T(8,128)(2,1)S(1)} %shard_map.110.after_ref.att_ref.refs_0_, bf16[1024,4096]{1,0:T(8,128)(2,1)S(1)} %get-tuple-element.35.refs_4_.w_ref, bf16[8,128,128]{2,1,0:T(8,128)(2,1)S(1)} %shard_map.111.refs_0_, ...), custom_call_target="tpu_custom_call" | custom-call | flops 1073741824 | bytes 8388608 | tf_op jit(solution)/shard_map/pallas_call | solution.py:495
  50.6 0.1 collective-permute-start.11
  50.6 0.8 collective-permute-start.19
  51.4 2.3 %collective-permute-done.13.refs_1_ = bf16[128,1024]{1,0:T(8,128)(2,1)S(1)} collective-permute-done((bf16[128,1024]{1,0:T(8,128)(2,1)S(1)}, bf16[128,1024]{1,0:T(8,128)(2,1)S(1)}, u32[]{:S(2)}, u32[]{:S(2)}) %collective-permute-start.13) | collective-permute-done | bytes 262176 | tf_op jit(solution)/shard_map/ppermute | solution.py:530
  53.7 1.1 %collective-permute-start.14 = (bf16[128,1024]{1,0:T(8,128)(2,1)S(1)}, bf16[128,1024]{1,0:T(8,128)(2,1)S(1)}, u32[]{:S(2)}, u32[]{:S(2)}) collective-permute-start(bf16[128,1024]{1,0:T(8,128)(2,1)S(1)} %collective-permute-done.13.refs_1_), channel_id=1, source_target_pairs={{0,8},{8,16},{16,24},{24,28},{28,20},{20,12},{12,4},{4,0},{1,9},{9... | collective-permute-start | bytes 786440 | tf_op jit(solution)/shard_map/ppermute | solution.py:530
  54.8 0.2 collective-permute-done.16.refs_2_
  55.0 1.0 %collective-permute-start.17 = (bf16[128,1024]{1,0:T(8,128)(2,1)S(1)}, bf16[128,1024]{1,0:T(8,128)(2,1)S(1)}, u32[]{:S(2)}, u32[]{:S(2)}) collective-permute-start(bf16[128,1024]{1,0:T(8,128)(2,1)S(1)} %collective-permute-done.16.refs_2_), channel_id=1, source_target_pairs={{8,0},{16,8},{24,16},{28,24},{20,28},{12,20},{4,12},{0,4},{9,1},{1... | collective-permute-start | bytes 786440 | tf_op jit(solution)/shard_map/ppermute | solution.py:531
  56.0 4.6 %collective-permute-done.19.refs_1_ = bf16[8,128,128]{2,1,0:T(8,128)(2,1)S(1)} collective-permute-done((bf16[8,128,128]{2,1,0:T(8,128)(2,1)S(1)}, bf16[8,128,128]{2,1,0:T(8,128)(2,1)S(1)}, u32[]{:S(2)}, u32[]{:S(2)}) %collective-permute-start.19) | collective-permute-done | bytes 262176 | tf_op jit(solution)/shard_map/ppermute | solution.py:44
  60.6 0.1 shard_map.117
  60.7 1.1 %collective-permute-start.20 = (bf16[8,128,128]{2,1,0:T(8,128)(2,1)S(1)}, bf16[8,128,128]{2,1,0:T(8,128)(2,1)S(1)}, u32[]{:S(2)}, u32[]{:S(2)}) collective-permute-start(bf16[8,128,128]{2,1,0:T(8,128)(2,1)S(1)} %shard_map.117), channel_id=1, source_target_pairs={{0,4},{4,0},{8,12},{12,8},{16,20},{20,16},{24,28},{28,24},{1,5},{5... | collective-permute-start | bytes 786440 | tf_op jit(solution)/shard_map/ppermute | solution.py:44
  61.8 1.6 %collective-permute-done.14.refs_3_ = bf16[128,1024]{1,0:T(8,128)(2,1)S(1)} collective-permute-done((bf16[128,1024]{1,0:T(8,128)(2,1)S(1)}, bf16[128,1024]{1,0:T(8,128)(2,1)S(1)}, u32[]{:S(2)}, u32[]{:S(2)}) %collective-permute-start.14) | collective-permute-done | bytes 262176 | tf_op jit(solution)/shard_map/ppermute | solution.py:530
  63.4 2.5 %collective-permute-start.15 = (bf16[128,1024]{1,0:T(8,128)(2,1)S(1)}, bf16[128,1024]{1,0:T(8,128)(2,1)S(1)}, u32[]{:S(2)}, u32[]{:S(2)}) collective-permute-start(bf16[128,1024]{1,0:T(8,128)(2,1)S(1)} %collective-permute-done.14.refs_3_), channel_id=1, source_target_pairs={{0,8},{8,16},{16,24},{24,28},{28,20},{20,12},{12,4},{4,0},{1,9},{9... | collective-permute-start | bytes 786440 | tf_op jit(solution)/shard_map/ppermute | solution.py:530
  65.9 0.0 collective-permute-done.17.refs_4_
  65.9 0.8 collective-permute-start.18
  66.7 0.0 collective-permute-done.11
  66.7 0.2 convert_add_fusion
  67.0 1.6 %collective-permute-start.12 = (bf16[1,128,1024]{2,1,0:T(8,128)(2,1)S(1)}, bf16[1,128,1024]{2,1,0:T(8,128)(2,1)S(1)}, u32[]{:S(2)}, u32[]{:S(2)}) collective-permute-start(bf16[1,128,1024]{2,1,0:T(8,128)(2,1)S(1)} %slice.29), channel_id=1, source_target_pairs={{0,2},{1,3},{2,0},{3,1},{4,6},{5,7},{6,4},{7,5},{8,10},{9,11},{10,... | collective-permute-start | bytes 786440 | tf_op jit(solution)/shard_map/ppermute | solution.py:325
  68.5 1.5 %shard_map.115.refs_2_ = f32[1024,512]{1,0:T(8,128)S(1)} custom-call(bf16[8,128,512]{2,1,0:T(8,128)(2,1)S(1)} %shard_map.113.refs_2_.cols_ref, bf16[128,1024]{1,0:T(8,128)(2,1)S(1)} %shard_map.110.after_ref.att_ref.refs_0_, bf16[128,1024]{1,0:T(8,128)(2,1)S(1)} %collective-permute-done.13.refs_1_, bf16[128,1024]{1,0:T(8,128)(2,1)S(1)} %collective-permute-done.16.refs_2_, ...), custom_call_target="tpu_custom_call" | custom-call | flops 671088640 | bytes 2097152 | tf_op jit(solution)/shard_map/pallas_call | solution.py:515
  70.1 3.5 %collective-permute-done.15.refs_0_ = bf16[128,1024]{1,0:T(8,128)(2,1)S(1)} collective-permute-done((bf16[128,1024]{1,0:T(8,128)(2,1)S(1)}, bf16[128,1024]{1,0:T(8,128)(2,1)S(1)}, u32[]{:S(2)}, u32[]{:S(2)}) %collective-permute-start.15) | collective-permute-done | bytes 262176 | tf_op jit(solution)/shard_map/ppermute | solution.py:530
  73.6 0.4 collective-permute-start.21
  74.0 0.0 collective-permute-done.18.refs_1_
  74.0 1.7 %collective-permute-start.22 = (bf16[64,1024]{1,0:T(8,128)(2,1)S(1)}, bf16[64,1024]{1,0:T(8,128)(2,1)S(1)}, u32[]{:S(2)}, u32[]{:S(2)}) collective-permute-start(bf16[64,1024]{1,0:T(8,128)(2,1)S(1)} %slice.22), channel_id=1, source_target_pairs={{8,0},{16,8},{24,16},{28,24},{20,28},{12,20},{4,12},{0,4},{9,1},{1... | collective-permute-start | bytes 393224 | tf_op jit(solution)/shard_map/ppermute | solution.py:541
  75.7 0.7 shard_map.116.after_ref.total_ref
  76.4 0.0 collective-permute-done.20.refs_2_
  76.5 1.7 %shard_map.118 = (f32[128,8,128]{2,1,0:T(8,128)}, f32[128,8,128]{2,1,0:T(8,128)}) custom-call(bf16[8,128,128]{2,1,0:T(8,128)(2,1)S(1)} %get-tuple-element.28.kh_ref, bf16[8,128,128]{2,1,0:T(8,128)(2,1)S(1)} %get-tuple-element.29.vh_ref, f32[8,128,128]{2,1,0:T(8,128)S(1)} %get-tuple-element.41.refs_3_.dkl_ref, f32[8,128,128]{2,1,0:T(8,128)S(1)} %get-tuple-element.47.dvl_ref, ...), custom_call_target="tpu_custom_call" | custom-call | flops 67108864 | bytes 2883584 | tf_op jit(solution)/shard_map/pallas_call | solution.py:543
  78.2 0.0 collective-permute-done.12
  78.2 0.8 fusion.1
  79.0 0.0 collective-permute-done.21.low_ref
  79.0 0.1 collective-permute-done.22.high_ref
  79.0 2.4 %shard_map.119 = f32[1024,512]{1,0:T(8,128)} custom-call(bf16[8,128,512]{2,1,0:T(8,128)(2,1)S(1)} %shard_map.113.refs_2_.cols_ref, bf16[64,1024]{1,0:T(8,128)(2,1)S(1)} %collective-permute-done.21.low_ref, bf16[64,1024]{1,0:T(8,128)(2,1)S(1)} %collective-permute-done.22.high_ref, f32[1024,512]{1,0:T(8,128)S(1)} %shard_map.116.after_ref.total_ref, ...), custom_call_target="tpu_custom_call" | custom-call | flops 134217728 | bytes 4194304 | tf_op jit(solution)/shard_map/pallas_call | solution.py:552
  (6 shorter events, 0.1 us)
Async XLA Ops:
  3.1 9.6 %collective-permute-start.4 = (bf16[128,1024]{1,0:T(8,128)(2,1)S(1)}, bf16[128,1024]{1,0:T(8,128)(2,1)S(1)}, u32[]{:S(2)}, u32[]{:S(2)}) collective-permute-start(bf16[128,1024]{1,0:T(8,128)(2,1)S(1)} %get-tuple-element.33.refs_0_), channel_id=1, source_target_pairs={{0,0},{1,10},{2,18},{3,24},{4,4},{5,14},{6,22},{7,28},{8,2},{9,8},... | collective-permute-start | bytes 786440 | tf_op jit(solution)/shard_map/ppermute | solution.py:344
  3.8 17.4 %collective-permute-start.3 = (bf16[128,1024]{1,0:T(8,128)(2,1)S(1)}, bf16[128,1024]{1,0:T(8,128)(2,1)S(1)}, u32[]{:S(2)}, u32[]{:S(2)}) collective-permute-start(bf16[128,1024]{1,0:T(8,128)(2,1)S(1)} %get-tuple-element.33.refs_0_), channel_id=1, source_target_pairs={{0,2},{1,3},{2,0},{3,1},{4,6},{5,7},{6,4},{7,5},{8,10},{9,11},{10,... | collective-permute-start | bytes 786440 | tf_op jit(solution)/shard_map/ppermute | solution.py:325
  10.6 10.9 %collective-permute-start = (bf16[8,128,128]{2,1,0:T(8,128)(2,1)S(1)}, bf16[8,128,128]{2,1,0:T(8,128)(2,1)S(1)}, u32[]{:S(2)}, u32[]{:S(2)}) collective-permute-start(bf16[8,128,128]{2,1,0:T(8,128)(2,1)S(1)} %get-tuple-element.30.running_ref), channel_id=1, source_target_pairs={{0,4},{4,0},{8,12},{12,8},{16,20},{20,16},{24,28},{28,24},{1,5},{5... | collective-permute-start | bytes 786440 | tf_op jit(solution)/shard_map/ppermute | solution.py:44
  12.1 15.5 %collective-permute-start.2 = (bf16[128,1024]{1,0:T(8,128)(2,1)S(1)}, bf16[128,1024]{1,0:T(8,128)(2,1)S(1)}, u32[]{:S(2)}, u32[]{:S(2)}) collective-permute-start(bf16[128,1024]{1,0:T(8,128)(2,1)S(1)} %get-tuple-element.33.refs_0_), channel_id=1, source_target_pairs={{0,1},{1,0},{2,3},{3,2},{4,5},{5,4},{6,7},{7,6},{8,9},{9,8},{10,11... | collective-permute-start | bytes 786440 | tf_op jit(solution)/shard_map/ppermute | solution.py:325
  21.1 6.5 %collective-permute-start.5 = (bf16[128,1024]{1,0:T(8,128)(2,1)S(1)}, bf16[128,1024]{1,0:T(8,128)(2,1)S(1)}, u32[]{:S(2)}, u32[]{:S(2)}) collective-permute-start(bf16[128,1024]{1,0:T(8,128)(2,1)S(1)} %shard_map.105), channel_id=1, source_target_pairs={{0,1},{1,0},{2,3},{3,2},{4,5},{5,4},{6,7},{7,6},{8,9},{9,8},{10,11... | collective-permute-start | bytes 786440 | tf_op jit(solution)/shard_map/ppermute | solution.py:325
  21.6 8.9 %collective-permute-start.1 = (bf16[8,128,128]{2,1,0:T(8,128)(2,1)S(1)}, bf16[8,128,128]{2,1,0:T(8,128)(2,1)S(1)}, u32[]{:S(2)}, u32[]{:S(2)}) collective-permute-start(bf16[8,128,128]{2,1,0:T(8,128)(2,1)S(1)} %shard_map.102.after_ref.refs_6_.running_ref), channel_id=1, source_target_pairs={{0,8},{8,0},{4,12},{12,4},{16,24},{24,16},{20,28},{28,20},{1,9},{9... | collective-permute-start | bytes 786440 | tf_op jit(solution)/shard_map/ppermute | solution.py:44
  22.5 11.0 %collective-permute-start.7 = (bf16[128,512]{1,0:T(8,128)(2,1)S(1)}, bf16[128,512]{1,0:T(8,128)(2,1)S(1)}, u32[]{:S(2)}, u32[]{:S(2)}) collective-permute-start(bf16[128,512]{1,0:T(8,128)(2,1)S(1)} %get-tuple-element.34.after_ref), channel_id=1, source_target_pairs={{0,4},{4,0},{8,12},{12,8},{16,20},{20,16},{24,28},{28,24},{1,5},{5... | collective-permute-start | bytes 393224 | tf_op jit(solution)/shard_map/ppermute | solution.py:408
  30.6 14.7 %collective-permute-start.6 = (bf16[8,128,128]{2,1,0:T(8,128)(2,1)S(1)}, bf16[8,128,128]{2,1,0:T(8,128)(2,1)S(1)}, u32[]{:S(2)}, u32[]{:S(2)}) collective-permute-start(bf16[8,128,128]{2,1,0:T(8,128)(2,1)S(1)} %shard_map.107.after_ref), channel_id=1, source_target_pairs={{0,16},{16,0},{4,20},{20,4},{8,24},{24,8},{12,28},{28,12},{1,17},{... | collective-permute-start | bytes 786440 | tf_op jit(solution)/shard_map/ppermute | solution.py:44
  33.5 15.6 %collective-permute-start.8 = (bf16[2,128,512]{2,1,0:T(8,128)(2,1)S(1)}, bf16[2,128,512]{2,1,0:T(8,128)(2,1)S(1)}, u32[]{:S(2)}, u32[]{:S(2)}) collective-permute-start(bf16[2,128,512]{2,1,0:T(8,128)(2,1)S(1)} %shard_map.109.refs_4_.refs_0_), channel_id=1, source_target_pairs={{0,1},{1,0},{2,3},{3,2},{4,5},{5,4},{6,7},{7,6},{8,9},{9,8},{10,11... | collective-permute-start | bytes 786440 | tf_op jit(solution)/shard_map/ppermute | solution.py:325
  33.6 15.6 %collective-permute-start.9 = (bf16[2,128,512]{2,1,0:T(8,128)(2,1)S(1)}, bf16[2,128,512]{2,1,0:T(8,128)(2,1)S(1)}, u32[]{:S(2)}, u32[]{:S(2)}) collective-permute-start(bf16[2,128,512]{2,1,0:T(8,128)(2,1)S(1)} %shard_map.109.refs_4_.refs_0_), channel_id=1, source_target_pairs={{0,2},{1,3},{2,0},{3,1},{4,6},{5,7},{6,4},{7,5},{8,10},{9,11},{10,... | collective-permute-start | bytes 786440 | tf_op jit(solution)/shard_map/ppermute | solution.py:325
  35.4 13.7 %collective-permute-start.10 = (bf16[2,128,512]{2,1,0:T(8,128)(2,1)S(1)}, bf16[2,128,512]{2,1,0:T(8,128)(2,1)S(1)}, u32[]{:S(2)}, u32[]{:S(2)}) collective-permute-start(bf16[2,128,512]{2,1,0:T(8,128)(2,1)S(1)} %shard_map.109.refs_4_.refs_0_), channel_id=1, source_target_pairs={{0,3},{1,2},{2,1},{3,0},{4,7},{5,6},{6,5},{7,4},{8,11},{9,10},{10,... | collective-permute-start | bytes 786440 | tf_op jit(solution)/shard_map/ppermute | solution.py:325
  45.7 8.1 %collective-permute-start.13 = (bf16[128,1024]{1,0:T(8,128)(2,1)S(1)}, bf16[128,1024]{1,0:T(8,128)(2,1)S(1)}, u32[]{:S(2)}, u32[]{:S(2)}) collective-permute-start(bf16[128,1024]{1,0:T(8,128)(2,1)S(1)} %shard_map.110.after_ref.att_ref.refs_0_), channel_id=1, source_target_pairs={{0,8},{8,16},{16,24},{24,28},{28,20},{20,12},{12,4},{4,0},{1,9},{9... | collective-permute-start | bytes 786440 | tf_op jit(solution)/shard_map/ppermute | solution.py:530
  46.4 8.5 %collective-permute-start.16 = (bf16[128,1024]{1,0:T(8,128)(2,1)S(1)}, bf16[128,1024]{1,0:T(8,128)(2,1)S(1)}, u32[]{:S(2)}, u32[]{:S(2)}) collective-permute-start(bf16[128,1024]{1,0:T(8,128)(2,1)S(1)} %shard_map.110.after_ref.att_ref.refs_0_), channel_id=1, source_target_pairs={{8,0},{16,8},{24,16},{28,24},{20,28},{12,20},{4,12},{0,4},{9,1},{1... | collective-permute-start | bytes 786440 | tf_op jit(solution)/shard_map/ppermute | solution.py:531
  50.6 16.2 %collective-permute-start.11 = (bf16[2,128,1024]{2,1,0:T(8,128)(2,1)S(1)}, bf16[2,128,1024]{2,1,0:T(8,128)(2,1)S(1)}, u32[]{:S(2)}, u32[]{:S(2)}) collective-permute-start(bf16[2,128,1024]{2,1,0:T(8,128)(2,1)S(1)} %get-tuple-element.46), channel_id=1, source_target_pairs={{0,1},{1,0},{2,3},{3,2},{4,5},{5,4},{6,7},{7,6},{8,9},{9,8},{10,11... | collective-permute-start | bytes 1572872 | tf_op jit(solution)/shard_map/ppermute | solution.py:325
  50.6 10.0 %collective-permute-start.19 = (bf16[8,128,128]{2,1,0:T(8,128)(2,1)S(1)}, bf16[8,128,128]{2,1,0:T(8,128)(2,1)S(1)}, u32[]{:S(2)}, u32[]{:S(2)}) collective-permute-start(bf16[8,128,128]{2,1,0:T(8,128)(2,1)S(1)} %shard_map.111.refs_0_), channel_id=1, source_target_pairs={{0,8},{8,0},{4,12},{12,4},{16,24},{24,16},{20,28},{28,20},{1,9},{9... | collective-permute-start | bytes 786440 | tf_op jit(solution)/shard_map/ppermute | solution.py:44
  53.7 9.7 %collective-permute-start.14 = (bf16[128,1024]{1,0:T(8,128)(2,1)S(1)}, bf16[128,1024]{1,0:T(8,128)(2,1)S(1)}, u32[]{:S(2)}, u32[]{:S(2)}) collective-permute-start(bf16[128,1024]{1,0:T(8,128)(2,1)S(1)} %collective-permute-done.13.refs_1_), channel_id=1, source_target_pairs={{0,8},{8,16},{16,24},{24,28},{28,20},{20,12},{12,4},{4,0},{1,9},{9... | collective-permute-start | bytes 786440 | tf_op jit(solution)/shard_map/ppermute | solution.py:530
  55.0 10.9 %collective-permute-start.17 = (bf16[128,1024]{1,0:T(8,128)(2,1)S(1)}, bf16[128,1024]{1,0:T(8,128)(2,1)S(1)}, u32[]{:S(2)}, u32[]{:S(2)}) collective-permute-start(bf16[128,1024]{1,0:T(8,128)(2,1)S(1)} %collective-permute-done.16.refs_2_), channel_id=1, source_target_pairs={{8,0},{16,8},{24,16},{28,24},{20,28},{12,20},{4,12},{0,4},{9,1},{1... | collective-permute-start | bytes 786440 | tf_op jit(solution)/shard_map/ppermute | solution.py:531
  60.7 15.7 %collective-permute-start.20 = (bf16[8,128,128]{2,1,0:T(8,128)(2,1)S(1)}, bf16[8,128,128]{2,1,0:T(8,128)(2,1)S(1)}, u32[]{:S(2)}, u32[]{:S(2)}) collective-permute-start(bf16[8,128,128]{2,1,0:T(8,128)(2,1)S(1)} %shard_map.117), channel_id=1, source_target_pairs={{0,4},{4,0},{8,12},{12,8},{16,20},{20,16},{24,28},{28,24},{1,5},{5... | collective-permute-start | bytes 786440 | tf_op jit(solution)/shard_map/ppermute | solution.py:44
  63.4 10.1 %collective-permute-start.15 = (bf16[128,1024]{1,0:T(8,128)(2,1)S(1)}, bf16[128,1024]{1,0:T(8,128)(2,1)S(1)}, u32[]{:S(2)}, u32[]{:S(2)}) collective-permute-start(bf16[128,1024]{1,0:T(8,128)(2,1)S(1)} %collective-permute-done.14.refs_3_), channel_id=1, source_target_pairs={{0,8},{8,16},{16,24},{24,28},{28,20},{20,12},{12,4},{4,0},{1,9},{9... | collective-permute-start | bytes 786440 | tf_op jit(solution)/shard_map/ppermute | solution.py:530
  65.9 8.1 %collective-permute-start.18 = (bf16[128,1024]{1,0:T(8,128)(2,1)S(1)}, bf16[128,1024]{1,0:T(8,128)(2,1)S(1)}, u32[]{:S(2)}, u32[]{:S(2)}) collective-permute-start(bf16[128,1024]{1,0:T(8,128)(2,1)S(1)} %collective-permute-done.17.refs_4_), channel_id=1, source_target_pairs={{8,0},{16,8},{24,16},{28,24},{20,28},{12,20},{4,12},{0,4},{9,1},{1... | collective-permute-start | bytes 786440 | tf_op jit(solution)/shard_map/ppermute | solution.py:531
  67.0 11.2 %collective-permute-start.12 = (bf16[1,128,1024]{2,1,0:T(8,128)(2,1)S(1)}, bf16[1,128,1024]{2,1,0:T(8,128)(2,1)S(1)}, u32[]{:S(2)}, u32[]{:S(2)}) collective-permute-start(bf16[1,128,1024]{2,1,0:T(8,128)(2,1)S(1)} %slice.29), channel_id=1, source_target_pairs={{0,2},{1,3},{2,0},{3,1},{4,6},{5,7},{6,4},{7,5},{8,10},{9,11},{10,... | collective-permute-start | bytes 786440 | tf_op jit(solution)/shard_map/ppermute | solution.py:325
  73.6 5.4 %collective-permute-start.21 = (bf16[64,1024]{1,0:T(8,128)(2,1)S(1)}, bf16[64,1024]{1,0:T(8,128)(2,1)S(1)}, u32[]{:S(2)}, u32[]{:S(2)}) collective-permute-start(bf16[64,1024]{1,0:T(8,128)(2,1)S(1)} %slice.21), channel_id=1, source_target_pairs={{0,8},{8,16},{16,24},{24,28},{28,20},{20,12},{12,4},{4,0},{1,9},{9... | collective-permute-start | bytes 393224 | tf_op jit(solution)/shard_map/ppermute | solution.py:540
  74.0 5.0 %collective-permute-start.22 = (bf16[64,1024]{1,0:T(8,128)(2,1)S(1)}, bf16[64,1024]{1,0:T(8,128)(2,1)S(1)}, u32[]{:S(2)}, u32[]{:S(2)}) collective-permute-start(bf16[64,1024]{1,0:T(8,128)(2,1)S(1)} %slice.22), channel_id=1, source_target_pairs={{8,0},{16,8},{24,16},{28,24},{20,28},{12,20},{4,12},{0,4},{9,1},{1... | collective-permute-start | bytes 393224 | tf_op jit(solution)/shard_map/ppermute | solution.py:541

commit v6 on v3

--- a/solution.py
+++ b/solution.py
@@ -48,11 +48,13 @@
     return pltpu.with_memory_space_constraint(array, pltpu.HBM)
 
 
-def state_kernel(k_hbm, v_hbm, grad_hbm, s_ref, kh_ref, vh_ref, grad_ref, k_ref, v_ref, sems):
+def state_kernel(k_hbm, v_hbm, grad_hbm, *refs):
+    s_ref, kh_ref, vh_ref, grad_ref, low_ref, k_ref, v_ref, sems = refs
     copies = [
         pltpu.make_async_copy(k_hbm, k_ref, sems.at[0]),
         pltpu.make_async_copy(v_hbm, v_ref, sems.at[1]),
         pltpu.make_async_copy(grad_hbm, grad_ref, sems.at[2]),
+        pltpu.make_async_copy(grad_hbm.at[pl.ds(0, low_ref.shape[0])], low_ref, sems.at[3]),
     ]
     for copy in copies:
         copy.start()
@@ -65,6 +67,7 @@
         vh_ref[h] = v
         s_ref[h] = mm(k, v, TN).astype(BF)
     copies[2].wait()
+    copies[3].wait()
 
 
 def weight_of(lam_ref, h, rows):
@@ -187,12 +190,20 @@
     return (turned << 1 & (1 << bits) - 1) | turned >> bits - 1
 
 
-def chunk_kernel(block_ref, after_ref, *outs):
-    del after_ref
+def relay_kernel(block_ref, after_ref, out_ref):
+    del after_ref
+    out_ref[...] = block_ref[...]
+
+
+def chunk_kernel(low_ref, high_ref, after_ref, *outs):
+    del after_ref
+    half = low_ref.shape[0]
     columns = outs[0].shape[1]
     low = lax.axis_index("seq") % len(outs)
     for r, out in enumerate(outs):
-        out[...] = block_ref[:, pl.ds(pl.multiple_of((low ^ r) * columns, columns), columns)]
+        at = pl.ds(pl.multiple_of((low ^ r) * columns, columns), columns)
+        out[:half] = low_ref[:, at]
+        out[half:] = high_ref[:, at]
 
 
 def stack_kernel(after_ref, *refs):
@@ -302,15 +313,16 @@
     moved_head = 2 * rows * width
     top = seq_bits - 1
 
-    own_state, kh, vh, own_grad = pl.pallas_call(
+    half = rows // 2
+    own_state, kh, vh, own_grad, own_low = pl.pallas_call(
         state_kernel,
-        out_shape=(head_state, per_head, per_head, like(out_grad.shape, BF)),
+        out_shape=(head_state, per_head, per_head, like(out_grad.shape, BF), like((half, width), BF)),
         in_specs=[ANY] * 3,
-        out_specs=(VMEM,) * 4,
+        out_specs=(VMEM,) * 5,
         scratch_shapes=[
             pltpu.VMEM(keys.shape, F32),
             pltpu.VMEM(keys.shape, F32),
-            pltpu.SemaphoreType.DMA((3,)),
+            pltpu.SemaphoreType.DMA((4,)),
         ],
         compiler_params=PARAMS,
         cost_estimate=cost(flops_head, 7 * moved_head),
@@ -326,19 +338,6 @@
                 blocks[i ^ 1 << digit] = to_group(blocks[i], 1 << digit)
         return [blocks[i] for i in range(heads)]
 
-    grad_blocks = [own_grad] + [to_group(own_grad, i) for i in range(1, heads)]
-
-    per = devices // heads
-    route = [
-        (
-            (high * per + low) * heads + group_at,
-            (group_at * per + low) * heads + turned_group(high, group_at, head_bits),
-        )
-        for high in range(heads)
-        for low in range(per)
-        for group_at in range(heads)
-    ]
-    turned = lax.ppermute(out_grad, ("seq", "head"), route)
     probs_t, att_local, qh, qw, lam, w = pl.pallas_call(
         local_kernel,
         out_shape=(
@@ -360,18 +359,39 @@
         cost_estimate=cost(2 * flops_head, 12 * moved_head),
     )(hbm(queries), kh, vh, hbm(level_weights), hbm(out_proj))
 
-    chunks = pl.pallas_call(
-        chunk_kernel,
-        out_shape=(like((rows, columns_dev), BF),) * per,
-        in_specs=[VMEM, ANY],
-        out_specs=(VMEM,) * per,
-        compiler_params=PARAMS,
-        cost_estimate=cost(0, 2 * moved_head),
-    )(turned, qw)
-    own_chunks = chunks
-    chunks = [chunks[0]] + [
-        lax.ppermute(chunks[r], "seq", [(at, at ^ r) for at in range(devices)])
-        for r in range(1, per)
+    def relayed(block):
+        return pl.pallas_call(
+            relay_kernel,
+            out_shape=like(block.shape, block.dtype),
+            in_specs=[VMEM, ANY],
+            out_specs=VMEM,
+            compiler_params=PARAMS,
+            cost_estimate=cost(0, 2 * moved_head),
+        )(block, qw)
+
+    grad_blocks = {0: own_grad}
+    for digit in reversed(range(head_bits)):
+        for i in sorted(grad_blocks):
+            block = relayed(grad_blocks[i]) if i else own_grad
+            grad_blocks[i ^ 1 << digit] = to_group(block, 1 << digit)
+    grad_blocks = [grad_blocks[i] for i in range(heads)]
+
+    per = devices // heads
+    def turn_route(shift):
+        return [
+            (
+                (high * per + low) * heads + (group_at ^ shift),
+                (group_at * per + low) * heads + turned_group(high, group_at, head_bits),
+            )
+            for high in range(heads)
+            for low in range(per)
+            for group_at in range(heads)
+        ]
+
+    axes, far = ("seq", "head"), heads // 2
+    turned = [
+        lax.ppermute(own_low, axes, turn_route(0)),
+        lax.ppermute(grad_blocks[far][half:], axes, turn_route(far)),
     ]
     partner_states = []
     running, arrived = own_state, None
@@ -384,7 +404,7 @@
                 out_specs=VMEM,
                 compiler_params=PARAMS,
                 cost_estimate=cost(0, 3 * moved_head),
-            )(running, arrived, own_chunks[-1])
+            )(running, arrived, qw)
         arrived = across(running, "seq", digit)
         partner_states.append(arrived)
 
@@ -395,7 +415,7 @@
         out_specs=(VMEM,) * (1 + seq_bits),
         compiler_params=PARAMS,
         cost_estimate=cost(2 * rows * width * out_proj.shape[1], 2 * width * out_proj.shape[1]),
-    )(*grad_blocks, w, qw, own_chunks[-1])
+    )(*grad_blocks, w, qw, running)
 
     meeting = pl.pallas_call(
         functools.partial(meet_kernel, top)
@@ -412,6 +432,18 @@
     landed = [across(meeting, "seq", top)]
     partner_states.append(landed[0])
 
+    chunks = pl.pallas_call(
+        chunk_kernel,
+        out_shape=(like((rows, columns_dev), BF),) * per,
+        in_specs=[VMEM, VMEM, ANY],
+        out_specs=(VMEM,) * per,
+        compiler_params=PARAMS,
+        cost_estimate=cost(0, 2 * moved_head),
+    )(*turned, gt)
+    chunks = [chunks[0]] + [
+        lax.ppermute(chunks[r], "seq", [(at, at ^ r) for at in range(devices)])
+        for r in range(1, per)
+    ]
     stacked = pl.pallas_call(
         stack_kernel,
         out_shape=like((per, rows, columns_dev), BF),
@@ -505,7 +537,7 @@
 
     blocks, offsets = [attended], [(0, 0, rows)]
     ahead = behind = attended
-    half, steps, total = rows // 2, devices // 2, None
+    steps, total = devices // 2, None
     for step in range(1, steps):
         ahead = lax.ppermute(ahead, "seq", forward)
         behind = lax.ppermute(behind, "seq", backward)

time: 79.1 us -> 78.6 us (level)
  waiting for transfers between devices: 27.3 us -> 25.9 us
  starting transfers between devices: 29.8 us -> 30.7 us
    ppermute x8, waiting for transfers between devices: 6.05 us -> 1.13 us  [to_group(): return lax.ppermute(block, 'head', [(at, at ^ i) for at in range(heads)])]
    ppermute x1 -> x2, starting transfers between devices: 1.61 us -> 4.58 us  [the longest x1 3.92 us: body(): lax.ppermute(grad_blocks[far][half:], axes, turn_route(far))]
    ppermute x8, starting transfers between devices: 9.21 us -> 7.1 us  [to_group(): return lax.ppermute(block, 'head', [(at, at ^ i) for at in range(heads)])]
    ppermute x1 -> x2, waiting for transfers between devices: 0.01 us -> 1.94 us  [the longest x1 1.94 us: body(): lax.ppermute(grad_blocks[far][half:], axes, turn_route(far))]
    ppermute x3, waiting for transfers between devices: 7.34 us -> 9.03 us  [body(): ahead = lax.ppermute(ahead, 'seq', forward)]
    ppermute x3, starting transfers between devices: 3.87 us -> 2.83 us  [body(): ahead = lax.ppermute(ahead, 'seq', forward)]
  transfers between devices with their start and end apart: 23 -> 24, of which waited for: 7 -> 8; matrix products, arithmetic and copies ran while one was open for 1% -> 1% of each run, Pallas kernels for 22% -> 19%
where the time goes in v6:
time: 78.6 us; the launch traced here: 78.5 us
  starting transfers between devices  30.7 us (39%)
  waiting for transfers between devices  25.9 us (33%)
  Pallas kernels  20.1 us (26%)
  other arithmetic  0.95 us (1%)
  between operations  0.85 us (1%)
    ppermute x5, waiting for transfers between devices, across(): return lax.ppermute(block, axis, route)  13.8 us
    ppermute x3, waiting for transfers between devices, body(): ahead = lax.ppermute(ahead, 'seq', forward)  9.03 us
    ppermute x5, starting transfers between devices, across(): return lax.ppermute(block, axis, route)  8.5 us
    ppermute x8, starting transfers between devices, to_group(): return lax.ppermute(block, 'head', [(at, at ^ i) for at in range(heads)])  7.1 us
    ppermute x3, starting transfers between devices, body(): behind = lax.ppermute(behind, 'seq', backward)  3.97 us
    ppermute x1, starting transfers between devices, body(): lax.ppermute(grad_blocks[far][half:], axes, turn_route(far))  3.92 us
    pallas_call x1, Pallas kernels, body(): pl.pallas_call(local_kernel, out_shape=(pltpu.VMEM((heads_dev, rows, rows...  3.66 us
    ppermute x3, starting transfers between devices, body(): ahead = lax.ppermute(ahead, 'seq', forward)  2.83 us
  transfers between devices with their start and end apart: 24, of which 8 were waited for; matrix products, arithmetic and copies ran while one was open for 1% of the time, Pallas kernels for 19%

profile of v6, /device:TPU:0, one launch (start us, length us, event | category | flops | bytes accessed | tf_op | source)
XLA Modules:
  0.0 78.5 jit_solution(4644710661919603364)
XLA Ops:
  0.6 2.5 %shard_map.101 = (bf16[8,128,128]{2,1,0:T(8,128)(2,1)S(1)}, bf16[8,128,128]{2,1,0:T(8,128)(2,1)S(1)}, bf16[8,128,128]{2,1,0:T(8,128)(2,1)S(1)}, bf16[128,1024]{1,0:T(8,128)(2,1)S(1)}, bf16[64,1024]{1,0:T(8,128)(2,1)S(1)}) custom-call(f32[128,8,128]{2,1,0:T(8,128)} %k_hbm.1, f32[128,8,128]{2,1,0:T(8,128)} %v_hbm.1, bf16[128,1024]{1,0:T(8,128)(2,1)} %grad_hbm.1), custom_call_target="tpu_custom_call" | custom-call | flops 33554432 | bytes 1835008 | tf_op jit(solution)/shard_map/pallas_call | solution.py:317
  3.1 3.0 %collective-permute-start.3 = (bf16[128,1024]{1,0:T(8,128)(2,1)S(1)}, bf16[128,1024]{1,0:T(8,128)(2,1)S(1)}, u32[]{:S(2)}, u32[]{:S(2)}) collective-permute-start(bf16[128,1024]{1,0:T(8,128)(2,1)S(1)} %get-tuple-element.34.refs_0_), channel_id=1, source_target_pairs={{0,2},{1,3},{2,0},{3,1},{4,6},{5,7},{6,4},{7,5},{8,10},{9,11},{10,... | collective-permute-start | bytes 786440 | tf_op jit(solution)/shard_map/ppermute | solution.py:332
  6.1 1.5 %collective-permute-start = (bf16[8,128,128]{2,1,0:T(8,128)(2,1)S(1)}, bf16[8,128,128]{2,1,0:T(8,128)(2,1)S(1)}, u32[]{:S(2)}, u32[]{:S(2)}) collective-permute-start(bf16[8,128,128]{2,1,0:T(8,128)(2,1)S(1)} %get-tuple-element.33.running_ref), channel_id=1, source_target_pairs={{0,4},{4,0},{8,12},{12,8},{16,20},{20,16},{24,28},{28,24},{1,5},{5... | collective-permute-start | bytes 786440 | tf_op jit(solution)/shard_map/ppermute | solution.py:44
  7.6 0.0 collective-permute-start.2
  7.6 3.7 %shard_map.102 = (bf16[8,128,128]{2,1,0:T(8,128)(2,1)S(1)}, f32[8,128,128]{2,1,0:T(8,128)S(1)}, bf16[8,128,128]{2,1,0:T(8,128)(2,1)S(1)}, bf16[3,8,128,128]{3,2,...) custom-call(f32[128,8,128]{2,1,0:T(8,128)} %q_hbm.1, ...), custom_call_target="tpu_custom_call" | custom-call | flops 67108864 | bytes 3145728 | tf_op jit(solution)/shard_map/pallas_call | solution.py:341
  11.3 1.1 %collective-permute-done.3.block_ref.refs_2_ = bf16[128,1024]{1,0:T(8,128)(2,1)S(1)} collective-permute-done((bf16[128,1024]{1,0:T(8,128)(2,1)S(1)}, bf16[128,1024]{1,0:T(8,128)(2,1)S(1)}, u32[]{:S(2)}, u32[]{:S(2)}) %collective-permute-start.3) | collective-permute-done | bytes 262176 | tf_op jit(solution)/shard_map/ppermute | solution.py:332
  12.4 0.1 collective-permute-start.4
  12.5 1.4 %collective-permute-done.arrived_ref.refs_0_ = bf16[8,128,128]{2,1,0:T(8,128)(2,1)S(1)} collective-permute-done((bf16[8,128,128]{2,1,0:T(8,128)(2,1)S(1)}, bf16[8,128,128]{2,1,0:T(8,128)(2,1)S(1)}, u32[]{:S(2)}, u32[]{:S(2)}) %collective-permute-start) | collective-permute-done | bytes 262176 | tf_op jit(solution)/shard_map/ppermute | solution.py:44
  13.9 0.1 shard_map.103.refs_6_.running_ref
  13.9 1.6 %collective-permute-start.1 = (bf16[8,128,128]{2,1,0:T(8,128)(2,1)S(1)}, bf16[8,128,128]{2,1,0:T(8,128)(2,1)S(1)}, u32[]{:S(2)}, u32[]{:S(2)}) collective-permute-start(bf16[8,128,128]{2,1,0:T(8,128)(2,1)S(1)} %shard_map.103.refs_6_.running_ref), channel_id=1, source_target_pairs={{0,8},{8,0},{4,12},{12,4},{16,24},{24,16},{20,28},{28,20},{1,9},{9... | collective-permute-start | bytes 786440 | tf_op jit(solution)/shard_map/ppermute | solution.py:44
  15.6 0.7 collective-permute-start.6
  16.3 3.9 %collective-permute-start.7 = (bf16[64,1024]{1,0:T(8,128)(2,1)S(1)}, bf16[64,1024]{1,0:T(8,128)(2,1)S(1)}, u32[]{:S(2)}, u32[]{:S(2)}) collective-permute-start(bf16[64,1024]{1,0:T(8,128)(2,1)S(1)} %slice.23), channel_id=1, source_target_pairs={{2,0},{3,10},{0,18},{1,24},{6,4},{7,14},{4,22},{5,28},{10,2},{11,8... | collective-permute-start | bytes 393224 | tf_op jit(solution)/shard_map/ppermute | solution.py:394
  20.2 0.0 collective-permute-done.2.refs_1_
  20.2 0.0 collective-permute-done.4.refs_3_
  20.2 2.8 %shard_map.105 = (bf16[1024,128]{1,0:T(8,128)(2,1)S(1)}, bf16[8,128,128]{2,1,0:T(8,128)(2,1)S(1)}, bf16[8,128,128]{2,1,0:T(8,128)(2,1)S(1)}, bf16[8,128,128]{2,1,0:T(8,128)(2,1)S(1)}) custom-call(bf16[128,1024]{1,0:T(8,128)(2,1)S(1)} %get-tuple-element.34.refs_0_, bf16[128,1024]{1,0:T(8,128)(2,1)S(1)} %collective-permute-done.2.refs_1_, ...), custom_call_target="tpu_custom_call" | custom-call | flops 1073741824 | bytes 8388608 | tf_op jit(solution)/shard_map/pallas_call | solution.py:411
  23.0 0.0 collective-permute-done.6.low_ref
  23.0 1.9 %collective-permute-done.7.high_ref = bf16[64,1024]{1,0:T(8,128)(2,1)S(1)} collective-permute-done((bf16[64,1024]{1,0:T(8,128)(2,1)S(1)}, bf16[64,1024]{1,0:T(8,128)(2,1)S(1)}, u32[]{:S(2)}, u32[]{:S(2)}) %collective-permute-start.7) | collective-permute-done | bytes 131104 | tf_op jit(solution)/shard_map/ppermute | solution.py:394
  25.0 1.6 %collective-permute-start.8 = (bf16[128,512]{1,0:T(8,128)(2,1)S(1)}, bf16[128,512]{1,0:T(8,128)(2,1)S(1)}, u32[]{:S(2)}, u32[]{:S(2)}) collective-permute-start(bf16[128,512]{1,0:T(8,128)(2,1)S(1)} %get-tuple-element.44), channel_id=1, source_target_pairs={{0,4},{4,0},{8,12},{12,8},{16,20},{20,16},{24,28},{28,24},{1,5},{5... | collective-permute-start | bytes 393224 | tf_op jit(solution)/shard_map/ppermute | solution.py:444
  26.6 0.0 collective-permute-done.1.arrived_ref.refs_1_
  26.6 0.1 shard_map.106.after_ref
  26.7 4.0 %collective-permute-start.5 = (bf16[8,128,128]{2,1,0:T(8,128)(2,1)S(1)}, bf16[8,128,128]{2,1,0:T(8,128)(2,1)S(1)}, u32[]{:S(2)}, u32[]{:S(2)}) collective-permute-start(bf16[8,128,128]{2,1,0:T(8,128)(2,1)S(1)} %shard_map.106.after_ref), channel_id=1, source_target_pairs={{0,16},{16,0},{4,20},{20,4},{8,24},{24,8},{12,28},{28,12},{1,17},{... | collective-permute-start | bytes 786440 | tf_op jit(solution)/shard_map/ppermute | solution.py:44
  30.7 0.0 collective-permute-done.8.refs_1_
  30.7 0.6 collective-permute-start.9
  31.3 2.1 %collective-permute-start.10 = (bf16[2,128,512]{2,1,0:T(8,128)(2,1)S(1)}, bf16[2,128,512]{2,1,0:T(8,128)(2,1)S(1)}, u32[]{:S(2)}, u32[]{:S(2)}) collective-permute-start(bf16[2,128,512]{2,1,0:T(8,128)(2,1)S(1)} %shard_map.109.refs_4_.refs_0_), channel_id=1, source_target_pairs={{0,2},{1,3},{2,0},{3,1},{4,6},{5,7},{6,4},{7,5},{8,10},{9,11},{10,... | collective-permute-start | bytes 786440 | tf_op jit(solution)/shard_map/ppermute | solution.py:332
  33.4 0.0 collective-permute-start.11
  33.4 1.3 %shard_map.107 = (f32[8,128,128]{2,1,0:T(8,128)S(1)}, f32[8,128,128]{2,1,0:T(8,128)S(1)}, f32[8,128,128]{2,1,0:T(8,128)S(1)}) custom-call(bf16[1024,128]{1,0:T(8,128)(2,1)S(1)} %get-tuple-element.37.gt_ref.after_ref, bf16[8,128,128]{2,1,0:T(8,128)(2,1)S(1)} %get-tuple-element.38.qh_ref, bf16[8,128,128]{2,1,0:T(8,128)(2,1)S(1)} %get-tuple-element.29.kh_ref, ...), custom_call_target="tpu_custom_call" | custom-call | flops 201326592 | bytes 3670016 | tf_op jit(solution)/shard_map/pallas_call | solution.py:466
  34.7 8.2 %collective-permute-done.5.refs_2_.refs_0_.state_ref = bf16[8,128,128]{2,1,0:T(8,128)(2,1)S(1)} collective-permute-done((bf16[8,128,128]{2,1,0:T(8,128)(2,1)S(1)}, bf16[8,128,128]{2,1,0:T(8,128)(2,1)S(1)}, u32[]{:S(2)}, u32[]{:S(2)}) %collective-permute-start.5) | collective-permute-done | bytes 262176 | tf_op jit(solution)/shard_map/ppermute | solution.py:44
  43.0 0.4 shard_map.110.after_ref.att_ref.refs_0_
  43.3 0.1 collective-permute-start.14
  43.4 2.0 %collective-permute-start.17 = (bf16[128,1024]{1,0:T(8,128)(2,1)S(1)}, bf16[128,1024]{1,0:T(8,128)(2,1)S(1)}, u32[]{:S(2)}, u32[]{:S(2)}) collective-permute-start(bf16[128,1024]{1,0:T(8,128)(2,1)S(1)} %shard_map.110.after_ref.att_ref.refs_0_), channel_id=1, source_target_pairs={{8,0},{16,8},{24,16},{28,24},{20,28},{12,20},{4,12},{0,4},{9,1},{1... | collective-permute-start | bytes 786440 | tf_op jit(solution)/shard_map/ppermute | solution.py:543
  45.4 0.1 shard_map.111.refs_0_
  45.5 1.3 %shard_map.112.refs_1_ = f32[128,8,128]{2,1,0:T(8,128)} custom-call(bf16[1024,128]{1,0:T(8,128)(2,1)S(1)} %get-tuple-element.37.gt_ref.after_ref, f32[5,8,128]{2,1,0:T(8,128)S(1)} %get-tuple-element.40.lam_ref, f32[8,128,128]{2,1,0:T(8,128)S(1)} %get-tuple-element.46.dql_ref, bf16[8,128,128]{2,1,0:T(8,128)(2,1)S(1)} %collective-permute-done.5.refs_2_.refs_0_.state_ref, ...), custom_call_target="tpu_custom_call" | custom-call | flops 33554432 | bytes 1572864 | tf_op jit(solution)/shard_map/pallas_call | solution.py:498
  46.8 0.0 collective-permute-done.9.refs_1_
  46.8 0.0 collective-permute-done.10.refs_2_
  46.8 0.0 collective-permute-done.11.refs_3_
  46.8 0.1 shard_map.113.refs_2_.cols_ref
  46.9 1.3 %shard_map.114 = (bf16[2,128,1024]{2,1,0:T(8,128)(2,1)S(1)}, f32[2,128,1024]{2,1,0:T(8,128)S(1)}) custom-call(bf16[128,1024]{1,0:T(8,128)(2,1)S(1)} %shard_map.110.after_ref.att_ref.refs_0_, bf16[1024,4096]{1,0:T(8,128)(2,1)S(1)} %get-tuple-element.35.refs_4_.w_ref, bf16[8,128,128]{2,1,0:T(8,128)(2,1)S(1)} %shard_map.111.refs_0_, ...), custom_call_target="tpu_custom_call" | custom-call | flops 1073741824 | bytes 8388608 | tf_op jit(solution)/shard_map/pallas_call | solution.py:507
  48.2 0.1 collective-permute-start.12
  48.3 0.7 collective-permute-start.20
  49.0 2.2 %collective-permute-done.14.refs_1_ = bf16[128,1024]{1,0:T(8,128)(2,1)S(1)} collective-permute-done((bf16[128,1024]{1,0:T(8,128)(2,1)S(1)}, bf16[128,1024]{1,0:T(8,128)(2,1)S(1)}, u32[]{:S(2)}, u32[]{:S(2)}) %collective-permute-start.14) | collective-permute-done | bytes 262176 | tf_op jit(solution)/shard_map/ppermute | solution.py:542
  51.3 0.3 collective-permute-start.15
  51.6 1.7 %collective-permute-start.18 = (bf16[128,1024]{1,0:T(8,128)(2,1)S(1)}, bf16[128,1024]{1,0:T(8,128)(2,1)S(1)}, u32[]{:S(2)}, u32[]{:S(2)}) collective-permute-start(bf16[128,1024]{1,0:T(8,128)(2,1)S(1)} %collective-permute-done.17.refs_2_), channel_id=1, source_target_pairs={{8,0},{16,8},{24,16},{28,24},{20,28},{12,20},{4,12},{0,4},{9,1},{1... | collective-permute-start | bytes 786440 | tf_op jit(solution)/shard_map/ppermute | solution.py:543
  53.3 4.2 %collective-permute-done.20.refs_1_ = bf16[8,128,128]{2,1,0:T(8,128)(2,1)S(1)} collective-permute-done((bf16[8,128,128]{2,1,0:T(8,128)(2,1)S(1)}, bf16[8,128,128]{2,1,0:T(8,128)(2,1)S(1)}, u32[]{:S(2)}, u32[]{:S(2)}) %collective-permute-start.20) | collective-permute-done | bytes 262176 | tf_op jit(solution)/shard_map/ppermute | solution.py:44
  57.5 0.1 shard_map.117
  57.6 0.6 collective-permute-start.21
  58.2 2.3 %collective-permute-done.15.refs_3_ = bf16[128,1024]{1,0:T(8,128)(2,1)S(1)} collective-permute-done((bf16[128,1024]{1,0:T(8,128)(2,1)S(1)}, bf16[128,1024]{1,0:T(8,128)(2,1)S(1)}, u32[]{:S(2)}, u32[]{:S(2)}) %collective-permute-start.15) | collective-permute-done | bytes 262176 | tf_op jit(solution)/shard_map/ppermute | solution.py:542
  60.5 2.5 %collective-permute-start.16 = (bf16[128,1024]{1,0:T(8,128)(2,1)S(1)}, bf16[128,1024]{1,0:T(8,128)(2,1)S(1)}, u32[]{:S(2)}, u32[]{:S(2)}) collective-permute-start(bf16[128,1024]{1,0:T(8,128)(2,1)S(1)} %collective-permute-done.15.refs_3_), channel_id=1, source_target_pairs={{0,8},{8,16},{16,24},{24,28},{28,20},{20,12},{12,4},{4,0},{1,9},{9... | collective-permute-start | bytes 786440 | tf_op jit(solution)/shard_map/ppermute | solution.py:542
  62.9 0.0 collective-permute-done.18.refs_4_
  63.0 0.2 collective-permute-start.19
  63.2 0.0 collective-permute-done.12
  63.2 0.2 convert_add_fusion
  63.4 1.2 %collective-permute-start.13 = (bf16[1,128,1024]{2,1,0:T(8,128)(2,1)S(1)}, bf16[1,128,1024]{2,1,0:T(8,128)(2,1)S(1)}, u32[]{:S(2)}, u32[]{:S(2)}) collective-permute-start(bf16[1,128,1024]{2,1,0:T(8,128)(2,1)S(1)} %slice.34), channel_id=1, source_target_pairs={{0,2},{1,3},{2,0},{3,1},{4,6},{5,7},{6,4},{7,5},{8,10},{9,11},{10,... | collective-permute-start | bytes 786440 | tf_op jit(solution)/shard_map/ppermute | solution.py:332
  64.7 1.5 %shard_map.115.refs_2_ = f32[1024,512]{1,0:T(8,128)S(1)} custom-call(bf16[8,128,512]{2,1,0:T(8,128)(2,1)S(1)} %shard_map.113.refs_2_.cols_ref, bf16[128,1024]{1,0:T(8,128)(2,1)S(1)} %shard_map.110.after_ref.att_ref.refs_0_, bf16[128,1024]{1,0:T(8,128)(2,1)S(1)} %collective-permute-done.14.refs_1_, bf16[128,1024]{1,0:T(8,128)(2,1)S(1)} %collective-permute-done.17.refs_2_, ...), custom_call_target="tpu_custom_call" | custom-call | flops 671088640 | bytes 2097152 | tf_op jit(solution)/shard_map/pallas_call | solution.py:527
  66.2 4.5 %collective-permute-done.16.refs_0_ = bf16[128,1024]{1,0:T(8,128)(2,1)S(1)} collective-permute-done((bf16[128,1024]{1,0:T(8,128)(2,1)S(1)}, bf16[128,1024]{1,0:T(8,128)(2,1)S(1)}, u32[]{:S(2)}, u32[]{:S(2)}) %collective-permute-start.16) | collective-permute-done | bytes 262176 | tf_op jit(solution)/shard_map/ppermute | solution.py:542
  70.7 0.1 collective-permute-start.22
  70.8 0.0 collective-permute-done.19.refs_1_
  70.8 2.1 %collective-permute-start.23 = (bf16[64,1024]{1,0:T(8,128)(2,1)S(1)}, bf16[64,1024]{1,0:T(8,128)(2,1)S(1)}, u32[]{:S(2)}, u32[]{:S(2)}) collective-permute-start(bf16[64,1024]{1,0:T(8,128)(2,1)S(1)} %slice.27), channel_id=1, source_target_pairs={{8,0},{16,8},{24,16},{28,24},{20,28},{12,20},{4,12},{0,4},{9,1},{1... | collective-permute-start | bytes 393224 | tf_op jit(solution)/shard_map/ppermute | solution.py:553
  72.9 0.7 shard_map.116.after_ref.total_ref
  73.6 1.7 %shard_map.118 = (f32[128,8,128]{2,1,0:T(8,128)}, f32[128,8,128]{2,1,0:T(8,128)}) custom-call(bf16[8,128,128]{2,1,0:T(8,128)(2,1)S(1)} %get-tuple-element.29.kh_ref, bf16[8,128,128]{2,1,0:T(8,128)(2,1)S(1)} %get-tuple-element.30.vh_ref, f32[8,128,128]{2,1,0:T(8,128)S(1)} %get-tuple-element.41.refs_3_.dkl_ref, f32[8,128,128]{2,1,0:T(8,128)S(1)} %get-tuple-element.49.dvl_ref, ...), custom_call_target="tpu_custom_call" | custom-call | flops 67108864 | bytes 2883584 | tf_op jit(solution)/shard_map/pallas_call | solution.py:555
  75.4 0.0 collective-permute-done.13
  75.4 0.8 fusion.1
  76.1 0.0 collective-permute-done.22.low_ref
  76.1 0.0 collective-permute-done.23.high_ref
  76.1 2.4 %shard_map.119 = f32[1024,512]{1,0:T(8,128)} custom-call(bf16[8,128,512]{2,1,0:T(8,128)(2,1)S(1)} %shard_map.113.refs_2_.cols_ref, bf16[64,1024]{1,0:T(8,128)(2,1)S(1)} %collective-permute-done.22.low_ref, bf16[64,1024]{1,0:T(8,128)(2,1)S(1)} %collective-permute-done.23.high_ref, f32[1024,512]{1,0:T(8,128)S(1)} %shard_map.116.after_ref.total_ref, ...), custom_call_target="tpu_custom_call" | custom-call | flops 134217728 | bytes 4194304 | tf_op jit(solution)/shard_map/pallas_call | solution.py:564
  (9 shorter events, 0.1 us)
Async XLA Ops:
  3.1 9.3 %collective-permute-start.3 = (bf16[128,1024]{1,0:T(8,128)(2,1)S(1)}, bf16[128,1024]{1,0:T(8,128)(2,1)S(1)}, u32[]{:S(2)}, u32[]{:S(2)}) collective-permute-start(bf16[128,1024]{1,0:T(8,128)(2,1)S(1)} %get-tuple-element.34.refs_0_), channel_id=1, source_target_pairs={{0,2},{1,3},{2,0},{3,1},{4,6},{5,7},{6,4},{7,5},{8,10},{9,11},{10,... | collective-permute-start | bytes 786440 | tf_op jit(solution)/shard_map/ppermute | solution.py:332
  6.1 7.8 %collective-permute-start = (bf16[8,128,128]{2,1,0:T(8,128)(2,1)S(1)}, bf16[8,128,128]{2,1,0:T(8,128)(2,1)S(1)}, u32[]{:S(2)}, u32[]{:S(2)}) collective-permute-start(bf16[8,128,128]{2,1,0:T(8,128)(2,1)S(1)} %get-tuple-element.33.running_ref), channel_id=1, source_target_pairs={{0,4},{4,0},{8,12},{12,8},{16,20},{20,16},{24,28},{28,24},{1,5},{5... | collective-permute-start | bytes 786440 | tf_op jit(solution)/shard_map/ppermute | solution.py:44
  7.6 12.6 %collective-permute-start.2 = (bf16[128,1024]{1,0:T(8,128)(2,1)S(1)}, bf16[128,1024]{1,0:T(8,128)(2,1)S(1)}, u32[]{:S(2)}, u32[]{:S(2)}) collective-permute-start(bf16[128,1024]{1,0:T(8,128)(2,1)S(1)} %get-tuple-element.34.refs_0_), channel_id=1, source_target_pairs={{0,1},{1,0},{2,3},{3,2},{4,5},{5,4},{6,7},{7,6},{8,9},{9,8},{10,11... | collective-permute-start | bytes 786440 | tf_op jit(solution)/shard_map/ppermute | solution.py:332
  12.4 7.8 %collective-permute-start.4 = (bf16[128,1024]{1,0:T(8,128)(2,1)S(1)}, bf16[128,1024]{1,0:T(8,128)(2,1)S(1)}, u32[]{:S(2)}, u32[]{:S(2)}) collective-permute-start(bf16[128,1024]{1,0:T(8,128)(2,1)S(1)} %shard_map.104), channel_id=1, source_target_pairs={{0,1},{1,0},{2,3},{3,2},{4,5},{5,4},{6,7},{7,6},{8,9},{9,8},{10,11... | collective-permute-start | bytes 786440 | tf_op jit(solution)/shard_map/ppermute | solution.py:332
  13.9 12.6 %collective-permute-start.1 = (bf16[8,128,128]{2,1,0:T(8,128)(2,1)S(1)}, bf16[8,128,128]{2,1,0:T(8,128)(2,1)S(1)}, u32[]{:S(2)}, u32[]{:S(2)}) collective-permute-start(bf16[8,128,128]{2,1,0:T(8,128)(2,1)S(1)} %shard_map.103.refs_6_.running_ref), channel_id=1, source_target_pairs={{0,8},{8,0},{4,12},{12,4},{16,24},{24,16},{20,28},{28,20},{1,9},{9... | collective-permute-start | bytes 786440 | tf_op jit(solution)/shard_map/ppermute | solution.py:44
  15.6 7.4 %collective-permute-start.6 = (bf16[64,1024]{1,0:T(8,128)(2,1)S(1)}, bf16[64,1024]{1,0:T(8,128)(2,1)S(1)}, u32[]{:S(2)}, u32[]{:S(2)}) collective-permute-start(bf16[64,1024]{1,0:T(8,128)(2,1)S(1)} %get-tuple-element.42), channel_id=1, source_target_pairs={{0,0},{1,10},{2,18},{3,24},{4,4},{5,14},{6,22},{7,28},{8,2},{9,8},... | collective-permute-start | bytes 393224 | tf_op jit(solution)/shard_map/ppermute | solution.py:393
  16.3 8.7 %collective-permute-start.7 = (bf16[64,1024]{1,0:T(8,128)(2,1)S(1)}, bf16[64,1024]{1,0:T(8,128)(2,1)S(1)}, u32[]{:S(2)}, u32[]{:S(2)}) collective-permute-start(bf16[64,1024]{1,0:T(8,128)(2,1)S(1)} %slice.23), channel_id=1, source_target_pairs={{2,0},{3,10},{0,18},{1,24},{6,4},{7,14},{4,22},{5,28},{10,2},{11,8... | collective-permute-start | bytes 393224 | tf_op jit(solution)/shard_map/ppermute | solution.py:394
  25.0 5.7 %collective-permute-start.8 = (bf16[128,512]{1,0:T(8,128)(2,1)S(1)}, bf16[128,512]{1,0:T(8,128)(2,1)S(1)}, u32[]{:S(2)}, u32[]{:S(2)}) collective-permute-start(bf16[128,512]{1,0:T(8,128)(2,1)S(1)} %get-tuple-element.44), channel_id=1, source_target_pairs={{0,4},{4,0},{8,12},{12,8},{16,20},{20,16},{24,28},{28,24},{1,5},{5... | collective-permute-start | bytes 393224 | tf_op jit(solution)/shard_map/ppermute | solution.py:444
  26.7 16.3 %collective-permute-start.5 = (bf16[8,128,128]{2,1,0:T(8,128)(2,1)S(1)}, bf16[8,128,128]{2,1,0:T(8,128)(2,1)S(1)}, u32[]{:S(2)}, u32[]{:S(2)}) collective-permute-start(bf16[8,128,128]{2,1,0:T(8,128)(2,1)S(1)} %shard_map.106.after_ref), channel_id=1, source_target_pairs={{0,16},{16,0},{4,20},{20,4},{8,24},{24,8},{12,28},{28,12},{1,17},{... | collective-permute-start | bytes 786440 | tf_op jit(solution)/shard_map/ppermute | solution.py:44
  30.7 16.1 %collective-permute-start.9 = (bf16[2,128,512]{2,1,0:T(8,128)(2,1)S(1)}, bf16[2,128,512]{2,1,0:T(8,128)(2,1)S(1)}, u32[]{:S(2)}, u32[]{:S(2)}) collective-permute-start(bf16[2,128,512]{2,1,0:T(8,128)(2,1)S(1)} %shard_map.109.refs_4_.refs_0_), channel_id=1, source_target_pairs={{0,1},{1,0},{2,3},{3,2},{4,5},{5,4},{6,7},{7,6},{8,9},{9,8},{10,11... | collective-permute-start | bytes 786440 | tf_op jit(solution)/shard_map/ppermute | solution.py:332
  31.3 15.5 %collective-permute-start.10 = (bf16[2,128,512]{2,1,0:T(8,128)(2,1)S(1)}, bf16[2,128,512]{2,1,0:T(8,128)(2,1)S(1)}, u32[]{:S(2)}, u32[]{:S(2)}) collective-permute-start(bf16[2,128,512]{2,1,0:T(8,128)(2,1)S(1)} %shard_map.109.refs_4_.refs_0_), channel_id=1, source_target_pairs={{0,2},{1,3},{2,0},{3,1},{4,6},{5,7},{6,4},{7,5},{8,10},{9,11},{10,... | collective-permute-start | bytes 786440 | tf_op jit(solution)/shard_map/ppermute | solution.py:332
  33.4 13.4 %collective-permute-start.11 = (bf16[2,128,512]{2,1,0:T(8,128)(2,1)S(1)}, bf16[2,128,512]{2,1,0:T(8,128)(2,1)S(1)}, u32[]{:S(2)}, u32[]{:S(2)}) collective-permute-start(bf16[2,128,512]{2,1,0:T(8,128)(2,1)S(1)} %shard_map.109.refs_4_.refs_0_), channel_id=1, source_target_pairs={{0,3},{1,2},{2,1},{3,0},{4,7},{5,6},{6,5},{7,4},{8,11},{9,10},{10,... | collective-permute-start | bytes 786440 | tf_op jit(solution)/shard_map/ppermute | solution.py:332
  43.3 7.9 %collective-permute-start.14 = (bf16[128,1024]{1,0:T(8,128)(2,1)S(1)}, bf16[128,1024]{1,0:T(8,128)(2,1)S(1)}, u32[]{:S(2)}, u32[]{:S(2)}) collective-permute-start(bf16[128,1024]{1,0:T(8,128)(2,1)S(1)} %shard_map.110.after_ref.att_ref.refs_0_), channel_id=1, source_target_pairs={{0,8},{8,16},{16,24},{24,28},{28,20},{20,12},{12,4},{4,0},{1,9},{9... | collective-permute-start | bytes 786440 | tf_op jit(solution)/shard_map/ppermute | solution.py:542
  43.4 8.2 %collective-permute-start.17 = (bf16[128,1024]{1,0:T(8,128)(2,1)S(1)}, bf16[128,1024]{1,0:T(8,128)(2,1)S(1)}, u32[]{:S(2)}, u32[]{:S(2)}) collective-permute-start(bf16[128,1024]{1,0:T(8,128)(2,1)S(1)} %shard_map.110.after_ref.att_ref.refs_0_), channel_id=1, source_target_pairs={{8,0},{16,8},{24,16},{28,24},{20,28},{12,20},{4,12},{0,4},{9,1},{1... | collective-permute-start | bytes 786440 | tf_op jit(solution)/shard_map/ppermute | solution.py:543
  48.2 14.9 %collective-permute-start.12 = (bf16[2,128,1024]{2,1,0:T(8,128)(2,1)S(1)}, bf16[2,128,1024]{2,1,0:T(8,128)(2,1)S(1)}, u32[]{:S(2)}, u32[]{:S(2)}) collective-permute-start(bf16[2,128,1024]{2,1,0:T(8,128)(2,1)S(1)} %get-tuple-element.48), channel_id=1, source_target_pairs={{0,1},{1,0},{2,3},{3,2},{4,5},{5,4},{6,7},{7,6},{8,9},{9,8},{10,11... | collective-permute-start | bytes 1572872 | tf_op jit(solution)/shard_map/ppermute | solution.py:332
  48.3 9.2 %collective-permute-start.20 = (bf16[8,128,128]{2,1,0:T(8,128)(2,1)S(1)}, bf16[8,128,128]{2,1,0:T(8,128)(2,1)S(1)}, u32[]{:S(2)}, u32[]{:S(2)}) collective-permute-start(bf16[8,128,128]{2,1,0:T(8,128)(2,1)S(1)} %shard_map.111.refs_0_), channel_id=1, source_target_pairs={{0,8},{8,0},{4,12},{12,4},{16,24},{24,16},{20,28},{28,20},{1,9},{9... | collective-permute-start | bytes 786440 | tf_op jit(solution)/shard_map/ppermute | solution.py:44
  51.3 9.2 %collective-permute-start.15 = (bf16[128,1024]{1,0:T(8,128)(2,1)S(1)}, bf16[128,1024]{1,0:T(8,128)(2,1)S(1)}, u32[]{:S(2)}, u32[]{:S(2)}) collective-permute-start(bf16[128,1024]{1,0:T(8,128)(2,1)S(1)} %collective-permute-done.14.refs_1_), channel_id=1, source_target_pairs={{0,8},{8,16},{16,24},{24,28},{28,20},{20,12},{12,4},{4,0},{1,9},{9... | collective-permute-start | bytes 786440 | tf_op jit(solution)/shard_map/ppermute | solution.py:542
  51.6 11.4 %collective-permute-start.18 = (bf16[128,1024]{1,0:T(8,128)(2,1)S(1)}, bf16[128,1024]{1,0:T(8,128)(2,1)S(1)}, u32[]{:S(2)}, u32[]{:S(2)}) collective-permute-start(bf16[128,1024]{1,0:T(8,128)(2,1)S(1)} %collective-permute-done.17.refs_2_), channel_id=1, source_target_pairs={{8,0},{16,8},{24,16},{28,24},{20,28},{12,20},{4,12},{0,4},{9,1},{1... | collective-permute-start | bytes 786440 | tf_op jit(solution)/shard_map/ppermute | solution.py:543
  57.6 16.0 %collective-permute-start.21 = (bf16[8,128,128]{2,1,0:T(8,128)(2,1)S(1)}, bf16[8,128,128]{2,1,0:T(8,128)(2,1)S(1)}, u32[]{:S(2)}, u32[]{:S(2)}) collective-permute-start(bf16[8,128,128]{2,1,0:T(8,128)(2,1)S(1)} %shard_map.117), channel_id=1, source_target_pairs={{0,4},{4,0},{8,12},{12,8},{16,20},{20,16},{24,28},{28,24},{1,5},{5... | collective-permute-start | bytes 786440 | tf_op jit(solution)/shard_map/ppermute | solution.py:44
  60.5 10.2 %collective-permute-start.16 = (bf16[128,1024]{1,0:T(8,128)(2,1)S(1)}, bf16[128,1024]{1,0:T(8,128)(2,1)S(1)}, u32[]{:S(2)}, u32[]{:S(2)}) collective-permute-start(bf16[128,1024]{1,0:T(8,128)(2,1)S(1)} %collective-permute-done.15.refs_3_), channel_id=1, source_target_pairs={{0,8},{8,16},{16,24},{24,28},{28,20},{20,12},{12,4},{4,0},{1,9},{9... | collective-permute-start | bytes 786440 | tf_op jit(solution)/shard_map/ppermute | solution.py:542
  63.0 7.8 %collective-permute-start.19 = (bf16[128,1024]{1,0:T(8,128)(2,1)S(1)}, bf16[128,1024]{1,0:T(8,128)(2,1)S(1)}, u32[]{:S(2)}, u32[]{:S(2)}) collective-permute-start(bf16[128,1024]{1,0:T(8,128)(2,1)S(1)} %collective-permute-done.18.refs_4_), channel_id=1, source_target_pairs={{8,0},{16,8},{24,16},{28,24},{20,28},{12,20},{4,12},{0,4},{9,1},{1... | collective-permute-start | bytes 786440 | tf_op jit(solution)/shard_map/ppermute | solution.py:543
  63.4 12.0 %collective-permute-start.13 = (bf16[1,128,1024]{2,1,0:T(8,128)(2,1)S(1)}, bf16[1,128,1024]{2,1,0:T(8,128)(2,1)S(1)}, u32[]{:S(2)}, u32[]{:S(2)}) collective-permute-start(bf16[1,128,1024]{2,1,0:T(8,128)(2,1)S(1)} %slice.34), channel_id=1, source_target_pairs={{0,2},{1,3},{2,0},{3,1},{4,6},{5,7},{6,4},{7,5},{8,10},{9,11},{10,... | collective-permute-start | bytes 786440 | tf_op jit(solution)/shard_map/ppermute | solution.py:332
  70.7 5.4 %collective-permute-start.22 = (bf16[64,1024]{1,0:T(8,128)(2,1)S(1)}, bf16[64,1024]{1,0:T(8,128)(2,1)S(1)}, u32[]{:S(2)}, u32[]{:S(2)}) collective-permute-start(bf16[64,1024]{1,0:T(8,128)(2,1)S(1)} %slice.26), channel_id=1, source_target_pairs={{0,8},{8,16},{16,24},{24,28},{28,20},{20,12},{12,4},{4,0},{1,9},{9... | collective-permute-start | bytes 393224 | tf_op jit(solution)/shard_map/ppermute | solution.py:552
  70.8 5.3 %collective-permute-start.23 = (bf16[64,1024]{1,0:T(8,128)(2,1)S(1)}, bf16[64,1024]{1,0:T(8,128)(2,1)S(1)}, u32[]{:S(2)}, u32[]{:S(2)}) collective-permute-start(bf16[64,1024]{1,0:T(8,128)(2,1)S(1)} %slice.27), channel_id=1, source_target_pairs={{8,0},{16,8},{24,16},{28,24},{20,28},{12,20},{4,12},{0,4},{9,1},{1... | collective-permute-start | bytes 393224 | tf_op jit(solution)/shard_map/ppermute | solution.py:553

commit v7 on v6

--- a/solution.py
+++ b/solution.py
@@ -439,7 +439,8 @@
         out_specs=(VMEM,) * per,
         compiler_params=PARAMS,
         cost_estimate=cost(0, 2 * moved_head),
-    )(*turned, gt)
+    )(*turned, meeting)
+    own_chunks = chunks
     chunks = [chunks[0]] + [
         lax.ppermute(chunks[r], "seq", [(at, at ^ r) for at in range(devices)])
         for r in range(1, per)
@@ -479,7 +480,7 @@
         out_specs=VMEM,
         compiler_params=PARAMS,
         cost_estimate=cost(seq_bits * flops_head, 8 * moved_head),
-    )(att_local, qw, *partner_states, key_local, stacked)
+    )(att_local, qw, *partner_states, key_local, own_chunks[-1])
 
     first_pending = attended
     for digit in reversed(range(top)):
@@ -507,11 +508,11 @@
     send, kept = pl.pallas_call(
         functools.partial(share_kernel, heads),
         out_shape=(like((heads // 2, rows, width), BF), like((heads // 2, rows, width), F32)),
-        in_specs=[VMEM, VMEM, ANY, ANY, ANY],
+        in_specs=[VMEM] * 2 + [ANY],
         out_specs=(VMEM,) * 2,
         compiler_params=PARAMS,
         cost_estimate=cost(2 * rows * width * out_proj.shape[1], 2 * width * out_proj.shape[1]),
-    )(attended, w, first_pending, hbm(query_grad), grad_columns)
+    )(attended, w, stacked)
     for digit in range(head_bits):
         kept = kept + to_group(send, 1 << digit).astype(F32)
         if digit < head_bits - 1:

time: 78.6 us -> 80.5 us (1.024)
  waiting for transfers between devices: 25.9 us -> 28 us
    ppermute x8, waiting for transfers between devices: 1.13 us -> 5.35 us  [to_group(): return lax.ppermute(block, 'head', [(at, at ^ i) for at in range(heads)])]
    ppermute x1, waiting for transfers between devices: 0.01 us -> 2.79 us  [body(): lax.ppermute(chunks[r], 'seq', [(at, at ^ r) for at in range(devices)])]
    ppermute x3, waiting for transfers between devices: 9.03 us -> 6.85 us  [body(): ahead = lax.ppermute(ahead, 'seq', forward)]
    ppermute x1, waiting for transfers between devices: 1.94 us -> 0.01 us  [body(): lax.ppermute(grad_blocks[far][half:], axes, turn_route(far))]
    ppermute x5, waiting for transfers between devices: 13.8 us -> 12.1 us  [across(): return lax.ppermute(block, axis, route)]
  transfers between devices with their start and end apart: 24 -> 24, of which waited for: 8 -> 11; matrix products, arithmetic and copies ran while one was open for 1% -> 1% of each run, Pallas kernels for 19% -> 17%
where the time goes in v7:
time: 80.5 us; the launch traced here: 80.3 us
  starting transfers between devices  30.4 us (38%)
  waiting for transfers between devices  28 us (35%)
  Pallas kernels  20.1 us (25%)
  other arithmetic  0.94 us (1%)
  between operations  0.86 us (1%)
    ppermute x5, waiting for transfers between devices, across(): return lax.ppermute(block, axis, route)  12.1 us
    ppermute x5, starting transfers between devices, across(): return lax.ppermute(block, axis, route)  8.21 us
    ppermute x3, waiting for transfers between devices, body(): ahead = lax.ppermute(ahead, 'seq', forward)  6.85 us
    ppermute x8, starting transfers between devices, to_group(): return lax.ppermute(block, 'head', [(at, at ^ i) for at in range(heads)])  6.61 us
    ppermute x8, waiting for transfers between devices, to_group(): return lax.ppermute(block, 'head', [(at, at ^ i) for at in range(heads)])  5.35 us
    ppermute x3, starting transfers between devices, body(): behind = lax.ppermute(behind, 'seq', backward)  4.54 us
    ppermute x1, starting transfers between devices, body(): lax.ppermute(grad_blocks[far][half:], axes, turn_route(far))  3.92 us
    pallas_call x1, Pallas kernels, body(): pl.pallas_call(local_kernel, out_shape=(pltpu.VMEM((heads_dev, rows, rows...  3.66 us
  transfers between devices with their start and end apart: 24, of which 11 were waited for; matrix products, arithmetic and copies ran while one was open for 1% of the time, Pallas kernels for 17%

profile of v7, /device:TPU:0, one launch (start us, length us, event | category | flops | bytes accessed | tf_op | source)
XLA Modules:
  0.0 80.3 jit_solution(9227327631188872926)
XLA Ops:
  0.6 2.5 %shard_map.101 = (bf16[8,128,128]{2,1,0:T(8,128)(2,1)S(1)}, bf16[8,128,128]{2,1,0:T(8,128)(2,1)S(1)}, bf16[8,128,128]{2,1,0:T(8,128)(2,1)S(1)}, bf16[128,1024]{1,0:T(8,128)(2,1)S(1)}, bf16[64,1024]{1,0:T(8,128)(2,1)S(1)}) custom-call(f32[128,8,128]{2,1,0:T(8,128)} %k_hbm.1, f32[128,8,128]{2,1,0:T(8,128)} %v_hbm.1, bf16[128,1024]{1,0:T(8,128)(2,1)} %grad_hbm.1), custom_call_target="tpu_custom_call" | custom-call | flops 33554432 | bytes 1835008 | tf_op jit(solution)/shard_map/pallas_call | solution.py:317
  3.1 3.0 %collective-permute-start.3 = (bf16[128,1024]{1,0:T(8,128)(2,1)S(1)}, bf16[128,1024]{1,0:T(8,128)(2,1)S(1)}, u32[]{:S(2)}, u32[]{:S(2)}) collective-permute-start(bf16[128,1024]{1,0:T(8,128)(2,1)S(1)} %get-tuple-element.34.refs_0_), channel_id=1, source_target_pairs={{0,2},{1,3},{2,0},{3,1},{4,6},{5,7},{6,4},{7,5},{8,10},{9,11},{10,... | collective-permute-start | bytes 786440 | tf_op jit(solution)/shard_map/ppermute | solution.py:332
  6.1 1.5 %collective-permute-start = (bf16[8,128,128]{2,1,0:T(8,128)(2,1)S(1)}, bf16[8,128,128]{2,1,0:T(8,128)(2,1)S(1)}, u32[]{:S(2)}, u32[]{:S(2)}) collective-permute-start(bf16[8,128,128]{2,1,0:T(8,128)(2,1)S(1)} %get-tuple-element.33.running_ref), channel_id=1, source_target_pairs={{0,4},{4,0},{8,12},{12,8},{16,20},{20,16},{24,28},{28,24},{1,5},{5... | collective-permute-start | bytes 786440 | tf_op jit(solution)/shard_map/ppermute | solution.py:44
  7.6 0.0 collective-permute-start.2
  7.6 3.7 %shard_map.102 = (bf16[8,128,128]{2,1,0:T(8,128)(2,1)S(1)}, f32[8,128,128]{2,1,0:T(8,128)S(1)}, bf16[8,128,128]{2,1,0:T(8,128)(2,1)S(1)}, bf16[3,8,128,128]{3,2,...) custom-call(f32[128,8,128]{2,1,0:T(8,128)} %q_hbm.1, ...), custom_call_target="tpu_custom_call" | custom-call | flops 67108864 | bytes 3145728 | tf_op jit(solution)/shard_map/pallas_call | solution.py:341
  11.3 1.1 %collective-permute-done.3.block_ref.refs_2_ = bf16[128,1024]{1,0:T(8,128)(2,1)S(1)} collective-permute-done((bf16[128,1024]{1,0:T(8,128)(2,1)S(1)}, bf16[128,1024]{1,0:T(8,128)(2,1)S(1)}, u32[]{:S(2)}, u32[]{:S(2)}) %collective-permute-start.3) | collective-permute-done | bytes 262176 | tf_op jit(solution)/shard_map/ppermute | solution.py:332
  12.4 0.1 collective-permute-start.4
  12.5 1.4 %collective-permute-done.arrived_ref.refs_0_ = bf16[8,128,128]{2,1,0:T(8,128)(2,1)S(1)} collective-permute-done((bf16[8,128,128]{2,1,0:T(8,128)(2,1)S(1)}, bf16[8,128,128]{2,1,0:T(8,128)(2,1)S(1)}, u32[]{:S(2)}, u32[]{:S(2)}) %collective-permute-start) | collective-permute-done | bytes 262176 | tf_op jit(solution)/shard_map/ppermute | solution.py:44
  13.9 0.1 shard_map.103.refs_6_.running_ref
  13.9 1.6 %collective-permute-start.1 = (bf16[8,128,128]{2,1,0:T(8,128)(2,1)S(1)}, bf16[8,128,128]{2,1,0:T(8,128)(2,1)S(1)}, u32[]{:S(2)}, u32[]{:S(2)}) collective-permute-start(bf16[8,128,128]{2,1,0:T(8,128)(2,1)S(1)} %shard_map.103.refs_6_.running_ref), channel_id=1, source_target_pairs={{0,8},{8,0},{4,12},{12,4},{16,24},{24,16},{20,28},{28,20},{1,9},{9... | collective-permute-start | bytes 786440 | tf_op jit(solution)/shard_map/ppermute | solution.py:44
  15.6 0.7 collective-permute-start.6
  16.3 3.9 %collective-permute-start.7 = (bf16[64,1024]{1,0:T(8,128)(2,1)S(1)}, bf16[64,1024]{1,0:T(8,128)(2,1)S(1)}, u32[]{:S(2)}, u32[]{:S(2)}) collective-permute-start(bf16[64,1024]{1,0:T(8,128)(2,1)S(1)} %slice.23), channel_id=1, source_target_pairs={{2,0},{3,10},{0,18},{1,24},{6,4},{7,14},{4,22},{5,28},{10,2},{11,8... | collective-permute-start | bytes 393224 | tf_op jit(solution)/shard_map/ppermute | solution.py:394
  20.2 0.0 collective-permute-done.2.refs_1_
  20.2 0.0 collective-permute-done.4.refs_3_
  20.2 2.8 %shard_map.105 = (bf16[1024,128]{1,0:T(8,128)(2,1)S(1)}, bf16[8,128,128]{2,1,0:T(8,128)(2,1)S(1)}, bf16[8,128,128]{2,1,0:T(8,128)(2,1)S(1)}, bf16[8,128,128]{2,1,0:T(8,128)(2,1)S(1)}) custom-call(bf16[128,1024]{1,0:T(8,128)(2,1)S(1)} %get-tuple-element.34.refs_0_, bf16[128,1024]{1,0:T(8,128)(2,1)S(1)} %collective-permute-done.2.refs_1_, ...), custom_call_target="tpu_custom_call" | custom-call | flops 1073741824 | bytes 8388608 | tf_op jit(solution)/shard_map/pallas_call | solution.py:411
  23.0 0.0 collective-permute-done.1.arrived_ref.refs_1_
  23.0 0.1 shard_map.106.after_ref
  23.1 3.4 %collective-permute-start.5 = (bf16[8,128,128]{2,1,0:T(8,128)(2,1)S(1)}, bf16[8,128,128]{2,1,0:T(8,128)(2,1)S(1)}, u32[]{:S(2)}, u32[]{:S(2)}) collective-permute-start(bf16[8,128,128]{2,1,0:T(8,128)(2,1)S(1)} %shard_map.106.after_ref), channel_id=1, source_target_pairs={{0,16},{16,0},{4,20},{20,4},{8,24},{24,8},{12,28},{28,12},{1,17},{... | collective-permute-start | bytes 786440 | tf_op jit(solution)/shard_map/ppermute | solution.py:44
  26.5 0.0 collective-permute-done.6.low_ref
  26.5 0.0 collective-permute-done.7.high_ref
  26.6 1.6 %collective-permute-start.8 = (bf16[128,512]{1,0:T(8,128)(2,1)S(1)}, bf16[128,512]{1,0:T(8,128)(2,1)S(1)}, u32[]{:S(2)}, u32[]{:S(2)}) collective-permute-start(bf16[128,512]{1,0:T(8,128)(2,1)S(1)} %get-tuple-element.43.refs_4_), channel_id=1, source_target_pairs={{0,4},{4,0},{8,12},{12,8},{16,20},{20,16},{24,28},{28,24},{1,5},{5... | collective-permute-start | bytes 393224 | tf_op jit(solution)/shard_map/ppermute | solution.py:445
  28.1 1.3 %shard_map.107 = (f32[8,128,128]{2,1,0:T(8,128)S(1)}, f32[8,128,128]{2,1,0:T(8,128)S(1)}, f32[8,128,128]{2,1,0:T(8,128)S(1)}) custom-call(bf16[1024,128]{1,0:T(8,128)(2,1)S(1)} %get-tuple-element.37.gt_ref, bf16[8,128,128]{2,1,0:T(8,128)(2,1)S(1)} %get-tuple-element.38.qh_ref, bf16[8,128,128]{2,1,0:T(8,128)(2,1)S(1)} %get-tuple-element.29.kh_ref, ...), custom_call_target="tpu_custom_call" | custom-call | flops 201326592 | bytes 3670016 | tf_op jit(solution)/shard_map/pallas_call | solution.py:467
  29.4 2.8 %collective-permute-done.8.refs_1_ = bf16[128,512]{1,0:T(8,128)(2,1)S(1)} collective-permute-done((bf16[128,512]{1,0:T(8,128)(2,1)S(1)}, bf16[128,512]{1,0:T(8,128)(2,1)S(1)}, u32[]{:S(2)}, u32[]{:S(2)}) %collective-permute-start.8) | collective-permute-done | bytes 131104 | tf_op jit(solution)/shard_map/ppermute | solution.py:445
  32.3 6.6 %collective-permute-done.5.refs_2_.state_ref.refs_0_ = bf16[8,128,128]{2,1,0:T(8,128)(2,1)S(1)} collective-permute-done((bf16[8,128,128]{2,1,0:T(8,128)(2,1)S(1)}, bf16[8,128,128]{2,1,0:T(8,128)(2,1)S(1)}, u32[]{:S(2)}, u32[]{:S(2)}) %collective-permute-start.5) | collective-permute-done | bytes 262176 | tf_op jit(solution)/shard_map/ppermute | solution.py:44
  38.9 0.4 shard_map.109.att_ref.after_ref.refs_0_
  39.2 1.3 %shard_map.111 = (bf16[2,128,1024]{2,1,0:T(8,128)(2,1)S(1)}, f32[2,128,1024]{2,1,0:T(8,128)S(1)}) custom-call(bf16[128,1024]{1,0:T(8,128)(2,1)S(1)} %shard_map.109.att_ref.after_ref.refs_0_, bf16[1024,4096]{1,0:T(8,128)(2,1)S(1)} %get-tuple-element.35.refs_4_.w_ref, bf16[2,128,512]{2,1,0:T(8,128)(2,1)S(1)} %shard_map.110.refs_0_), custom_call_target="tpu_custom_call" | custom-call | flops 1073741824 | bytes 8388608 | tf_op jit(solution)/shard_map/pallas_call | solution.py:508
  40.5 0.1 collective-permute-start.9
  40.6 0.1 collective-permute-start.14
  40.7 2.0 %collective-permute-start.17 = (bf16[128,1024]{1,0:T(8,128)(2,1)S(1)}, bf16[128,1024]{1,0:T(8,128)(2,1)S(1)}, u32[]{:S(2)}, u32[]{:S(2)}) collective-permute-start(bf16[128,1024]{1,0:T(8,128)(2,1)S(1)} %shard_map.109.att_ref.after_ref.refs_0_), channel_id=1, source_target_pairs={{8,0},{16,8},{24,16},{28,24},{20,28},{12,20},{4,12},{0,4},{9,1},{1... | collective-permute-start | bytes 786440 | tf_op jit(solution)/shard_map/ppermute | solution.py:544
  42.7 0.1 shard_map.116
  42.8 0.2 collective-permute-start.20
  42.9 0.0 collective-permute-start.11
  42.9 6.4 %collective-permute-done.14.refs_1_ = bf16[128,1024]{1,0:T(8,128)(2,1)S(1)} collective-permute-done((bf16[128,1024]{1,0:T(8,128)(2,1)S(1)}, bf16[128,1024]{1,0:T(8,128)(2,1)S(1)}, u32[]{:S(2)}, u32[]{:S(2)}) %collective-permute-start.14) | collective-permute-done | bytes 262176 | tf_op jit(solution)/shard_map/ppermute | solution.py:543
  49.3 0.6 collective-permute-start.15
  49.9 0.0 collective-permute-done.17.refs_2_
  49.9 1.5 %collective-permute-start.18 = (bf16[128,1024]{1,0:T(8,128)(2,1)S(1)}, bf16[128,1024]{1,0:T(8,128)(2,1)S(1)}, u32[]{:S(2)}, u32[]{:S(2)}) collective-permute-start(bf16[128,1024]{1,0:T(8,128)(2,1)S(1)} %collective-permute-done.17.refs_2_), channel_id=1, source_target_pairs={{8,0},{16,8},{24,16},{28,24},{20,28},{12,20},{4,12},{0,4},{9,1},{1... | collective-permute-start | bytes 786440 | tf_op jit(solution)/shard_map/ppermute | solution.py:544
  51.3 4.1 %collective-permute-done.20.refs_1_ = bf16[8,128,128]{2,1,0:T(8,128)(2,1)S(1)} collective-permute-done((bf16[8,128,128]{2,1,0:T(8,128)(2,1)S(1)}, bf16[8,128,128]{2,1,0:T(8,128)(2,1)S(1)}, u32[]{:S(2)}, u32[]{:S(2)}) %collective-permute-start.20) | collective-permute-done | bytes 262176 | tf_op jit(solution)/shard_map/ppermute | solution.py:44
  55.5 1.7 %collective-permute-start.12 = (bf16[2,128,512]{2,1,0:T(8,128)(2,1)S(1)}, bf16[2,128,512]{2,1,0:T(8,128)(2,1)S(1)}, u32[]{:S(2)}, u32[]{:S(2)}) collective-permute-start(bf16[2,128,512]{2,1,0:T(8,128)(2,1)S(1)} %shard_map.110.refs_0_), channel_id=1, source_target_pairs={{0,2},{1,3},{2,0},{3,1},{4,6},{5,7},{6,4},{7,5},{8,10},{9,11},{10,... | collective-permute-start | bytes 786440 | tf_op jit(solution)/shard_map/ppermute | solution.py:332
  57.2 0.1 shard_map.117
  57.3 0.0 collective-permute-done.11.refs_1_
  57.3 0.1 collective-permute-start.13
  57.4 0.0 collective-permute-done.9
  57.4 1.5 %collective-permute-start.21 = (bf16[8,128,128]{2,1,0:T(8,128)(2,1)S(1)}, bf16[8,128,128]{2,1,0:T(8,128)(2,1)S(1)}, u32[]{:S(2)}, u32[]{:S(2)}) collective-permute-start(bf16[8,128,128]{2,1,0:T(8,128)(2,1)S(1)} %shard_map.117), channel_id=1, source_target_pairs={{0,4},{4,0},{8,12},{12,8},{16,20},{20,16},{24,28},{28,24},{1,5},{5... | collective-permute-start | bytes 786440 | tf_op jit(solution)/shard_map/ppermute | solution.py:44
  58.9 2.1 %collective-permute-start.16 = (bf16[128,1024]{1,0:T(8,128)(2,1)S(1)}, bf16[128,1024]{1,0:T(8,128)(2,1)S(1)}, u32[]{:S(2)}, u32[]{:S(2)}) collective-permute-start(bf16[128,1024]{1,0:T(8,128)(2,1)S(1)} %collective-permute-done.15.refs_3_), channel_id=1, source_target_pairs={{0,8},{8,16},{16,24},{24,28},{28,20},{20,12},{12,4},{4,0},{1,9},{9... | collective-permute-start | bytes 786440 | tf_op jit(solution)/shard_map/ppermute | solution.py:543
  61.0 0.0 collective-permute-done.18.refs_4_
  61.0 1.1 %collective-permute-start.19 = (bf16[128,1024]{1,0:T(8,128)(2,1)S(1)}, bf16[128,1024]{1,0:T(8,128)(2,1)S(1)}, u32[]{:S(2)}, u32[]{:S(2)}) collective-permute-start(bf16[128,1024]{1,0:T(8,128)(2,1)S(1)} %collective-permute-done.18.refs_4_), channel_id=1, source_target_pairs={{8,0},{16,8},{24,16},{28,24},{20,28},{12,20},{4,12},{0,4},{9,1},{1... | collective-permute-start | bytes 786440 | tf_op jit(solution)/shard_map/ppermute | solution.py:544
  62.1 0.2 convert_add_fusion
  62.3 2.4 %collective-permute-done.12.refs_2_ = bf16[2,128,512]{2,1,0:T(8,128)(2,1)S(1)} collective-permute-done((bf16[2,128,512]{2,1,0:T(8,128)(2,1)S(1)}, bf16[2,128,512]{2,1,0:T(8,128)(2,1)S(1)}, u32[]{:S(2)}, u32[]{:S(2)}) %collective-permute-start.12) | collective-permute-done | bytes 262176 | tf_op jit(solution)/shard_map/ppermute | solution.py:332
  64.7 1.7 %collective-permute-start.10 = (bf16[1,128,1024]{2,1,0:T(8,128)(2,1)S(1)}, bf16[1,128,1024]{2,1,0:T(8,128)(2,1)S(1)}, u32[]{:S(2)}, u32[]{:S(2)}) collective-permute-start(bf16[1,128,1024]{2,1,0:T(8,128)(2,1)S(1)} %slice.34), channel_id=1, source_target_pairs={{0,2},{1,3},{2,0},{3,1},{4,6},{5,7},{6,4},{7,5},{8,10},{9,11},{10,... | collective-permute-start | bytes 786440 | tf_op jit(solution)/shard_map/ppermute | solution.py:332
  66.4 1.3 %shard_map.112 = f32[128,8,128]{2,1,0:T(8,128)} custom-call(bf16[1024,128]{1,0:T(8,128)(2,1)S(1)} %get-tuple-element.37.gt_ref, f32[5,8,128]{2,1,0:T(8,128)S(1)} %get-tuple-element.40.lam_ref, f32[8,128,128]{2,1,0:T(8,128)S(1)} %get-tuple-element.47.dql_ref, bf16[8,128,128]{2,1,0:T(8,128)(2,1)S(1)} %collective-permute-done.5.refs_2_.state_ref.refs_0_, ...), custom_call_target="tpu_custom_call" | custom-call | flops 33554432 | bytes 1572864 | tf_op jit(solution)/shard_map/pallas_call | solution.py:499
  67.7 1.8 %collective-permute-done.13.refs_3_ = bf16[2,128,512]{2,1,0:T(8,128)(2,1)S(1)} collective-permute-done((bf16[2,128,512]{2,1,0:T(8,128)(2,1)S(1)}, bf16[2,128,512]{2,1,0:T(8,128)(2,1)S(1)}, u32[]{:S(2)}, u32[]{:S(2)}) %collective-permute-start.13) | collective-permute-done | bytes 262176 | tf_op jit(solution)/shard_map/ppermute | solution.py:332
  69.6 0.1 shard_map.113.cols_ref
  69.6 1.5 %shard_map.114.refs_2_ = f32[1024,512]{1,0:T(8,128)S(1)} custom-call(bf16[8,128,512]{2,1,0:T(8,128)(2,1)S(1)} %shard_map.113.cols_ref, bf16[128,1024]{1,0:T(8,128)(2,1)S(1)} %shard_map.109.att_ref.after_ref.refs_0_, bf16[128,1024]{1,0:T(8,128)(2,1)S(1)} %collective-permute-done.14.refs_1_, bf16[128,1024]{1,0:T(8,128)(2,1)S(1)} %collective-permute-done.17.refs_2_, ...), custom_call_target="tpu_custom_call" | custom-call | flops 671088640 | bytes 2097152 | tf_op jit(solution)/shard_map/pallas_call | solution.py:528
  71.2 0.5 collective-permute-done.16.refs_0_
  71.7 0.1 collective-permute-start.22
  71.7 0.0 collective-permute-done.19.refs_1_
  71.8 2.1 %collective-permute-start.23 = (bf16[64,1024]{1,0:T(8,128)(2,1)S(1)}, bf16[64,1024]{1,0:T(8,128)(2,1)S(1)}, u32[]{:S(2)}, u32[]{:S(2)}) collective-permute-start(bf16[64,1024]{1,0:T(8,128)(2,1)S(1)} %slice.27), channel_id=1, source_target_pairs={{8,0},{16,8},{24,16},{28,24},{20,28},{12,20},{4,12},{0,4},{9,1},{1... | collective-permute-start | bytes 393224 | tf_op jit(solution)/shard_map/ppermute | solution.py:554
  73.8 0.7 shard_map.115.after_ref.total_ref
  74.6 1.7 %shard_map.118 = (f32[128,8,128]{2,1,0:T(8,128)}, f32[128,8,128]{2,1,0:T(8,128)}) custom-call(bf16[8,128,128]{2,1,0:T(8,128)(2,1)S(1)} %get-tuple-element.29.kh_ref, bf16[8,128,128]{2,1,0:T(8,128)(2,1)S(1)} %get-tuple-element.30.vh_ref, f32[8,128,128]{2,1,0:T(8,128)S(1)} %get-tuple-element.41.refs_3_.dkl_ref, f32[8,128,128]{2,1,0:T(8,128)S(1)} %get-tuple-element.48.dvl_ref, ...), custom_call_target="tpu_custom_call" | custom-call | flops 67108864 | bytes 2883584 | tf_op jit(solution)/shard_map/pallas_call | solution.py:556
  76.3 0.0 collective-permute-done.10
  76.3 0.8 fusion.1
  77.1 0.5 collective-permute-done.22.low_ref
  77.6 0.4 collective-permute-done.23.high_ref
  78.0 2.4 %shard_map.119 = f32[1024,512]{1,0:T(8,128)} custom-call(bf16[8,128,512]{2,1,0:T(8,128)(2,1)S(1)} %shard_map.113.cols_ref, bf16[64,1024]{1,0:T(8,128)(2,1)S(1)} %collective-permute-done.22.low_ref, bf16[64,1024]{1,0:T(8,128)(2,1)S(1)} %collective-permute-done.23.high_ref, f32[1024,512]{1,0:T(8,128)S(1)} %shard_map.115.after_ref.total_ref, ...), custom_call_target="tpu_custom_call" | custom-call | flops 134217728 | bytes 4194304 | tf_op jit(solution)/shard_map/pallas_call | solution.py:565
  (9 shorter events, 0.1 us)
Async XLA Ops:
  3.1 9.3 %collective-permute-start.3 = (bf16[128,1024]{1,0:T(8,128)(2,1)S(1)}, bf16[128,1024]{1,0:T(8,128)(2,1)S(1)}, u32[]{:S(2)}, u32[]{:S(2)}) collective-permute-start(bf16[128,1024]{1,0:T(8,128)(2,1)S(1)} %get-tuple-element.34.refs_0_), channel_id=1, source_target_pairs={{0,2},{1,3},{2,0},{3,1},{4,6},{5,7},{6,4},{7,5},{8,10},{9,11},{10,... | collective-permute-start | bytes 786440 | tf_op jit(solution)/shard_map/ppermute | solution.py:332
  6.1 7.8 %collective-permute-start = (bf16[8,128,128]{2,1,0:T(8,128)(2,1)S(1)}, bf16[8,128,128]{2,1,0:T(8,128)(2,1)S(1)}, u32[]{:S(2)}, u32[]{:S(2)}) collective-permute-start(bf16[8,128,128]{2,1,0:T(8,128)(2,1)S(1)} %get-tuple-element.33.running_ref), channel_id=1, source_target_pairs={{0,4},{4,0},{8,12},{12,8},{16,20},{20,16},{24,28},{28,24},{1,5},{5... | collective-permute-start | bytes 786440 | tf_op jit(solution)/shard_map/ppermute | solution.py:44
  7.6 12.6 %collective-permute-start.2 = (bf16[128,1024]{1,0:T(8,128)(2,1)S(1)}, bf16[128,1024]{1,0:T(8,128)(2,1)S(1)}, u32[]{:S(2)}, u32[]{:S(2)}) collective-permute-start(bf16[128,1024]{1,0:T(8,128)(2,1)S(1)} %get-tuple-element.34.refs_0_), channel_id=1, source_target_pairs={{0,1},{1,0},{2,3},{3,2},{4,5},{5,4},{6,7},{7,6},{8,9},{9,8},{10,11... | collective-permute-start | bytes 786440 | tf_op jit(solution)/shard_map/ppermute | solution.py:332
  12.4 7.8 %collective-permute-start.4 = (bf16[128,1024]{1,0:T(8,128)(2,1)S(1)}, bf16[128,1024]{1,0:T(8,128)(2,1)S(1)}, u32[]{:S(2)}, u32[]{:S(2)}) collective-permute-start(bf16[128,1024]{1,0:T(8,128)(2,1)S(1)} %shard_map.104), channel_id=1, source_target_pairs={{0,1},{1,0},{2,3},{3,2},{4,5},{5,4},{6,7},{7,6},{8,9},{9,8},{10,11... | collective-permute-start | bytes 786440 | tf_op jit(solution)/shard_map/ppermute | solution.py:332
  13.9 9.1 %collective-permute-start.1 = (bf16[8,128,128]{2,1,0:T(8,128)(2,1)S(1)}, bf16[8,128,128]{2,1,0:T(8,128)(2,1)S(1)}, u32[]{:S(2)}, u32[]{:S(2)}) collective-permute-start(bf16[8,128,128]{2,1,0:T(8,128)(2,1)S(1)} %shard_map.103.refs_6_.running_ref), channel_id=1, source_target_pairs={{0,8},{8,0},{4,12},{12,4},{16,24},{24,16},{20,28},{28,20},{1,9},{9... | collective-permute-start | bytes 786440 | tf_op jit(solution)/shard_map/ppermute | solution.py:44
  15.6 11.0 %collective-permute-start.6 = (bf16[64,1024]{1,0:T(8,128)(2,1)S(1)}, bf16[64,1024]{1,0:T(8,128)(2,1)S(1)}, u32[]{:S(2)}, u32[]{:S(2)}) collective-permute-start(bf16[64,1024]{1,0:T(8,128)(2,1)S(1)} %get-tuple-element.42), channel_id=1, source_target_pairs={{0,0},{1,10},{2,18},{3,24},{4,4},{5,14},{6,22},{7,28},{8,2},{9,8},... | collective-permute-start | bytes 393224 | tf_op jit(solution)/shard_map/ppermute | solution.py:393
  16.3 10.3 %collective-permute-start.7 = (bf16[64,1024]{1,0:T(8,128)(2,1)S(1)}, bf16[64,1024]{1,0:T(8,128)(2,1)S(1)}, u32[]{:S(2)}, u32[]{:S(2)}) collective-permute-start(bf16[64,1024]{1,0:T(8,128)(2,1)S(1)} %slice.23), channel_id=1, source_target_pairs={{2,0},{3,10},{0,18},{1,24},{6,4},{7,14},{4,22},{5,28},{10,2},{11,8... | collective-permute-start | bytes 393224 | tf_op jit(solution)/shard_map/ppermute | solution.py:394
  23.1 15.7 %collective-permute-start.5 = (bf16[8,128,128]{2,1,0:T(8,128)(2,1)S(1)}, bf16[8,128,128]{2,1,0:T(8,128)(2,1)S(1)}, u32[]{:S(2)}, u32[]{:S(2)}) collective-permute-start(bf16[8,128,128]{2,1,0:T(8,128)(2,1)S(1)} %shard_map.106.after_ref), channel_id=1, source_target_pairs={{0,16},{16,0},{4,20},{20,4},{8,24},{24,8},{12,28},{28,12},{1,17},{... | collective-permute-start | bytes 786440 | tf_op jit(solution)/shard_map/ppermute | solution.py:44
  26.6 5.7 %collective-permute-start.8 = (bf16[128,512]{1,0:T(8,128)(2,1)S(1)}, bf16[128,512]{1,0:T(8,128)(2,1)S(1)}, u32[]{:S(2)}, u32[]{:S(2)}) collective-permute-start(bf16[128,512]{1,0:T(8,128)(2,1)S(1)} %get-tuple-element.43.refs_4_), channel_id=1, source_target_pairs={{0,4},{4,0},{8,12},{12,8},{16,20},{20,16},{24,28},{28,24},{1,5},{5... | collective-permute-start | bytes 393224 | tf_op jit(solution)/shard_map/ppermute | solution.py:445
  40.5 16.9 %collective-permute-start.9 = (bf16[2,128,1024]{2,1,0:T(8,128)(2,1)S(1)}, bf16[2,128,1024]{2,1,0:T(8,128)(2,1)S(1)}, u32[]{:S(2)}, u32[]{:S(2)}) collective-permute-start(bf16[2,128,1024]{2,1,0:T(8,128)(2,1)S(1)} %get-tuple-element.46), channel_id=1, source_target_pairs={{0,1},{1,0},{2,3},{3,2},{4,5},{5,4},{6,7},{7,6},{8,9},{9,8},{10,11... | collective-permute-start | bytes 1572872 | tf_op jit(solution)/shard_map/ppermute | solution.py:332
  40.6 8.7 %collective-permute-start.14 = (bf16[128,1024]{1,0:T(8,128)(2,1)S(1)}, bf16[128,1024]{1,0:T(8,128)(2,1)S(1)}, u32[]{:S(2)}, u32[]{:S(2)}) collective-permute-start(bf16[128,1024]{1,0:T(8,128)(2,1)S(1)} %shard_map.109.att_ref.after_ref.refs_0_), channel_id=1, source_target_pairs={{0,8},{8,16},{16,24},{24,28},{28,20},{20,12},{12,4},{4,0},{1,9},{9... | collective-permute-start | bytes 786440 | tf_op jit(solution)/shard_map/ppermute | solution.py:543
  40.7 9.2 %collective-permute-start.17 = (bf16[128,1024]{1,0:T(8,128)(2,1)S(1)}, bf16[128,1024]{1,0:T(8,128)(2,1)S(1)}, u32[]{:S(2)}, u32[]{:S(2)}) collective-permute-start(bf16[128,1024]{1,0:T(8,128)(2,1)S(1)} %shard_map.109.att_ref.after_ref.refs_0_), channel_id=1, source_target_pairs={{8,0},{16,8},{24,16},{28,24},{20,28},{12,20},{4,12},{0,4},{9,1},{1... | collective-permute-start | bytes 786440 | tf_op jit(solution)/shard_map/ppermute | solution.py:544
  42.8 12.7 %collective-permute-start.20 = (bf16[8,128,128]{2,1,0:T(8,128)(2,1)S(1)}, bf16[8,128,128]{2,1,0:T(8,128)(2,1)S(1)}, u32[]{:S(2)}, u32[]{:S(2)}) collective-permute-start(bf16[8,128,128]{2,1,0:T(8,128)(2,1)S(1)} %shard_map.116), channel_id=1, source_target_pairs={{0,8},{8,0},{4,12},{12,4},{16,24},{24,16},{20,28},{28,20},{1,9},{9... | collective-permute-start | bytes 786440 | tf_op jit(solution)/shard_map/ppermute | solution.py:44
  42.9 14.4 %collective-permute-start.11 = (bf16[2,128,512]{2,1,0:T(8,128)(2,1)S(1)}, bf16[2,128,512]{2,1,0:T(8,128)(2,1)S(1)}, u32[]{:S(2)}, u32[]{:S(2)}) collective-permute-start(bf16[2,128,512]{2,1,0:T(8,128)(2,1)S(1)} %shard_map.110.refs_0_), channel_id=1, source_target_pairs={{0,1},{1,0},{2,3},{3,2},{4,5},{5,4},{6,7},{7,6},{8,9},{9,8},{10,11... | collective-permute-start | bytes 786440 | tf_op jit(solution)/shard_map/ppermute | solution.py:332
  49.3 9.6 %collective-permute-start.15 = (bf16[128,1024]{1,0:T(8,128)(2,1)S(1)}, bf16[128,1024]{1,0:T(8,128)(2,1)S(1)}, u32[]{:S(2)}, u32[]{:S(2)}) collective-permute-start(bf16[128,1024]{1,0:T(8,128)(2,1)S(1)} %collective-permute-done.14.refs_1_), channel_id=1, source_target_pairs={{0,8},{8,16},{16,24},{24,28},{28,20},{20,12},{12,4},{4,0},{1,9},{9... | collective-permute-start | bytes 786440 | tf_op jit(solution)/shard_map/ppermute | solution.py:543
  49.9 11.1 %collective-permute-start.18 = (bf16[128,1024]{1,0:T(8,128)(2,1)S(1)}, bf16[128,1024]{1,0:T(8,128)(2,1)S(1)}, u32[]{:S(2)}, u32[]{:S(2)}) collective-permute-start(bf16[128,1024]{1,0:T(8,128)(2,1)S(1)} %collective-permute-done.17.refs_2_), channel_id=1, source_target_pairs={{8,0},{16,8},{24,16},{28,24},{20,28},{12,20},{4,12},{0,4},{9,1},{1... | collective-permute-start | bytes 786440 | tf_op jit(solution)/shard_map/ppermute | solution.py:544
  55.5 9.2 %collective-permute-start.12 = (bf16[2,128,512]{2,1,0:T(8,128)(2,1)S(1)}, bf16[2,128,512]{2,1,0:T(8,128)(2,1)S(1)}, u32[]{:S(2)}, u32[]{:S(2)}) collective-permute-start(bf16[2,128,512]{2,1,0:T(8,128)(2,1)S(1)} %shard_map.110.refs_0_), channel_id=1, source_target_pairs={{0,2},{1,3},{2,0},{3,1},{4,6},{5,7},{6,4},{7,5},{8,10},{9,11},{10,... | collective-permute-start | bytes 786440 | tf_op jit(solution)/shard_map/ppermute | solution.py:332
  57.3 12.2 %collective-permute-start.13 = (bf16[2,128,512]{2,1,0:T(8,128)(2,1)S(1)}, bf16[2,128,512]{2,1,0:T(8,128)(2,1)S(1)}, u32[]{:S(2)}, u32[]{:S(2)}) collective-permute-start(bf16[2,128,512]{2,1,0:T(8,128)(2,1)S(1)} %shard_map.110.refs_0_), channel_id=1, source_target_pairs={{0,3},{1,2},{2,1},{3,0},{4,7},{5,6},{6,5},{7,4},{8,11},{9,10},{10,... | collective-permute-start | bytes 786440 | tf_op jit(solution)/shard_map/ppermute | solution.py:332
  57.4 17.2 %collective-permute-start.21 = (bf16[8,128,128]{2,1,0:T(8,128)(2,1)S(1)}, bf16[8,128,128]{2,1,0:T(8,128)(2,1)S(1)}, u32[]{:S(2)}, u32[]{:S(2)}) collective-permute-start(bf16[8,128,128]{2,1,0:T(8,128)(2,1)S(1)} %shard_map.117), channel_id=1, source_target_pairs={{0,4},{4,0},{8,12},{12,8},{16,20},{20,16},{24,28},{28,24},{1,5},{5... | collective-permute-start | bytes 786440 | tf_op jit(solution)/shard_map/ppermute | solution.py:44
  58.9 12.8 %collective-permute-start.16 = (bf16[128,1024]{1,0:T(8,128)(2,1)S(1)}, bf16[128,1024]{1,0:T(8,128)(2,1)S(1)}, u32[]{:S(2)}, u32[]{:S(2)}) collective-permute-start(bf16[128,1024]{1,0:T(8,128)(2,1)S(1)} %collective-permute-done.15.refs_3_), channel_id=1, source_target_pairs={{0,8},{8,16},{16,24},{24,28},{28,20},{20,12},{12,4},{4,0},{1,9},{9... | collective-permute-start | bytes 786440 | tf_op jit(solution)/shard_map/ppermute | solution.py:543
  61.0 10.8 %collective-permute-start.19 = (bf16[128,1024]{1,0:T(8,128)(2,1)S(1)}, bf16[128,1024]{1,0:T(8,128)(2,1)S(1)}, u32[]{:S(2)}, u32[]{:S(2)}) collective-permute-start(bf16[128,1024]{1,0:T(8,128)(2,1)S(1)} %collective-permute-done.18.refs_4_), channel_id=1, source_target_pairs={{8,0},{16,8},{24,16},{28,24},{20,28},{12,20},{4,12},{0,4},{9,1},{1... | collective-permute-start | bytes 786440 | tf_op jit(solution)/shard_map/ppermute | solution.py:544
  64.7 11.6 %collective-permute-start.10 = (bf16[1,128,1024]{2,1,0:T(8,128)(2,1)S(1)}, bf16[1,128,1024]{2,1,0:T(8,128)(2,1)S(1)}, u32[]{:S(2)}, u32[]{:S(2)}) collective-permute-start(bf16[1,128,1024]{2,1,0:T(8,128)(2,1)S(1)} %slice.34), channel_id=1, source_target_pairs={{0,2},{1,3},{2,0},{3,1},{4,6},{5,7},{6,4},{7,5},{8,10},{9,11},{10,... | collective-permute-start | bytes 786440 | tf_op jit(solution)/shard_map/ppermute | solution.py:332
  71.7 5.9 %collective-permute-start.22 = (bf16[64,1024]{1,0:T(8,128)(2,1)S(1)}, bf16[64,1024]{1,0:T(8,128)(2,1)S(1)}, u32[]{:S(2)}, u32[]{:S(2)}) collective-permute-start(bf16[64,1024]{1,0:T(8,128)(2,1)S(1)} %slice.26), channel_id=1, source_target_pairs={{0,8},{8,16},{16,24},{24,28},{28,20},{20,12},{12,4},{4,0},{1,9},{9... | collective-permute-start | bytes 393224 | tf_op jit(solution)/shard_map/ppermute | solution.py:553
  71.8 6.2 %collective-permute-start.23 = (bf16[64,1024]{1,0:T(8,128)(2,1)S(1)}, bf16[64,1024]{1,0:T(8,128)(2,1)S(1)}, u32[]{:S(2)}, u32[]{:S(2)}) collective-permute-start(bf16[64,1024]{1,0:T(8,128)(2,1)S(1)} %slice.27), channel_id=1, source_target_pairs={{8,0},{16,8},{24,16},{28,24},{20,28},{12,20},{4,12},{0,4},{9,1},{1... | collective-permute-start | bytes 393224 | tf_op jit(solution)/shard_map/ppermute | solution.py:554

commit v8 on v7

--- a/solution.py
+++ b/solution.py
@@ -453,7 +453,7 @@
         compiler_params=PARAMS,
         cost_estimate=cost(0, 2 * moved_head),
     )(meeting, *chunks)
-    column_blocks = [stacked] + [to_group(stacked, i) for i in range(1, heads)]
+    column_blocks = every_group(stacked)
 
     grad_columns = pl.pallas_call(
         functools.partial(columns_kernel, heads),

time: 80.5 us -> 77.9 us (0.968)
  waiting for transfers between devices: 28 us -> 25 us
    ppermute x8, waiting for transfers between devices: 5.35 us -> 1.13 us  [to_group(): return lax.ppermute(block, 'head', [(at, at ^ i) for at in range(heads)])]
    ppermute x3, waiting for transfers between devices: 6.85 us -> 8.92 us  [body(): ahead = lax.ppermute(ahead, 'seq', forward)]
  transfers between devices with their start and end apart: 24 -> 24, of which waited for: 11 -> 8; matrix products, arithmetic and copies ran while one was open for 1% -> 1% of each run, Pallas kernels for 17% -> 17%
where the time goes in v8:
time: 77.9 us; the launch traced here: 77.8 us
  starting transfers between devices  30.9 us (40%)
  waiting for transfers between devices  25 us (32%)
  Pallas kernels  20 us (26%)
  other arithmetic  0.94 us (1%)
  between operations  0.85 us (1%)
    ppermute x5, waiting for transfers between devices, across(): return lax.ppermute(block, axis, route)  12.1 us
    ppermute x3, waiting for transfers between devices, body(): ahead = lax.ppermute(ahead, 'seq', forward)  8.92 us
    ppermute x5, starting transfers between devices, across(): return lax.ppermute(block, axis, route)  8.2 us
    ppermute x8, starting transfers between devices, to_group(): return lax.ppermute(block, 'head', [(at, at ^ i) for at in range(heads)])  6.6 us
    ppermute x3, starting transfers between devices, body(): behind = lax.ppermute(behind, 'seq', backward)  4.68 us
    ppermute x1, starting transfers between devices, body(): lax.ppermute(grad_blocks[far][half:], axes, turn_route(far))  3.92 us
    pallas_call x1, Pallas kernels, body(): pl.pallas_call(local_kernel, out_shape=(pltpu.VMEM((heads_dev, rows, rows...  3.66 us
    ppermute x3, starting transfers between devices, body(): ahead = lax.ppermute(ahead, 'seq', forward)  3.15 us
  transfers between devices with their start and end apart: 24, of which 8 were waited for; matrix products, arithmetic and copies ran while one was open for 1% of the time, Pallas kernels for 17%

profile of v8, /device:TPU:0, one launch (start us, length us, event | category | flops | bytes accessed | tf_op | source)
XLA Modules:
  0.0 77.8 jit_solution(13034074447564068937)
XLA Ops:
  0.6 2.5 %shard_map.101 = (bf16[8,128,128]{2,1,0:T(8,128)(2,1)S(1)}, bf16[8,128,128]{2,1,0:T(8,128)(2,1)S(1)}, bf16[8,128,128]{2,1,0:T(8,128)(2,1)S(1)}, bf16[128,1024]{1,0:T(8,128)(2,1)S(1)}, bf16[64,1024]{1,0:T(8,128)(2,1)S(1)}) custom-call(f32[128,8,128]{2,1,0:T(8,128)} %k_hbm.1, f32[128,8,128]{2,1,0:T(8,128)} %v_hbm.1, bf16[128,1024]{1,0:T(8,128)(2,1)} %grad_hbm.1), custom_call_target="tpu_custom_call" | custom-call | flops 33554432 | bytes 1835008 | tf_op jit(solution)/shard_map/pallas_call | solution.py:317
  3.1 3.0 %collective-permute-start.3 = (bf16[128,1024]{1,0:T(8,128)(2,1)S(1)}, bf16[128,1024]{1,0:T(8,128)(2,1)S(1)}, u32[]{:S(2)}, u32[]{:S(2)}) collective-permute-start(bf16[128,1024]{1,0:T(8,128)(2,1)S(1)} %get-tuple-element.34.refs_0_), channel_id=1, source_target_pairs={{0,2},{1,3},{2,0},{3,1},{4,6},{5,7},{6,4},{7,5},{8,10},{9,11},{10,... | collective-permute-start | bytes 786440 | tf_op jit(solution)/shard_map/ppermute | solution.py:332
  6.1 1.5 %collective-permute-start = (bf16[8,128,128]{2,1,0:T(8,128)(2,1)S(1)}, bf16[8,128,128]{2,1,0:T(8,128)(2,1)S(1)}, u32[]{:S(2)}, u32[]{:S(2)}) collective-permute-start(bf16[8,128,128]{2,1,0:T(8,128)(2,1)S(1)} %get-tuple-element.33.running_ref), channel_id=1, source_target_pairs={{0,4},{4,0},{8,12},{12,8},{16,20},{20,16},{24,28},{28,24},{1,5},{5... | collective-permute-start | bytes 786440 | tf_op jit(solution)/shard_map/ppermute | solution.py:44
  7.6 0.0 collective-permute-start.2
  7.6 3.7 %shard_map.102 = (bf16[8,128,128]{2,1,0:T(8,128)(2,1)S(1)}, f32[8,128,128]{2,1,0:T(8,128)S(1)}, bf16[8,128,128]{2,1,0:T(8,128)(2,1)S(1)}, bf16[3,8,128,128]{3,2,...) custom-call(f32[128,8,128]{2,1,0:T(8,128)} %q_hbm.1, ...), custom_call_target="tpu_custom_call" | custom-call | flops 67108864 | bytes 3145728 | tf_op jit(solution)/shard_map/pallas_call | solution.py:341
  11.3 1.1 %collective-permute-done.3.block_ref.refs_2_ = bf16[128,1024]{1,0:T(8,128)(2,1)S(1)} collective-permute-done((bf16[128,1024]{1,0:T(8,128)(2,1)S(1)}, bf16[128,1024]{1,0:T(8,128)(2,1)S(1)}, u32[]{:S(2)}, u32[]{:S(2)}) %collective-permute-start.3) | collective-permute-done | bytes 262176 | tf_op jit(solution)/shard_map/ppermute | solution.py:332
  12.4 0.1 collective-permute-start.4
  12.5 1.4 %collective-permute-done.arrived_ref.refs_0_ = bf16[8,128,128]{2,1,0:T(8,128)(2,1)S(1)} collective-permute-done((bf16[8,128,128]{2,1,0:T(8,128)(2,1)S(1)}, bf16[8,128,128]{2,1,0:T(8,128)(2,1)S(1)}, u32[]{:S(2)}, u32[]{:S(2)}) %collective-permute-start) | collective-permute-done | bytes 262176 | tf_op jit(solution)/shard_map/ppermute | solution.py:44
  13.9 0.1 shard_map.103.refs_6_.running_ref
  13.9 1.6 %collective-permute-start.1 = (bf16[8,128,128]{2,1,0:T(8,128)(2,1)S(1)}, bf16[8,128,128]{2,1,0:T(8,128)(2,1)S(1)}, u32[]{:S(2)}, u32[]{:S(2)}) collective-permute-start(bf16[8,128,128]{2,1,0:T(8,128)(2,1)S(1)} %shard_map.103.refs_6_.running_ref), channel_id=1, source_target_pairs={{0,8},{8,0},{4,12},{12,4},{16,24},{24,16},{20,28},{28,20},{1,9},{9... | collective-permute-start | bytes 786440 | tf_op jit(solution)/shard_map/ppermute | solution.py:44
  15.6 0.7 collective-permute-start.6
  16.3 3.9 %collective-permute-start.7 = (bf16[64,1024]{1,0:T(8,128)(2,1)S(1)}, bf16[64,1024]{1,0:T(8,128)(2,1)S(1)}, u32[]{:S(2)}, u32[]{:S(2)}) collective-permute-start(bf16[64,1024]{1,0:T(8,128)(2,1)S(1)} %slice.23), channel_id=1, source_target_pairs={{2,0},{3,10},{0,18},{1,24},{6,4},{7,14},{4,22},{5,28},{10,2},{11,8... | collective-permute-start | bytes 393224 | tf_op jit(solution)/shard_map/ppermute | solution.py:394
  20.2 0.0 collective-permute-done.2.refs_1_
  20.2 0.0 collective-permute-done.4.refs_3_
  20.2 2.8 %shard_map.105 = (bf16[1024,128]{1,0:T(8,128)(2,1)S(1)}, bf16[8,128,128]{2,1,0:T(8,128)(2,1)S(1)}, bf16[8,128,128]{2,1,0:T(8,128)(2,1)S(1)}, bf16[8,128,128]{2,1,0:T(8,128)(2,1)S(1)}) custom-call(bf16[128,1024]{1,0:T(8,128)(2,1)S(1)} %get-tuple-element.34.refs_0_, bf16[128,1024]{1,0:T(8,128)(2,1)S(1)} %collective-permute-done.2.refs_1_, ...), custom_call_target="tpu_custom_call" | custom-call | flops 1073741824 | bytes 8388608 | tf_op jit(solution)/shard_map/pallas_call | solution.py:411
  23.0 0.0 collective-permute-done.1.arrived_ref.refs_1_
  23.0 0.1 shard_map.106.after_ref
  23.1 3.4 %collective-permute-start.5 = (bf16[8,128,128]{2,1,0:T(8,128)(2,1)S(1)}, bf16[8,128,128]{2,1,0:T(8,128)(2,1)S(1)}, u32[]{:S(2)}, u32[]{:S(2)}) collective-permute-start(bf16[8,128,128]{2,1,0:T(8,128)(2,1)S(1)} %shard_map.106.after_ref), channel_id=1, source_target_pairs={{0,16},{16,0},{4,20},{20,4},{8,24},{24,8},{12,28},{28,12},{1,17},{... | collective-permute-start | bytes 786440 | tf_op jit(solution)/shard_map/ppermute | solution.py:44
  26.5 0.0 collective-permute-done.6.low_ref
  26.5 0.0 collective-permute-done.7.high_ref
  26.6 1.6 %collective-permute-start.8 = (bf16[128,512]{1,0:T(8,128)(2,1)S(1)}, bf16[128,512]{1,0:T(8,128)(2,1)S(1)}, u32[]{:S(2)}, u32[]{:S(2)}) collective-permute-start(bf16[128,512]{1,0:T(8,128)(2,1)S(1)} %get-tuple-element.43.refs_4_), channel_id=1, source_target_pairs={{0,4},{4,0},{8,12},{12,8},{16,20},{20,16},{24,28},{28,24},{1,5},{5... | collective-permute-start | bytes 393224 | tf_op jit(solution)/shard_map/ppermute | solution.py:445
  28.1 1.3 %shard_map.107 = (f32[8,128,128]{2,1,0:T(8,128)S(1)}, f32[8,128,128]{2,1,0:T(8,128)S(1)}, f32[8,128,128]{2,1,0:T(8,128)S(1)}) custom-call(bf16[1024,128]{1,0:T(8,128)(2,1)S(1)} %get-tuple-element.37.gt_ref, bf16[8,128,128]{2,1,0:T(8,128)(2,1)S(1)} %get-tuple-element.38.qh_ref, bf16[8,128,128]{2,1,0:T(8,128)(2,1)S(1)} %get-tuple-element.29.kh_ref, ...), custom_call_target="tpu_custom_call" | custom-call | flops 201326592 | bytes 3670016 | tf_op jit(solution)/shard_map/pallas_call | solution.py:467
  29.4 2.8 %collective-permute-done.8.refs_1_ = bf16[128,512]{1,0:T(8,128)(2,1)S(1)} collective-permute-done((bf16[128,512]{1,0:T(8,128)(2,1)S(1)}, bf16[128,512]{1,0:T(8,128)(2,1)S(1)}, u32[]{:S(2)}, u32[]{:S(2)}) %collective-permute-start.8) | collective-permute-done | bytes 131104 | tf_op jit(solution)/shard_map/ppermute | solution.py:445
  32.3 6.6 %collective-permute-done.5.refs_2_.state_ref.refs_0_ = bf16[8,128,128]{2,1,0:T(8,128)(2,1)S(1)} collective-permute-done((bf16[8,128,128]{2,1,0:T(8,128)(2,1)S(1)}, bf16[8,128,128]{2,1,0:T(8,128)(2,1)S(1)}, u32[]{:S(2)}, u32[]{:S(2)}) %collective-permute-start.5) | collective-permute-done | bytes 262176 | tf_op jit(solution)/shard_map/ppermute | solution.py:44
  38.9 0.4 shard_map.109.att_ref.after_ref.refs_0_
  39.2 1.3 %shard_map.111 = (bf16[2,128,1024]{2,1,0:T(8,128)(2,1)S(1)}, f32[2,128,1024]{2,1,0:T(8,128)S(1)}) custom-call(bf16[128,1024]{1,0:T(8,128)(2,1)S(1)} %shard_map.109.att_ref.after_ref.refs_0_, bf16[1024,4096]{1,0:T(8,128)(2,1)S(1)} %get-tuple-element.35.refs_4_.w_ref, bf16[2,128,512]{2,1,0:T(8,128)(2,1)S(1)} %shard_map.110.refs_0_), custom_call_target="tpu_custom_call" | custom-call | flops 1073741824 | bytes 8388608 | tf_op jit(solution)/shard_map/pallas_call | solution.py:508
  40.5 0.1 collective-permute-start.9
  40.6 0.1 collective-permute-start.14
  40.7 2.0 %collective-permute-start.17 = (bf16[128,1024]{1,0:T(8,128)(2,1)S(1)}, bf16[128,1024]{1,0:T(8,128)(2,1)S(1)}, u32[]{:S(2)}, u32[]{:S(2)}) collective-permute-start(bf16[128,1024]{1,0:T(8,128)(2,1)S(1)} %shard_map.109.att_ref.after_ref.refs_0_), channel_id=1, source_target_pairs={{8,0},{16,8},{24,16},{28,24},{20,28},{12,20},{4,12},{0,4},{9,1},{1... | collective-permute-start | bytes 786440 | tf_op jit(solution)/shard_map/ppermute | solution.py:544
  42.7 1.7 %collective-permute-start.12 = (bf16[2,128,512]{2,1,0:T(8,128)(2,1)S(1)}, bf16[2,128,512]{2,1,0:T(8,128)(2,1)S(1)}, u32[]{:S(2)}, u32[]{:S(2)}) collective-permute-start(bf16[2,128,512]{2,1,0:T(8,128)(2,1)S(1)} %shard_map.110.refs_0_), channel_id=1, source_target_pairs={{0,2},{1,3},{2,0},{3,1},{4,6},{5,7},{6,4},{7,5},{8,10},{9,11},{10,... | collective-permute-start | bytes 786440 | tf_op jit(solution)/shard_map/ppermute | solution.py:332
  44.4 0.1 shard_map.116
  44.5 0.2 collective-permute-start.20
  44.6 4.7 %collective-permute-done.14.refs_1_ = bf16[128,1024]{1,0:T(8,128)(2,1)S(1)} collective-permute-done((bf16[128,1024]{1,0:T(8,128)(2,1)S(1)}, bf16[128,1024]{1,0:T(8,128)(2,1)S(1)}, u32[]{:S(2)}, u32[]{:S(2)}) %collective-permute-start.14) | collective-permute-done | bytes 262176 | tf_op jit(solution)/shard_map/ppermute | solution.py:543
  49.3 0.6 collective-permute-start.15
  49.9 0.0 collective-permute-done.17.refs_2_
  49.9 1.5 %collective-permute-start.18 = (bf16[128,1024]{1,0:T(8,128)(2,1)S(1)}, bf16[128,1024]{1,0:T(8,128)(2,1)S(1)}, u32[]{:S(2)}, u32[]{:S(2)}) collective-permute-start(bf16[128,1024]{1,0:T(8,128)(2,1)S(1)} %collective-permute-done.17.refs_2_), channel_id=1, source_target_pairs={{8,0},{16,8},{24,16},{28,24},{20,28},{12,20},{4,12},{0,4},{9,1},{1... | collective-permute-start | bytes 786440 | tf_op jit(solution)/shard_map/ppermute | solution.py:544
  51.3 0.0 collective-permute-done.12.refs_2_
  51.3 0.0 collective-permute-start.11
  51.4 4.1 %collective-permute-done.20.refs_1_ = bf16[8,128,128]{2,1,0:T(8,128)(2,1)S(1)} collective-permute-done((bf16[8,128,128]{2,1,0:T(8,128)(2,1)S(1)}, bf16[8,128,128]{2,1,0:T(8,128)(2,1)S(1)}, u32[]{:S(2)}, u32[]{:S(2)}) %collective-permute-start.20) | collective-permute-done | bytes 262176 | tf_op jit(solution)/shard_map/ppermute | solution.py:44
  55.5 0.0 collective-permute-start.13
  55.5 0.1 shard_map.117
  55.6 0.0 collective-permute-done.9
  55.6 1.5 %collective-permute-start.21 = (bf16[8,128,128]{2,1,0:T(8,128)(2,1)S(1)}, bf16[8,128,128]{2,1,0:T(8,128)(2,1)S(1)}, u32[]{:S(2)}, u32[]{:S(2)}) collective-permute-start(bf16[8,128,128]{2,1,0:T(8,128)(2,1)S(1)} %shard_map.117), channel_id=1, source_target_pairs={{0,4},{4,0},{8,12},{12,8},{16,20},{20,16},{24,28},{28,24},{1,5},{5... | collective-permute-start | bytes 786440 | tf_op jit(solution)/shard_map/ppermute | solution.py:44
  57.1 1.2 %collective-permute-done.15.refs_3_ = bf16[128,1024]{1,0:T(8,128)(2,1)S(1)} collective-permute-done((bf16[128,1024]{1,0:T(8,128)(2,1)S(1)}, bf16[128,1024]{1,0:T(8,128)(2,1)S(1)}, u32[]{:S(2)}, u32[]{:S(2)}) %collective-permute-start.15) | collective-permute-done | bytes 262176 | tf_op jit(solution)/shard_map/ppermute | solution.py:543
  58.4 2.5 %collective-permute-start.16 = (bf16[128,1024]{1,0:T(8,128)(2,1)S(1)}, bf16[128,1024]{1,0:T(8,128)(2,1)S(1)}, u32[]{:S(2)}, u32[]{:S(2)}) collective-permute-start(bf16[128,1024]{1,0:T(8,128)(2,1)S(1)} %collective-permute-done.15.refs_3_), channel_id=1, source_target_pairs={{0,8},{8,16},{16,24},{24,28},{28,20},{20,12},{12,4},{4,0},{1,9},{9... | collective-permute-start | bytes 786440 | tf_op jit(solution)/shard_map/ppermute | solution.py:543
  60.8 0.0 collective-permute-done.18.refs_4_
  60.8 1.2 %collective-permute-start.19 = (bf16[128,1024]{1,0:T(8,128)(2,1)S(1)}, bf16[128,1024]{1,0:T(8,128)(2,1)S(1)}, u32[]{:S(2)}, u32[]{:S(2)}) collective-permute-start(bf16[128,1024]{1,0:T(8,128)(2,1)S(1)} %collective-permute-done.18.refs_4_), channel_id=1, source_target_pairs={{8,0},{16,8},{24,16},{28,24},{20,28},{12,20},{4,12},{0,4},{9,1},{1... | collective-permute-start | bytes 786440 | tf_op jit(solution)/shard_map/ppermute | solution.py:544
  62.1 0.2 convert_add_fusion
  62.3 1.8 %collective-permute-start.10 = (bf16[1,128,1024]{2,1,0:T(8,128)(2,1)S(1)}, bf16[1,128,1024]{2,1,0:T(8,128)(2,1)S(1)}, u32[]{:S(2)}, u32[]{:S(2)}) collective-permute-start(bf16[1,128,1024]{2,1,0:T(8,128)(2,1)S(1)} %slice.34), channel_id=1, source_target_pairs={{0,2},{1,3},{2,0},{3,1},{4,6},{5,7},{6,4},{7,5},{8,10},{9,11},{10,... | collective-permute-start | bytes 786440 | tf_op jit(solution)/shard_map/ppermute | solution.py:332
  64.1 1.3 %shard_map.112 = f32[128,8,128]{2,1,0:T(8,128)} custom-call(bf16[1024,128]{1,0:T(8,128)(2,1)S(1)} %get-tuple-element.37.gt_ref, f32[5,8,128]{2,1,0:T(8,128)S(1)} %get-tuple-element.40.lam_ref, f32[8,128,128]{2,1,0:T(8,128)S(1)} %get-tuple-element.47.dql_ref, bf16[8,128,128]{2,1,0:T(8,128)(2,1)S(1)} %collective-permute-done.5.refs_2_.state_ref.refs_0_, ...), custom_call_target="tpu_custom_call" | custom-call | flops 33554432 | bytes 1572864 | tf_op jit(solution)/shard_map/pallas_call | solution.py:499
  65.4 0.0 collective-permute-done.13.refs_3_
  65.4 0.1 shard_map.113.cols_ref
  65.5 1.5 %shard_map.114.refs_2_ = f32[1024,512]{1,0:T(8,128)S(1)} custom-call(bf16[8,128,512]{2,1,0:T(8,128)(2,1)S(1)} %shard_map.113.cols_ref, bf16[128,1024]{1,0:T(8,128)(2,1)S(1)} %shard_map.109.att_ref.after_ref.refs_0_, bf16[128,1024]{1,0:T(8,128)(2,1)S(1)} %collective-permute-done.14.refs_1_, bf16[128,1024]{1,0:T(8,128)(2,1)S(1)} %collective-permute-done.17.refs_2_, ...), custom_call_target="tpu_custom_call" | custom-call | flops 671088640 | bytes 2097152 | tf_op jit(solution)/shard_map/pallas_call | solution.py:528
  67.0 3.0 %collective-permute-done.16.refs_0_ = bf16[128,1024]{1,0:T(8,128)(2,1)S(1)} collective-permute-done((bf16[128,1024]{1,0:T(8,128)(2,1)S(1)}, bf16[128,1024]{1,0:T(8,128)(2,1)S(1)}, u32[]{:S(2)}, u32[]{:S(2)}) %collective-permute-start.16) | collective-permute-done | bytes 262176 | tf_op jit(solution)/shard_map/ppermute | solution.py:543
  70.0 0.1 collective-permute-start.22
  70.1 0.0 collective-permute-done.19.refs_1_
  70.1 2.1 %collective-permute-start.23 = (bf16[64,1024]{1,0:T(8,128)(2,1)S(1)}, bf16[64,1024]{1,0:T(8,128)(2,1)S(1)}, u32[]{:S(2)}, u32[]{:S(2)}) collective-permute-start(bf16[64,1024]{1,0:T(8,128)(2,1)S(1)} %slice.27), channel_id=1, source_target_pairs={{8,0},{16,8},{24,16},{28,24},{20,28},{12,20},{4,12},{0,4},{9,1},{1... | collective-permute-start | bytes 393224 | tf_op jit(solution)/shard_map/ppermute | solution.py:554
  72.2 0.7 shard_map.115.after_ref.total_ref
  72.9 1.7 %shard_map.118 = (f32[128,8,128]{2,1,0:T(8,128)}, f32[128,8,128]{2,1,0:T(8,128)}) custom-call(bf16[8,128,128]{2,1,0:T(8,128)(2,1)S(1)} %get-tuple-element.29.kh_ref, bf16[8,128,128]{2,1,0:T(8,128)(2,1)S(1)} %get-tuple-element.30.vh_ref, f32[8,128,128]{2,1,0:T(8,128)S(1)} %get-tuple-element.41.refs_3_.dkl_ref, f32[8,128,128]{2,1,0:T(8,128)S(1)} %get-tuple-element.48.dvl_ref, ...), custom_call_target="tpu_custom_call" | custom-call | flops 67108864 | bytes 2883584 | tf_op jit(solution)/shard_map/pallas_call | solution.py:556
  74.7 0.0 collective-permute-done.10
  74.7 0.8 fusion.1
  75.4 0.0 collective-permute-done.22.low_ref
  75.4 0.0 collective-permute-done.23.high_ref
  75.4 2.3 %shard_map.119 = f32[1024,512]{1,0:T(8,128)} custom-call(bf16[8,128,512]{2,1,0:T(8,128)(2,1)S(1)} %shard_map.113.cols_ref, bf16[64,1024]{1,0:T(8,128)(2,1)S(1)} %collective-permute-done.22.low_ref, bf16[64,1024]{1,0:T(8,128)(2,1)S(1)} %collective-permute-done.23.high_ref, f32[1024,512]{1,0:T(8,128)S(1)} %shard_map.115.after_ref.total_ref, ...), custom_call_target="tpu_custom_call" | custom-call | flops 134217728 | bytes 4194304 | tf_op jit(solution)/shard_map/pallas_call | solution.py:565
  (9 shorter events, 0.1 us)
Async XLA Ops:
  3.1 9.3 %collective-permute-start.3 = (bf16[128,1024]{1,0:T(8,128)(2,1)S(1)}, bf16[128,1024]{1,0:T(8,128)(2,1)S(1)}, u32[]{:S(2)}, u32[]{:S(2)}) collective-permute-start(bf16[128,1024]{1,0:T(8,128)(2,1)S(1)} %get-tuple-element.34.refs_0_), channel_id=1, source_target_pairs={{0,2},{1,3},{2,0},{3,1},{4,6},{5,7},{6,4},{7,5},{8,10},{9,11},{10,... | collective-permute-start | bytes 786440 | tf_op jit(solution)/shard_map/ppermute | solution.py:332
  6.1 7.8 %collective-permute-start = (bf16[8,128,128]{2,1,0:T(8,128)(2,1)S(1)}, bf16[8,128,128]{2,1,0:T(8,128)(2,1)S(1)}, u32[]{:S(2)}, u32[]{:S(2)}) collective-permute-start(bf16[8,128,128]{2,1,0:T(8,128)(2,1)S(1)} %get-tuple-element.33.running_ref), channel_id=1, source_target_pairs={{0,4},{4,0},{8,12},{12,8},{16,20},{20,16},{24,28},{28,24},{1,5},{5... | collective-permute-start | bytes 786440 | tf_op jit(solution)/shard_map/ppermute | solution.py:44
  7.6 12.6 %collective-permute-start.2 = (bf16[128,1024]{1,0:T(8,128)(2,1)S(1)}, bf16[128,1024]{1,0:T(8,128)(2,1)S(1)}, u32[]{:S(2)}, u32[]{:S(2)}) collective-permute-start(bf16[128,1024]{1,0:T(8,128)(2,1)S(1)} %get-tuple-element.34.refs_0_), channel_id=1, source_target_pairs={{0,1},{1,0},{2,3},{3,2},{4,5},{5,4},{6,7},{7,6},{8,9},{9,8},{10,11... | collective-permute-start | bytes 786440 | tf_op jit(solution)/shard_map/ppermute | solution.py:332
  12.4 7.8 %collective-permute-start.4 = (bf16[128,1024]{1,0:T(8,128)(2,1)S(1)}, bf16[128,1024]{1,0:T(8,128)(2,1)S(1)}, u32[]{:S(2)}, u32[]{:S(2)}) collective-permute-start(bf16[128,1024]{1,0:T(8,128)(2,1)S(1)} %shard_map.104), channel_id=1, source_target_pairs={{0,1},{1,0},{2,3},{3,2},{4,5},{5,4},{6,7},{7,6},{8,9},{9,8},{10,11... | collective-permute-start | bytes 786440 | tf_op jit(solution)/shard_map/ppermute | solution.py:332
  13.9 9.1 %collective-permute-start.1 = (bf16[8,128,128]{2,1,0:T(8,128)(2,1)S(1)}, bf16[8,128,128]{2,1,0:T(8,128)(2,1)S(1)}, u32[]{:S(2)}, u32[]{:S(2)}) collective-permute-start(bf16[8,128,128]{2,1,0:T(8,128)(2,1)S(1)} %shard_map.103.refs_6_.running_ref), channel_id=1, source_target_pairs={{0,8},{8,0},{4,12},{12,4},{16,24},{24,16},{20,28},{28,20},{1,9},{9... | collective-permute-start | bytes 786440 | tf_op jit(solution)/shard_map/ppermute | solution.py:44
  15.6 11.0 %collective-permute-start.6 = (bf16[64,1024]{1,0:T(8,128)(2,1)S(1)}, bf16[64,1024]{1,0:T(8,128)(2,1)S(1)}, u32[]{:S(2)}, u32[]{:S(2)}) collective-permute-start(bf16[64,1024]{1,0:T(8,128)(2,1)S(1)} %get-tuple-element.42), channel_id=1, source_target_pairs={{0,0},{1,10},{2,18},{3,24},{4,4},{5,14},{6,22},{7,28},{8,2},{9,8},... | collective-permute-start | bytes 393224 | tf_op jit(solution)/shard_map/ppermute | solution.py:393
  16.3 10.3 %collective-permute-start.7 = (bf16[64,1024]{1,0:T(8,128)(2,1)S(1)}, bf16[64,1024]{1,0:T(8,128)(2,1)S(1)}, u32[]{:S(2)}, u32[]{:S(2)}) collective-permute-start(bf16[64,1024]{1,0:T(8,128)(2,1)S(1)} %slice.23), channel_id=1, source_target_pairs={{2,0},{3,10},{0,18},{1,24},{6,4},{7,14},{4,22},{5,28},{10,2},{11,8... | collective-permute-start | bytes 393224 | tf_op jit(solution)/shard_map/ppermute | solution.py:394
  23.1 15.7 %collective-permute-start.5 = (bf16[8,128,128]{2,1,0:T(8,128)(2,1)S(1)}, bf16[8,128,128]{2,1,0:T(8,128)(2,1)S(1)}, u32[]{:S(2)}, u32[]{:S(2)}) collective-permute-start(bf16[8,128,128]{2,1,0:T(8,128)(2,1)S(1)} %shard_map.106.after_ref), channel_id=1, source_target_pairs={{0,16},{16,0},{4,20},{20,4},{8,24},{24,8},{12,28},{28,12},{1,17},{... | collective-permute-start | bytes 786440 | tf_op jit(solution)/shard_map/ppermute | solution.py:44
  26.6 5.7 %collective-permute-start.8 = (bf16[128,512]{1,0:T(8,128)(2,1)S(1)}, bf16[128,512]{1,0:T(8,128)(2,1)S(1)}, u32[]{:S(2)}, u32[]{:S(2)}) collective-permute-start(bf16[128,512]{1,0:T(8,128)(2,1)S(1)} %get-tuple-element.43.refs_4_), channel_id=1, source_target_pairs={{0,4},{4,0},{8,12},{12,8},{16,20},{20,16},{24,28},{28,24},{1,5},{5... | collective-permute-start | bytes 393224 | tf_op jit(solution)/shard_map/ppermute | solution.py:445
  40.5 15.1 %collective-permute-start.9 = (bf16[2,128,1024]{2,1,0:T(8,128)(2,1)S(1)}, bf16[2,128,1024]{2,1,0:T(8,128)(2,1)S(1)}, u32[]{:S(2)}, u32[]{:S(2)}) collective-permute-start(bf16[2,128,1024]{2,1,0:T(8,128)(2,1)S(1)} %get-tuple-element.46), channel_id=1, source_target_pairs={{0,1},{1,0},{2,3},{3,2},{4,5},{5,4},{6,7},{7,6},{8,9},{9,8},{10,11... | collective-permute-start | bytes 1572872 | tf_op jit(solution)/shard_map/ppermute | solution.py:332
  40.6 8.7 %collective-permute-start.14 = (bf16[128,1024]{1,0:T(8,128)(2,1)S(1)}, bf16[128,1024]{1,0:T(8,128)(2,1)S(1)}, u32[]{:S(2)}, u32[]{:S(2)}) collective-permute-start(bf16[128,1024]{1,0:T(8,128)(2,1)S(1)} %shard_map.109.att_ref.after_ref.refs_0_), channel_id=1, source_target_pairs={{0,8},{8,16},{16,24},{24,28},{28,20},{20,12},{12,4},{4,0},{1,9},{9... | collective-permute-start | bytes 786440 | tf_op jit(solution)/shard_map/ppermute | solution.py:543
  40.7 9.2 %collective-permute-start.17 = (bf16[128,1024]{1,0:T(8,128)(2,1)S(1)}, bf16[128,1024]{1,0:T(8,128)(2,1)S(1)}, u32[]{:S(2)}, u32[]{:S(2)}) collective-permute-start(bf16[128,1024]{1,0:T(8,128)(2,1)S(1)} %shard_map.109.att_ref.after_ref.refs_0_), channel_id=1, source_target_pairs={{8,0},{16,8},{24,16},{28,24},{20,28},{12,20},{4,12},{0,4},{9,1},{1... | collective-permute-start | bytes 786440 | tf_op jit(solution)/shard_map/ppermute | solution.py:544
  42.7 8.7 %collective-permute-start.12 = (bf16[2,128,512]{2,1,0:T(8,128)(2,1)S(1)}, bf16[2,128,512]{2,1,0:T(8,128)(2,1)S(1)}, u32[]{:S(2)}, u32[]{:S(2)}) collective-permute-start(bf16[2,128,512]{2,1,0:T(8,128)(2,1)S(1)} %shard_map.110.refs_0_), channel_id=1, source_target_pairs={{0,2},{1,3},{2,0},{3,1},{4,6},{5,7},{6,4},{7,5},{8,10},{9,11},{10,... | collective-permute-start | bytes 786440 | tf_op jit(solution)/shard_map/ppermute | solution.py:332
  44.5 11.0 %collective-permute-start.20 = (bf16[8,128,128]{2,1,0:T(8,128)(2,1)S(1)}, bf16[8,128,128]{2,1,0:T(8,128)(2,1)S(1)}, u32[]{:S(2)}, u32[]{:S(2)}) collective-permute-start(bf16[8,128,128]{2,1,0:T(8,128)(2,1)S(1)} %shard_map.116), channel_id=1, source_target_pairs={{0,8},{8,0},{4,12},{12,4},{16,24},{24,16},{20,28},{28,20},{1,9},{9... | collective-permute-start | bytes 786440 | tf_op jit(solution)/shard_map/ppermute | solution.py:44
  49.3 9.0 %collective-permute-start.15 = (bf16[128,1024]{1,0:T(8,128)(2,1)S(1)}, bf16[128,1024]{1,0:T(8,128)(2,1)S(1)}, u32[]{:S(2)}, u32[]{:S(2)}) collective-permute-start(bf16[128,1024]{1,0:T(8,128)(2,1)S(1)} %collective-permute-done.14.refs_1_), channel_id=1, source_target_pairs={{0,8},{8,16},{16,24},{24,28},{28,20},{20,12},{12,4},{4,0},{1,9},{9... | collective-permute-start | bytes 786440 | tf_op jit(solution)/shard_map/ppermute | solution.py:543
  49.9 10.9 %collective-permute-start.18 = (bf16[128,1024]{1,0:T(8,128)(2,1)S(1)}, bf16[128,1024]{1,0:T(8,128)(2,1)S(1)}, u32[]{:S(2)}, u32[]{:S(2)}) collective-permute-start(bf16[128,1024]{1,0:T(8,128)(2,1)S(1)} %collective-permute-done.17.refs_2_), channel_id=1, source_target_pairs={{8,0},{16,8},{24,16},{28,24},{20,28},{12,20},{4,12},{0,4},{9,1},{1... | collective-permute-start | bytes 786440 | tf_op jit(solution)/shard_map/ppermute | solution.py:544
  51.3 11.0 %collective-permute-start.11 = (bf16[2,128,512]{2,1,0:T(8,128)(2,1)S(1)}, bf16[2,128,512]{2,1,0:T(8,128)(2,1)S(1)}, u32[]{:S(2)}, u32[]{:S(2)}) collective-permute-start(bf16[2,128,512]{2,1,0:T(8,128)(2,1)S(1)} %shard_map.110.refs_0_), channel_id=1, source_target_pairs={{0,1},{1,0},{2,3},{3,2},{4,5},{5,4},{6,7},{7,6},{8,9},{9,8},{10,11... | collective-permute-start | bytes 786440 | tf_op jit(solution)/shard_map/ppermute | solution.py:332
  55.5 9.9 %collective-permute-start.13 = (bf16[2,128,512]{2,1,0:T(8,128)(2,1)S(1)}, bf16[2,128,512]{2,1,0:T(8,128)(2,1)S(1)}, u32[]{:S(2)}, u32[]{:S(2)}) collective-permute-start(bf16[2,128,512]{2,1,0:T(8,128)(2,1)S(1)} %collective-permute-done.12.refs_2_), channel_id=1, source_target_pairs={{0,1},{1,0},{2,3},{3,2},{4,5},{5,4},{6,7},{7,6},{8,9},{9,8},{10,11... | collective-permute-start | bytes 786440 | tf_op jit(solution)/shard_map/ppermute | solution.py:332
  55.6 17.3 %collective-permute-start.21 = (bf16[8,128,128]{2,1,0:T(8,128)(2,1)S(1)}, bf16[8,128,128]{2,1,0:T(8,128)(2,1)S(1)}, u32[]{:S(2)}, u32[]{:S(2)}) collective-permute-start(bf16[8,128,128]{2,1,0:T(8,128)(2,1)S(1)} %shard_map.117), channel_id=1, source_target_pairs={{0,4},{4,0},{8,12},{12,8},{16,20},{20,16},{24,28},{28,24},{1,5},{5... | collective-permute-start | bytes 786440 | tf_op jit(solution)/shard_map/ppermute | solution.py:44
  58.4 11.7 %collective-permute-start.16 = (bf16[128,1024]{1,0:T(8,128)(2,1)S(1)}, bf16[128,1024]{1,0:T(8,128)(2,1)S(1)}, u32[]{:S(2)}, u32[]{:S(2)}) collective-permute-start(bf16[128,1024]{1,0:T(8,128)(2,1)S(1)} %collective-permute-done.15.refs_3_), channel_id=1, source_target_pairs={{0,8},{8,16},{16,24},{24,28},{28,20},{20,12},{12,4},{4,0},{1,9},{9... | collective-permute-start | bytes 786440 | tf_op jit(solution)/shard_map/ppermute | solution.py:543
  60.8 9.3 %collective-permute-start.19 = (bf16[128,1024]{1,0:T(8,128)(2,1)S(1)}, bf16[128,1024]{1,0:T(8,128)(2,1)S(1)}, u32[]{:S(2)}, u32[]{:S(2)}) collective-permute-start(bf16[128,1024]{1,0:T(8,128)(2,1)S(1)} %collective-permute-done.18.refs_4_), channel_id=1, source_target_pairs={{8,0},{16,8},{24,16},{28,24},{20,28},{12,20},{4,12},{0,4},{9,1},{1... | collective-permute-start | bytes 786440 | tf_op jit(solution)/shard_map/ppermute | solution.py:544
  62.3 12.3 %collective-permute-start.10 = (bf16[1,128,1024]{2,1,0:T(8,128)(2,1)S(1)}, bf16[1,128,1024]{2,1,0:T(8,128)(2,1)S(1)}, u32[]{:S(2)}, u32[]{:S(2)}) collective-permute-start(bf16[1,128,1024]{2,1,0:T(8,128)(2,1)S(1)} %slice.34), channel_id=1, source_target_pairs={{0,2},{1,3},{2,0},{3,1},{4,6},{5,7},{6,4},{7,5},{8,10},{9,11},{10,... | collective-permute-start | bytes 786440 | tf_op jit(solution)/shard_map/ppermute | solution.py:332
  70.0 5.4 %collective-permute-start.22 = (bf16[64,1024]{1,0:T(8,128)(2,1)S(1)}, bf16[64,1024]{1,0:T(8,128)(2,1)S(1)}, u32[]{:S(2)}, u32[]{:S(2)}) collective-permute-start(bf16[64,1024]{1,0:T(8,128)(2,1)S(1)} %slice.26), channel_id=1, source_target_pairs={{0,8},{8,16},{16,24},{24,28},{28,20},{20,12},{12,4},{4,0},{1,9},{9... | collective-permute-start | bytes 393224 | tf_op jit(solution)/shard_map/ppermute | solution.py:553
  70.1 5.3 %collective-permute-start.23 = (bf16[64,1024]{1,0:T(8,128)(2,1)S(1)}, bf16[64,1024]{1,0:T(8,128)(2,1)S(1)}, u32[]{:S(2)}, u32[]{:S(2)}) collective-permute-start(bf16[64,1024]{1,0:T(8,128)(2,1)S(1)} %slice.27), channel_id=1, source_target_pairs={{8,0},{16,8},{24,16},{28,24},{20,28},{12,20},{4,12},{0,4},{9,1},{1... | collective-permute-start | bytes 393224 | tf_op jit(solution)/shard_map/ppermute | solution.py:554

commit v9 on v8

--- a/solution.py
+++ b/solution.py
@@ -260,13 +260,12 @@
         dv_ref[:, h, :] = dvl_ref[h] + mm(kh_ref[h], late, NT)
 
 
-def share_kernel(blocks, att_ref, w_ref, *refs):
-    send_ref, kept_ref = refs[-2:]
-    width = send_ref.shape[2]
-    for i in range(blocks):
-        out = send_ref if i % 2 else kept_ref
+def share_kernel(offsets, att_ref, w_ref, after_ref, out_ref):
+    del after_ref
+    width = out_ref.shape[2]
+    for n, i in enumerate(offsets):
         column = pl.multiple_of((lax.axis_index("head") ^ i) * width, width)
-        out[i // 2] = mm(att_ref[...], w_ref[:, pl.ds(column, width)], NN).astype(out.dtype)
+        out_ref[n] = mm(att_ref[...], w_ref[:, pl.ds(column, width)], NN).astype(out_ref.dtype)
 
 
 def ring_owner(place, offset, devices):
@@ -505,14 +504,20 @@
         cost_estimate=cost(flops_head, 6 * moved_head),
     )(gt, lam, query_local, partner_states[top], attended)
 
-    send, kept = pl.pallas_call(
-        functools.partial(share_kernel, heads),
-        out_shape=(like((heads // 2, rows, width), BF), like((heads // 2, rows, width), F32)),
-        in_specs=[VMEM] * 2 + [ANY],
-        out_specs=(VMEM,) * 2,
-        compiler_params=PARAMS,
-        cost_estimate=cost(2 * rows * width * out_proj.shape[1], 2 * width * out_proj.shape[1]),
-    )(attended, w, stacked)
+    def share(offsets, kind, after):
+        return pl.pallas_call(
+            functools.partial(share_kernel, offsets),
+            out_shape=like((len(offsets), rows, width), kind),
+            in_specs=[VMEM, VMEM, ANY],
+            out_specs=VMEM,
+            compiler_params=PARAMS,
+            cost_estimate=cost(
+                2 * rows * width * len(offsets) * width, 2 * width * len(offsets) * width
+            ),
+        )(attended, w, after)
+
+    send = share(range(1, heads, 2), BF, stacked)
+    kept = share(range(0, heads, 2), F32, first_pending)
     for digit in range(head_bits):
         kept = kept + to_group(send, 1 << digit).astype(F32)
         if digit < head_bits - 1:

time: 77.9 us -> 77.4 us (level)
  waiting for transfers between devices: 25 us -> 24.2 us
    ppermute x5, waiting for transfers between devices: 12.1 us -> 11.3 us  [across(): return lax.ppermute(block, axis, route)]
  transfers between devices with their start and end apart: 24 -> 24, of which waited for: 8 -> 8; matrix products, arithmetic and copies ran while one was open for 1% -> 1% of each run, Pallas kernels for 17% -> 19%
where the time goes in v9:
time: 77.4 us; the launch traced here: 77.3 us
  starting transfers between devices  31 us (40%)
  waiting for transfers between devices  24.2 us (31%)
  Pallas kernels  20.2 us (26%)
  other arithmetic  0.94 us (1%)
  between operations  0.88 us (1%)
    ppermute x5, waiting for transfers between devices, across(): return lax.ppermute(block, axis, route)  11.3 us
    ppermute x3, waiting for transfers between devices, body(): ahead = lax.ppermute(ahead, 'seq', forward)  8.91 us
    ppermute x5, starting transfers between devices, across(): return lax.ppermute(block, axis, route)  8.18 us
    ppermute x8, starting transfers between devices, to_group(): return lax.ppermute(block, 'head', [(at, at ^ i) for at in range(heads)])  6.69 us
    ppermute x3, starting transfers between devices, body(): behind = lax.ppermute(behind, 'seq', backward)  4.6 us
    ppermute x1, starting transfers between devices, body(): lax.ppermute(grad_blocks[far][half:], axes, turn_route(far))  3.92 us
    pallas_call x1, Pallas kernels, body(): pl.pallas_call(local_kernel, out_shape=(pltpu.VMEM((heads_dev, rows, rows...  3.66 us
    ppermute x3, starting transfers between devices, body(): ahead = lax.ppermute(ahead, 'seq', forward)  3.23 us
  transfers between devices with their start and end apart: 24, of which 8 were waited for; matrix products, arithmetic and copies ran while one was open for 1% of the time, Pallas kernels for 19%

profile of v9, /device:TPU:0, one launch (start us, length us, event | category | flops | bytes accessed | tf_op | source)
XLA Modules:
  0.0 77.3 jit_solution(16939293253878586193)
XLA Ops:
  0.6 2.5 %shard_map.101 = (bf16[8,128,128]{2,1,0:T(8,128)(2,1)S(1)}, bf16[8,128,128]{2,1,0:T(8,128)(2,1)S(1)}, bf16[8,128,128]{2,1,0:T(8,128)(2,1)S(1)}, bf16[128,1024]{1,0:T(8,128)(2,1)S(1)}, bf16[64,1024]{1,0:T(8,128)(2,1)S(1)}) custom-call(f32[128,8,128]{2,1,0:T(8,128)} %k_hbm.1, f32[128,8,128]{2,1,0:T(8,128)} %v_hbm.1, bf16[128,1024]{1,0:T(8,128)(2,1)} %grad_hbm.1), custom_call_target="tpu_custom_call" | custom-call | flops 33554432 | bytes 1835008 | tf_op jit(solution)/shard_map/pallas_call | solution.py:316
  3.1 3.0 %collective-permute-start.3 = (bf16[128,1024]{1,0:T(8,128)(2,1)S(1)}, bf16[128,1024]{1,0:T(8,128)(2,1)S(1)}, u32[]{:S(2)}, u32[]{:S(2)}) collective-permute-start(bf16[128,1024]{1,0:T(8,128)(2,1)S(1)} %get-tuple-element.32.refs_0_), channel_id=1, source_target_pairs={{0,2},{1,3},{2,0},{3,1},{4,6},{5,7},{6,4},{7,5},{8,10},{9,11},{10,... | collective-permute-start | bytes 786440 | tf_op jit(solution)/shard_map/ppermute | solution.py:331
  6.1 1.5 %collective-permute-start = (bf16[8,128,128]{2,1,0:T(8,128)(2,1)S(1)}, bf16[8,128,128]{2,1,0:T(8,128)(2,1)S(1)}, u32[]{:S(2)}, u32[]{:S(2)}) collective-permute-start(bf16[8,128,128]{2,1,0:T(8,128)(2,1)S(1)} %get-tuple-element.31.running_ref), channel_id=1, source_target_pairs={{0,4},{4,0},{8,12},{12,8},{16,20},{20,16},{24,28},{28,24},{1,5},{5... | collective-permute-start | bytes 786440 | tf_op jit(solution)/shard_map/ppermute | solution.py:44
  7.6 0.0 collective-permute-start.2
  7.6 3.7 %shard_map.102 = (bf16[8,128,128]{2,1,0:T(8,128)(2,1)S(1)}, f32[8,128,128]{2,1,0:T(8,128)S(1)}, bf16[8,128,128]{2,1,0:T(8,128)(2,1)S(1)}, bf16[3,8,128,128]{3,2,...) custom-call(f32[128,8,128]{2,1,0:T(8,128)} %q_hbm.1, ...), custom_call_target="tpu_custom_call" | custom-call | flops 67108864 | bytes 3145728 | tf_op jit(solution)/shard_map/pallas_call | solution.py:340
  11.3 1.1 %collective-permute-done.3.block_ref.refs_2_ = bf16[128,1024]{1,0:T(8,128)(2,1)S(1)} collective-permute-done((bf16[128,1024]{1,0:T(8,128)(2,1)S(1)}, bf16[128,1024]{1,0:T(8,128)(2,1)S(1)}, u32[]{:S(2)}, u32[]{:S(2)}) %collective-permute-start.3) | collective-permute-done | bytes 262176 | tf_op jit(solution)/shard_map/ppermute | solution.py:331
  12.4 0.1 collective-permute-start.4
  12.5 1.4 %collective-permute-done.arrived_ref.refs_0_ = bf16[8,128,128]{2,1,0:T(8,128)(2,1)S(1)} collective-permute-done((bf16[8,128,128]{2,1,0:T(8,128)(2,1)S(1)}, bf16[8,128,128]{2,1,0:T(8,128)(2,1)S(1)}, u32[]{:S(2)}, u32[]{:S(2)}) %collective-permute-start) | collective-permute-done | bytes 262176 | tf_op jit(solution)/shard_map/ppermute | solution.py:44
  13.9 0.1 shard_map.103.refs_6_.running_ref
  13.9 1.6 %collective-permute-start.1 = (bf16[8,128,128]{2,1,0:T(8,128)(2,1)S(1)}, bf16[8,128,128]{2,1,0:T(8,128)(2,1)S(1)}, u32[]{:S(2)}, u32[]{:S(2)}) collective-permute-start(bf16[8,128,128]{2,1,0:T(8,128)(2,1)S(1)} %shard_map.103.refs_6_.running_ref), channel_id=1, source_target_pairs={{0,8},{8,0},{4,12},{12,4},{16,24},{24,16},{20,28},{28,20},{1,9},{9... | collective-permute-start | bytes 786440 | tf_op jit(solution)/shard_map/ppermute | solution.py:44
  15.6 0.7 collective-permute-start.6
  16.3 3.9 %collective-permute-start.7 = (bf16[64,1024]{1,0:T(8,128)(2,1)S(1)}, bf16[64,1024]{1,0:T(8,128)(2,1)S(1)}, u32[]{:S(2)}, u32[]{:S(2)}) collective-permute-start(bf16[64,1024]{1,0:T(8,128)(2,1)S(1)} %slice.23), channel_id=1, source_target_pairs={{2,0},{3,10},{0,18},{1,24},{6,4},{7,14},{4,22},{5,28},{10,2},{11,8... | collective-permute-start | bytes 393224 | tf_op jit(solution)/shard_map/ppermute | solution.py:393
  20.2 0.0 collective-permute-done.2.refs_1_
  20.2 0.0 collective-permute-done.4.refs_3_
  20.2 2.8 %shard_map.105 = (bf16[1024,128]{1,0:T(8,128)(2,1)S(1)}, bf16[8,128,128]{2,1,0:T(8,128)(2,1)S(1)}, bf16[8,128,128]{2,1,0:T(8,128)(2,1)S(1)}, bf16[8,128,128]{2,1,0:T(8,128)(2,1)S(1)}) custom-call(bf16[128,1024]{1,0:T(8,128)(2,1)S(1)} %get-tuple-element.32.refs_0_, bf16[128,1024]{1,0:T(8,128)(2,1)S(1)} %collective-permute-done.2.refs_1_, ...), custom_call_target="tpu_custom_call" | custom-call | flops 1073741824 | bytes 8388608 | tf_op jit(solution)/shard_map/pallas_call | solution.py:410
  23.0 0.0 collective-permute-done.1.arrived_ref.refs_1_
  23.0 0.1 shard_map.106.after_ref
  23.1 3.4 %collective-permute-start.5 = (bf16[8,128,128]{2,1,0:T(8,128)(2,1)S(1)}, bf16[8,128,128]{2,1,0:T(8,128)(2,1)S(1)}, u32[]{:S(2)}, u32[]{:S(2)}) collective-permute-start(bf16[8,128,128]{2,1,0:T(8,128)(2,1)S(1)} %shard_map.106.after_ref), channel_id=1, source_target_pairs={{0,16},{16,0},{4,20},{20,4},{8,24},{24,8},{12,28},{28,12},{1,17},{... | collective-permute-start | bytes 786440 | tf_op jit(solution)/shard_map/ppermute | solution.py:44
  26.5 0.0 collective-permute-done.6.low_ref
  26.5 1.6 %collective-permute-start.8 = (bf16[128,512]{1,0:T(8,128)(2,1)S(1)}, bf16[128,512]{1,0:T(8,128)(2,1)S(1)}, u32[]{:S(2)}, u32[]{:S(2)}) collective-permute-start(bf16[128,512]{1,0:T(8,128)(2,1)S(1)} %get-tuple-element.41.refs_4_), channel_id=1, source_target_pairs={{0,4},{4,0},{8,12},{12,8},{16,20},{20,16},{24,28},{28,24},{1,5},{5... | collective-permute-start | bytes 393224 | tf_op jit(solution)/shard_map/ppermute | solution.py:444
  28.1 1.3 %shard_map.107 = (f32[8,128,128]{2,1,0:T(8,128)S(1)}, f32[8,128,128]{2,1,0:T(8,128)S(1)}, f32[8,128,128]{2,1,0:T(8,128)S(1)}) custom-call(bf16[1024,128]{1,0:T(8,128)(2,1)S(1)} %get-tuple-element.35.gt_ref, bf16[8,128,128]{2,1,0:T(8,128)(2,1)S(1)} %get-tuple-element.36.qh_ref, bf16[8,128,128]{2,1,0:T(8,128)(2,1)S(1)} %get-tuple-element.27.kh_ref, ...), custom_call_target="tpu_custom_call" | custom-call | flops 201326592 | bytes 3670016 | tf_op jit(solution)/shard_map/pallas_call | solution.py:466
  29.4 2.8 %collective-permute-done.8.refs_1_ = bf16[128,512]{1,0:T(8,128)(2,1)S(1)} collective-permute-done((bf16[128,512]{1,0:T(8,128)(2,1)S(1)}, bf16[128,512]{1,0:T(8,128)(2,1)S(1)}, u32[]{:S(2)}, u32[]{:S(2)}) %collective-permute-start.8) | collective-permute-done | bytes 131104 | tf_op jit(solution)/shard_map/ppermute | solution.py:444
  32.3 6.6 %collective-permute-done.5.refs_2_.refs_0_.state_ref = bf16[8,128,128]{2,1,0:T(8,128)(2,1)S(1)} collective-permute-done((bf16[8,128,128]{2,1,0:T(8,128)(2,1)S(1)}, bf16[8,128,128]{2,1,0:T(8,128)(2,1)S(1)}, u32[]{:S(2)}, u32[]{:S(2)}) %collective-permute-start.5) | collective-permute-done | bytes 262176 | tf_op jit(solution)/shard_map/ppermute | solution.py:44
  38.9 0.4 shard_map.109.after_ref.att_ref.refs_0_
  39.2 0.7 shard_map.113
  40.0 0.1 collective-permute-start.9
  40.1 0.1 collective-permute-start.14
  40.2 1.9 %collective-permute-start.17 = (bf16[128,1024]{1,0:T(8,128)(2,1)S(1)}, bf16[128,1024]{1,0:T(8,128)(2,1)S(1)}, u32[]{:S(2)}, u32[]{:S(2)}) collective-permute-start(bf16[128,1024]{1,0:T(8,128)(2,1)S(1)} %shard_map.109.after_ref.att_ref.refs_0_), channel_id=1, source_target_pairs={{8,0},{16,8},{24,16},{28,24},{20,28},{12,20},{4,12},{0,4},{9,1},{1... | collective-permute-start | bytes 786440 | tf_op jit(solution)/shard_map/ppermute | solution.py:549
  42.1 1.7 %collective-permute-start.12 = (bf16[2,128,512]{2,1,0:T(8,128)(2,1)S(1)}, bf16[2,128,512]{2,1,0:T(8,128)(2,1)S(1)}, u32[]{:S(2)}, u32[]{:S(2)}) collective-permute-start(bf16[2,128,512]{2,1,0:T(8,128)(2,1)S(1)} %shard_map.112.after_ref.refs_0_), channel_id=1, source_target_pairs={{0,2},{1,3},{2,0},{3,1},{4,6},{5,7},{6,4},{7,5},{8,10},{9,11},{10,... | collective-permute-start | bytes 786440 | tf_op jit(solution)/shard_map/ppermute | solution.py:331
  43.8 0.1 shard_map.110.after_ref
  43.9 0.2 collective-permute-start.20
  44.1 4.7 %collective-permute-done.14.refs_1_ = bf16[128,1024]{1,0:T(8,128)(2,1)S(1)} collective-permute-done((bf16[128,1024]{1,0:T(8,128)(2,1)S(1)}, bf16[128,1024]{1,0:T(8,128)(2,1)S(1)}, u32[]{:S(2)}, u32[]{:S(2)}) %collective-permute-start.14) | collective-permute-done | bytes 262176 | tf_op jit(solution)/shard_map/ppermute | solution.py:548
  48.8 0.6 collective-permute-start.15
  49.4 0.0 collective-permute-done.17.refs_2_
  49.4 1.4 %collective-permute-start.18 = (bf16[128,1024]{1,0:T(8,128)(2,1)S(1)}, bf16[128,1024]{1,0:T(8,128)(2,1)S(1)}, u32[]{:S(2)}, u32[]{:S(2)}) collective-permute-start(bf16[128,1024]{1,0:T(8,128)(2,1)S(1)} %collective-permute-done.17.refs_2_), channel_id=1, source_target_pairs={{8,0},{16,8},{24,16},{28,24},{20,28},{12,20},{4,12},{0,4},{9,1},{1... | collective-permute-start | bytes 786440 | tf_op jit(solution)/shard_map/ppermute | solution.py:549
  50.8 0.7 shard_map.111
  51.5 0.0 collective-permute-done.12.refs_2_
  51.5 0.1 collective-permute-start.11
  51.6 3.3 %collective-permute-done.20.refs_1_ = bf16[8,128,128]{2,1,0:T(8,128)(2,1)S(1)} collective-permute-done((bf16[8,128,128]{2,1,0:T(8,128)(2,1)S(1)}, bf16[8,128,128]{2,1,0:T(8,128)(2,1)S(1)}, u32[]{:S(2)}, u32[]{:S(2)}) %collective-permute-start.20) | collective-permute-done | bytes 262176 | tf_op jit(solution)/shard_map/ppermute | solution.py:44
  55.0 0.1 shard_map.118
  55.1 0.0 collective-permute-done.9
  55.1 1.5 %collective-permute-start.21 = (bf16[8,128,128]{2,1,0:T(8,128)(2,1)S(1)}, bf16[8,128,128]{2,1,0:T(8,128)(2,1)S(1)}, u32[]{:S(2)}, u32[]{:S(2)}) collective-permute-start(bf16[8,128,128]{2,1,0:T(8,128)(2,1)S(1)} %shard_map.118), channel_id=1, source_target_pairs={{0,4},{4,0},{8,12},{12,8},{16,20},{20,16},{24,28},{28,24},{1,5},{5... | collective-permute-start | bytes 786440 | tf_op jit(solution)/shard_map/ppermute | solution.py:44
  56.6 1.2 %collective-permute-done.15.refs_3_ = bf16[128,1024]{1,0:T(8,128)(2,1)S(1)} collective-permute-done((bf16[128,1024]{1,0:T(8,128)(2,1)S(1)}, bf16[128,1024]{1,0:T(8,128)(2,1)S(1)}, u32[]{:S(2)}, u32[]{:S(2)}) %collective-permute-start.15) | collective-permute-done | bytes 262176 | tf_op jit(solution)/shard_map/ppermute | solution.py:548
  57.8 2.5 %collective-permute-start.16 = (bf16[128,1024]{1,0:T(8,128)(2,1)S(1)}, bf16[128,1024]{1,0:T(8,128)(2,1)S(1)}, u32[]{:S(2)}, u32[]{:S(2)}) collective-permute-start(bf16[128,1024]{1,0:T(8,128)(2,1)S(1)} %collective-permute-done.15.refs_3_), channel_id=1, source_target_pairs={{0,8},{8,16},{16,24},{24,28},{28,20},{20,12},{12,4},{4,0},{1,9},{9... | collective-permute-start | bytes 786440 | tf_op jit(solution)/shard_map/ppermute | solution.py:548
  60.3 0.0 collective-permute-done.18.refs_4_
  60.3 1.2 %collective-permute-start.19 = (bf16[128,1024]{1,0:T(8,128)(2,1)S(1)}, bf16[128,1024]{1,0:T(8,128)(2,1)S(1)}, u32[]{:S(2)}, u32[]{:S(2)}) collective-permute-start(bf16[128,1024]{1,0:T(8,128)(2,1)S(1)} %collective-permute-done.18.refs_4_), channel_id=1, source_target_pairs={{8,0},{16,8},{24,16},{28,24},{20,28},{12,20},{4,12},{0,4},{9,1},{1... | collective-permute-start | bytes 786440 | tf_op jit(solution)/shard_map/ppermute | solution.py:549
  61.5 0.2 convert_add_fusion
  61.8 0.0 collective-permute-done.11.refs_1_
  61.8 1.8 %collective-permute-start.10 = (bf16[1,128,1024]{2,1,0:T(8,128)(2,1)S(1)}, bf16[1,128,1024]{2,1,0:T(8,128)(2,1)S(1)}, u32[]{:S(2)}, u32[]{:S(2)}) collective-permute-start(bf16[1,128,1024]{2,1,0:T(8,128)(2,1)S(1)} %slice.34), channel_id=1, source_target_pairs={{0,2},{1,3},{2,0},{3,1},{4,6},{5,7},{6,4},{7,5},{8,10},{9,11},{10,... | collective-permute-start | bytes 786440 | tf_op jit(solution)/shard_map/ppermute | solution.py:331
  63.5 1.3 %shard_map.114 = f32[128,8,128]{2,1,0:T(8,128)} custom-call(bf16[1024,128]{1,0:T(8,128)(2,1)S(1)} %get-tuple-element.35.gt_ref, f32[5,8,128]{2,1,0:T(8,128)S(1)} %get-tuple-element.38.lam_ref, f32[8,128,128]{2,1,0:T(8,128)S(1)} %get-tuple-element.44.dql_ref, bf16[8,128,128]{2,1,0:T(8,128)(2,1)S(1)} %collective-permute-done.5.refs_2_.refs_0_.state_ref, ...), custom_call_target="tpu_custom_call" | custom-call | flops 33554432 | bytes 1572864 | tf_op jit(solution)/shard_map/pallas_call | solution.py:498
  64.9 0.0 collective-permute-done.13.refs_3_
  64.9 0.1 shard_map.115.cols_ref
  65.0 1.5 %shard_map.116.refs_2_ = f32[1024,512]{1,0:T(8,128)S(1)} custom-call(bf16[8,128,512]{2,1,0:T(8,128)(2,1)S(1)} %shard_map.115.cols_ref, bf16[128,1024]{1,0:T(8,128)(2,1)S(1)} %shard_map.109.after_ref.att_ref.refs_0_, bf16[128,1024]{1,0:T(8,128)(2,1)S(1)} %collective-permute-done.14.refs_1_, bf16[128,1024]{1,0:T(8,128)(2,1)S(1)} %collective-permute-done.17.refs_2_, ...), custom_call_target="tpu_custom_call" | custom-call | flops 671088640 | bytes 2097152 | tf_op jit(solution)/shard_map/pallas_call | solution.py:533
  66.5 3.0 %collective-permute-done.16.refs_0_ = bf16[128,1024]{1,0:T(8,128)(2,1)S(1)} collective-permute-done((bf16[128,1024]{1,0:T(8,128)(2,1)S(1)}, bf16[128,1024]{1,0:T(8,128)(2,1)S(1)}, u32[]{:S(2)}, u32[]{:S(2)}) %collective-permute-start.16) | collective-permute-done | bytes 262176 | tf_op jit(solution)/shard_map/ppermute | solution.py:548
  69.5 0.1 collective-permute-start.22
  69.6 0.0 collective-permute-done.19.refs_1_
  69.6 2.1 %collective-permute-start.23 = (bf16[64,1024]{1,0:T(8,128)(2,1)S(1)}, bf16[64,1024]{1,0:T(8,128)(2,1)S(1)}, u32[]{:S(2)}, u32[]{:S(2)}) collective-permute-start(bf16[64,1024]{1,0:T(8,128)(2,1)S(1)} %slice.27), channel_id=1, source_target_pairs={{8,0},{16,8},{24,16},{28,24},{20,28},{12,20},{4,12},{0,4},{9,1},{1... | collective-permute-start | bytes 393224 | tf_op jit(solution)/shard_map/ppermute | solution.py:559
  71.7 0.7 shard_map.117.after_ref.total_ref
  72.4 0.0 collective-permute-done.21.refs_2_
  72.4 1.7 %shard_map.119 = (f32[128,8,128]{2,1,0:T(8,128)}, f32[128,8,128]{2,1,0:T(8,128)}) custom-call(bf16[8,128,128]{2,1,0:T(8,128)(2,1)S(1)} %get-tuple-element.27.kh_ref, bf16[8,128,128]{2,1,0:T(8,128)(2,1)S(1)} %get-tuple-element.28.vh_ref, f32[8,128,128]{2,1,0:T(8,128)S(1)} %get-tuple-element.39.refs_3_.dkl_ref, f32[8,128,128]{2,1,0:T(8,128)S(1)} %get-tuple-element.45.dvl_ref, ...), custom_call_target="tpu_custom_call" | custom-call | flops 67108864 | bytes 2883584 | tf_op jit(solution)/shard_map/pallas_call | solution.py:561
  74.1 0.8 fusion.1
  74.9 0.0 collective-permute-done.22.low_ref
  74.9 0.0 collective-permute-done.23.high_ref
  74.9 2.3 %shard_map.120 = f32[1024,512]{1,0:T(8,128)} custom-call(bf16[8,128,512]{2,1,0:T(8,128)(2,1)S(1)} %shard_map.115.cols_ref, bf16[64,1024]{1,0:T(8,128)(2,1)S(1)} %collective-permute-done.22.low_ref, bf16[64,1024]{1,0:T(8,128)(2,1)S(1)} %collective-permute-done.23.high_ref, f32[1024,512]{1,0:T(8,128)S(1)} %shard_map.117.after_ref.total_ref, ...), custom_call_target="tpu_custom_call" | custom-call | flops 134217728 | bytes 4194304 | tf_op jit(solution)/shard_map/pallas_call | solution.py:570
  (10 shorter events, 0.1 us)
Async XLA Ops:
  3.1 9.3 %collective-permute-start.3 = (bf16[128,1024]{1,0:T(8,128)(2,1)S(1)}, bf16[128,1024]{1,0:T(8,128)(2,1)S(1)}, u32[]{:S(2)}, u32[]{:S(2)}) collective-permute-start(bf16[128,1024]{1,0:T(8,128)(2,1)S(1)} %get-tuple-element.32.refs_0_), channel_id=1, source_target_pairs={{0,2},{1,3},{2,0},{3,1},{4,6},{5,7},{6,4},{7,5},{8,10},{9,11},{10,... | collective-permute-start | bytes 786440 | tf_op jit(solution)/shard_map/ppermute | solution.py:331
  6.1 7.8 %collective-permute-start = (bf16[8,128,128]{2,1,0:T(8,128)(2,1)S(1)}, bf16[8,128,128]{2,1,0:T(8,128)(2,1)S(1)}, u32[]{:S(2)}, u32[]{:S(2)}) collective-permute-start(bf16[8,128,128]{2,1,0:T(8,128)(2,1)S(1)} %get-tuple-element.31.running_ref), channel_id=1, source_target_pairs={{0,4},{4,0},{8,12},{12,8},{16,20},{20,16},{24,28},{28,24},{1,5},{5... | collective-permute-start | bytes 786440 | tf_op jit(solution)/shard_map/ppermute | solution.py:44
  7.6 12.6 %collective-permute-start.2 = (bf16[128,1024]{1,0:T(8,128)(2,1)S(1)}, bf16[128,1024]{1,0:T(8,128)(2,1)S(1)}, u32[]{:S(2)}, u32[]{:S(2)}) collective-permute-start(bf16[128,1024]{1,0:T(8,128)(2,1)S(1)} %get-tuple-element.32.refs_0_), channel_id=1, source_target_pairs={{0,1},{1,0},{2,3},{3,2},{4,5},{5,4},{6,7},{7,6},{8,9},{9,8},{10,11... | collective-permute-start | bytes 786440 | tf_op jit(solution)/shard_map/ppermute | solution.py:331
  12.4 7.8 %collective-permute-start.4 = (bf16[128,1024]{1,0:T(8,128)(2,1)S(1)}, bf16[128,1024]{1,0:T(8,128)(2,1)S(1)}, u32[]{:S(2)}, u32[]{:S(2)}) collective-permute-start(bf16[128,1024]{1,0:T(8,128)(2,1)S(1)} %shard_map.104), channel_id=1, source_target_pairs={{0,1},{1,0},{2,3},{3,2},{4,5},{5,4},{6,7},{7,6},{8,9},{9,8},{10,11... | collective-permute-start | bytes 786440 | tf_op jit(solution)/shard_map/ppermute | solution.py:331
  13.9 9.1 %collective-permute-start.1 = (bf16[8,128,128]{2,1,0:T(8,128)(2,1)S(1)}, bf16[8,128,128]{2,1,0:T(8,128)(2,1)S(1)}, u32[]{:S(2)}, u32[]{:S(2)}) collective-permute-start(bf16[8,128,128]{2,1,0:T(8,128)(2,1)S(1)} %shard_map.103.refs_6_.running_ref), channel_id=1, source_target_pairs={{0,8},{8,0},{4,12},{12,4},{16,24},{24,16},{20,28},{28,20},{1,9},{9... | collective-permute-start | bytes 786440 | tf_op jit(solution)/shard_map/ppermute | solution.py:44
  15.6 10.9 %collective-permute-start.6 = (bf16[64,1024]{1,0:T(8,128)(2,1)S(1)}, bf16[64,1024]{1,0:T(8,128)(2,1)S(1)}, u32[]{:S(2)}, u32[]{:S(2)}) collective-permute-start(bf16[64,1024]{1,0:T(8,128)(2,1)S(1)} %get-tuple-element.40), channel_id=1, source_target_pairs={{0,0},{1,10},{2,18},{3,24},{4,4},{5,14},{6,22},{7,28},{8,2},{9,8},... | collective-permute-start | bytes 393224 | tf_op jit(solution)/shard_map/ppermute | solution.py:392
  16.3 10.3 %collective-permute-start.7 = (bf16[64,1024]{1,0:T(8,128)(2,1)S(1)}, bf16[64,1024]{1,0:T(8,128)(2,1)S(1)}, u32[]{:S(2)}, u32[]{:S(2)}) collective-permute-start(bf16[64,1024]{1,0:T(8,128)(2,1)S(1)} %slice.23), channel_id=1, source_target_pairs={{2,0},{3,10},{0,18},{1,24},{6,4},{7,14},{4,22},{5,28},{10,2},{11,8... | collective-permute-start | bytes 393224 | tf_op jit(solution)/shard_map/ppermute | solution.py:393
  23.1 15.7 %collective-permute-start.5 = (bf16[8,128,128]{2,1,0:T(8,128)(2,1)S(1)}, bf16[8,128,128]{2,1,0:T(8,128)(2,1)S(1)}, u32[]{:S(2)}, u32[]{:S(2)}) collective-permute-start(bf16[8,128,128]{2,1,0:T(8,128)(2,1)S(1)} %shard_map.106.after_ref), channel_id=1, source_target_pairs={{0,16},{16,0},{4,20},{20,4},{8,24},{24,8},{12,28},{28,12},{1,17},{... | collective-permute-start | bytes 786440 | tf_op jit(solution)/shard_map/ppermute | solution.py:44
  26.5 5.7 %collective-permute-start.8 = (bf16[128,512]{1,0:T(8,128)(2,1)S(1)}, bf16[128,512]{1,0:T(8,128)(2,1)S(1)}, u32[]{:S(2)}, u32[]{:S(2)}) collective-permute-start(bf16[128,512]{1,0:T(8,128)(2,1)S(1)} %get-tuple-element.41.refs_4_), channel_id=1, source_target_pairs={{0,4},{4,0},{8,12},{12,8},{16,20},{20,16},{24,28},{28,24},{1,5},{5... | collective-permute-start | bytes 393224 | tf_op jit(solution)/shard_map/ppermute | solution.py:444
  40.0 15.1 %collective-permute-start.9 = (bf16[2,128,1024]{2,1,0:T(8,128)(2,1)S(1)}, bf16[2,128,1024]{2,1,0:T(8,128)(2,1)S(1)}, u32[]{:S(2)}, u32[]{:S(2)}) collective-permute-start(bf16[2,128,1024]{2,1,0:T(8,128)(2,1)S(1)} %shard_map.113), channel_id=1, source_target_pairs={{0,1},{1,0},{2,3},{3,2},{4,5},{5,4},{6,7},{7,6},{8,9},{9,8},{10,11... | collective-permute-start | bytes 1572872 | tf_op jit(solution)/shard_map/ppermute | solution.py:331
  40.1 8.7 %collective-permute-start.14 = (bf16[128,1024]{1,0:T(8,128)(2,1)S(1)}, bf16[128,1024]{1,0:T(8,128)(2,1)S(1)}, u32[]{:S(2)}, u32[]{:S(2)}) collective-permute-start(bf16[128,1024]{1,0:T(8,128)(2,1)S(1)} %shard_map.109.after_ref.att_ref.refs_0_), channel_id=1, source_target_pairs={{0,8},{8,16},{16,24},{24,28},{28,20},{20,12},{12,4},{4,0},{1,9},{9... | collective-permute-start | bytes 786440 | tf_op jit(solution)/shard_map/ppermute | solution.py:548
  40.2 9.2 %collective-permute-start.17 = (bf16[128,1024]{1,0:T(8,128)(2,1)S(1)}, bf16[128,1024]{1,0:T(8,128)(2,1)S(1)}, u32[]{:S(2)}, u32[]{:S(2)}) collective-permute-start(bf16[128,1024]{1,0:T(8,128)(2,1)S(1)} %shard_map.109.after_ref.att_ref.refs_0_), channel_id=1, source_target_pairs={{8,0},{16,8},{24,16},{28,24},{20,28},{12,20},{4,12},{0,4},{9,1},{1... | collective-permute-start | bytes 786440 | tf_op jit(solution)/shard_map/ppermute | solution.py:549
  42.1 9.4 %collective-permute-start.12 = (bf16[2,128,512]{2,1,0:T(8,128)(2,1)S(1)}, bf16[2,128,512]{2,1,0:T(8,128)(2,1)S(1)}, u32[]{:S(2)}, u32[]{:S(2)}) collective-permute-start(bf16[2,128,512]{2,1,0:T(8,128)(2,1)S(1)} %shard_map.112.after_ref.refs_0_), channel_id=1, source_target_pairs={{0,2},{1,3},{2,0},{3,1},{4,6},{5,7},{6,4},{7,5},{8,10},{9,11},{10,... | collective-permute-start | bytes 786440 | tf_op jit(solution)/shard_map/ppermute | solution.py:331
  43.9 11.0 %collective-permute-start.20 = (bf16[8,128,128]{2,1,0:T(8,128)(2,1)S(1)}, bf16[8,128,128]{2,1,0:T(8,128)(2,1)S(1)}, u32[]{:S(2)}, u32[]{:S(2)}) collective-permute-start(bf16[8,128,128]{2,1,0:T(8,128)(2,1)S(1)} %shard_map.110.after_ref), channel_id=1, source_target_pairs={{0,8},{8,0},{4,12},{12,4},{16,24},{24,16},{20,28},{28,20},{1,9},{9... | collective-permute-start | bytes 786440 | tf_op jit(solution)/shard_map/ppermute | solution.py:44
  48.8 9.0 %collective-permute-start.15 = (bf16[128,1024]{1,0:T(8,128)(2,1)S(1)}, bf16[128,1024]{1,0:T(8,128)(2,1)S(1)}, u32[]{:S(2)}, u32[]{:S(2)}) collective-permute-start(bf16[128,1024]{1,0:T(8,128)(2,1)S(1)} %collective-permute-done.14.refs_1_), channel_id=1, source_target_pairs={{0,8},{8,16},{16,24},{24,28},{28,20},{20,12},{12,4},{4,0},{1,9},{9... | collective-permute-start | bytes 786440 | tf_op jit(solution)/shard_map/ppermute | solution.py:548
  49.4 10.9 %collective-permute-start.18 = (bf16[128,1024]{1,0:T(8,128)(2,1)S(1)}, bf16[128,1024]{1,0:T(8,128)(2,1)S(1)}, u32[]{:S(2)}, u32[]{:S(2)}) collective-permute-start(bf16[128,1024]{1,0:T(8,128)(2,1)S(1)} %collective-permute-done.17.refs_2_), channel_id=1, source_target_pairs={{8,0},{16,8},{24,16},{28,24},{20,28},{12,20},{4,12},{0,4},{9,1},{1... | collective-permute-start | bytes 786440 | tf_op jit(solution)/shard_map/ppermute | solution.py:549
  51.5 10.2 %collective-permute-start.11 = (bf16[2,128,512]{2,1,0:T(8,128)(2,1)S(1)}, bf16[2,128,512]{2,1,0:T(8,128)(2,1)S(1)}, u32[]{:S(2)}, u32[]{:S(2)}) collective-permute-start(bf16[2,128,512]{2,1,0:T(8,128)(2,1)S(1)} %shard_map.112.after_ref.refs_0_), channel_id=1, source_target_pairs={{0,1},{1,0},{2,3},{3,2},{4,5},{5,4},{6,7},{7,6},{8,9},{9,8},{10,11... | collective-permute-start | bytes 786440 | tf_op jit(solution)/shard_map/ppermute | solution.py:331
  55.0 9.9 %collective-permute-start.13 = (bf16[2,128,512]{2,1,0:T(8,128)(2,1)S(1)}, bf16[2,128,512]{2,1,0:T(8,128)(2,1)S(1)}, u32[]{:S(2)}, u32[]{:S(2)}) collective-permute-start(bf16[2,128,512]{2,1,0:T(8,128)(2,1)S(1)} %collective-permute-done.12.refs_2_), channel_id=1, source_target_pairs={{0,1},{1,0},{2,3},{3,2},{4,5},{5,4},{6,7},{7,6},{8,9},{9,8},{10,11... | collective-permute-start | bytes 786440 | tf_op jit(solution)/shard_map/ppermute | solution.py:331
  55.1 17.3 %collective-permute-start.21 = (bf16[8,128,128]{2,1,0:T(8,128)(2,1)S(1)}, bf16[8,128,128]{2,1,0:T(8,128)(2,1)S(1)}, u32[]{:S(2)}, u32[]{:S(2)}) collective-permute-start(bf16[8,128,128]{2,1,0:T(8,128)(2,1)S(1)} %shard_map.118), channel_id=1, source_target_pairs={{0,4},{4,0},{8,12},{12,8},{16,20},{20,16},{24,28},{28,24},{1,5},{5... | collective-permute-start | bytes 786440 | tf_op jit(solution)/shard_map/ppermute | solution.py:44
  57.8 11.7 %collective-permute-start.16 = (bf16[128,1024]{1,0:T(8,128)(2,1)S(1)}, bf16[128,1024]{1,0:T(8,128)(2,1)S(1)}, u32[]{:S(2)}, u32[]{:S(2)}) collective-permute-start(bf16[128,1024]{1,0:T(8,128)(2,1)S(1)} %collective-permute-done.15.refs_3_), channel_id=1, source_target_pairs={{0,8},{8,16},{16,24},{24,28},{28,20},{20,12},{12,4},{4,0},{1,9},{9... | collective-permute-start | bytes 786440 | tf_op jit(solution)/shard_map/ppermute | solution.py:548
  60.3 9.3 %collective-permute-start.19 = (bf16[128,1024]{1,0:T(8,128)(2,1)S(1)}, bf16[128,1024]{1,0:T(8,128)(2,1)S(1)}, u32[]{:S(2)}, u32[]{:S(2)}) collective-permute-start(bf16[128,1024]{1,0:T(8,128)(2,1)S(1)} %collective-permute-done.18.refs_4_), channel_id=1, source_target_pairs={{8,0},{16,8},{24,16},{28,24},{20,28},{12,20},{4,12},{0,4},{9,1},{1... | collective-permute-start | bytes 786440 | tf_op jit(solution)/shard_map/ppermute | solution.py:549
  61.8 12.4 %collective-permute-start.10 = (bf16[1,128,1024]{2,1,0:T(8,128)(2,1)S(1)}, bf16[1,128,1024]{2,1,0:T(8,128)(2,1)S(1)}, u32[]{:S(2)}, u32[]{:S(2)}) collective-permute-start(bf16[1,128,1024]{2,1,0:T(8,128)(2,1)S(1)} %slice.34), channel_id=1, source_target_pairs={{0,2},{1,3},{2,0},{3,1},{4,6},{5,7},{6,4},{7,5},{8,10},{9,11},{10,... | collective-permute-start | bytes 786440 | tf_op jit(solution)/shard_map/ppermute | solution.py:331
  69.5 5.4 %collective-permute-start.22 = (bf16[64,1024]{1,0:T(8,128)(2,1)S(1)}, bf16[64,1024]{1,0:T(8,128)(2,1)S(1)}, u32[]{:S(2)}, u32[]{:S(2)}) collective-permute-start(bf16[64,1024]{1,0:T(8,128)(2,1)S(1)} %slice.26), channel_id=1, source_target_pairs={{0,8},{8,16},{16,24},{24,28},{28,20},{20,12},{12,4},{4,0},{1,9},{9... | collective-permute-start | bytes 393224 | tf_op jit(solution)/shard_map/ppermute | solution.py:558
  69.6 5.3 %collective-permute-start.23 = (bf16[64,1024]{1,0:T(8,128)(2,1)S(1)}, bf16[64,1024]{1,0:T(8,128)(2,1)S(1)}, u32[]{:S(2)}, u32[]{:S(2)}) collective-permute-start(bf16[64,1024]{1,0:T(8,128)(2,1)S(1)} %slice.27), channel_id=1, source_target_pairs={{8,0},{16,8},{24,16},{28,24},{20,28},{12,20},{4,12},{0,4},{9,1},{1... | collective-permute-start | bytes 393224 | tf_op jit(solution)/shard_map/ppermute | solution.py:559

commit v10 on v9

--- a/solution.py
+++ b/solution.py
@@ -283,16 +283,23 @@
     refs[-1][...] = total
 
 
-def last_kernel(
-    offset, devices, cols_ref, low_ref, high_ref, total_ref, after_ref, out_ref, held
-):
-    del after_ref
-    half, block = low_ref.shape[0], out_ref.shape[0]
-    at = pl.ds(pl.multiple_of(pl.program_id(0) * block, block), block)
-    held[:half] = low_ref[:, at]
-    held[half:] = high_ref[:, at]
-    owner = ring_owner(lax.axis_index("seq"), offset, devices)
-    out_ref[...] = total_ref[at, :] + mm(held[...], cols_ref[owner], TN)
+def last_kernel(offset, devices, cols_ref, low_ref, high_ref, total_ref, after_ref, out_hbm, *refs):
+    del after_ref
+    held, result, sems = refs
+    half = low_ref.shape[0]
+    held[:half] = low_ref[...]
+    held[half:] = high_ref[...]
+    cols = cols_ref[ring_owner(lax.axis_index("seq"), offset, devices)]
+    pieces = sems.shape[0]
+    block = held.shape[1] // pieces
+    copies = []
+    for i in range(pieces):
+        at = pl.ds(i * block, block)
+        result[at, :] = total_ref[at, :] + mm(held[:, at], cols, TN)
+        copies.append(pltpu.make_async_copy(result.at[at], out_hbm.at[at], sems.at[i]))
+        copies[-1].start()
+    for copy in copies:
+        copy.wait()
 
 
 def body(queries, keys, values, level_weights, out_proj, out_grad):
@@ -566,20 +573,16 @@
         compiler_params=PARAMS,
         cost_estimate=cost(2 * flops_head, 11 * moved_head),
     )(kh, vh, key_local, value_local, total, *landed)
-    quarter_rows = width // 4
     proj_grad = pl.pallas_call(
         functools.partial(last_kernel, steps, devices),
         out_shape=like((width, columns_dev), F32),
-        grid=(4,),
-        in_specs=[
-            VMEM,
-            VMEM,
-            VMEM,
-            VMEM,
-            ANY,
+        in_specs=[VMEM] * 4 + [ANY],
+        out_specs=ANY,
+        scratch_shapes=[
+            pltpu.VMEM((rows, width), BF),
+            pltpu.VMEM((width, columns_dev), F32),
+            pltpu.SemaphoreType.DMA((4,)),
         ],
-        out_specs=pl.BlockSpec((quarter_rows, columns_dev), lambda i: (i, 0)),
-        scratch_shapes=[pltpu.VMEM((rows, quarter_rows), BF)],
         compiler_params=PARAMS,
         cost_estimate=cost(2 * rows * width * columns_dev, 8 * width * columns_dev),
     )(grad_columns, *last, total, hbm(key_grad))

time: 77.4 us -> 76.7 us (level)
  no operation moved by 1% of the time
where the time goes in v10:
time: 76.7 us; the launch traced here: 76.5 us
  starting transfers between devices  31 us (40%)
  waiting for transfers between devices  24.2 us (32%)
  Pallas kernels  19.5 us (25%)
  other arithmetic  0.94 us (1%)
  between operations  0.88 us (1%)
    ppermute x5, waiting for transfers between devices, across(): return lax.ppermute(block, axis, route)  11.3 us
    ppermute x3, waiting for transfers between devices, body(): ahead = lax.ppermute(ahead, 'seq', forward)  8.91 us
    ppermute x5, starting transfers between devices, across(): return lax.ppermute(block, axis, route)  8.18 us
    ppermute x8, starting transfers between devices, to_group(): return lax.ppermute(block, 'head', [(at, at ^ i) for at in range(heads)])  6.69 us
    ppermute x3, starting transfers between devices, body(): behind = lax.ppermute(behind, 'seq', backward)  4.6 us
    ppermute x1, starting transfers between devices, body(): lax.ppermute(grad_blocks[far][half:], axes, turn_route(far))  3.92 us
    pallas_call x1, Pallas kernels, body(): pl.pallas_call(local_kernel, out_shape=(pltpu.VMEM((heads_dev, rows, rows...  3.66 us
    ppermute x3, starting transfers between devices, body(): ahead = lax.ppermute(ahead, 'seq', forward)  3.23 us
  transfers between devices with their start and end apart: 24, of which 8 were waited for; matrix products, arithmetic and copies ran while one was open for 1% of the time, Pallas kernels for 19%

profile of v10, /device:TPU:0, one launch (start us, length us, event | category | flops | bytes accessed | tf_op | source)
XLA Modules:
  0.0 76.5 jit_solution(499964192068856203)
XLA Ops:
  0.6 2.5 %shard_map.101 = (bf16[8,128,128]{2,1,0:T(8,128)(2,1)S(1)}, bf16[8,128,128]{2,1,0:T(8,128)(2,1)S(1)}, bf16[8,128,128]{2,1,0:T(8,128)(2,1)S(1)}, bf16[128,1024]{1,0:T(8,128)(2,1)S(1)}, bf16[64,1024]{1,0:T(8,128)(2,1)S(1)}) custom-call(f32[128,8,128]{2,1,0:T(8,128)} %k_hbm.1, f32[128,8,128]{2,1,0:T(8,128)} %v_hbm.1, bf16[128,1024]{1,0:T(8,128)(2,1)} %grad_hbm.1), custom_call_target="tpu_custom_call" | custom-call | flops 33554432 | bytes 1835008 | tf_op jit(solution)/shard_map/pallas_call | solution.py:323
  3.1 3.0 %collective-permute-start.3 = (bf16[128,1024]{1,0:T(8,128)(2,1)S(1)}, bf16[128,1024]{1,0:T(8,128)(2,1)S(1)}, u32[]{:S(2)}, u32[]{:S(2)}) collective-permute-start(bf16[128,1024]{1,0:T(8,128)(2,1)S(1)} %get-tuple-element.32.refs_0_), channel_id=1, source_target_pairs={{0,2},{1,3},{2,0},{3,1},{4,6},{5,7},{6,4},{7,5},{8,10},{9,11},{10,... | collective-permute-start | bytes 786440 | tf_op jit(solution)/shard_map/ppermute | solution.py:338
  6.1 1.5 %collective-permute-start = (bf16[8,128,128]{2,1,0:T(8,128)(2,1)S(1)}, bf16[8,128,128]{2,1,0:T(8,128)(2,1)S(1)}, u32[]{:S(2)}, u32[]{:S(2)}) collective-permute-start(bf16[8,128,128]{2,1,0:T(8,128)(2,1)S(1)} %get-tuple-element.31.running_ref), channel_id=1, source_target_pairs={{0,4},{4,0},{8,12},{12,8},{16,20},{20,16},{24,28},{28,24},{1,5},{5... | collective-permute-start | bytes 786440 | tf_op jit(solution)/shard_map/ppermute | solution.py:44
  7.6 0.0 collective-permute-start.2
  7.6 3.7 %shard_map.102 = (bf16[8,128,128]{2,1,0:T(8,128)(2,1)S(1)}, f32[8,128,128]{2,1,0:T(8,128)S(1)}, bf16[8,128,128]{2,1,0:T(8,128)(2,1)S(1)}, bf16[3,8,128,128]{3,2,...) custom-call(f32[128,8,128]{2,1,0:T(8,128)} %q_hbm.1, ...), custom_call_target="tpu_custom_call" | custom-call | flops 67108864 | bytes 3145728 | tf_op jit(solution)/shard_map/pallas_call | solution.py:347
  11.3 1.1 %collective-permute-done.3.block_ref.refs_2_ = bf16[128,1024]{1,0:T(8,128)(2,1)S(1)} collective-permute-done((bf16[128,1024]{1,0:T(8,128)(2,1)S(1)}, bf16[128,1024]{1,0:T(8,128)(2,1)S(1)}, u32[]{:S(2)}, u32[]{:S(2)}) %collective-permute-start.3) | collective-permute-done | bytes 262176 | tf_op jit(solution)/shard_map/ppermute | solution.py:338
  12.4 0.1 collective-permute-start.4
  12.5 1.4 %collective-permute-done.arrived_ref.refs_0_ = bf16[8,128,128]{2,1,0:T(8,128)(2,1)S(1)} collective-permute-done((bf16[8,128,128]{2,1,0:T(8,128)(2,1)S(1)}, bf16[8,128,128]{2,1,0:T(8,128)(2,1)S(1)}, u32[]{:S(2)}, u32[]{:S(2)}) %collective-permute-start) | collective-permute-done | bytes 262176 | tf_op jit(solution)/shard_map/ppermute | solution.py:44
  13.9 0.1 shard_map.103.refs_6_.running_ref
  13.9 1.6 %collective-permute-start.1 = (bf16[8,128,128]{2,1,0:T(8,128)(2,1)S(1)}, bf16[8,128,128]{2,1,0:T(8,128)(2,1)S(1)}, u32[]{:S(2)}, u32[]{:S(2)}) collective-permute-start(bf16[8,128,128]{2,1,0:T(8,128)(2,1)S(1)} %shard_map.103.refs_6_.running_ref), channel_id=1, source_target_pairs={{0,8},{8,0},{4,12},{12,4},{16,24},{24,16},{20,28},{28,20},{1,9},{9... | collective-permute-start | bytes 786440 | tf_op jit(solution)/shard_map/ppermute | solution.py:44
  15.6 0.7 collective-permute-start.6
  16.3 3.9 %collective-permute-start.7 = (bf16[64,1024]{1,0:T(8,128)(2,1)S(1)}, bf16[64,1024]{1,0:T(8,128)(2,1)S(1)}, u32[]{:S(2)}, u32[]{:S(2)}) collective-permute-start(bf16[64,1024]{1,0:T(8,128)(2,1)S(1)} %slice.23), channel_id=1, source_target_pairs={{2,0},{3,10},{0,18},{1,24},{6,4},{7,14},{4,22},{5,28},{10,2},{11,8... | collective-permute-start | bytes 393224 | tf_op jit(solution)/shard_map/ppermute | solution.py:400
  20.2 0.0 collective-permute-done.2.refs_1_
  20.2 0.0 collective-permute-done.4.refs_3_
  20.2 2.8 %shard_map.105 = (bf16[1024,128]{1,0:T(8,128)(2,1)S(1)}, bf16[8,128,128]{2,1,0:T(8,128)(2,1)S(1)}, bf16[8,128,128]{2,1,0:T(8,128)(2,1)S(1)}, bf16[8,128,128]{2,1,0:T(8,128)(2,1)S(1)}) custom-call(bf16[128,1024]{1,0:T(8,128)(2,1)S(1)} %get-tuple-element.32.refs_0_, bf16[128,1024]{1,0:T(8,128)(2,1)S(1)} %collective-permute-done.2.refs_1_, ...), custom_call_target="tpu_custom_call" | custom-call | flops 1073741824 | bytes 8388608 | tf_op jit(solution)/shard_map/pallas_call | solution.py:417
  23.0 0.0 collective-permute-done.1.arrived_ref.refs_1_
  23.0 0.1 shard_map.106.after_ref
  23.1 3.4 %collective-permute-start.5 = (bf16[8,128,128]{2,1,0:T(8,128)(2,1)S(1)}, bf16[8,128,128]{2,1,0:T(8,128)(2,1)S(1)}, u32[]{:S(2)}, u32[]{:S(2)}) collective-permute-start(bf16[8,128,128]{2,1,0:T(8,128)(2,1)S(1)} %shard_map.106.after_ref), channel_id=1, source_target_pairs={{0,16},{16,0},{4,20},{20,4},{8,24},{24,8},{12,28},{28,12},{1,17},{... | collective-permute-start | bytes 786440 | tf_op jit(solution)/shard_map/ppermute | solution.py:44
  26.5 0.0 collective-permute-done.6.low_ref
  26.5 0.0 collective-permute-done.7.high_ref
  26.5 1.6 %collective-permute-start.8 = (bf16[128,512]{1,0:T(8,128)(2,1)S(1)}, bf16[128,512]{1,0:T(8,128)(2,1)S(1)}, u32[]{:S(2)}, u32[]{:S(2)}) collective-permute-start(bf16[128,512]{1,0:T(8,128)(2,1)S(1)} %get-tuple-element.41.refs_4_), channel_id=1, source_target_pairs={{0,4},{4,0},{8,12},{12,8},{16,20},{20,16},{24,28},{28,24},{1,5},{5... | collective-permute-start | bytes 393224 | tf_op jit(solution)/shard_map/ppermute | solution.py:451
  28.1 1.3 %shard_map.107 = (f32[8,128,128]{2,1,0:T(8,128)S(1)}, f32[8,128,128]{2,1,0:T(8,128)S(1)}, f32[8,128,128]{2,1,0:T(8,128)S(1)}) custom-call(bf16[1024,128]{1,0:T(8,128)(2,1)S(1)} %get-tuple-element.35.gt_ref, bf16[8,128,128]{2,1,0:T(8,128)(2,1)S(1)} %get-tuple-element.36.qh_ref, bf16[8,128,128]{2,1,0:T(8,128)(2,1)S(1)} %get-tuple-element.27.kh_ref, ...), custom_call_target="tpu_custom_call" | custom-call | flops 201326592 | bytes 3670016 | tf_op jit(solution)/shard_map/pallas_call | solution.py:473
  29.4 2.8 %collective-permute-done.8.refs_1_ = bf16[128,512]{1,0:T(8,128)(2,1)S(1)} collective-permute-done((bf16[128,512]{1,0:T(8,128)(2,1)S(1)}, bf16[128,512]{1,0:T(8,128)(2,1)S(1)}, u32[]{:S(2)}, u32[]{:S(2)}) %collective-permute-start.8) | collective-permute-done | bytes 131104 | tf_op jit(solution)/shard_map/ppermute | solution.py:451
  32.3 6.6 %collective-permute-done.5.refs_2_.refs_0_.state_ref = bf16[8,128,128]{2,1,0:T(8,128)(2,1)S(1)} collective-permute-done((bf16[8,128,128]{2,1,0:T(8,128)(2,1)S(1)}, bf16[8,128,128]{2,1,0:T(8,128)(2,1)S(1)}, u32[]{:S(2)}, u32[]{:S(2)}) %collective-permute-start.5) | collective-permute-done | bytes 262176 | tf_op jit(solution)/shard_map/ppermute | solution.py:44
  38.9 0.4 shard_map.109.after_ref.att_ref.refs_0_
  39.2 0.7 shard_map.113
  40.0 0.1 collective-permute-start.9
  40.1 0.1 collective-permute-start.14
  40.2 1.9 %collective-permute-start.17 = (bf16[128,1024]{1,0:T(8,128)(2,1)S(1)}, bf16[128,1024]{1,0:T(8,128)(2,1)S(1)}, u32[]{:S(2)}, u32[]{:S(2)}) collective-permute-start(bf16[128,1024]{1,0:T(8,128)(2,1)S(1)} %shard_map.109.after_ref.att_ref.refs_0_), channel_id=1, source_target_pairs={{8,0},{16,8},{24,16},{28,24},{20,28},{12,20},{4,12},{0,4},{9,1},{1... | collective-permute-start | bytes 786440 | tf_op jit(solution)/shard_map/ppermute | solution.py:556
  42.1 1.7 %collective-permute-start.12 = (bf16[2,128,512]{2,1,0:T(8,128)(2,1)S(1)}, bf16[2,128,512]{2,1,0:T(8,128)(2,1)S(1)}, u32[]{:S(2)}, u32[]{:S(2)}) collective-permute-start(bf16[2,128,512]{2,1,0:T(8,128)(2,1)S(1)} %shard_map.112.after_ref.refs_0_), channel_id=1, source_target_pairs={{0,2},{1,3},{2,0},{3,1},{4,6},{5,7},{6,4},{7,5},{8,10},{9,11},{10,... | collective-permute-start | bytes 786440 | tf_op jit(solution)/shard_map/ppermute | solution.py:338
  43.8 0.1 shard_map.110.after_ref
  43.9 0.2 collective-permute-start.20
  44.1 4.7 %collective-permute-done.14.refs_1_ = bf16[128,1024]{1,0:T(8,128)(2,1)S(1)} collective-permute-done((bf16[128,1024]{1,0:T(8,128)(2,1)S(1)}, bf16[128,1024]{1,0:T(8,128)(2,1)S(1)}, u32[]{:S(2)}, u32[]{:S(2)}) %collective-permute-start.14) | collective-permute-done | bytes 262176 | tf_op jit(solution)/shard_map/ppermute | solution.py:555
  48.8 0.6 collective-permute-start.15
  49.4 0.0 collective-permute-done.17.refs_2_
  49.4 1.4 %collective-permute-start.18 = (bf16[128,1024]{1,0:T(8,128)(2,1)S(1)}, bf16[128,1024]{1,0:T(8,128)(2,1)S(1)}, u32[]{:S(2)}, u32[]{:S(2)}) collective-permute-start(bf16[128,1024]{1,0:T(8,128)(2,1)S(1)} %collective-permute-done.17.refs_2_), channel_id=1, source_target_pairs={{8,0},{16,8},{24,16},{28,24},{20,28},{12,20},{4,12},{0,4},{9,1},{1... | collective-permute-start | bytes 786440 | tf_op jit(solution)/shard_map/ppermute | solution.py:556
  50.8 0.7 shard_map.111
  51.5 0.0 collective-permute-done.12.refs_2_
  51.5 0.1 collective-permute-start.11
  51.6 3.3 %collective-permute-done.20.refs_1_ = bf16[8,128,128]{2,1,0:T(8,128)(2,1)S(1)} collective-permute-done((bf16[8,128,128]{2,1,0:T(8,128)(2,1)S(1)}, bf16[8,128,128]{2,1,0:T(8,128)(2,1)S(1)}, u32[]{:S(2)}, u32[]{:S(2)}) %collective-permute-start.20) | collective-permute-done | bytes 262176 | tf_op jit(solution)/shard_map/ppermute | solution.py:44
  55.0 0.1 shard_map.118
  55.1 1.5 %collective-permute-start.21 = (bf16[8,128,128]{2,1,0:T(8,128)(2,1)S(1)}, bf16[8,128,128]{2,1,0:T(8,128)(2,1)S(1)}, u32[]{:S(2)}, u32[]{:S(2)}) collective-permute-start(bf16[8,128,128]{2,1,0:T(8,128)(2,1)S(1)} %shard_map.118), channel_id=1, source_target_pairs={{0,4},{4,0},{8,12},{12,8},{16,20},{20,16},{24,28},{28,24},{1,5},{5... | collective-permute-start | bytes 786440 | tf_op jit(solution)/shard_map/ppermute | solution.py:44
  56.6 1.2 %collective-permute-done.15.refs_3_ = bf16[128,1024]{1,0:T(8,128)(2,1)S(1)} collective-permute-done((bf16[128,1024]{1,0:T(8,128)(2,1)S(1)}, bf16[128,1024]{1,0:T(8,128)(2,1)S(1)}, u32[]{:S(2)}, u32[]{:S(2)}) %collective-permute-start.15) | collective-permute-done | bytes 262176 | tf_op jit(solution)/shard_map/ppermute | solution.py:555
  57.8 2.5 %collective-permute-start.16 = (bf16[128,1024]{1,0:T(8,128)(2,1)S(1)}, bf16[128,1024]{1,0:T(8,128)(2,1)S(1)}, u32[]{:S(2)}, u32[]{:S(2)}) collective-permute-start(bf16[128,1024]{1,0:T(8,128)(2,1)S(1)} %collective-permute-done.15.refs_3_), channel_id=1, source_target_pairs={{0,8},{8,16},{16,24},{24,28},{28,20},{20,12},{12,4},{4,0},{1,9},{9... | collective-permute-start | bytes 786440 | tf_op jit(solution)/shard_map/ppermute | solution.py:555
  60.3 0.0 collective-permute-done.18.refs_4_
  60.3 1.2 %collective-permute-start.19 = (bf16[128,1024]{1,0:T(8,128)(2,1)S(1)}, bf16[128,1024]{1,0:T(8,128)(2,1)S(1)}, u32[]{:S(2)}, u32[]{:S(2)}) collective-permute-start(bf16[128,1024]{1,0:T(8,128)(2,1)S(1)} %collective-permute-done.18.refs_4_), channel_id=1, source_target_pairs={{8,0},{16,8},{24,16},{28,24},{20,28},{12,20},{4,12},{0,4},{9,1},{1... | collective-permute-start | bytes 786440 | tf_op jit(solution)/shard_map/ppermute | solution.py:556
  61.5 0.2 convert_add_fusion
  61.8 0.0 collective-permute-done.11.refs_1_
  61.8 1.8 %collective-permute-start.10 = (bf16[1,128,1024]{2,1,0:T(8,128)(2,1)S(1)}, bf16[1,128,1024]{2,1,0:T(8,128)(2,1)S(1)}, u32[]{:S(2)}, u32[]{:S(2)}) collective-permute-start(bf16[1,128,1024]{2,1,0:T(8,128)(2,1)S(1)} %slice.34), channel_id=1, source_target_pairs={{0,2},{1,3},{2,0},{3,1},{4,6},{5,7},{6,4},{7,5},{8,10},{9,11},{10,... | collective-permute-start | bytes 786440 | tf_op jit(solution)/shard_map/ppermute | solution.py:338
  63.5 1.3 %shard_map.114 = f32[128,8,128]{2,1,0:T(8,128)} custom-call(bf16[1024,128]{1,0:T(8,128)(2,1)S(1)} %get-tuple-element.35.gt_ref, f32[5,8,128]{2,1,0:T(8,128)S(1)} %get-tuple-element.38.lam_ref, f32[8,128,128]{2,1,0:T(8,128)S(1)} %get-tuple-element.44.dql_ref, bf16[8,128,128]{2,1,0:T(8,128)(2,1)S(1)} %collective-permute-done.5.refs_2_.refs_0_.state_ref, ...), custom_call_target="tpu_custom_call" | custom-call | flops 33554432 | bytes 1572864 | tf_op jit(solution)/shard_map/pallas_call | solution.py:505
  64.9 0.1 shard_map.115.cols_ref
  65.0 1.5 %shard_map.116.refs_2_ = f32[1024,512]{1,0:T(8,128)S(1)} custom-call(bf16[8,128,512]{2,1,0:T(8,128)(2,1)S(1)} %shard_map.115.cols_ref, bf16[128,1024]{1,0:T(8,128)(2,1)S(1)} %shard_map.109.after_ref.att_ref.refs_0_, bf16[128,1024]{1,0:T(8,128)(2,1)S(1)} %collective-permute-done.14.refs_1_, bf16[128,1024]{1,0:T(8,128)(2,1)S(1)} %collective-permute-done.17.refs_2_, ...), custom_call_target="tpu_custom_call" | custom-call | flops 671088640 | bytes 2097152 | tf_op jit(solution)/shard_map/pallas_call | solution.py:540
  66.5 3.0 %collective-permute-done.16.refs_0_ = bf16[128,1024]{1,0:T(8,128)(2,1)S(1)} collective-permute-done((bf16[128,1024]{1,0:T(8,128)(2,1)S(1)}, bf16[128,1024]{1,0:T(8,128)(2,1)S(1)}, u32[]{:S(2)}, u32[]{:S(2)}) %collective-permute-start.16) | collective-permute-done | bytes 262176 | tf_op jit(solution)/shard_map/ppermute | solution.py:555
  69.5 0.1 collective-permute-start.22
  69.6 0.0 collective-permute-done.19.refs_1_
  69.6 2.1 %collective-permute-start.23 = (bf16[64,1024]{1,0:T(8,128)(2,1)S(1)}, bf16[64,1024]{1,0:T(8,128)(2,1)S(1)}, u32[]{:S(2)}, u32[]{:S(2)}) collective-permute-start(bf16[64,1024]{1,0:T(8,128)(2,1)S(1)} %slice.27), channel_id=1, source_target_pairs={{8,0},{16,8},{24,16},{28,24},{20,28},{12,20},{4,12},{0,4},{9,1},{1... | collective-permute-start | bytes 393224 | tf_op jit(solution)/shard_map/ppermute | solution.py:566
  71.7 0.7 shard_map.117.after_ref.total_ref
  72.4 0.0 collective-permute-done.21.refs_2_
  72.4 1.7 %shard_map.119 = (f32[128,8,128]{2,1,0:T(8,128)}, f32[128,8,128]{2,1,0:T(8,128)}) custom-call(bf16[8,128,128]{2,1,0:T(8,128)(2,1)S(1)} %get-tuple-element.27.kh_ref, bf16[8,128,128]{2,1,0:T(8,128)(2,1)S(1)} %get-tuple-element.28.vh_ref, f32[8,128,128]{2,1,0:T(8,128)S(1)} %get-tuple-element.39.refs_3_.dkl_ref, f32[8,128,128]{2,1,0:T(8,128)S(1)} %get-tuple-element.45.dvl_ref, ...), custom_call_target="tpu_custom_call" | custom-call | flops 67108864 | bytes 2883584 | tf_op jit(solution)/shard_map/pallas_call | solution.py:568
  74.1 0.0 collective-permute-done.10
  74.1 0.8 fusion.1
  74.9 0.0 collective-permute-done.22.low_ref
  74.9 0.0 collective-permute-done.23.high_ref
  74.9 1.6 %shard_map.120 = f32[1024,512]{1,0:T(8,128)} custom-call(bf16[8,128,512]{2,1,0:T(8,128)(2,1)S(1)} %shard_map.115.cols_ref, bf16[64,1024]{1,0:T(8,128)(2,1)S(1)} %collective-permute-done.22.low_ref, bf16[64,1024]{1,0:T(8,128)(2,1)S(1)} %collective-permute-done.23.high_ref, f32[1024,512]{1,0:T(8,128)S(1)} %shard_map.117.after_ref.total_ref, ...), custom_call_target="tpu_custom_call" | custom-call | flops 134217728 | bytes 4194304 | tf_op jit(solution)/shard_map/pallas_call | solution.py:576
  (10 shorter events, 0.1 us)
Async XLA Ops:
  3.1 9.3 %collective-permute-start.3 = (bf16[128,1024]{1,0:T(8,128)(2,1)S(1)}, bf16[128,1024]{1,0:T(8,128)(2,1)S(1)}, u32[]{:S(2)}, u32[]{:S(2)}) collective-permute-start(bf16[128,1024]{1,0:T(8,128)(2,1)S(1)} %get-tuple-element.32.refs_0_), channel_id=1, source_target_pairs={{0,2},{1,3},{2,0},{3,1},{4,6},{5,7},{6,4},{7,5},{8,10},{9,11},{10,... | collective-permute-start | bytes 786440 | tf_op jit(solution)/shard_map/ppermute | solution.py:338
  6.1 7.8 %collective-permute-start = (bf16[8,128,128]{2,1,0:T(8,128)(2,1)S(1)}, bf16[8,128,128]{2,1,0:T(8,128)(2,1)S(1)}, u32[]{:S(2)}, u32[]{:S(2)}) collective-permute-start(bf16[8,128,128]{2,1,0:T(8,128)(2,1)S(1)} %get-tuple-element.31.running_ref), channel_id=1, source_target_pairs={{0,4},{4,0},{8,12},{12,8},{16,20},{20,16},{24,28},{28,24},{1,5},{5... | collective-permute-start | bytes 786440 | tf_op jit(solution)/shard_map/ppermute | solution.py:44
  7.6 12.6 %collective-permute-start.2 = (bf16[128,1024]{1,0:T(8,128)(2,1)S(1)}, bf16[128,1024]{1,0:T(8,128)(2,1)S(1)}, u32[]{:S(2)}, u32[]{:S(2)}) collective-permute-start(bf16[128,1024]{1,0:T(8,128)(2,1)S(1)} %get-tuple-element.32.refs_0_), channel_id=1, source_target_pairs={{0,1},{1,0},{2,3},{3,2},{4,5},{5,4},{6,7},{7,6},{8,9},{9,8},{10,11... | collective-permute-start | bytes 786440 | tf_op jit(solution)/shard_map/ppermute | solution.py:338
  12.4 7.8 %collective-permute-start.4 = (bf16[128,1024]{1,0:T(8,128)(2,1)S(1)}, bf16[128,1024]{1,0:T(8,128)(2,1)S(1)}, u32[]{:S(2)}, u32[]{:S(2)}) collective-permute-start(bf16[128,1024]{1,0:T(8,128)(2,1)S(1)} %shard_map.104), channel_id=1, source_target_pairs={{0,1},{1,0},{2,3},{3,2},{4,5},{5,4},{6,7},{7,6},{8,9},{9,8},{10,11... | collective-permute-start | bytes 786440 | tf_op jit(solution)/shard_map/ppermute | solution.py:338
  13.9 9.1 %collective-permute-start.1 = (bf16[8,128,128]{2,1,0:T(8,128)(2,1)S(1)}, bf16[8,128,128]{2,1,0:T(8,128)(2,1)S(1)}, u32[]{:S(2)}, u32[]{:S(2)}) collective-permute-start(bf16[8,128,128]{2,1,0:T(8,128)(2,1)S(1)} %shard_map.103.refs_6_.running_ref), channel_id=1, source_target_pairs={{0,8},{8,0},{4,12},{12,4},{16,24},{24,16},{20,28},{28,20},{1,9},{9... | collective-permute-start | bytes 786440 | tf_op jit(solution)/shard_map/ppermute | solution.py:44
  15.6 10.9 %collective-permute-start.6 = (bf16[64,1024]{1,0:T(8,128)(2,1)S(1)}, bf16[64,1024]{1,0:T(8,128)(2,1)S(1)}, u32[]{:S(2)}, u32[]{:S(2)}) collective-permute-start(bf16[64,1024]{1,0:T(8,128)(2,1)S(1)} %get-tuple-element.40), channel_id=1, source_target_pairs={{0,0},{1,10},{2,18},{3,24},{4,4},{5,14},{6,22},{7,28},{8,2},{9,8},... | collective-permute-start | bytes 393224 | tf_op jit(solution)/shard_map/ppermute | solution.py:399
  16.3 10.3 %collective-permute-start.7 = (bf16[64,1024]{1,0:T(8,128)(2,1)S(1)}, bf16[64,1024]{1,0:T(8,128)(2,1)S(1)}, u32[]{:S(2)}, u32[]{:S(2)}) collective-permute-start(bf16[64,1024]{1,0:T(8,128)(2,1)S(1)} %slice.23), channel_id=1, source_target_pairs={{2,0},{3,10},{0,18},{1,24},{6,4},{7,14},{4,22},{5,28},{10,2},{11,8... | collective-permute-start | bytes 393224 | tf_op jit(solution)/shard_map/ppermute | solution.py:400
  23.1 15.7 %collective-permute-start.5 = (bf16[8,128,128]{2,1,0:T(8,128)(2,1)S(1)}, bf16[8,128,128]{2,1,0:T(8,128)(2,1)S(1)}, u32[]{:S(2)}, u32[]{:S(2)}) collective-permute-start(bf16[8,128,128]{2,1,0:T(8,128)(2,1)S(1)} %shard_map.106.after_ref), channel_id=1, source_target_pairs={{0,16},{16,0},{4,20},{20,4},{8,24},{24,8},{12,28},{28,12},{1,17},{... | collective-permute-start | bytes 786440 | tf_op jit(solution)/shard_map/ppermute | solution.py:44
  26.5 5.7 %collective-permute-start.8 = (bf16[128,512]{1,0:T(8,128)(2,1)S(1)}, bf16[128,512]{1,0:T(8,128)(2,1)S(1)}, u32[]{:S(2)}, u32[]{:S(2)}) collective-permute-start(bf16[128,512]{1,0:T(8,128)(2,1)S(1)} %get-tuple-element.41.refs_4_), channel_id=1, source_target_pairs={{0,4},{4,0},{8,12},{12,8},{16,20},{20,16},{24,28},{28,24},{1,5},{5... | collective-permute-start | bytes 393224 | tf_op jit(solution)/shard_map/ppermute | solution.py:451
  40.0 15.1 %collective-permute-start.9 = (bf16[2,128,1024]{2,1,0:T(8,128)(2,1)S(1)}, bf16[2,128,1024]{2,1,0:T(8,128)(2,1)S(1)}, u32[]{:S(2)}, u32[]{:S(2)}) collective-permute-start(bf16[2,128,1024]{2,1,0:T(8,128)(2,1)S(1)} %shard_map.113), channel_id=1, source_target_pairs={{0,1},{1,0},{2,3},{3,2},{4,5},{5,4},{6,7},{7,6},{8,9},{9,8},{10,11... | collective-permute-start | bytes 1572872 | tf_op jit(solution)/shard_map/ppermute | solution.py:338
  40.1 8.7 %collective-permute-start.14 = (bf16[128,1024]{1,0:T(8,128)(2,1)S(1)}, bf16[128,1024]{1,0:T(8,128)(2,1)S(1)}, u32[]{:S(2)}, u32[]{:S(2)}) collective-permute-start(bf16[128,1024]{1,0:T(8,128)(2,1)S(1)} %shard_map.109.after_ref.att_ref.refs_0_), channel_id=1, source_target_pairs={{0,8},{8,16},{16,24},{24,28},{28,20},{20,12},{12,4},{4,0},{1,9},{9... | collective-permute-start | bytes 786440 | tf_op jit(solution)/shard_map/ppermute | solution.py:555
  40.2 9.2 %collective-permute-start.17 = (bf16[128,1024]{1,0:T(8,128)(2,1)S(1)}, bf16[128,1024]{1,0:T(8,128)(2,1)S(1)}, u32[]{:S(2)}, u32[]{:S(2)}) collective-permute-start(bf16[128,1024]{1,0:T(8,128)(2,1)S(1)} %shard_map.109.after_ref.att_ref.refs_0_), channel_id=1, source_target_pairs={{8,0},{16,8},{24,16},{28,24},{20,28},{12,20},{4,12},{0,4},{9,1},{1... | collective-permute-start | bytes 786440 | tf_op jit(solution)/shard_map/ppermute | solution.py:556
  42.1 9.4 %collective-permute-start.12 = (bf16[2,128,512]{2,1,0:T(8,128)(2,1)S(1)}, bf16[2,128,512]{2,1,0:T(8,128)(2,1)S(1)}, u32[]{:S(2)}, u32[]{:S(2)}) collective-permute-start(bf16[2,128,512]{2,1,0:T(8,128)(2,1)S(1)} %shard_map.112.after_ref.refs_0_), channel_id=1, source_target_pairs={{0,2},{1,3},{2,0},{3,1},{4,6},{5,7},{6,4},{7,5},{8,10},{9,11},{10,... | collective-permute-start | bytes 786440 | tf_op jit(solution)/shard_map/ppermute | solution.py:338
  43.9 11.0 %collective-permute-start.20 = (bf16[8,128,128]{2,1,0:T(8,128)(2,1)S(1)}, bf16[8,128,128]{2,1,0:T(8,128)(2,1)S(1)}, u32[]{:S(2)}, u32[]{:S(2)}) collective-permute-start(bf16[8,128,128]{2,1,0:T(8,128)(2,1)S(1)} %shard_map.110.after_ref), channel_id=1, source_target_pairs={{0,8},{8,0},{4,12},{12,4},{16,24},{24,16},{20,28},{28,20},{1,9},{9... | collective-permute-start | bytes 786440 | tf_op jit(solution)/shard_map/ppermute | solution.py:44
  48.8 9.0 %collective-permute-start.15 = (bf16[128,1024]{1,0:T(8,128)(2,1)S(1)}, bf16[128,1024]{1,0:T(8,128)(2,1)S(1)}, u32[]{:S(2)}, u32[]{:S(2)}) collective-permute-start(bf16[128,1024]{1,0:T(8,128)(2,1)S(1)} %collective-permute-done.14.refs_1_), channel_id=1, source_target_pairs={{0,8},{8,16},{16,24},{24,28},{28,20},{20,12},{12,4},{4,0},{1,9},{9... | collective-permute-start | bytes 786440 | tf_op jit(solution)/shard_map/ppermute | solution.py:555
  49.4 10.9 %collective-permute-start.18 = (bf16[128,1024]{1,0:T(8,128)(2,1)S(1)}, bf16[128,1024]{1,0:T(8,128)(2,1)S(1)}, u32[]{:S(2)}, u32[]{:S(2)}) collective-permute-start(bf16[128,1024]{1,0:T(8,128)(2,1)S(1)} %collective-permute-done.17.refs_2_), channel_id=1, source_target_pairs={{8,0},{16,8},{24,16},{28,24},{20,28},{12,20},{4,12},{0,4},{9,1},{1... | collective-permute-start | bytes 786440 | tf_op jit(solution)/shard_map/ppermute | solution.py:556
  51.5 10.2 %collective-permute-start.11 = (bf16[2,128,512]{2,1,0:T(8,128)(2,1)S(1)}, bf16[2,128,512]{2,1,0:T(8,128)(2,1)S(1)}, u32[]{:S(2)}, u32[]{:S(2)}) collective-permute-start(bf16[2,128,512]{2,1,0:T(8,128)(2,1)S(1)} %shard_map.112.after_ref.refs_0_), channel_id=1, source_target_pairs={{0,1},{1,0},{2,3},{3,2},{4,5},{5,4},{6,7},{7,6},{8,9},{9,8},{10,11... | collective-permute-start | bytes 786440 | tf_op jit(solution)/shard_map/ppermute | solution.py:338
  55.0 9.9 %collective-permute-start.13 = (bf16[2,128,512]{2,1,0:T(8,128)(2,1)S(1)}, bf16[2,128,512]{2,1,0:T(8,128)(2,1)S(1)}, u32[]{:S(2)}, u32[]{:S(2)}) collective-permute-start(bf16[2,128,512]{2,1,0:T(8,128)(2,1)S(1)} %collective-permute-done.12.refs_2_), channel_id=1, source_target_pairs={{0,1},{1,0},{2,3},{3,2},{4,5},{5,4},{6,7},{7,6},{8,9},{9,8},{10,11... | collective-permute-start | bytes 786440 | tf_op jit(solution)/shard_map/ppermute | solution.py:338
  55.1 17.3 %collective-permute-start.21 = (bf16[8,128,128]{2,1,0:T(8,128)(2,1)S(1)}, bf16[8,128,128]{2,1,0:T(8,128)(2,1)S(1)}, u32[]{:S(2)}, u32[]{:S(2)}) collective-permute-start(bf16[8,128,128]{2,1,0:T(8,128)(2,1)S(1)} %shard_map.118), channel_id=1, source_target_pairs={{0,4},{4,0},{8,12},{12,8},{16,20},{20,16},{24,28},{28,24},{1,5},{5... | collective-permute-start | bytes 786440 | tf_op jit(solution)/shard_map/ppermute | solution.py:44
  57.8 11.7 %collective-permute-start.16 = (bf16[128,1024]{1,0:T(8,128)(2,1)S(1)}, bf16[128,1024]{1,0:T(8,128)(2,1)S(1)}, u32[]{:S(2)}, u32[]{:S(2)}) collective-permute-start(bf16[128,1024]{1,0:T(8,128)(2,1)S(1)} %collective-permute-done.15.refs_3_), channel_id=1, source_target_pairs={{0,8},{8,16},{16,24},{24,28},{28,20},{20,12},{12,4},{4,0},{1,9},{9... | collective-permute-start | bytes 786440 | tf_op jit(solution)/shard_map/ppermute | solution.py:555
  60.3 9.3 %collective-permute-start.19 = (bf16[128,1024]{1,0:T(8,128)(2,1)S(1)}, bf16[128,1024]{1,0:T(8,128)(2,1)S(1)}, u32[]{:S(2)}, u32[]{:S(2)}) collective-permute-start(bf16[128,1024]{1,0:T(8,128)(2,1)S(1)} %collective-permute-done.18.refs_4_), channel_id=1, source_target_pairs={{8,0},{16,8},{24,16},{28,24},{20,28},{12,20},{4,12},{0,4},{9,1},{1... | collective-permute-start | bytes 786440 | tf_op jit(solution)/shard_map/ppermute | solution.py:556
  61.8 12.4 %collective-permute-start.10 = (bf16[1,128,1024]{2,1,0:T(8,128)(2,1)S(1)}, bf16[1,128,1024]{2,1,0:T(8,128)(2,1)S(1)}, u32[]{:S(2)}, u32[]{:S(2)}) collective-permute-start(bf16[1,128,1024]{2,1,0:T(8,128)(2,1)S(1)} %slice.34), channel_id=1, source_target_pairs={{0,2},{1,3},{2,0},{3,1},{4,6},{5,7},{6,4},{7,5},{8,10},{9,11},{10,... | collective-permute-start | bytes 786440 | tf_op jit(solution)/shard_map/ppermute | solution.py:338
  69.5 5.4 %collective-permute-start.22 = (bf16[64,1024]{1,0:T(8,128)(2,1)S(1)}, bf16[64,1024]{1,0:T(8,128)(2,1)S(1)}, u32[]{:S(2)}, u32[]{:S(2)}) collective-permute-start(bf16[64,1024]{1,0:T(8,128)(2,1)S(1)} %slice.26), channel_id=1, source_target_pairs={{0,8},{8,16},{16,24},{24,28},{28,20},{20,12},{12,4},{4,0},{1,9},{9... | collective-permute-start | bytes 393224 | tf_op jit(solution)/shard_map/ppermute | solution.py:565
  69.6 5.3 %collective-permute-start.23 = (bf16[64,1024]{1,0:T(8,128)(2,1)S(1)}, bf16[64,1024]{1,0:T(8,128)(2,1)S(1)}, u32[]{:S(2)}, u32[]{:S(2)}) collective-permute-start(bf16[64,1024]{1,0:T(8,128)(2,1)S(1)} %slice.27), channel_id=1, source_target_pairs={{8,0},{16,8},{24,16},{28,24},{20,28},{12,20},{4,12},{0,4},{9,1},{1... | collective-permute-start | bytes 393224 | tf_op jit(solution)/shard_map/ppermute | solution.py:566

commit v11 on v10

--- a/solution.py
+++ b/solution.py
@@ -274,7 +274,8 @@
     return jnp.where(at < devices // 2, 2 * at, 2 * (devices - 1 - at) + 1)
 
 
-def proj_kernel(offsets, devices, first, cols_ref, *refs):
+def proj_kernel(offsets, devices, first, cols_ref, after_ref, *refs):
+    del after_ref
     total = None if first else refs[len(offsets)][...]
     for i, (offset, low, high) in enumerate(offsets):
         owner = ring_owner(lax.axis_index("seq"), offset, devices)
@@ -531,6 +532,15 @@
             send, kept = kept[1::2].astype(BF), kept[0::2]
     mixed = kept[0].astype(BF)
 
+    key_grad, value_grad = pl.pallas_call(
+        functools.partial(later_grad_kernel, top),
+        out_shape=(like((rows, heads_dev, head_dim), F32),) * 2,
+        in_specs=[VMEM] * 4 + [ANY] + [VMEM] * seq_bits,
+        out_specs=(VMEM,) * 2,
+        compiler_params=PARAMS,
+        cost_estimate=cost(2 * flops_head, 11 * moved_head),
+    )(kh, vh, key_local, value_local, attended, *landed)
+
     ring = list(range(0, devices, 2)) + list(range(devices - 1, 0, -2))
     forward = [(ring[i], ring[(i + 1) % devices]) for i in range(devices)]
     backward = [(b, a) for a, b in forward]
@@ -540,13 +550,13 @@
         return pl.pallas_call(
             functools.partial(proj_kernel, offsets, devices, total is None),
             out_shape=pltpu.VMEM((width, columns_dev), F32),
-            in_specs=[VMEM] * (1 + len(operands)),
+            in_specs=[VMEM, ANY] + [VMEM] * len(operands),
             out_specs=VMEM,
             compiler_params=PARAMS,
             cost_estimate=cost(
                 2 * len(blocks) * rows * width * columns_dev, 4 * width * columns_dev
             ),
-        )(grad_columns, *operands)
+        )(grad_columns, hbm(key_grad), *operands)
 
     blocks, offsets = [attended], [(0, 0, rows)]
     ahead = behind = attended
@@ -565,14 +575,6 @@
         lax.ppermute(ahead[:half], "seq", forward),
         lax.ppermute(behind[half:], "seq", backward),
     ]
-    key_grad, value_grad = pl.pallas_call(
-        functools.partial(later_grad_kernel, top),
-        out_shape=(like((rows, heads_dev, head_dim), F32),) * 2,
-        in_specs=[VMEM] * 4 + [ANY] + [VMEM] * seq_bits,
-        out_specs=(VMEM,) * 2,
-        compiler_params=PARAMS,
-        cost_estimate=cost(2 * flops_head, 11 * moved_head),
-    )(kh, vh, key_local, value_local, total, *landed)
     proj_grad = pl.pallas_call(
         functools.partial(last_kernel, steps, devices),
         out_shape=like((width, columns_dev), F32),

time: 76.7 us -> 76.5 us (level)
    ppermute x3, waiting for transfers between devices: 8.91 us -> 7.15 us  [body(): ahead = lax.ppermute(ahead, 'seq', forward)]
    ppermute x1, waiting for transfers between devices: 0.01 us -> 1.53 us  [body(): lax.ppermute(ahead[:half], 'seq', forward)]
  transfers between devices with their start and end apart: 24 -> 24, of which waited for: 8 -> 10; matrix products, arithmetic and copies ran while one was open for 1% -> 1% of each run, Pallas kernels for 19% -> 19%
where the time goes in v11:
time: 76.5 us; the launch traced here: 76.4 us
  starting transfers between devices  31 us (41%)
  waiting for transfers between devices  24 us (31%)
  Pallas kernels  19.5 us (25%)
  other arithmetic  0.95 us (1%)
  between operations  0.87 us (1%)
    ppermute x5, waiting for transfers between devices, across(): return lax.ppermute(block, axis, route)  11.3 us
    ppermute x5, starting transfers between devices, across(): return lax.ppermute(block, axis, route)  8.19 us
    ppermute x3, waiting for transfers between devices, body(): ahead = lax.ppermute(ahead, 'seq', forward)  7.15 us
    ppermute x8, starting transfers between devices, to_group(): return lax.ppermute(block, 'head', [(at, at ^ i) for at in range(heads)])  6.7 us
    ppermute x3, starting transfers between devices, body(): behind = lax.ppermute(behind, 'seq', backward)  4.58 us
    ppermute x1, starting transfers between devices, body(): lax.ppermute(grad_blocks[far][half:], axes, turn_route(far))  3.92 us
    pallas_call x1, Pallas kernels, body(): pl.pallas_call(local_kernel, out_shape=(pltpu.VMEM((heads_dev, rows, rows...  3.66 us
    ppermute x3, starting transfers between devices, body(): ahead = lax.ppermute(ahead, 'seq', forward)  3.25 us
  transfers between devices with their start and end apart: 24, of which 10 were waited for; matrix products, arithmetic and copies ran while one was open for 1% of the time, Pallas kernels for 19%

profile of v11, /device:TPU:0, one launch (start us, length us, event | category | flops | bytes accessed | tf_op | source)
XLA Modules:
  0.0 76.4 jit_solution(13692508835035457680)
XLA Ops:
  0.6 2.5 %shard_map.101 = (bf16[8,128,128]{2,1,0:T(8,128)(2,1)S(1)}, bf16[8,128,128]{2,1,0:T(8,128)(2,1)S(1)}, bf16[8,128,128]{2,1,0:T(8,128)(2,1)S(1)}, bf16[128,1024]{1,0:T(8,128)(2,1)S(1)}, bf16[64,1024]{1,0:T(8,128)(2,1)S(1)}) custom-call(f32[128,8,128]{2,1,0:T(8,128)} %k_hbm.1, f32[128,8,128]{2,1,0:T(8,128)} %v_hbm.1, bf16[128,1024]{1,0:T(8,128)(2,1)} %grad_hbm.1), custom_call_target="tpu_custom_call" | custom-call | flops 33554432 | bytes 1835008 | tf_op jit(solution)/shard_map/pallas_call | solution.py:324
  3.1 3.0 %collective-permute-start.3 = (bf16[128,1024]{1,0:T(8,128)(2,1)S(1)}, bf16[128,1024]{1,0:T(8,128)(2,1)S(1)}, u32[]{:S(2)}, u32[]{:S(2)}) collective-permute-start(bf16[128,1024]{1,0:T(8,128)(2,1)S(1)} %get-tuple-element.32.refs_0_), channel_id=1, source_target_pairs={{0,2},{1,3},{2,0},{3,1},{4,6},{5,7},{6,4},{7,5},{8,10},{9,11},{10,... | collective-permute-start | bytes 786440 | tf_op jit(solution)/shard_map/ppermute | solution.py:339
  6.1 1.5 %collective-permute-start = (bf16[8,128,128]{2,1,0:T(8,128)(2,1)S(1)}, bf16[8,128,128]{2,1,0:T(8,128)(2,1)S(1)}, u32[]{:S(2)}, u32[]{:S(2)}) collective-permute-start(bf16[8,128,128]{2,1,0:T(8,128)(2,1)S(1)} %get-tuple-element.31.running_ref), channel_id=1, source_target_pairs={{0,4},{4,0},{8,12},{12,8},{16,20},{20,16},{24,28},{28,24},{1,5},{5... | collective-permute-start | bytes 786440 | tf_op jit(solution)/shard_map/ppermute | solution.py:44
  7.6 0.0 collective-permute-start.2
  7.6 3.7 %shard_map.102 = (bf16[8,128,128]{2,1,0:T(8,128)(2,1)S(1)}, f32[8,128,128]{2,1,0:T(8,128)S(1)}, bf16[8,128,128]{2,1,0:T(8,128)(2,1)S(1)}, bf16[3,8,128,128]{3,2,...) custom-call(f32[128,8,128]{2,1,0:T(8,128)} %q_hbm.1, ...), custom_call_target="tpu_custom_call" | custom-call | flops 67108864 | bytes 3145728 | tf_op jit(solution)/shard_map/pallas_call | solution.py:348
  11.3 1.1 %collective-permute-done.3.block_ref.refs_2_ = bf16[128,1024]{1,0:T(8,128)(2,1)S(1)} collective-permute-done((bf16[128,1024]{1,0:T(8,128)(2,1)S(1)}, bf16[128,1024]{1,0:T(8,128)(2,1)S(1)}, u32[]{:S(2)}, u32[]{:S(2)}) %collective-permute-start.3) | collective-permute-done | bytes 262176 | tf_op jit(solution)/shard_map/ppermute | solution.py:339
  12.4 0.1 collective-permute-start.4
  12.5 1.4 %collective-permute-done.arrived_ref.refs_0_ = bf16[8,128,128]{2,1,0:T(8,128)(2,1)S(1)} collective-permute-done((bf16[8,128,128]{2,1,0:T(8,128)(2,1)S(1)}, bf16[8,128,128]{2,1,0:T(8,128)(2,1)S(1)}, u32[]{:S(2)}, u32[]{:S(2)}) %collective-permute-start) | collective-permute-done | bytes 262176 | tf_op jit(solution)/shard_map/ppermute | solution.py:44
  13.9 0.1 shard_map.103.refs_6_.running_ref
  13.9 1.6 %collective-permute-start.1 = (bf16[8,128,128]{2,1,0:T(8,128)(2,1)S(1)}, bf16[8,128,128]{2,1,0:T(8,128)(2,1)S(1)}, u32[]{:S(2)}, u32[]{:S(2)}) collective-permute-start(bf16[8,128,128]{2,1,0:T(8,128)(2,1)S(1)} %shard_map.103.refs_6_.running_ref), channel_id=1, source_target_pairs={{0,8},{8,0},{4,12},{12,4},{16,24},{24,16},{20,28},{28,20},{1,9},{9... | collective-permute-start | bytes 786440 | tf_op jit(solution)/shard_map/ppermute | solution.py:44
  15.6 0.7 collective-permute-start.6
  16.3 3.9 %collective-permute-start.7 = (bf16[64,1024]{1,0:T(8,128)(2,1)S(1)}, bf16[64,1024]{1,0:T(8,128)(2,1)S(1)}, u32[]{:S(2)}, u32[]{:S(2)}) collective-permute-start(bf16[64,1024]{1,0:T(8,128)(2,1)S(1)} %slice.23), channel_id=1, source_target_pairs={{2,0},{3,10},{0,18},{1,24},{6,4},{7,14},{4,22},{5,28},{10,2},{11,8... | collective-permute-start | bytes 393224 | tf_op jit(solution)/shard_map/ppermute | solution.py:401
  20.2 0.0 collective-permute-done.2.refs_1_
  20.2 0.0 collective-permute-done.4.refs_3_
  20.2 2.8 %shard_map.105 = (bf16[1024,128]{1,0:T(8,128)(2,1)S(1)}, bf16[8,128,128]{2,1,0:T(8,128)(2,1)S(1)}, bf16[8,128,128]{2,1,0:T(8,128)(2,1)S(1)}, bf16[8,128,128]{2,1,0:T(8,128)(2,1)S(1)}) custom-call(bf16[128,1024]{1,0:T(8,128)(2,1)S(1)} %get-tuple-element.32.refs_0_, bf16[128,1024]{1,0:T(8,128)(2,1)S(1)} %collective-permute-done.2.refs_1_, ...), custom_call_target="tpu_custom_call" | custom-call | flops 1073741824 | bytes 8388608 | tf_op jit(solution)/shard_map/pallas_call | solution.py:418
  23.0 0.0 collective-permute-done.1.arrived_ref.refs_1_
  23.0 0.1 shard_map.106.after_ref
  23.1 3.4 %collective-permute-start.5 = (bf16[8,128,128]{2,1,0:T(8,128)(2,1)S(1)}, bf16[8,128,128]{2,1,0:T(8,128)(2,1)S(1)}, u32[]{:S(2)}, u32[]{:S(2)}) collective-permute-start(bf16[8,128,128]{2,1,0:T(8,128)(2,1)S(1)} %shard_map.106.after_ref), channel_id=1, source_target_pairs={{0,16},{16,0},{4,20},{20,4},{8,24},{24,8},{12,28},{28,12},{1,17},{... | collective-permute-start | bytes 786440 | tf_op jit(solution)/shard_map/ppermute | solution.py:44
  26.5 0.0 collective-permute-done.6.low_ref
  26.5 0.0 collective-permute-done.7.high_ref
  26.5 1.6 %collective-permute-start.8 = (bf16[128,512]{1,0:T(8,128)(2,1)S(1)}, bf16[128,512]{1,0:T(8,128)(2,1)S(1)}, u32[]{:S(2)}, u32[]{:S(2)}) collective-permute-start(bf16[128,512]{1,0:T(8,128)(2,1)S(1)} %get-tuple-element.41.refs_4_), channel_id=1, source_target_pairs={{0,4},{4,0},{8,12},{12,8},{16,20},{20,16},{24,28},{28,24},{1,5},{5... | collective-permute-start | bytes 393224 | tf_op jit(solution)/shard_map/ppermute | solution.py:452
  28.1 1.3 %shard_map.107 = (f32[8,128,128]{2,1,0:T(8,128)S(1)}, f32[8,128,128]{2,1,0:T(8,128)S(1)}, f32[8,128,128]{2,1,0:T(8,128)S(1)}) custom-call(bf16[1024,128]{1,0:T(8,128)(2,1)S(1)} %get-tuple-element.35.gt_ref, bf16[8,128,128]{2,1,0:T(8,128)(2,1)S(1)} %get-tuple-element.36.qh_ref, bf16[8,128,128]{2,1,0:T(8,128)(2,1)S(1)} %get-tuple-element.27.kh_ref, ...), custom_call_target="tpu_custom_call" | custom-call | flops 201326592 | bytes 3670016 | tf_op jit(solution)/shard_map/pallas_call | solution.py:474
  29.4 2.8 %collective-permute-done.8.refs_1_ = bf16[128,512]{1,0:T(8,128)(2,1)S(1)} collective-permute-done((bf16[128,512]{1,0:T(8,128)(2,1)S(1)}, bf16[128,512]{1,0:T(8,128)(2,1)S(1)}, u32[]{:S(2)}, u32[]{:S(2)}) %collective-permute-start.8) | collective-permute-done | bytes 131104 | tf_op jit(solution)/shard_map/ppermute | solution.py:452
  32.3 6.6 %collective-permute-done.5.refs_2_.refs_0_.state_ref = bf16[8,128,128]{2,1,0:T(8,128)(2,1)S(1)} collective-permute-done((bf16[8,128,128]{2,1,0:T(8,128)(2,1)S(1)}, bf16[8,128,128]{2,1,0:T(8,128)(2,1)S(1)}, u32[]{:S(2)}, u32[]{:S(2)}) %collective-permute-start.5) | collective-permute-done | bytes 262176 | tf_op jit(solution)/shard_map/ppermute | solution.py:44
  38.9 0.4 shard_map.109.after_ref.att_ref.refs_0_
  39.2 0.7 shard_map.113
  40.0 0.1 collective-permute-start.9
  40.0 0.1 collective-permute-start.16
  40.2 1.9 %collective-permute-start.20 = (bf16[128,1024]{1,0:T(8,128)(2,1)S(1)}, bf16[128,1024]{1,0:T(8,128)(2,1)S(1)}, u32[]{:S(2)}, u32[]{:S(2)}) collective-permute-start(bf16[128,1024]{1,0:T(8,128)(2,1)S(1)} %shard_map.109.after_ref.att_ref.refs_0_), channel_id=1, source_target_pairs={{8,0},{16,8},{24,16},{28,24},{20,28},{12,20},{4,12},{0,4},{9,1},{1... | collective-permute-start | bytes 786440 | tf_op jit(solution)/shard_map/ppermute | solution.py:566
  42.1 1.7 %collective-permute-start.14 = (bf16[2,128,512]{2,1,0:T(8,128)(2,1)S(1)}, bf16[2,128,512]{2,1,0:T(8,128)(2,1)S(1)}, u32[]{:S(2)}, u32[]{:S(2)}) collective-permute-start(bf16[2,128,512]{2,1,0:T(8,128)(2,1)S(1)} %shard_map.112.after_ref.refs_0_), channel_id=1, source_target_pairs={{0,2},{1,3},{2,0},{3,1},{4,6},{5,7},{6,4},{7,5},{8,10},{9,11},{10,... | collective-permute-start | bytes 786440 | tf_op jit(solution)/shard_map/ppermute | solution.py:339
  43.8 0.1 shard_map.110.after_ref
  43.9 0.2 collective-permute-start.11
  44.1 4.7 %collective-permute-done.16.refs_1_ = bf16[128,1024]{1,0:T(8,128)(2,1)S(1)} collective-permute-done((bf16[128,1024]{1,0:T(8,128)(2,1)S(1)}, bf16[128,1024]{1,0:T(8,128)(2,1)S(1)}, u32[]{:S(2)}, u32[]{:S(2)}) %collective-permute-start.16) | collective-permute-done | bytes 262176 | tf_op jit(solution)/shard_map/ppermute | solution.py:565
  48.7 0.6 collective-permute-start.17
  49.4 0.0 collective-permute-done.20.refs_2_
  49.4 1.4 %collective-permute-start.21 = (bf16[128,1024]{1,0:T(8,128)(2,1)S(1)}, bf16[128,1024]{1,0:T(8,128)(2,1)S(1)}, u32[]{:S(2)}, u32[]{:S(2)}) collective-permute-start(bf16[128,1024]{1,0:T(8,128)(2,1)S(1)} %collective-permute-done.20.refs_2_), channel_id=1, source_target_pairs={{8,0},{16,8},{24,16},{28,24},{20,28},{12,20},{4,12},{0,4},{9,1},{1... | collective-permute-start | bytes 786440 | tf_op jit(solution)/shard_map/ppermute | solution.py:566
  50.8 0.7 shard_map.111
  51.5 0.0 collective-permute-done.14.refs_2_
  51.5 0.1 collective-permute-start.13
  51.6 3.3 %collective-permute-done.11.refs_1_ = bf16[8,128,128]{2,1,0:T(8,128)(2,1)S(1)} collective-permute-done((bf16[8,128,128]{2,1,0:T(8,128)(2,1)S(1)}, bf16[8,128,128]{2,1,0:T(8,128)(2,1)S(1)}, u32[]{:S(2)}, u32[]{:S(2)}) %collective-permute-start.11) | collective-permute-done | bytes 262176 | tf_op jit(solution)/shard_map/ppermute | solution.py:44
  54.9 0.0 collective-permute-start.15
  54.9 0.1 shard_map.115
  55.1 0.0 collective-permute-done.9
  55.1 1.5 %collective-permute-start.12 = (bf16[8,128,128]{2,1,0:T(8,128)(2,1)S(1)}, bf16[8,128,128]{2,1,0:T(8,128)(2,1)S(1)}, u32[]{:S(2)}, u32[]{:S(2)}) collective-permute-start(bf16[8,128,128]{2,1,0:T(8,128)(2,1)S(1)} %shard_map.115), channel_id=1, source_target_pairs={{0,4},{4,0},{8,12},{12,8},{16,20},{20,16},{24,28},{28,24},{1,5},{5... | collective-permute-start | bytes 786440 | tf_op jit(solution)/shard_map/ppermute | solution.py:44
  56.5 1.2 %collective-permute-done.17.refs_3_ = bf16[128,1024]{1,0:T(8,128)(2,1)S(1)} collective-permute-done((bf16[128,1024]{1,0:T(8,128)(2,1)S(1)}, bf16[128,1024]{1,0:T(8,128)(2,1)S(1)}, u32[]{:S(2)}, u32[]{:S(2)}) %collective-permute-start.17) | collective-permute-done | bytes 262176 | tf_op jit(solution)/shard_map/ppermute | solution.py:565
  57.8 2.5 %collective-permute-start.18 = (bf16[128,1024]{1,0:T(8,128)(2,1)S(1)}, bf16[128,1024]{1,0:T(8,128)(2,1)S(1)}, u32[]{:S(2)}, u32[]{:S(2)}) collective-permute-start(bf16[128,1024]{1,0:T(8,128)(2,1)S(1)} %collective-permute-done.17.refs_3_), channel_id=1, source_target_pairs={{0,8},{8,16},{16,24},{24,28},{28,20},{20,12},{12,4},{4,0},{1,9},{9... | collective-permute-start | bytes 786440 | tf_op jit(solution)/shard_map/ppermute | solution.py:565
  60.3 1.2 %collective-permute-start.22 = (bf16[128,1024]{1,0:T(8,128)(2,1)S(1)}, bf16[128,1024]{1,0:T(8,128)(2,1)S(1)}, u32[]{:S(2)}, u32[]{:S(2)}) collective-permute-start(bf16[128,1024]{1,0:T(8,128)(2,1)S(1)} %collective-permute-done.21.refs_4_), channel_id=1, source_target_pairs={{8,0},{16,8},{24,16},{28,24},{20,28},{12,20},{4,12},{0,4},{9,1},{1... | collective-permute-start | bytes 786440 | tf_op jit(solution)/shard_map/ppermute | solution.py:566
  61.5 0.2 convert_add_fusion
  61.8 0.0 collective-permute-done.13.refs_1_
  61.8 1.8 %collective-permute-start.10 = (bf16[1,128,1024]{2,1,0:T(8,128)(2,1)S(1)}, bf16[1,128,1024]{2,1,0:T(8,128)(2,1)S(1)}, u32[]{:S(2)}, u32[]{:S(2)}) collective-permute-start(bf16[1,128,1024]{2,1,0:T(8,128)(2,1)S(1)} %slice.34), channel_id=1, source_target_pairs={{0,2},{1,3},{2,0},{3,1},{4,6},{5,7},{6,4},{7,5},{8,10},{9,11},{10,... | collective-permute-start | bytes 786440 | tf_op jit(solution)/shard_map/ppermute | solution.py:339
  63.5 1.3 %shard_map.114 = f32[128,8,128]{2,1,0:T(8,128)} custom-call(bf16[1024,128]{1,0:T(8,128)(2,1)S(1)} %get-tuple-element.35.gt_ref, f32[5,8,128]{2,1,0:T(8,128)S(1)} %get-tuple-element.38.lam_ref, f32[8,128,128]{2,1,0:T(8,128)S(1)} %get-tuple-element.44.dql_ref, bf16[8,128,128]{2,1,0:T(8,128)(2,1)S(1)} %collective-permute-done.5.refs_2_.refs_0_.state_ref, ...), custom_call_target="tpu_custom_call" | custom-call | flops 33554432 | bytes 1572864 | tf_op jit(solution)/shard_map/pallas_call | solution.py:506
  64.9 0.0 collective-permute-done.15.refs_3_
  64.9 0.1 shard_map.117.cols_ref
  65.0 0.0 collective-permute-done.12.refs_2_
  65.0 1.7 %shard_map.116 = (f32[128,8,128]{2,1,0:T(8,128)}, f32[128,8,128]{2,1,0:T(8,128)}) custom-call(bf16[8,128,128]{2,1,0:T(8,128)(2,1)S(1)} %get-tuple-element.27.kh_ref, bf16[8,128,128]{2,1,0:T(8,128)(2,1)S(1)} %get-tuple-element.28.vh_ref, f32[8,128,128]{2,1,0:T(8,128)S(1)} %get-tuple-element.39.refs_3_.dkl_ref, f32[8,128,128]{2,1,0:T(8,128)S(1)} %get-tuple-element.45.dvl_ref, ...), custom_call_target="tpu_custom_call" | custom-call | flops 67108864 | bytes 2883584 | tf_op jit(solution)/shard_map/pallas_call | solution.py:535
  66.7 1.5 %shard_map.118.refs_2_ = f32[1024,512]{1,0:T(8,128)S(1)} custom-call(bf16[8,128,512]{2,1,0:T(8,128)(2,1)S(1)} %shard_map.117.cols_ref, f32[128,8,128]{2,1,0:T(8,128)} %get-tuple-element.24.after_ref, bf16[128,1024]{1,0:T(8,128)(2,1)S(1)} %shard_map.109.after_ref.att_ref.refs_0_, bf16[128,1024]{1,0:T(8,128)(2,1)S(1)} %collective-permute-done.16.refs_1_, ...), custom_call_target="tpu_custom_call" | custom-call | flops 671088640 | bytes 2097152 | tf_op jit(solution)/shard_map/pallas_call | solution.py:550
  68.2 1.2 %collective-permute-done.18.refs_0_ = bf16[128,1024]{1,0:T(8,128)(2,1)S(1)} collective-permute-done((bf16[128,1024]{1,0:T(8,128)(2,1)S(1)}, bf16[128,1024]{1,0:T(8,128)(2,1)S(1)}, u32[]{:S(2)}, u32[]{:S(2)}) %collective-permute-start.18) | collective-permute-done | bytes 262176 | tf_op jit(solution)/shard_map/ppermute | solution.py:565
  69.5 0.1 collective-permute-start.19
  69.6 2.1 %collective-permute-start.23 = (bf16[64,1024]{1,0:T(8,128)(2,1)S(1)}, bf16[64,1024]{1,0:T(8,128)(2,1)S(1)}, u32[]{:S(2)}, u32[]{:S(2)}) collective-permute-start(bf16[64,1024]{1,0:T(8,128)(2,1)S(1)} %slice.27), channel_id=1, source_target_pairs={{8,0},{16,8},{24,16},{28,24},{20,28},{12,20},{4,12},{0,4},{9,1},{1... | collective-permute-start | bytes 393224 | tf_op jit(solution)/shard_map/ppermute | solution.py:576
  71.6 0.8 fusion.1
  72.4 0.7 shard_map.119.total_ref
  73.1 1.5 %collective-permute-done.19.low_ref = bf16[64,1024]{1,0:T(8,128)(2,1)S(1)} collective-permute-done((bf16[64,1024]{1,0:T(8,128)(2,1)S(1)}, bf16[64,1024]{1,0:T(8,128)(2,1)S(1)}, u32[]{:S(2)}, u32[]{:S(2)}) %collective-permute-start.19) | collective-permute-done | bytes 131104 | tf_op jit(solution)/shard_map/ppermute | solution.py:575
  74.7 0.1 collective-permute-done.23.high_ref
  74.8 1.6 %shard_map.120 = f32[1024,512]{1,0:T(8,128)} custom-call(bf16[8,128,512]{2,1,0:T(8,128)(2,1)S(1)} %shard_map.117.cols_ref, bf16[64,1024]{1,0:T(8,128)(2,1)S(1)} %collective-permute-done.19.low_ref, bf16[64,1024]{1,0:T(8,128)(2,1)S(1)} %collective-permute-done.23.high_ref, f32[1024,512]{1,0:T(8,128)S(1)} %shard_map.119.total_ref, ...), custom_call_target="tpu_custom_call" | custom-call | flops 134217728 | bytes 4194304 | tf_op jit(solution)/shard_map/pallas_call | solution.py:578
  (10 shorter events, 0.1 us)
Async XLA Ops:
  3.1 9.3 %collective-permute-start.3 = (bf16[128,1024]{1,0:T(8,128)(2,1)S(1)}, bf16[128,1024]{1,0:T(8,128)(2,1)S(1)}, u32[]{:S(2)}, u32[]{:S(2)}) collective-permute-start(bf16[128,1024]{1,0:T(8,128)(2,1)S(1)} %get-tuple-element.32.refs_0_), channel_id=1, source_target_pairs={{0,2},{1,3},{2,0},{3,1},{4,6},{5,7},{6,4},{7,5},{8,10},{9,11},{10,... | collective-permute-start | bytes 786440 | tf_op jit(solution)/shard_map/ppermute | solution.py:339
  6.1 7.8 %collective-permute-start = (bf16[8,128,128]{2,1,0:T(8,128)(2,1)S(1)}, bf16[8,128,128]{2,1,0:T(8,128)(2,1)S(1)}, u32[]{:S(2)}, u32[]{:S(2)}) collective-permute-start(bf16[8,128,128]{2,1,0:T(8,128)(2,1)S(1)} %get-tuple-element.31.running_ref), channel_id=1, source_target_pairs={{0,4},{4,0},{8,12},{12,8},{16,20},{20,16},{24,28},{28,24},{1,5},{5... | collective-permute-start | bytes 786440 | tf_op jit(solution)/shard_map/ppermute | solution.py:44
  7.6 12.6 %collective-permute-start.2 = (bf16[128,1024]{1,0:T(8,128)(2,1)S(1)}, bf16[128,1024]{1,0:T(8,128)(2,1)S(1)}, u32[]{:S(2)}, u32[]{:S(2)}) collective-permute-start(bf16[128,1024]{1,0:T(8,128)(2,1)S(1)} %get-tuple-element.32.refs_0_), channel_id=1, source_target_pairs={{0,1},{1,0},{2,3},{3,2},{4,5},{5,4},{6,7},{7,6},{8,9},{9,8},{10,11... | collective-permute-start | bytes 786440 | tf_op jit(solution)/shard_map/ppermute | solution.py:339
  12.4 7.8 %collective-permute-start.4 = (bf16[128,1024]{1,0:T(8,128)(2,1)S(1)}, bf16[128,1024]{1,0:T(8,128)(2,1)S(1)}, u32[]{:S(2)}, u32[]{:S(2)}) collective-permute-start(bf16[128,1024]{1,0:T(8,128)(2,1)S(1)} %shard_map.104), channel_id=1, source_target_pairs={{0,1},{1,0},{2,3},{3,2},{4,5},{5,4},{6,7},{7,6},{8,9},{9,8},{10,11... | collective-permute-start | bytes 786440 | tf_op jit(solution)/shard_map/ppermute | solution.py:339
  13.9 9.1 %collective-permute-start.1 = (bf16[8,128,128]{2,1,0:T(8,128)(2,1)S(1)}, bf16[8,128,128]{2,1,0:T(8,128)(2,1)S(1)}, u32[]{:S(2)}, u32[]{:S(2)}) collective-permute-start(bf16[8,128,128]{2,1,0:T(8,128)(2,1)S(1)} %shard_map.103.refs_6_.running_ref), channel_id=1, source_target_pairs={{0,8},{8,0},{4,12},{12,4},{16,24},{24,16},{20,28},{28,20},{1,9},{9... | collective-permute-start | bytes 786440 | tf_op jit(solution)/shard_map/ppermute | solution.py:44
  15.6 10.9 %collective-permute-start.6 = (bf16[64,1024]{1,0:T(8,128)(2,1)S(1)}, bf16[64,1024]{1,0:T(8,128)(2,1)S(1)}, u32[]{:S(2)}, u32[]{:S(2)}) collective-permute-start(bf16[64,1024]{1,0:T(8,128)(2,1)S(1)} %get-tuple-element.40), channel_id=1, source_target_pairs={{0,0},{1,10},{2,18},{3,24},{4,4},{5,14},{6,22},{7,28},{8,2},{9,8},... | collective-permute-start | bytes 393224 | tf_op jit(solution)/shard_map/ppermute | solution.py:400
  16.3 10.3 %collective-permute-start.7 = (bf16[64,1024]{1,0:T(8,128)(2,1)S(1)}, bf16[64,1024]{1,0:T(8,128)(2,1)S(1)}, u32[]{:S(2)}, u32[]{:S(2)}) collective-permute-start(bf16[64,1024]{1,0:T(8,128)(2,1)S(1)} %slice.23), channel_id=1, source_target_pairs={{2,0},{3,10},{0,18},{1,24},{6,4},{7,14},{4,22},{5,28},{10,2},{11,8... | collective-permute-start | bytes 393224 | tf_op jit(solution)/shard_map/ppermute | solution.py:401
  23.1 15.7 %collective-permute-start.5 = (bf16[8,128,128]{2,1,0:T(8,128)(2,1)S(1)}, bf16[8,128,128]{2,1,0:T(8,128)(2,1)S(1)}, u32[]{:S(2)}, u32[]{:S(2)}) collective-permute-start(bf16[8,128,128]{2,1,0:T(8,128)(2,1)S(1)} %shard_map.106.after_ref), channel_id=1, source_target_pairs={{0,16},{16,0},{4,20},{20,4},{8,24},{24,8},{12,28},{28,12},{1,17},{... | collective-permute-start | bytes 786440 | tf_op jit(solution)/shard_map/ppermute | solution.py:44
  26.5 5.7 %collective-permute-start.8 = (bf16[128,512]{1,0:T(8,128)(2,1)S(1)}, bf16[128,512]{1,0:T(8,128)(2,1)S(1)}, u32[]{:S(2)}, u32[]{:S(2)}) collective-permute-start(bf16[128,512]{1,0:T(8,128)(2,1)S(1)} %get-tuple-element.41.refs_4_), channel_id=1, source_target_pairs={{0,4},{4,0},{8,12},{12,8},{16,20},{20,16},{24,28},{28,24},{1,5},{5... | collective-permute-start | bytes 393224 | tf_op jit(solution)/shard_map/ppermute | solution.py:452
  40.0 15.1 %collective-permute-start.9 = (bf16[2,128,1024]{2,1,0:T(8,128)(2,1)S(1)}, bf16[2,128,1024]{2,1,0:T(8,128)(2,1)S(1)}, u32[]{:S(2)}, u32[]{:S(2)}) collective-permute-start(bf16[2,128,1024]{2,1,0:T(8,128)(2,1)S(1)} %shard_map.113), channel_id=1, source_target_pairs={{0,1},{1,0},{2,3},{3,2},{4,5},{5,4},{6,7},{7,6},{8,9},{9,8},{10,11... | collective-permute-start | bytes 1572872 | tf_op jit(solution)/shard_map/ppermute | solution.py:339
  40.0 8.7 %collective-permute-start.16 = (bf16[128,1024]{1,0:T(8,128)(2,1)S(1)}, bf16[128,1024]{1,0:T(8,128)(2,1)S(1)}, u32[]{:S(2)}, u32[]{:S(2)}) collective-permute-start(bf16[128,1024]{1,0:T(8,128)(2,1)S(1)} %shard_map.109.after_ref.att_ref.refs_0_), channel_id=1, source_target_pairs={{0,8},{8,16},{16,24},{24,28},{28,20},{20,12},{12,4},{4,0},{1,9},{9... | collective-permute-start | bytes 786440 | tf_op jit(solution)/shard_map/ppermute | solution.py:565
  40.2 9.2 %collective-permute-start.20 = (bf16[128,1024]{1,0:T(8,128)(2,1)S(1)}, bf16[128,1024]{1,0:T(8,128)(2,1)S(1)}, u32[]{:S(2)}, u32[]{:S(2)}) collective-permute-start(bf16[128,1024]{1,0:T(8,128)(2,1)S(1)} %shard_map.109.after_ref.att_ref.refs_0_), channel_id=1, source_target_pairs={{8,0},{16,8},{24,16},{28,24},{20,28},{12,20},{4,12},{0,4},{9,1},{1... | collective-permute-start | bytes 786440 | tf_op jit(solution)/shard_map/ppermute | solution.py:566
  42.1 9.4 %collective-permute-start.14 = (bf16[2,128,512]{2,1,0:T(8,128)(2,1)S(1)}, bf16[2,128,512]{2,1,0:T(8,128)(2,1)S(1)}, u32[]{:S(2)}, u32[]{:S(2)}) collective-permute-start(bf16[2,128,512]{2,1,0:T(8,128)(2,1)S(1)} %shard_map.112.after_ref.refs_0_), channel_id=1, source_target_pairs={{0,2},{1,3},{2,0},{3,1},{4,6},{5,7},{6,4},{7,5},{8,10},{9,11},{10,... | collective-permute-start | bytes 786440 | tf_op jit(solution)/shard_map/ppermute | solution.py:339
  43.9 11.0 %collective-permute-start.11 = (bf16[8,128,128]{2,1,0:T(8,128)(2,1)S(1)}, bf16[8,128,128]{2,1,0:T(8,128)(2,1)S(1)}, u32[]{:S(2)}, u32[]{:S(2)}) collective-permute-start(bf16[8,128,128]{2,1,0:T(8,128)(2,1)S(1)} %shard_map.110.after_ref), channel_id=1, source_target_pairs={{0,8},{8,0},{4,12},{12,4},{16,24},{24,16},{20,28},{28,20},{1,9},{9... | collective-permute-start | bytes 786440 | tf_op jit(solution)/shard_map/ppermute | solution.py:44
  48.7 9.0 %collective-permute-start.17 = (bf16[128,1024]{1,0:T(8,128)(2,1)S(1)}, bf16[128,1024]{1,0:T(8,128)(2,1)S(1)}, u32[]{:S(2)}, u32[]{:S(2)}) collective-permute-start(bf16[128,1024]{1,0:T(8,128)(2,1)S(1)} %collective-permute-done.16.refs_1_), channel_id=1, source_target_pairs={{0,8},{8,16},{16,24},{24,28},{28,20},{20,12},{12,4},{4,0},{1,9},{9... | collective-permute-start | bytes 786440 | tf_op jit(solution)/shard_map/ppermute | solution.py:565
  49.4 10.9 %collective-permute-start.21 = (bf16[128,1024]{1,0:T(8,128)(2,1)S(1)}, bf16[128,1024]{1,0:T(8,128)(2,1)S(1)}, u32[]{:S(2)}, u32[]{:S(2)}) collective-permute-start(bf16[128,1024]{1,0:T(8,128)(2,1)S(1)} %collective-permute-done.20.refs_2_), channel_id=1, source_target_pairs={{8,0},{16,8},{24,16},{28,24},{20,28},{12,20},{4,12},{0,4},{9,1},{1... | collective-permute-start | bytes 786440 | tf_op jit(solution)/shard_map/ppermute | solution.py:566
  51.5 10.2 %collective-permute-start.13 = (bf16[2,128,512]{2,1,0:T(8,128)(2,1)S(1)}, bf16[2,128,512]{2,1,0:T(8,128)(2,1)S(1)}, u32[]{:S(2)}, u32[]{:S(2)}) collective-permute-start(bf16[2,128,512]{2,1,0:T(8,128)(2,1)S(1)} %shard_map.112.after_ref.refs_0_), channel_id=1, source_target_pairs={{0,1},{1,0},{2,3},{3,2},{4,5},{5,4},{6,7},{7,6},{8,9},{9,8},{10,11... | collective-permute-start | bytes 786440 | tf_op jit(solution)/shard_map/ppermute | solution.py:339
  54.9 9.9 %collective-permute-start.15 = (bf16[2,128,512]{2,1,0:T(8,128)(2,1)S(1)}, bf16[2,128,512]{2,1,0:T(8,128)(2,1)S(1)}, u32[]{:S(2)}, u32[]{:S(2)}) collective-permute-start(bf16[2,128,512]{2,1,0:T(8,128)(2,1)S(1)} %collective-permute-done.14.refs_2_), channel_id=1, source_target_pairs={{0,1},{1,0},{2,3},{3,2},{4,5},{5,4},{6,7},{7,6},{8,9},{9,8},{10,11... | collective-permute-start | bytes 786440 | tf_op jit(solution)/shard_map/ppermute | solution.py:339
  55.1 9.9 %collective-permute-start.12 = (bf16[8,128,128]{2,1,0:T(8,128)(2,1)S(1)}, bf16[8,128,128]{2,1,0:T(8,128)(2,1)S(1)}, u32[]{:S(2)}, u32[]{:S(2)}) collective-permute-start(bf16[8,128,128]{2,1,0:T(8,128)(2,1)S(1)} %shard_map.115), channel_id=1, source_target_pairs={{0,4},{4,0},{8,12},{12,8},{16,20},{20,16},{24,28},{28,24},{1,5},{5... | collective-permute-start | bytes 786440 | tf_op jit(solution)/shard_map/ppermute | solution.py:44
  57.8 11.7 %collective-permute-start.18 = (bf16[128,1024]{1,0:T(8,128)(2,1)S(1)}, bf16[128,1024]{1,0:T(8,128)(2,1)S(1)}, u32[]{:S(2)}, u32[]{:S(2)}) collective-permute-start(bf16[128,1024]{1,0:T(8,128)(2,1)S(1)} %collective-permute-done.17.refs_3_), channel_id=1, source_target_pairs={{0,8},{8,16},{16,24},{24,28},{28,20},{20,12},{12,4},{4,0},{1,9},{9... | collective-permute-start | bytes 786440 | tf_op jit(solution)/shard_map/ppermute | solution.py:565
  60.3 9.3 %collective-permute-start.22 = (bf16[128,1024]{1,0:T(8,128)(2,1)S(1)}, bf16[128,1024]{1,0:T(8,128)(2,1)S(1)}, u32[]{:S(2)}, u32[]{:S(2)}) collective-permute-start(bf16[128,1024]{1,0:T(8,128)(2,1)S(1)} %collective-permute-done.21.refs_4_), channel_id=1, source_target_pairs={{8,0},{16,8},{24,16},{28,24},{20,28},{12,20},{4,12},{0,4},{9,1},{1... | collective-permute-start | bytes 786440 | tf_op jit(solution)/shard_map/ppermute | solution.py:566
  61.8 9.9 %collective-permute-start.10 = (bf16[1,128,1024]{2,1,0:T(8,128)(2,1)S(1)}, bf16[1,128,1024]{2,1,0:T(8,128)(2,1)S(1)}, u32[]{:S(2)}, u32[]{:S(2)}) collective-permute-start(bf16[1,128,1024]{2,1,0:T(8,128)(2,1)S(1)} %slice.34), channel_id=1, source_target_pairs={{0,2},{1,3},{2,0},{3,1},{4,6},{5,7},{6,4},{7,5},{8,10},{9,11},{10,... | collective-permute-start | bytes 786440 | tf_op jit(solution)/shard_map/ppermute | solution.py:339
  69.5 5.2 %collective-permute-start.19 = (bf16[64,1024]{1,0:T(8,128)(2,1)S(1)}, bf16[64,1024]{1,0:T(8,128)(2,1)S(1)}, u32[]{:S(2)}, u32[]{:S(2)}) collective-permute-start(bf16[64,1024]{1,0:T(8,128)(2,1)S(1)} %slice.26), channel_id=1, source_target_pairs={{0,8},{8,16},{16,24},{24,28},{28,20},{20,12},{12,4},{4,0},{1,9},{9... | collective-permute-start | bytes 393224 | tf_op jit(solution)/shard_map/ppermute | solution.py:575
  69.6 5.2 %collective-permute-start.23 = (bf16[64,1024]{1,0:T(8,128)(2,1)S(1)}, bf16[64,1024]{1,0:T(8,128)(2,1)S(1)}, u32[]{:S(2)}, u32[]{:S(2)}) collective-permute-start(bf16[64,1024]{1,0:T(8,128)(2,1)S(1)} %slice.27), channel_id=1, source_target_pairs={{8,0},{16,8},{24,16},{28,24},{20,28},{12,20},{4,12},{0,4},{9,1},{1... | collective-permute-start | bytes 393224 | tf_op jit(solution)/shard_map/ppermute | solution.py:576

commit v12 on v11

--- a/solution.py
+++ b/solution.py
@@ -190,6 +190,13 @@
     return (turned << 1 & (1 << bits) - 1) | turned >> bits - 1
 
 
+def feed_kernel(own_ref, far_ref, after_ref, low_ref, high_ref):
+    del after_ref
+    half = low_ref.shape[0]
+    low_ref[...] = own_ref[:half]
+    high_ref[...] = far_ref[half:]
+
+
 def relay_kernel(block_ref, after_ref, out_ref):
     del after_ref
     out_ref[...] = block_ref[...]
@@ -383,23 +390,6 @@
             grad_blocks[i ^ 1 << digit] = to_group(block, 1 << digit)
     grad_blocks = [grad_blocks[i] for i in range(heads)]
 
-    per = devices // heads
-    def turn_route(shift):
-        return [
-            (
-                (high * per + low) * heads + (group_at ^ shift),
-                (group_at * per + low) * heads + turned_group(high, group_at, head_bits),
-            )
-            for high in range(heads)
-            for low in range(per)
-            for group_at in range(heads)
-        ]
-
-    axes, far = ("seq", "head"), heads // 2
-    turned = [
-        lax.ppermute(own_low, axes, turn_route(0)),
-        lax.ppermute(grad_blocks[far][half:], axes, turn_route(far)),
-    ]
     partner_states = []
     running, arrived = own_state, None
     for digit in range(top):
@@ -424,6 +414,31 @@
         cost_estimate=cost(2 * rows * width * out_proj.shape[1], 2 * width * out_proj.shape[1]),
     )(*grad_blocks, w, qw, running)
 
+    per = devices // heads
+    def turn_route(shift):
+        return [
+            (
+                (high * per + low) * heads + (group_at ^ shift),
+                (group_at * per + low) * heads + turned_group(high, group_at, head_bits),
+            )
+            for high in range(heads)
+            for low in range(per)
+            for group_at in range(heads)
+        ]
+
+    axes, far = ("seq", "head"), heads // 2
+    low_rows, high_rows = pl.pallas_call(
+        feed_kernel,
+        out_shape=(like((half, width), BF),) * 2,
+        in_specs=[VMEM, VMEM, ANY],
+        out_specs=(VMEM,) * 2,
+        compiler_params=PARAMS,
+        cost_estimate=cost(0, 2 * moved_head),
+    )(own_grad, grad_blocks[far], gt)
+    turned = [
+        lax.ppermute(low_rows, axes, turn_route(0)),
+        lax.ppermute(high_rows, axes, turn_route(far)),
+    ]
     meeting = pl.pallas_call(
         functools.partial(meet_kernel, top)
         if arrived is not None

time: 76.5 us -> 86.6 us (1.13)
  waiting for transfers between devices: 24 us -> 30.4 us
  starting transfers between devices: 31 us -> 34.1 us
    ppermute x8, starting transfers between devices: 6.7 us -> 12 us  [to_group(): return lax.ppermute(block, 'head', [(at, at ^ i) for at in range(heads)])]
    ppermute x5, waiting for transfers between devices: 11.3 us -> 16.1 us  [across(): return lax.ppermute(block, axis, route)]
    ppermute x2, waiting for transfers between devices: 0.01 us -> 3.5 us  [the longest x1 3.49 us: body(): lax.ppermute(high_rows, axes, turn_route(far))]
    ppermute x3, waiting for transfers between devices: 0.01 us -> 2.93 us  [body(): behind = lax.ppermute(behind, 'seq', backward)]
    ppermute x3, starting transfers between devices: 4.58 us -> 1.69 us  [body(): behind = lax.ppermute(behind, 'seq', backward)]
    ppermute x1, waiting for transfers between devices: 2.8 us -> 0.01 us  [body(): lax.ppermute(chunks[r], 'seq', [(at, at ^ r) for at in range(devices)])]
    ppermute x3, waiting for transfers between devices: 7.15 us -> 5.13 us  [body(): ahead = lax.ppermute(ahead, 'seq', forward)]
    ppermute x3, starting transfers between devices: 3.25 us -> 4.97 us  [body(): ahead = lax.ppermute(ahead, 'seq', forward)]
  transfers between devices with their start and end apart: 24 -> 24, of which waited for: 10 -> 13; matrix products, arithmetic and copies ran while one was open for 1% -> 1% of each run, Pallas kernels for 19% -> 17%
where the time goes in v12:
time: 86.6 us; the launch traced here: 86.5 us
  starting transfers between devices  34.1 us (39%)
  waiting for transfers between devices  30.4 us (35%)
  Pallas kernels  20.1 us (23%)
  other arithmetic  0.95 us (1%)
    ppermute x5, waiting for transfers between devices, across(): return lax.ppermute(block, axis, route)  16.1 us
    ppermute x8, starting transfers between devices, to_group(): return lax.ppermute(block, 'head', [(at, at ^ i) for at in range(heads)])  12 us
    ppermute x5, starting transfers between devices, across(): return lax.ppermute(block, axis, route)  8.48 us
    ppermute x3, waiting for transfers between devices, body(): ahead = lax.ppermute(ahead, 'seq', forward)  5.13 us
    ppermute x3, starting transfers between devices, body(): ahead = lax.ppermute(ahead, 'seq', forward)  4.97 us
    pallas_call x1, Pallas kernels, body(): pl.pallas_call(local_kernel, out_shape=(pltpu.VMEM((heads_dev, rows, rows...  3.66 us
    ppermute x1, waiting for transfers between devices, body(): lax.ppermute(high_rows, axes, turn_route(far))  3.49 us
    pallas_call x1, Pallas kernels, body(): pl.pallas_call(state_kernel, out_shape=(head_state, per_head, per_head, l...  3.11 us
  transfers between devices with their start and end apart: 24, of which 13 were waited for; matrix products, arithmetic and copies ran while one was open for 1% of the time, Pallas kernels for 17%

profile of v12, /device:TPU:0, one launch (start us, length us, event | category | flops | bytes accessed | tf_op | source)
XLA Modules:
  0.0 86.5 jit_solution(17290029557864326653)
XLA Ops:
  0.6 3.1 %shard_map.101 = (bf16[8,128,128]{2,1,0:T(8,128)(2,1)S(1)}, bf16[8,128,128]{2,1,0:T(8,128)(2,1)S(1)}, bf16[8,128,128]{2,1,0:T(8,128)(2,1)S(1)}, bf16[128,1024]{1,0:T(8,128)(2,1)S(1)}, bf16[64,1024]{1,0:T(8,128)(2,1)}) custom-call(f32[128,8,128]{2,1,0:T(8,128)} %k_hbm.1, f32[128,8,128]{2,1,0:T(8,128)} %v_hbm.1, bf16[128,1024]{1,0:T(8,128)(2,1)} %grad_hbm.1), custom_call_target="tpu_custom_call" | custom-call | flops 33554432 | bytes 1835008 | tf_op jit(solution)/shard_map/pallas_call | solution.py:331
  3.8 3.0 %collective-permute-start.3 = (bf16[128,1024]{1,0:T(8,128)(2,1)S(1)}, bf16[128,1024]{1,0:T(8,128)(2,1)S(1)}, u32[]{:S(2)}, u32[]{:S(2)}) collective-permute-start(bf16[128,1024]{1,0:T(8,128)(2,1)S(1)} %get-tuple-element.33.refs_0_.own_ref), channel_id=1, source_target_pairs={{0,2},{1,3},{2,0},{3,1},{4,6},{5,7},{6,4},{7,5},{8,10},{9,11},{10,... | collective-permute-start | bytes 786440 | tf_op jit(solution)/shard_map/ppermute | solution.py:346
  6.8 1.5 %collective-permute-start = (bf16[8,128,128]{2,1,0:T(8,128)(2,1)S(1)}, bf16[8,128,128]{2,1,0:T(8,128)(2,1)S(1)}, u32[]{:S(2)}, u32[]{:S(2)}) collective-permute-start(bf16[8,128,128]{2,1,0:T(8,128)(2,1)S(1)} %get-tuple-element.32.running_ref), channel_id=1, source_target_pairs={{0,4},{4,0},{8,12},{12,8},{16,20},{20,16},{24,28},{28,24},{1,5},{5... | collective-permute-start | bytes 786440 | tf_op jit(solution)/shard_map/ppermute | solution.py:44
  8.3 0.0 collective-permute-start.2
  8.3 3.7 %shard_map.102 = (bf16[8,128,128]{2,1,0:T(8,128)(2,1)S(1)}, f32[8,128,128]{2,1,0:T(8,128)S(1)}, bf16[8,128,128]{2,1,0:T(8,128)(2,1)S(1)}, bf16[3,8,128,128]{3,2,...) custom-call(f32[128,8,128]{2,1,0:T(8,128)} %q_hbm.1, ...), custom_call_target="tpu_custom_call" | custom-call | flops 67108864 | bytes 3145728 | tf_op jit(solution)/shard_map/pallas_call | solution.py:355
  12.0 1.1 %collective-permute-done.3.block_ref.refs_2_.far_ref = bf16[128,1024]{1,0:T(8,128)(2,1)S(1)} collective-permute-done((bf16[128,1024]{1,0:T(8,128)(2,1)S(1)}, bf16[128,1024]{1,0:T(8,128)(2,1)S(1)}, u32[]{:S(2)}, u32[]{:S(2)}) %collective-permute-start.3) | collective-permute-done | bytes 262176 | tf_op jit(solution)/shard_map/ppermute | solution.py:346
  13.1 0.1 collective-permute-start.4
  13.2 1.4 %collective-permute-done.arrived_ref.refs_0_ = bf16[8,128,128]{2,1,0:T(8,128)(2,1)S(1)} collective-permute-done((bf16[8,128,128]{2,1,0:T(8,128)(2,1)S(1)}, bf16[8,128,128]{2,1,0:T(8,128)(2,1)S(1)}, u32[]{:S(2)}, u32[]{:S(2)}) %collective-permute-start) | collective-permute-done | bytes 262176 | tf_op jit(solution)/shard_map/ppermute | solution.py:44
  14.5 0.1 shard_map.103.refs_6_.running_ref
  14.6 1.6 %collective-permute-start.1 = (bf16[8,128,128]{2,1,0:T(8,128)(2,1)S(1)}, bf16[8,128,128]{2,1,0:T(8,128)(2,1)S(1)}, u32[]{:S(2)}, u32[]{:S(2)}) collective-permute-start(bf16[8,128,128]{2,1,0:T(8,128)(2,1)S(1)} %shard_map.103.refs_6_.running_ref), channel_id=1, source_target_pairs={{0,8},{8,0},{4,12},{12,4},{16,24},{24,16},{20,28},{28,20},{1,9},{9... | collective-permute-start | bytes 786440 | tf_op jit(solution)/shard_map/ppermute | solution.py:44
  16.2 0.0 collective-permute-done.2.refs_1_
  16.2 0.0 collective-permute-done.4.refs_3_
  16.2 2.8 %shard_map.105 = (bf16[1024,128]{1,0:T(8,128)(2,1)S(1)}, bf16[8,128,128]{2,1,0:T(8,128)(2,1)S(1)}, bf16[8,128,128]{2,1,0:T(8,128)(2,1)S(1)}, bf16[8,128,128]{2,1,0:T(8,128)(2,1)S(1)}) custom-call(bf16[128,1024]{1,0:T(8,128)(2,1)S(1)} %get-tuple-element.33.refs_0_.own_ref, bf16[128,1024]{1,0:T(8,128)(2,1)S(1)} %collective-permute-done.2.refs_1_, ...), custom_call_target="tpu_custom_call" | custom-call | flops 1073741824 | bytes 8388608 | tf_op jit(solution)/shard_map/pallas_call | solution.py:408
  19.1 3.0 %collective-permute-done.1.arrived_ref.refs_1_ = bf16[8,128,128]{2,1,0:T(8,128)(2,1)S(1)} collective-permute-done((bf16[8,128,128]{2,1,0:T(8,128)(2,1)S(1)}, bf16[8,128,128]{2,1,0:T(8,128)(2,1)S(1)}, u32[]{:S(2)}, u32[]{:S(2)}) %collective-permute-start.1) | collective-permute-done | bytes 262176 | tf_op jit(solution)/shard_map/ppermute | solution.py:44
  22.1 0.1 shard_map.106.after_ref
  22.2 2.8 %collective-permute-start.5 = (bf16[8,128,128]{2,1,0:T(8,128)(2,1)S(1)}, bf16[8,128,128]{2,1,0:T(8,128)(2,1)S(1)}, u32[]{:S(2)}, u32[]{:S(2)}) collective-permute-start(bf16[8,128,128]{2,1,0:T(8,128)(2,1)S(1)} %shard_map.106.after_ref), channel_id=1, source_target_pairs={{0,16},{16,0},{4,20},{20,4},{8,24},{24,8},{12,28},{28,12},{1,17},{... | collective-permute-start | bytes 786440 | tf_op jit(solution)/shard_map/ppermute | solution.py:44
  25.0 0.7 collective-permute-start.6
  25.7 2.6 %collective-permute-start.7 = (bf16[64,1024]{1,0:T(8,128)(2,1)S(1)}, bf16[64,1024]{1,0:T(8,128)(2,1)S(1)}, u32[]{:S(2)}, u32[]{:S(2)}) collective-permute-start(bf16[64,1024]{1,0:T(8,128)(2,1)S(1)} %get-tuple-element.42), channel_id=1, source_target_pairs={{2,0},{3,10},{0,18},{1,24},{6,4},{7,14},{4,22},{5,28},{10,2},{11,8... | collective-permute-start | bytes 393224 | tf_op jit(solution)/shard_map/ppermute | solution.py:440
  28.3 0.0 collective-permute-done.6.low_ref
  28.3 3.5 %collective-permute-done.7.high_ref = bf16[64,1024]{1,0:T(8,128)(2,1)S(1)} collective-permute-done((bf16[64,1024]{1,0:T(8,128)(2,1)S(1)}, bf16[64,1024]{1,0:T(8,128)(2,1)S(1)}, u32[]{:S(2)}, u32[]{:S(2)}) %collective-permute-start.7) | collective-permute-done | bytes 131104 | tf_op jit(solution)/shard_map/ppermute | solution.py:440
  31.8 1.6 %collective-permute-start.8 = (bf16[128,512]{1,0:T(8,128)(2,1)S(1)}, bf16[128,512]{1,0:T(8,128)(2,1)S(1)}, u32[]{:S(2)}, u32[]{:S(2)}) collective-permute-start(bf16[128,512]{1,0:T(8,128)(2,1)S(1)} %get-tuple-element.43.refs_4_), channel_id=1, source_target_pairs={{0,4},{4,0},{8,12},{12,8},{16,20},{20,16},{24,28},{28,24},{1,5},{5... | collective-permute-start | bytes 393224 | tf_op jit(solution)/shard_map/ppermute | solution.py:467
  33.4 1.3 %shard_map.107 = (f32[8,128,128]{2,1,0:T(8,128)S(1)}, f32[8,128,128]{2,1,0:T(8,128)S(1)}, f32[8,128,128]{2,1,0:T(8,128)S(1)}) custom-call(bf16[1024,128]{1,0:T(8,128)(2,1)S(1)} %get-tuple-element.36.gt_ref.after_ref, bf16[8,128,128]{2,1,0:T(8,128)(2,1)S(1)} %get-tuple-element.37.qh_ref, bf16[8,128,128]{2,1,0:T(8,128)(2,1)S(1)} %get-tuple-element.28.kh_ref, ...), custom_call_target="tpu_custom_call" | custom-call | flops 201326592 | bytes 3670016 | tf_op jit(solution)/shard_map/pallas_call | solution.py:489
  34.7 5.0 %collective-permute-done.5.refs_2_.refs_0_.state_ref = bf16[8,128,128]{2,1,0:T(8,128)(2,1)S(1)} collective-permute-done((bf16[8,128,128]{2,1,0:T(8,128)(2,1)S(1)}, bf16[8,128,128]{2,1,0:T(8,128)(2,1)S(1)}, u32[]{:S(2)}, u32[]{:S(2)}) %collective-permute-start.5) | collective-permute-done | bytes 262176 | tf_op jit(solution)/shard_map/ppermute | solution.py:44
  39.6 0.4 shard_map.110.after_ref.att_ref.refs_0_
  40.0 0.0 collective-permute-done.8.refs_1_
  40.0 0.7 shard_map.114
  40.8 7.2 %collective-permute-start.9 = (bf16[2,128,1024]{2,1,0:T(8,128)(2,1)S(1)}, bf16[2,128,1024]{2,1,0:T(8,128)(2,1)S(1)}, u32[]{:S(2)}, u32[]{:S(2)}) collective-permute-start(bf16[2,128,1024]{2,1,0:T(8,128)(2,1)S(1)} %shard_map.114), channel_id=1, source_target_pairs={{0,1},{1,0},{2,3},{3,2},{4,5},{5,4},{6,7},{7,6},{8,9},{9,8},{10,11... | collective-permute-start | bytes 1572872 | tf_op jit(solution)/shard_map/ppermute | solution.py:346
  48.0 0.3 collective-permute-start.16
  48.3 1.7 %collective-permute-start.20 = (bf16[128,1024]{1,0:T(8,128)(2,1)S(1)}, bf16[128,1024]{1,0:T(8,128)(2,1)S(1)}, u32[]{:S(2)}, u32[]{:S(2)}) collective-permute-start(bf16[128,1024]{1,0:T(8,128)(2,1)S(1)} %shard_map.110.after_ref.att_ref.refs_0_), channel_id=1, source_target_pairs={{8,0},{16,8},{24,16},{28,24},{20,28},{12,20},{4,12},{0,4},{9,1},{1... | collective-permute-start | bytes 786440 | tf_op jit(solution)/shard_map/ppermute | solution.py:581
  50.0 0.1 shard_map.111.after_ref
  50.1 2.4 %collective-permute-start.11 = (bf16[8,128,128]{2,1,0:T(8,128)(2,1)S(1)}, bf16[8,128,128]{2,1,0:T(8,128)(2,1)S(1)}, u32[]{:S(2)}, u32[]{:S(2)}) collective-permute-start(bf16[8,128,128]{2,1,0:T(8,128)(2,1)S(1)} %shard_map.111.after_ref), channel_id=1, source_target_pairs={{0,8},{8,0},{4,12},{12,4},{16,24},{24,16},{20,28},{28,20},{1,9},{9... | collective-permute-start | bytes 786440 | tf_op jit(solution)/shard_map/ppermute | solution.py:44
  52.5 0.6 collective-permute-start.14
  53.1 3.2 %collective-permute-done.16.refs_1_ = bf16[128,1024]{1,0:T(8,128)(2,1)S(1)} collective-permute-done((bf16[128,1024]{1,0:T(8,128)(2,1)S(1)}, bf16[128,1024]{1,0:T(8,128)(2,1)S(1)}, u32[]{:S(2)}, u32[]{:S(2)}) %collective-permute-start.16) | collective-permute-done | bytes 262176 | tf_op jit(solution)/shard_map/ppermute | solution.py:580
  56.2 2.3 %collective-permute-start.17 = (bf16[128,1024]{1,0:T(8,128)(2,1)S(1)}, bf16[128,1024]{1,0:T(8,128)(2,1)S(1)}, u32[]{:S(2)}, u32[]{:S(2)}) collective-permute-start(bf16[128,1024]{1,0:T(8,128)(2,1)S(1)} %collective-permute-done.16.refs_1_), channel_id=1, source_target_pairs={{0,8},{8,16},{16,24},{24,28},{28,20},{20,12},{12,4},{4,0},{1,9},{9... | collective-permute-start | bytes 786440 | tf_op jit(solution)/shard_map/ppermute | solution.py:580
  58.5 0.9 %collective-permute-done.20.refs_2_ = bf16[128,1024]{1,0:T(8,128)(2,1)S(1)} collective-permute-done((bf16[128,1024]{1,0:T(8,128)(2,1)S(1)}, bf16[128,1024]{1,0:T(8,128)(2,1)S(1)}, u32[]{:S(2)}, u32[]{:S(2)}) %collective-permute-start.20) | collective-permute-done | bytes 262176 | tf_op jit(solution)/shard_map/ppermute | solution.py:581
  59.4 0.0 collective-permute-start.21
  59.4 0.7 shard_map.112
  60.2 4.9 %collective-permute-done.11.refs_1_ = bf16[8,128,128]{2,1,0:T(8,128)(2,1)S(1)} collective-permute-done((bf16[8,128,128]{2,1,0:T(8,128)(2,1)S(1)}, bf16[8,128,128]{2,1,0:T(8,128)(2,1)S(1)}, u32[]{:S(2)}, u32[]{:S(2)}) %collective-permute-start.11) | collective-permute-done | bytes 262176 | tf_op jit(solution)/shard_map/ppermute | solution.py:44
  65.0 0.0 collective-permute-start.13
  65.0 0.1 shard_map.116
  65.2 0.0 collective-permute-done.14.refs_2_
  65.2 0.1 collective-permute-start.12
  65.3 0.6 collective-permute-start.15
  65.8 0.0 collective-permute-done.17.refs_3_
  65.8 2.3 %collective-permute-start.18 = (bf16[128,1024]{1,0:T(8,128)(2,1)S(1)}, bf16[128,1024]{1,0:T(8,128)(2,1)S(1)}, u32[]{:S(2)}, u32[]{:S(2)}) collective-permute-start(bf16[128,1024]{1,0:T(8,128)(2,1)S(1)} %collective-permute-done.17.refs_3_), channel_id=1, source_target_pairs={{0,8},{8,16},{16,24},{24,28},{28,20},{20,12},{12,4},{4,0},{1,9},{9... | collective-permute-start | bytes 786440 | tf_op jit(solution)/shard_map/ppermute | solution.py:580
  68.2 2.0 %collective-permute-done.21.refs_4_ = bf16[128,1024]{1,0:T(8,128)(2,1)S(1)} collective-permute-done((bf16[128,1024]{1,0:T(8,128)(2,1)S(1)}, bf16[128,1024]{1,0:T(8,128)(2,1)S(1)}, u32[]{:S(2)}, u32[]{:S(2)}) %collective-permute-start.21) | collective-permute-done | bytes 262176 | tf_op jit(solution)/shard_map/ppermute | solution.py:581
  70.2 0.2 convert_add_fusion
  70.5 0.6 collective-permute-start.10
  71.1 1.3 %shard_map.115 = f32[128,8,128]{2,1,0:T(8,128)} custom-call(bf16[1024,128]{1,0:T(8,128)(2,1)S(1)} %get-tuple-element.36.gt_ref.after_ref, f32[5,8,128]{2,1,0:T(8,128)S(1)} %get-tuple-element.39.lam_ref, f32[8,128,128]{2,1,0:T(8,128)S(1)} %get-tuple-element.46.dql_ref, bf16[8,128,128]{2,1,0:T(8,128)(2,1)S(1)} %collective-permute-done.5.refs_2_.refs_0_.state_ref, ...), custom_call_target="tpu_custom_call" | custom-call | flops 33554432 | bytes 1572864 | tf_op jit(solution)/shard_map/pallas_call | solution.py:521
  72.4 0.0 collective-permute-done.15.refs_3_
  72.4 0.1 shard_map.118.cols_ref
  72.5 1.8 %collective-permute-done.12.refs_2_ = bf16[8,128,128]{2,1,0:T(8,128)(2,1)S(1)} collective-permute-done((bf16[8,128,128]{2,1,0:T(8,128)(2,1)S(1)}, bf16[8,128,128]{2,1,0:T(8,128)(2,1)S(1)}, u32[]{:S(2)}, u32[]{:S(2)}) %collective-permute-start.12) | collective-permute-done | bytes 262176 | tf_op jit(solution)/shard_map/ppermute | solution.py:44
  74.3 1.7 %shard_map.117 = (f32[128,8,128]{2,1,0:T(8,128)}, f32[128,8,128]{2,1,0:T(8,128)}) custom-call(bf16[8,128,128]{2,1,0:T(8,128)(2,1)S(1)} %get-tuple-element.28.kh_ref, bf16[8,128,128]{2,1,0:T(8,128)(2,1)S(1)} %get-tuple-element.29.vh_ref, f32[8,128,128]{2,1,0:T(8,128)S(1)} %get-tuple-element.40.refs_3_.dkl_ref, f32[8,128,128]{2,1,0:T(8,128)S(1)} %get-tuple-element.47.dvl_ref, ...), custom_call_target="tpu_custom_call" | custom-call | flops 67108864 | bytes 2883584 | tf_op jit(solution)/shard_map/pallas_call | solution.py:550
  76.1 1.5 %shard_map.119.refs_2_ = f32[1024,512]{1,0:T(8,128)S(1)} custom-call(bf16[8,128,512]{2,1,0:T(8,128)(2,1)S(1)} %shard_map.118.cols_ref, f32[128,8,128]{2,1,0:T(8,128)} %get-tuple-element.25.after_ref, bf16[128,1024]{1,0:T(8,128)(2,1)S(1)} %shard_map.110.after_ref.att_ref.refs_0_, bf16[128,1024]{1,0:T(8,128)(2,1)S(1)} %collective-permute-done.16.refs_1_, ...), custom_call_target="tpu_custom_call" | custom-call | flops 671088640 | bytes 2097152 | tf_op jit(solution)/shard_map/pallas_call | solution.py:565
  77.6 2.0 %collective-permute-done.18.refs_0_ = bf16[128,1024]{1,0:T(8,128)(2,1)S(1)} collective-permute-done((bf16[128,1024]{1,0:T(8,128)(2,1)S(1)}, bf16[128,1024]{1,0:T(8,128)(2,1)S(1)}, u32[]{:S(2)}, u32[]{:S(2)}) %collective-permute-start.18) | collective-permute-done | bytes 262176 | tf_op jit(solution)/shard_map/ppermute | solution.py:580
  79.6 0.1 collective-permute-start.19
  79.7 0.0 collective-permute-done.22.refs_1_
  79.7 2.1 %collective-permute-start.23 = (bf16[64,1024]{1,0:T(8,128)(2,1)S(1)}, bf16[64,1024]{1,0:T(8,128)(2,1)S(1)}, u32[]{:S(2)}, u32[]{:S(2)}) collective-permute-start(bf16[64,1024]{1,0:T(8,128)(2,1)S(1)} %slice.22), channel_id=1, source_target_pairs={{8,0},{16,8},{24,16},{28,24},{20,28},{12,20},{4,12},{0,4},{9,1},{1... | collective-permute-start | bytes 393224 | tf_op jit(solution)/shard_map/ppermute | solution.py:591
  81.7 0.0 collective-permute-done.10
  81.7 0.8 fusion.1
  82.5 0.7 shard_map.120.total_ref
  83.2 1.5 %collective-permute-done.19.low_ref = bf16[64,1024]{1,0:T(8,128)(2,1)S(1)} collective-permute-done((bf16[64,1024]{1,0:T(8,128)(2,1)S(1)}, bf16[64,1024]{1,0:T(8,128)(2,1)S(1)}, u32[]{:S(2)}, u32[]{:S(2)}) %collective-permute-start.19) | collective-permute-done | bytes 131104 | tf_op jit(solution)/shard_map/ppermute | solution.py:590
  84.8 0.1 collective-permute-done.23.high_ref
  84.9 1.6 %shard_map.121 = f32[1024,512]{1,0:T(8,128)} custom-call(bf16[8,128,512]{2,1,0:T(8,128)(2,1)S(1)} %shard_map.118.cols_ref, bf16[64,1024]{1,0:T(8,128)(2,1)S(1)} %collective-permute-done.19.low_ref, bf16[64,1024]{1,0:T(8,128)(2,1)S(1)} %collective-permute-done.23.high_ref, f32[1024,512]{1,0:T(8,128)S(1)} %shard_map.120.total_ref, ...), custom_call_target="tpu_custom_call" | custom-call | flops 134217728 | bytes 4194304 | tf_op jit(solution)/shard_map/pallas_call | solution.py:593
  (10 shorter events, 0.1 us)
Async XLA Ops:
  3.8 9.3 %collective-permute-start.3 = (bf16[128,1024]{1,0:T(8,128)(2,1)S(1)}, bf16[128,1024]{1,0:T(8,128)(2,1)S(1)}, u32[]{:S(2)}, u32[]{:S(2)}) collective-permute-start(bf16[128,1024]{1,0:T(8,128)(2,1)S(1)} %get-tuple-element.33.refs_0_.own_ref), channel_id=1, source_target_pairs={{0,2},{1,3},{2,0},{3,1},{4,6},{5,7},{6,4},{7,5},{8,10},{9,11},{10,... | collective-permute-start | bytes 786440 | tf_op jit(solution)/shard_map/ppermute | solution.py:346
  6.8 7.8 %collective-permute-start = (bf16[8,128,128]{2,1,0:T(8,128)(2,1)S(1)}, bf16[8,128,128]{2,1,0:T(8,128)(2,1)S(1)}, u32[]{:S(2)}, u32[]{:S(2)}) collective-permute-start(bf16[8,128,128]{2,1,0:T(8,128)(2,1)S(1)} %get-tuple-element.32.running_ref), channel_id=1, source_target_pairs={{0,4},{4,0},{8,12},{12,8},{16,20},{20,16},{24,28},{28,24},{1,5},{5... | collective-permute-start | bytes 786440 | tf_op jit(solution)/shard_map/ppermute | solution.py:44
  8.3 8.0 %collective-permute-start.2 = (bf16[128,1024]{1,0:T(8,128)(2,1)S(1)}, bf16[128,1024]{1,0:T(8,128)(2,1)S(1)}, u32[]{:S(2)}, u32[]{:S(2)}) collective-permute-start(bf16[128,1024]{1,0:T(8,128)(2,1)S(1)} %get-tuple-element.33.refs_0_.own_ref), channel_id=1, source_target_pairs={{0,1},{1,0},{2,3},{3,2},{4,5},{5,4},{6,7},{7,6},{8,9},{9,8},{10,11... | collective-permute-start | bytes 786440 | tf_op jit(solution)/shard_map/ppermute | solution.py:346
  13.1 3.2 %collective-permute-start.4 = (bf16[128,1024]{1,0:T(8,128)(2,1)S(1)}, bf16[128,1024]{1,0:T(8,128)(2,1)S(1)}, u32[]{:S(2)}, u32[]{:S(2)}) collective-permute-start(bf16[128,1024]{1,0:T(8,128)(2,1)S(1)} %shard_map.104), channel_id=1, source_target_pairs={{0,1},{1,0},{2,3},{3,2},{4,5},{5,4},{6,7},{7,6},{8,9},{9,8},{10,11... | collective-permute-start | bytes 786440 | tf_op jit(solution)/shard_map/ppermute | solution.py:346
  14.6 7.5 %collective-permute-start.1 = (bf16[8,128,128]{2,1,0:T(8,128)(2,1)S(1)}, bf16[8,128,128]{2,1,0:T(8,128)(2,1)S(1)}, u32[]{:S(2)}, u32[]{:S(2)}) collective-permute-start(bf16[8,128,128]{2,1,0:T(8,128)(2,1)S(1)} %shard_map.103.refs_6_.running_ref), channel_id=1, source_target_pairs={{0,8},{8,0},{4,12},{12,4},{16,24},{24,16},{20,28},{28,20},{1,9},{9... | collective-permute-start | bytes 786440 | tf_op jit(solution)/shard_map/ppermute | solution.py:44
  22.2 17.4 %collective-permute-start.5 = (bf16[8,128,128]{2,1,0:T(8,128)(2,1)S(1)}, bf16[8,128,128]{2,1,0:T(8,128)(2,1)S(1)}, u32[]{:S(2)}, u32[]{:S(2)}) collective-permute-start(bf16[8,128,128]{2,1,0:T(8,128)(2,1)S(1)} %shard_map.106.after_ref), channel_id=1, source_target_pairs={{0,16},{16,0},{4,20},{20,4},{8,24},{24,8},{12,28},{28,12},{1,17},{... | collective-permute-start | bytes 786440 | tf_op jit(solution)/shard_map/ppermute | solution.py:44
  25.0 3.3 %collective-permute-start.6 = (bf16[64,1024]{1,0:T(8,128)(2,1)S(1)}, bf16[64,1024]{1,0:T(8,128)(2,1)S(1)}, u32[]{:S(2)}, u32[]{:S(2)}) collective-permute-start(bf16[64,1024]{1,0:T(8,128)(2,1)S(1)} %get-tuple-element.41), channel_id=1, source_target_pairs={{0,0},{1,10},{2,18},{3,24},{4,4},{5,14},{6,22},{7,28},{8,2},{9,8},... | collective-permute-start | bytes 393224 | tf_op jit(solution)/shard_map/ppermute | solution.py:439
  25.7 6.1 %collective-permute-start.7 = (bf16[64,1024]{1,0:T(8,128)(2,1)S(1)}, bf16[64,1024]{1,0:T(8,128)(2,1)S(1)}, u32[]{:S(2)}, u32[]{:S(2)}) collective-permute-start(bf16[64,1024]{1,0:T(8,128)(2,1)S(1)} %get-tuple-element.42), channel_id=1, source_target_pairs={{2,0},{3,10},{0,18},{1,24},{6,4},{7,14},{4,22},{5,28},{10,2},{11,8... | collective-permute-start | bytes 393224 | tf_op jit(solution)/shard_map/ppermute | solution.py:440
  31.8 8.2 %collective-permute-start.8 = (bf16[128,512]{1,0:T(8,128)(2,1)S(1)}, bf16[128,512]{1,0:T(8,128)(2,1)S(1)}, u32[]{:S(2)}, u32[]{:S(2)}) collective-permute-start(bf16[128,512]{1,0:T(8,128)(2,1)S(1)} %get-tuple-element.43.refs_4_), channel_id=1, source_target_pairs={{0,4},{4,0},{8,12},{12,8},{16,20},{20,16},{24,28},{28,24},{1,5},{5... | collective-permute-start | bytes 393224 | tf_op jit(solution)/shard_map/ppermute | solution.py:467
  40.8 24.5 %collective-permute-start.9 = (bf16[2,128,1024]{2,1,0:T(8,128)(2,1)S(1)}, bf16[2,128,1024]{2,1,0:T(8,128)(2,1)S(1)}, u32[]{:S(2)}, u32[]{:S(2)}) collective-permute-start(bf16[2,128,1024]{2,1,0:T(8,128)(2,1)S(1)} %shard_map.114), channel_id=1, source_target_pairs={{0,1},{1,0},{2,3},{3,2},{4,5},{5,4},{6,7},{7,6},{8,9},{9,8},{10,11... | collective-permute-start | bytes 1572872 | tf_op jit(solution)/shard_map/ppermute | solution.py:346
  48.0 8.3 %collective-permute-start.16 = (bf16[128,1024]{1,0:T(8,128)(2,1)S(1)}, bf16[128,1024]{1,0:T(8,128)(2,1)S(1)}, u32[]{:S(2)}, u32[]{:S(2)}) collective-permute-start(bf16[128,1024]{1,0:T(8,128)(2,1)S(1)} %shard_map.110.after_ref.att_ref.refs_0_), channel_id=1, source_target_pairs={{0,8},{8,16},{16,24},{24,28},{28,20},{20,12},{12,4},{4,0},{1,9},{9... | collective-permute-start | bytes 786440 | tf_op jit(solution)/shard_map/ppermute | solution.py:580
  48.3 11.1 %collective-permute-start.20 = (bf16[128,1024]{1,0:T(8,128)(2,1)S(1)}, bf16[128,1024]{1,0:T(8,128)(2,1)S(1)}, u32[]{:S(2)}, u32[]{:S(2)}) collective-permute-start(bf16[128,1024]{1,0:T(8,128)(2,1)S(1)} %shard_map.110.after_ref.att_ref.refs_0_), channel_id=1, source_target_pairs={{8,0},{16,8},{24,16},{28,24},{20,28},{12,20},{4,12},{0,4},{9,1},{1... | collective-permute-start | bytes 786440 | tf_op jit(solution)/shard_map/ppermute | solution.py:581
  50.1 15.0 %collective-permute-start.11 = (bf16[8,128,128]{2,1,0:T(8,128)(2,1)S(1)}, bf16[8,128,128]{2,1,0:T(8,128)(2,1)S(1)}, u32[]{:S(2)}, u32[]{:S(2)}) collective-permute-start(bf16[8,128,128]{2,1,0:T(8,128)(2,1)S(1)} %shard_map.111.after_ref), channel_id=1, source_target_pairs={{0,8},{8,0},{4,12},{12,4},{16,24},{24,16},{20,28},{28,20},{1,9},{9... | collective-permute-start | bytes 786440 | tf_op jit(solution)/shard_map/ppermute | solution.py:44
  52.5 12.7 %collective-permute-start.14 = (bf16[2,128,512]{2,1,0:T(8,128)(2,1)S(1)}, bf16[2,128,512]{2,1,0:T(8,128)(2,1)S(1)}, u32[]{:S(2)}, u32[]{:S(2)}) collective-permute-start(bf16[2,128,512]{2,1,0:T(8,128)(2,1)S(1)} %shard_map.113.after_ref.refs_0_), channel_id=1, source_target_pairs={{0,2},{1,3},{2,0},{3,1},{4,6},{5,7},{6,4},{7,5},{8,10},{9,11},{10,... | collective-permute-start | bytes 786440 | tf_op jit(solution)/shard_map/ppermute | solution.py:346
  56.2 9.6 %collective-permute-start.17 = (bf16[128,1024]{1,0:T(8,128)(2,1)S(1)}, bf16[128,1024]{1,0:T(8,128)(2,1)S(1)}, u32[]{:S(2)}, u32[]{:S(2)}) collective-permute-start(bf16[128,1024]{1,0:T(8,128)(2,1)S(1)} %collective-permute-done.16.refs_1_), channel_id=1, source_target_pairs={{0,8},{8,16},{16,24},{24,28},{28,20},{20,12},{12,4},{4,0},{1,9},{9... | collective-permute-start | bytes 786440 | tf_op jit(solution)/shard_map/ppermute | solution.py:580
  59.4 10.8 %collective-permute-start.21 = (bf16[128,1024]{1,0:T(8,128)(2,1)S(1)}, bf16[128,1024]{1,0:T(8,128)(2,1)S(1)}, u32[]{:S(2)}, u32[]{:S(2)}) collective-permute-start(bf16[128,1024]{1,0:T(8,128)(2,1)S(1)} %collective-permute-done.20.refs_2_), channel_id=1, source_target_pairs={{8,0},{16,8},{24,16},{28,24},{20,28},{12,20},{4,12},{0,4},{9,1},{1... | collective-permute-start | bytes 786440 | tf_op jit(solution)/shard_map/ppermute | solution.py:581
  65.0 5.4 %collective-permute-start.13 = (bf16[2,128,512]{2,1,0:T(8,128)(2,1)S(1)}, bf16[2,128,512]{2,1,0:T(8,128)(2,1)S(1)}, u32[]{:S(2)}, u32[]{:S(2)}) collective-permute-start(bf16[2,128,512]{2,1,0:T(8,128)(2,1)S(1)} %shard_map.113.after_ref.refs_0_), channel_id=1, source_target_pairs={{0,1},{1,0},{2,3},{3,2},{4,5},{5,4},{6,7},{7,6},{8,9},{9,8},{10,11... | collective-permute-start | bytes 786440 | tf_op jit(solution)/shard_map/ppermute | solution.py:346
  65.2 9.2 %collective-permute-start.12 = (bf16[8,128,128]{2,1,0:T(8,128)(2,1)S(1)}, bf16[8,128,128]{2,1,0:T(8,128)(2,1)S(1)}, u32[]{:S(2)}, u32[]{:S(2)}) collective-permute-start(bf16[8,128,128]{2,1,0:T(8,128)(2,1)S(1)} %shard_map.116), channel_id=1, source_target_pairs={{0,4},{4,0},{8,12},{12,8},{16,20},{20,16},{24,28},{28,24},{1,5},{5... | collective-permute-start | bytes 786440 | tf_op jit(solution)/shard_map/ppermute | solution.py:44
  65.3 7.1 %collective-permute-start.15 = (bf16[2,128,512]{2,1,0:T(8,128)(2,1)S(1)}, bf16[2,128,512]{2,1,0:T(8,128)(2,1)S(1)}, u32[]{:S(2)}, u32[]{:S(2)}) collective-permute-start(bf16[2,128,512]{2,1,0:T(8,128)(2,1)S(1)} %collective-permute-done.14.refs_2_), channel_id=1, source_target_pairs={{0,1},{1,0},{2,3},{3,2},{4,5},{5,4},{6,7},{7,6},{8,9},{9,8},{10,11... | collective-permute-start | bytes 786440 | tf_op jit(solution)/shard_map/ppermute | solution.py:346
  65.8 13.7 %collective-permute-start.18 = (bf16[128,1024]{1,0:T(8,128)(2,1)S(1)}, bf16[128,1024]{1,0:T(8,128)(2,1)S(1)}, u32[]{:S(2)}, u32[]{:S(2)}) collective-permute-start(bf16[128,1024]{1,0:T(8,128)(2,1)S(1)} %collective-permute-done.17.refs_3_), channel_id=1, source_target_pairs={{0,8},{8,16},{16,24},{24,28},{28,20},{20,12},{12,4},{4,0},{1,9},{9... | collective-permute-start | bytes 786440 | tf_op jit(solution)/shard_map/ppermute | solution.py:580
  70.2 9.5 %collective-permute-start.22 = (bf16[128,1024]{1,0:T(8,128)(2,1)S(1)}, bf16[128,1024]{1,0:T(8,128)(2,1)S(1)}, u32[]{:S(2)}, u32[]{:S(2)}) collective-permute-start(bf16[128,1024]{1,0:T(8,128)(2,1)S(1)} %collective-permute-done.21.refs_4_), channel_id=1, source_target_pairs={{8,0},{16,8},{24,16},{28,24},{20,28},{12,20},{4,12},{0,4},{9,1},{1... | collective-permute-start | bytes 786440 | tf_op jit(solution)/shard_map/ppermute | solution.py:581
  70.5 11.3 %collective-permute-start.10 = (bf16[1,128,1024]{2,1,0:T(8,128)(2,1)S(1)}, bf16[1,128,1024]{2,1,0:T(8,128)(2,1)S(1)}, u32[]{:S(2)}, u32[]{:S(2)}) collective-permute-start(bf16[1,128,1024]{2,1,0:T(8,128)(2,1)S(1)} %slice.29), channel_id=1, source_target_pairs={{0,2},{1,3},{2,0},{3,1},{4,6},{5,7},{6,4},{7,5},{8,10},{9,11},{10,... | collective-permute-start | bytes 786440 | tf_op jit(solution)/shard_map/ppermute | solution.py:346
  79.6 5.2 %collective-permute-start.19 = (bf16[64,1024]{1,0:T(8,128)(2,1)S(1)}, bf16[64,1024]{1,0:T(8,128)(2,1)S(1)}, u32[]{:S(2)}, u32[]{:S(2)}) collective-permute-start(bf16[64,1024]{1,0:T(8,128)(2,1)S(1)} %slice.21), channel_id=1, source_target_pairs={{0,8},{8,16},{16,24},{24,28},{28,20},{20,12},{12,4},{4,0},{1,9},{9... | collective-permute-start | bytes 393224 | tf_op jit(solution)/shard_map/ppermute | solution.py:590
  79.7 5.2 %collective-permute-start.23 = (bf16[64,1024]{1,0:T(8,128)(2,1)S(1)}, bf16[64,1024]{1,0:T(8,128)(2,1)S(1)}, u32[]{:S(2)}, u32[]{:S(2)}) collective-permute-start(bf16[64,1024]{1,0:T(8,128)(2,1)S(1)} %slice.22), channel_id=1, source_target_pairs={{8,0},{16,8},{24,16},{28,24},{20,28},{12,20},{4,12},{0,4},{9,1},{1... | collective-permute-start | bytes 393224 | tf_op jit(solution)/shard_map/ppermute | solution.py:591

commit v13 on v11

--- a/solution.py
+++ b/solution.py
@@ -260,8 +260,8 @@
         dv_ref[:, h, :] = dvl_ref[h] + mm(kh_ref[h], late, NT)
 
 
-def share_kernel(offsets, att_ref, w_ref, after_ref, out_ref):
-    del after_ref
+def share_kernel(offsets, att_ref, w_ref, *refs):
+    out_ref = refs[-1]
     width = out_ref.shape[2]
     for n, i in enumerate(offsets):
         column = pl.multiple_of((lax.axis_index("head") ^ i) * width, width)
@@ -512,20 +512,20 @@
         cost_estimate=cost(flops_head, 6 * moved_head),
     )(gt, lam, query_local, partner_states[top], attended)
 
-    def share(offsets, kind, after):
+    def share(offsets, kind, *after):
         return pl.pallas_call(
             functools.partial(share_kernel, offsets),
             out_shape=like((len(offsets), rows, width), kind),
-            in_specs=[VMEM, VMEM, ANY],
+            in_specs=[VMEM] * 2 + [ANY] * len(after),
             out_specs=VMEM,
             compiler_params=PARAMS,
             cost_estimate=cost(
                 2 * rows * width * len(offsets) * width, 2 * width * len(offsets) * width
             ),
-        )(attended, w, after)
+        )(attended, w, *after)
 
     send = share(range(1, heads, 2), BF, stacked)
-    kept = share(range(0, heads, 2), F32, first_pending)
+    kept = share(range(0, heads, 2), F32, first_pending, hbm(query_grad))
     for digit in range(head_bits):
         kept = kept + to_group(send, 1 << digit).astype(F32)
         if digit < head_bits - 1:

time: 76.5 us -> 76.5 us (level)
  transfers between devices with their start and end apart: 24 -> 24, of which waited for: 10 -> 11; matrix products, arithmetic and copies ran while one was open for 1% -> 1% of each run, Pallas kernels for 19% -> 19%
where the time goes in v13:
time: 76.5 us; the launch traced here: 76.4 us
  starting transfers between devices  31 us (41%)
  waiting for transfers between devices  24 us (31%)
  Pallas kernels  19.5 us (25%)
  other arithmetic  0.95 us (1%)
  between operations  0.87 us (1%)
    ppermute x5, waiting for transfers between devices, across(): return lax.ppermute(block, axis, route)  10.6 us
    ppermute x5, starting transfers between devices, across(): return lax.ppermute(block, axis, route)  8.19 us
    ppermute x3, waiting for transfers between devices, body(): ahead = lax.ppermute(ahead, 'seq', forward)  7.87 us
    ppermute x8, starting transfers between devices, to_group(): return lax.ppermute(block, 'head', [(at, at ^ i) for at in range(heads)])  6.7 us
    ppermute x3, starting transfers between devices, body(): behind = lax.ppermute(behind, 'seq', backward)  4.58 us
    ppermute x1, starting transfers between devices, body(): lax.ppermute(grad_blocks[far][half:], axes, turn_route(far))  3.92 us
    pallas_call x1, Pallas kernels, body(): pl.pallas_call(local_kernel, out_shape=(pltpu.VMEM((heads_dev, rows, rows...  3.66 us
    ppermute x3, starting transfers between devices, body(): ahead = lax.ppermute(ahead, 'seq', forward)  3.25 us
  transfers between devices with their start and end apart: 24, of which 11 were waited for; matrix products, arithmetic and copies ran while one was open for 1% of the time, Pallas kernels for 19%

profile of v13, /device:TPU:0, one launch (start us, length us, event | category | flops | bytes accessed | tf_op | source)
XLA Modules:
  0.0 76.4 jit_solution(14268088886643512067)
XLA Ops:
  0.6 2.5 %shard_map.101 = (bf16[8,128,128]{2,1,0:T(8,128)(2,1)S(1)}, bf16[8,128,128]{2,1,0:T(8,128)(2,1)S(1)}, bf16[8,128,128]{2,1,0:T(8,128)(2,1)S(1)}, bf16[128,1024]{1,0:T(8,128)(2,1)S(1)}, bf16[64,1024]{1,0:T(8,128)(2,1)S(1)}) custom-call(f32[128,8,128]{2,1,0:T(8,128)} %k_hbm.1, f32[128,8,128]{2,1,0:T(8,128)} %v_hbm.1, bf16[128,1024]{1,0:T(8,128)(2,1)} %grad_hbm.1), custom_call_target="tpu_custom_call" | custom-call | flops 33554432 | bytes 1835008 | tf_op jit(solution)/shard_map/pallas_call | solution.py:324
  3.1 3.0 %collective-permute-start.3 = (bf16[128,1024]{1,0:T(8,128)(2,1)S(1)}, bf16[128,1024]{1,0:T(8,128)(2,1)S(1)}, u32[]{:S(2)}, u32[]{:S(2)}) collective-permute-start(bf16[128,1024]{1,0:T(8,128)(2,1)S(1)} %get-tuple-element.32.refs_0_), channel_id=1, source_target_pairs={{0,2},{1,3},{2,0},{3,1},{4,6},{5,7},{6,4},{7,5},{8,10},{9,11},{10,... | collective-permute-start | bytes 786440 | tf_op jit(solution)/shard_map/ppermute | solution.py:339
  6.1 1.5 %collective-permute-start = (bf16[8,128,128]{2,1,0:T(8,128)(2,1)S(1)}, bf16[8,128,128]{2,1,0:T(8,128)(2,1)S(1)}, u32[]{:S(2)}, u32[]{:S(2)}) collective-permute-start(bf16[8,128,128]{2,1,0:T(8,128)(2,1)S(1)} %get-tuple-element.31.running_ref), channel_id=1, source_target_pairs={{0,4},{4,0},{8,12},{12,8},{16,20},{20,16},{24,28},{28,24},{1,5},{5... | collective-permute-start | bytes 786440 | tf_op jit(solution)/shard_map/ppermute | solution.py:44
  7.6 0.0 collective-permute-start.2
  7.6 3.7 %shard_map.102 = (bf16[8,128,128]{2,1,0:T(8,128)(2,1)S(1)}, f32[8,128,128]{2,1,0:T(8,128)S(1)}, bf16[8,128,128]{2,1,0:T(8,128)(2,1)S(1)}, bf16[3,8,128,128]{3,2,...) custom-call(f32[128,8,128]{2,1,0:T(8,128)} %q_hbm.1, ...), custom_call_target="tpu_custom_call" | custom-call | flops 67108864 | bytes 3145728 | tf_op jit(solution)/shard_map/pallas_call | solution.py:348
  11.3 1.1 %collective-permute-done.3.block_ref.refs_2_ = bf16[128,1024]{1,0:T(8,128)(2,1)S(1)} collective-permute-done((bf16[128,1024]{1,0:T(8,128)(2,1)S(1)}, bf16[128,1024]{1,0:T(8,128)(2,1)S(1)}, u32[]{:S(2)}, u32[]{:S(2)}) %collective-permute-start.3) | collective-permute-done | bytes 262176 | tf_op jit(solution)/shard_map/ppermute | solution.py:339
  12.4 0.1 collective-permute-start.4
  12.5 1.4 %collective-permute-done.arrived_ref.refs_0_ = bf16[8,128,128]{2,1,0:T(8,128)(2,1)S(1)} collective-permute-done((bf16[8,128,128]{2,1,0:T(8,128)(2,1)S(1)}, bf16[8,128,128]{2,1,0:T(8,128)(2,1)S(1)}, u32[]{:S(2)}, u32[]{:S(2)}) %collective-permute-start) | collective-permute-done | bytes 262176 | tf_op jit(solution)/shard_map/ppermute | solution.py:44
  13.9 0.1 shard_map.103.refs_6_.running_ref
  13.9 1.6 %collective-permute-start.1 = (bf16[8,128,128]{2,1,0:T(8,128)(2,1)S(1)}, bf16[8,128,128]{2,1,0:T(8,128)(2,1)S(1)}, u32[]{:S(2)}, u32[]{:S(2)}) collective-permute-start(bf16[8,128,128]{2,1,0:T(8,128)(2,1)S(1)} %shard_map.103.refs_6_.running_ref), channel_id=1, source_target_pairs={{0,8},{8,0},{4,12},{12,4},{16,24},{24,16},{20,28},{28,20},{1,9},{9... | collective-permute-start | bytes 786440 | tf_op jit(solution)/shard_map/ppermute | solution.py:44
  15.6 0.7 collective-permute-start.6
  16.3 3.9 %collective-permute-start.7 = (bf16[64,1024]{1,0:T(8,128)(2,1)S(1)}, bf16[64,1024]{1,0:T(8,128)(2,1)S(1)}, u32[]{:S(2)}, u32[]{:S(2)}) collective-permute-start(bf16[64,1024]{1,0:T(8,128)(2,1)S(1)} %slice.23), channel_id=1, source_target_pairs={{2,0},{3,10},{0,18},{1,24},{6,4},{7,14},{4,22},{5,28},{10,2},{11,8... | collective-permute-start | bytes 393224 | tf_op jit(solution)/shard_map/ppermute | solution.py:401
  20.2 0.0 collective-permute-done.2.refs_1_
  20.2 0.0 collective-permute-done.4.refs_3_
  20.2 2.8 %shard_map.105 = (bf16[1024,128]{1,0:T(8,128)(2,1)S(1)}, bf16[8,128,128]{2,1,0:T(8,128)(2,1)S(1)}, bf16[8,128,128]{2,1,0:T(8,128)(2,1)S(1)}, bf16[8,128,128]{2,1,0:T(8,128)(2,1)S(1)}) custom-call(bf16[128,1024]{1,0:T(8,128)(2,1)S(1)} %get-tuple-element.32.refs_0_, bf16[128,1024]{1,0:T(8,128)(2,1)S(1)} %collective-permute-done.2.refs_1_, ...), custom_call_target="tpu_custom_call" | custom-call | flops 1073741824 | bytes 8388608 | tf_op jit(solution)/shard_map/pallas_call | solution.py:418
  23.0 0.0 collective-permute-done.1.arrived_ref.refs_1_
  23.0 0.1 shard_map.106.after_ref
  23.1 3.4 %collective-permute-start.5 = (bf16[8,128,128]{2,1,0:T(8,128)(2,1)S(1)}, bf16[8,128,128]{2,1,0:T(8,128)(2,1)S(1)}, u32[]{:S(2)}, u32[]{:S(2)}) collective-permute-start(bf16[8,128,128]{2,1,0:T(8,128)(2,1)S(1)} %shard_map.106.after_ref), channel_id=1, source_target_pairs={{0,16},{16,0},{4,20},{20,4},{8,24},{24,8},{12,28},{28,12},{1,17},{... | collective-permute-start | bytes 786440 | tf_op jit(solution)/shard_map/ppermute | solution.py:44
  26.5 0.0 collective-permute-done.6.low_ref
  26.5 0.0 collective-permute-done.7.high_ref
  26.5 1.6 %collective-permute-start.8 = (bf16[128,512]{1,0:T(8,128)(2,1)S(1)}, bf16[128,512]{1,0:T(8,128)(2,1)S(1)}, u32[]{:S(2)}, u32[]{:S(2)}) collective-permute-start(bf16[128,512]{1,0:T(8,128)(2,1)S(1)} %get-tuple-element.41.refs_4_), channel_id=1, source_target_pairs={{0,4},{4,0},{8,12},{12,8},{16,20},{20,16},{24,28},{28,24},{1,5},{5... | collective-permute-start | bytes 393224 | tf_op jit(solution)/shard_map/ppermute | solution.py:452
  28.1 1.3 %shard_map.107 = (f32[8,128,128]{2,1,0:T(8,128)S(1)}, f32[8,128,128]{2,1,0:T(8,128)S(1)}, f32[8,128,128]{2,1,0:T(8,128)S(1)}) custom-call(bf16[1024,128]{1,0:T(8,128)(2,1)S(1)} %get-tuple-element.35.gt_ref, bf16[8,128,128]{2,1,0:T(8,128)(2,1)S(1)} %get-tuple-element.36.qh_ref, bf16[8,128,128]{2,1,0:T(8,128)(2,1)S(1)} %get-tuple-element.27.kh_ref, ...), custom_call_target="tpu_custom_call" | custom-call | flops 201326592 | bytes 3670016 | tf_op jit(solution)/shard_map/pallas_call | solution.py:474
  29.4 2.8 %collective-permute-done.8.refs_1_ = bf16[128,512]{1,0:T(8,128)(2,1)S(1)} collective-permute-done((bf16[128,512]{1,0:T(8,128)(2,1)S(1)}, bf16[128,512]{1,0:T(8,128)(2,1)S(1)}, u32[]{:S(2)}, u32[]{:S(2)}) %collective-permute-start.8) | collective-permute-done | bytes 131104 | tf_op jit(solution)/shard_map/ppermute | solution.py:452
  32.3 6.6 %collective-permute-done.5.refs_2_.refs_0_.state_ref = bf16[8,128,128]{2,1,0:T(8,128)(2,1)S(1)} collective-permute-done((bf16[8,128,128]{2,1,0:T(8,128)(2,1)S(1)}, bf16[8,128,128]{2,1,0:T(8,128)(2,1)S(1)}, u32[]{:S(2)}, u32[]{:S(2)}) %collective-permute-start.5) | collective-permute-done | bytes 262176 | tf_op jit(solution)/shard_map/ppermute | solution.py:44
  38.9 0.4 shard_map.109.after_ref.att_ref.refs_0_
  39.2 0.7 shard_map.114
  40.0 0.1 collective-permute-start.9
  40.0 0.1 collective-permute-start.16
  40.2 1.9 %collective-permute-start.20 = (bf16[128,1024]{1,0:T(8,128)(2,1)S(1)}, bf16[128,1024]{1,0:T(8,128)(2,1)S(1)}, u32[]{:S(2)}, u32[]{:S(2)}) collective-permute-start(bf16[128,1024]{1,0:T(8,128)(2,1)S(1)} %shard_map.109.after_ref.att_ref.refs_0_), channel_id=1, source_target_pairs={{8,0},{16,8},{24,16},{28,24},{20,28},{12,20},{4,12},{0,4},{9,1},{1... | collective-permute-start | bytes 786440 | tf_op jit(solution)/shard_map/ppermute | solution.py:566
  42.1 1.7 %collective-permute-start.14 = (bf16[2,128,512]{2,1,0:T(8,128)(2,1)S(1)}, bf16[2,128,512]{2,1,0:T(8,128)(2,1)S(1)}, u32[]{:S(2)}, u32[]{:S(2)}) collective-permute-start(bf16[2,128,512]{2,1,0:T(8,128)(2,1)S(1)} %shard_map.113.refs_0_), channel_id=1, source_target_pairs={{0,2},{1,3},{2,0},{3,1},{4,6},{5,7},{6,4},{7,5},{8,10},{9,11},{10,... | collective-permute-start | bytes 786440 | tf_op jit(solution)/shard_map/ppermute | solution.py:339
  43.8 0.1 shard_map.110.refs_0_
  43.9 0.2 collective-permute-start.11
  44.1 4.7 %collective-permute-done.16.refs_1_ = bf16[128,1024]{1,0:T(8,128)(2,1)S(1)} collective-permute-done((bf16[128,1024]{1,0:T(8,128)(2,1)S(1)}, bf16[128,1024]{1,0:T(8,128)(2,1)S(1)}, u32[]{:S(2)}, u32[]{:S(2)}) %collective-permute-start.16) | collective-permute-done | bytes 262176 | tf_op jit(solution)/shard_map/ppermute | solution.py:565
  48.7 0.6 collective-permute-start.17
  49.4 0.0 collective-permute-done.20.refs_2_
  49.4 1.4 %collective-permute-start.21 = (bf16[128,1024]{1,0:T(8,128)(2,1)S(1)}, bf16[128,1024]{1,0:T(8,128)(2,1)S(1)}, u32[]{:S(2)}, u32[]{:S(2)}) collective-permute-start(bf16[128,1024]{1,0:T(8,128)(2,1)S(1)} %collective-permute-done.20.refs_2_), channel_id=1, source_target_pairs={{8,0},{16,8},{24,16},{28,24},{20,28},{12,20},{4,12},{0,4},{9,1},{1... | collective-permute-start | bytes 786440 | tf_op jit(solution)/shard_map/ppermute | solution.py:566
  50.8 1.3 %shard_map.111.refs_1_ = f32[128,8,128]{2,1,0:T(8,128)} custom-call(bf16[1024,128]{1,0:T(8,128)(2,1)S(1)} %get-tuple-element.35.gt_ref, f32[5,8,128]{2,1,0:T(8,128)S(1)} %get-tuple-element.38.lam_ref, f32[8,128,128]{2,1,0:T(8,128)S(1)} %get-tuple-element.43.dql_ref, bf16[8,128,128]{2,1,0:T(8,128)(2,1)S(1)} %collective-permute-done.5.refs_2_.refs_0_.state_ref, ...), custom_call_target="tpu_custom_call" | custom-call | flops 33554432 | bytes 1572864 | tf_op jit(solution)/shard_map/pallas_call | solution.py:506
  52.1 0.7 shard_map.112
  52.8 0.0 collective-permute-done.14.refs_2_
  52.8 0.1 collective-permute-start.13
  52.9 2.0 %collective-permute-done.11.refs_1_ = bf16[8,128,128]{2,1,0:T(8,128)(2,1)S(1)} collective-permute-done((bf16[8,128,128]{2,1,0:T(8,128)(2,1)S(1)}, bf16[8,128,128]{2,1,0:T(8,128)(2,1)S(1)}, u32[]{:S(2)}, u32[]{:S(2)}) %collective-permute-start.11) | collective-permute-done | bytes 262176 | tf_op jit(solution)/shard_map/ppermute | solution.py:44
  54.9 0.0 collective-permute-start.15
  54.9 0.1 shard_map.115
  55.1 0.0 collective-permute-done.9
  55.1 1.5 %collective-permute-start.12 = (bf16[8,128,128]{2,1,0:T(8,128)(2,1)S(1)}, bf16[8,128,128]{2,1,0:T(8,128)(2,1)S(1)}, u32[]{:S(2)}, u32[]{:S(2)}) collective-permute-start(bf16[8,128,128]{2,1,0:T(8,128)(2,1)S(1)} %shard_map.115), channel_id=1, source_target_pairs={{0,4},{4,0},{8,12},{12,8},{16,20},{20,16},{24,28},{28,24},{1,5},{5... | collective-permute-start | bytes 786440 | tf_op jit(solution)/shard_map/ppermute | solution.py:44
  56.5 1.2 %collective-permute-done.17.refs_3_ = bf16[128,1024]{1,0:T(8,128)(2,1)S(1)} collective-permute-done((bf16[128,1024]{1,0:T(8,128)(2,1)S(1)}, bf16[128,1024]{1,0:T(8,128)(2,1)S(1)}, u32[]{:S(2)}, u32[]{:S(2)}) %collective-permute-start.17) | collective-permute-done | bytes 262176 | tf_op jit(solution)/shard_map/ppermute | solution.py:565
  57.8 2.5 %collective-permute-start.18 = (bf16[128,1024]{1,0:T(8,128)(2,1)S(1)}, bf16[128,1024]{1,0:T(8,128)(2,1)S(1)}, u32[]{:S(2)}, u32[]{:S(2)}) collective-permute-start(bf16[128,1024]{1,0:T(8,128)(2,1)S(1)} %collective-permute-done.17.refs_3_), channel_id=1, source_target_pairs={{0,8},{8,16},{16,24},{24,28},{28,20},{20,12},{12,4},{4,0},{1,9},{9... | collective-permute-start | bytes 786440 | tf_op jit(solution)/shard_map/ppermute | solution.py:565
  60.3 0.0 collective-permute-done.21.refs_4_
  60.3 1.2 %collective-permute-start.22 = (bf16[128,1024]{1,0:T(8,128)(2,1)S(1)}, bf16[128,1024]{1,0:T(8,128)(2,1)S(1)}, u32[]{:S(2)}, u32[]{:S(2)}) collective-permute-start(bf16[128,1024]{1,0:T(8,128)(2,1)S(1)} %collective-permute-done.21.refs_4_), channel_id=1, source_target_pairs={{8,0},{16,8},{24,16},{28,24},{20,28},{12,20},{4,12},{0,4},{9,1},{1... | collective-permute-start | bytes 786440 | tf_op jit(solution)/shard_map/ppermute | solution.py:566
  61.5 0.2 convert_add_fusion
  61.8 0.0 collective-permute-done.13.refs_1_
  61.8 1.8 %collective-permute-start.10 = (bf16[1,128,1024]{2,1,0:T(8,128)(2,1)S(1)}, bf16[1,128,1024]{2,1,0:T(8,128)(2,1)S(1)}, u32[]{:S(2)}, u32[]{:S(2)}) collective-permute-start(bf16[1,128,1024]{2,1,0:T(8,128)(2,1)S(1)} %slice.34), channel_id=1, source_target_pairs={{0,2},{1,3},{2,0},{3,1},{4,6},{5,7},{6,4},{7,5},{8,10},{9,11},{10,... | collective-permute-start | bytes 786440 | tf_op jit(solution)/shard_map/ppermute | solution.py:339
  63.5 0.1 shard_map.117.cols_ref
  63.6 0.6 collective-permute-done.12.refs_2_
  64.2 1.7 %shard_map.116 = (f32[128,8,128]{2,1,0:T(8,128)}, f32[128,8,128]{2,1,0:T(8,128)}) custom-call(bf16[8,128,128]{2,1,0:T(8,128)(2,1)S(1)} %get-tuple-element.27.kh_ref, bf16[8,128,128]{2,1,0:T(8,128)(2,1)S(1)} %get-tuple-element.28.vh_ref, f32[8,128,128]{2,1,0:T(8,128)S(1)} %get-tuple-element.39.refs_3_.dkl_ref, f32[8,128,128]{2,1,0:T(8,128)S(1)} %get-tuple-element.45.dvl_ref, ...), custom_call_target="tpu_custom_call" | custom-call | flops 67108864 | bytes 2883584 | tf_op jit(solution)/shard_map/pallas_call | solution.py:535
  66.0 1.5 %shard_map.118.refs_2_ = f32[1024,512]{1,0:T(8,128)S(1)} custom-call(bf16[8,128,512]{2,1,0:T(8,128)(2,1)S(1)} %shard_map.117.cols_ref, f32[128,8,128]{2,1,0:T(8,128)} %get-tuple-element.24.after_ref, bf16[128,1024]{1,0:T(8,128)(2,1)S(1)} %shard_map.109.after_ref.att_ref.refs_0_, bf16[128,1024]{1,0:T(8,128)(2,1)S(1)} %collective-permute-done.16.refs_1_, ...), custom_call_target="tpu_custom_call" | custom-call | flops 671088640 | bytes 2097152 | tf_op jit(solution)/shard_map/pallas_call | solution.py:550
  67.5 2.0 %collective-permute-done.18.refs_0_ = bf16[128,1024]{1,0:T(8,128)(2,1)S(1)} collective-permute-done((bf16[128,1024]{1,0:T(8,128)(2,1)S(1)}, bf16[128,1024]{1,0:T(8,128)(2,1)S(1)}, u32[]{:S(2)}, u32[]{:S(2)}) %collective-permute-start.18) | collective-permute-done | bytes 262176 | tf_op jit(solution)/shard_map/ppermute | solution.py:565
  69.5 0.1 collective-permute-start.19
  69.6 2.1 %collective-permute-start.23 = (bf16[64,1024]{1,0:T(8,128)(2,1)S(1)}, bf16[64,1024]{1,0:T(8,128)(2,1)S(1)}, u32[]{:S(2)}, u32[]{:S(2)}) collective-permute-start(bf16[64,1024]{1,0:T(8,128)(2,1)S(1)} %slice.27), channel_id=1, source_target_pairs={{8,0},{16,8},{24,16},{28,24},{20,28},{12,20},{4,12},{0,4},{9,1},{1... | collective-permute-start | bytes 393224 | tf_op jit(solution)/shard_map/ppermute | solution.py:576
  71.6 0.8 fusion.1
  72.4 0.7 shard_map.119.total_ref
  73.1 1.5 %collective-permute-done.19.low_ref = bf16[64,1024]{1,0:T(8,128)(2,1)S(1)} collective-permute-done((bf16[64,1024]{1,0:T(8,128)(2,1)S(1)}, bf16[64,1024]{1,0:T(8,128)(2,1)S(1)}, u32[]{:S(2)}, u32[]{:S(2)}) %collective-permute-start.19) | collective-permute-done | bytes 131104 | tf_op jit(solution)/shard_map/ppermute | solution.py:575
  74.7 0.1 collective-permute-done.23.high_ref
  74.8 1.6 %shard_map.120 = f32[1024,512]{1,0:T(8,128)} custom-call(bf16[8,128,512]{2,1,0:T(8,128)(2,1)S(1)} %shard_map.117.cols_ref, bf16[64,1024]{1,0:T(8,128)(2,1)S(1)} %collective-permute-done.19.low_ref, bf16[64,1024]{1,0:T(8,128)(2,1)S(1)} %collective-permute-done.23.high_ref, f32[1024,512]{1,0:T(8,128)S(1)} %shard_map.119.total_ref, ...), custom_call_target="tpu_custom_call" | custom-call | flops 134217728 | bytes 4194304 | tf_op jit(solution)/shard_map/pallas_call | solution.py:578
  (10 shorter events, 0.1 us)
Async XLA Ops:
  3.1 9.3 %collective-permute-start.3 = (bf16[128,1024]{1,0:T(8,128)(2,1)S(1)}, bf16[128,1024]{1,0:T(8,128)(2,1)S(1)}, u32[]{:S(2)}, u32[]{:S(2)}) collective-permute-start(bf16[128,1024]{1,0:T(8,128)(2,1)S(1)} %get-tuple-element.32.refs_0_), channel_id=1, source_target_pairs={{0,2},{1,3},{2,0},{3,1},{4,6},{5,7},{6,4},{7,5},{8,10},{9,11},{10,... | collective-permute-start | bytes 786440 | tf_op jit(solution)/shard_map/ppermute | solution.py:339
  6.1 7.8 %collective-permute-start = (bf16[8,128,128]{2,1,0:T(8,128)(2,1)S(1)}, bf16[8,128,128]{2,1,0:T(8,128)(2,1)S(1)}, u32[]{:S(2)}, u32[]{:S(2)}) collective-permute-start(bf16[8,128,128]{2,1,0:T(8,128)(2,1)S(1)} %get-tuple-element.31.running_ref), channel_id=1, source_target_pairs={{0,4},{4,0},{8,12},{12,8},{16,20},{20,16},{24,28},{28,24},{1,5},{5... | collective-permute-start | bytes 786440 | tf_op jit(solution)/shard_map/ppermute | solution.py:44
  7.6 12.6 %collective-permute-start.2 = (bf16[128,1024]{1,0:T(8,128)(2,1)S(1)}, bf16[128,1024]{1,0:T(8,128)(2,1)S(1)}, u32[]{:S(2)}, u32[]{:S(2)}) collective-permute-start(bf16[128,1024]{1,0:T(8,128)(2,1)S(1)} %get-tuple-element.32.refs_0_), channel_id=1, source_target_pairs={{0,1},{1,0},{2,3},{3,2},{4,5},{5,4},{6,7},{7,6},{8,9},{9,8},{10,11... | collective-permute-start | bytes 786440 | tf_op jit(solution)/shard_map/ppermute | solution.py:339
  12.4 7.8 %collective-permute-start.4 = (bf16[128,1024]{1,0:T(8,128)(2,1)S(1)}, bf16[128,1024]{1,0:T(8,128)(2,1)S(1)}, u32[]{:S(2)}, u32[]{:S(2)}) collective-permute-start(bf16[128,1024]{1,0:T(8,128)(2,1)S(1)} %shard_map.104), channel_id=1, source_target_pairs={{0,1},{1,0},{2,3},{3,2},{4,5},{5,4},{6,7},{7,6},{8,9},{9,8},{10,11... | collective-permute-start | bytes 786440 | tf_op jit(solution)/shard_map/ppermute | solution.py:339
  13.9 9.1 %collective-permute-start.1 = (bf16[8,128,128]{2,1,0:T(8,128)(2,1)S(1)}, bf16[8,128,128]{2,1,0:T(8,128)(2,1)S(1)}, u32[]{:S(2)}, u32[]{:S(2)}) collective-permute-start(bf16[8,128,128]{2,1,0:T(8,128)(2,1)S(1)} %shard_map.103.refs_6_.running_ref), channel_id=1, source_target_pairs={{0,8},{8,0},{4,12},{12,4},{16,24},{24,16},{20,28},{28,20},{1,9},{9... | collective-permute-start | bytes 786440 | tf_op jit(solution)/shard_map/ppermute | solution.py:44
  15.6 10.9 %collective-permute-start.6 = (bf16[64,1024]{1,0:T(8,128)(2,1)S(1)}, bf16[64,1024]{1,0:T(8,128)(2,1)S(1)}, u32[]{:S(2)}, u32[]{:S(2)}) collective-permute-start(bf16[64,1024]{1,0:T(8,128)(2,1)S(1)} %get-tuple-element.40), channel_id=1, source_target_pairs={{0,0},{1,10},{2,18},{3,24},{4,4},{5,14},{6,22},{7,28},{8,2},{9,8},... | collective-permute-start | bytes 393224 | tf_op jit(solution)/shard_map/ppermute | solution.py:400
  16.3 10.3 %collective-permute-start.7 = (bf16[64,1024]{1,0:T(8,128)(2,1)S(1)}, bf16[64,1024]{1,0:T(8,128)(2,1)S(1)}, u32[]{:S(2)}, u32[]{:S(2)}) collective-permute-start(bf16[64,1024]{1,0:T(8,128)(2,1)S(1)} %slice.23), channel_id=1, source_target_pairs={{2,0},{3,10},{0,18},{1,24},{6,4},{7,14},{4,22},{5,28},{10,2},{11,8... | collective-permute-start | bytes 393224 | tf_op jit(solution)/shard_map/ppermute | solution.py:401
  23.1 15.7 %collective-permute-start.5 = (bf16[8,128,128]{2,1,0:T(8,128)(2,1)S(1)}, bf16[8,128,128]{2,1,0:T(8,128)(2,1)S(1)}, u32[]{:S(2)}, u32[]{:S(2)}) collective-permute-start(bf16[8,128,128]{2,1,0:T(8,128)(2,1)S(1)} %shard_map.106.after_ref), channel_id=1, source_target_pairs={{0,16},{16,0},{4,20},{20,4},{8,24},{24,8},{12,28},{28,12},{1,17},{... | collective-permute-start | bytes 786440 | tf_op jit(solution)/shard_map/ppermute | solution.py:44
  26.5 5.7 %collective-permute-start.8 = (bf16[128,512]{1,0:T(8,128)(2,1)S(1)}, bf16[128,512]{1,0:T(8,128)(2,1)S(1)}, u32[]{:S(2)}, u32[]{:S(2)}) collective-permute-start(bf16[128,512]{1,0:T(8,128)(2,1)S(1)} %get-tuple-element.41.refs_4_), channel_id=1, source_target_pairs={{0,4},{4,0},{8,12},{12,8},{16,20},{20,16},{24,28},{28,24},{1,5},{5... | collective-permute-start | bytes 393224 | tf_op jit(solution)/shard_map/ppermute | solution.py:452
  40.0 15.1 %collective-permute-start.9 = (bf16[2,128,1024]{2,1,0:T(8,128)(2,1)S(1)}, bf16[2,128,1024]{2,1,0:T(8,128)(2,1)S(1)}, u32[]{:S(2)}, u32[]{:S(2)}) collective-permute-start(bf16[2,128,1024]{2,1,0:T(8,128)(2,1)S(1)} %shard_map.114), channel_id=1, source_target_pairs={{0,1},{1,0},{2,3},{3,2},{4,5},{5,4},{6,7},{7,6},{8,9},{9,8},{10,11... | collective-permute-start | bytes 1572872 | tf_op jit(solution)/shard_map/ppermute | solution.py:339
  40.0 8.7 %collective-permute-start.16 = (bf16[128,1024]{1,0:T(8,128)(2,1)S(1)}, bf16[128,1024]{1,0:T(8,128)(2,1)S(1)}, u32[]{:S(2)}, u32[]{:S(2)}) collective-permute-start(bf16[128,1024]{1,0:T(8,128)(2,1)S(1)} %shard_map.109.after_ref.att_ref.refs_0_), channel_id=1, source_target_pairs={{0,8},{8,16},{16,24},{24,28},{28,20},{20,12},{12,4},{4,0},{1,9},{9... | collective-permute-start | bytes 786440 | tf_op jit(solution)/shard_map/ppermute | solution.py:565
  40.2 9.2 %collective-permute-start.20 = (bf16[128,1024]{1,0:T(8,128)(2,1)S(1)}, bf16[128,1024]{1,0:T(8,128)(2,1)S(1)}, u32[]{:S(2)}, u32[]{:S(2)}) collective-permute-start(bf16[128,1024]{1,0:T(8,128)(2,1)S(1)} %shard_map.109.after_ref.att_ref.refs_0_), channel_id=1, source_target_pairs={{8,0},{16,8},{24,16},{28,24},{20,28},{12,20},{4,12},{0,4},{9,1},{1... | collective-permute-start | bytes 786440 | tf_op jit(solution)/shard_map/ppermute | solution.py:566
  42.1 10.7 %collective-permute-start.14 = (bf16[2,128,512]{2,1,0:T(8,128)(2,1)S(1)}, bf16[2,128,512]{2,1,0:T(8,128)(2,1)S(1)}, u32[]{:S(2)}, u32[]{:S(2)}) collective-permute-start(bf16[2,128,512]{2,1,0:T(8,128)(2,1)S(1)} %shard_map.113.refs_0_), channel_id=1, source_target_pairs={{0,2},{1,3},{2,0},{3,1},{4,6},{5,7},{6,4},{7,5},{8,10},{9,11},{10,... | collective-permute-start | bytes 786440 | tf_op jit(solution)/shard_map/ppermute | solution.py:339
  43.9 11.0 %collective-permute-start.11 = (bf16[8,128,128]{2,1,0:T(8,128)(2,1)S(1)}, bf16[8,128,128]{2,1,0:T(8,128)(2,1)S(1)}, u32[]{:S(2)}, u32[]{:S(2)}) collective-permute-start(bf16[8,128,128]{2,1,0:T(8,128)(2,1)S(1)} %shard_map.110.refs_0_), channel_id=1, source_target_pairs={{0,8},{8,0},{4,12},{12,4},{16,24},{24,16},{20,28},{28,20},{1,9},{9... | collective-permute-start | bytes 786440 | tf_op jit(solution)/shard_map/ppermute | solution.py:44
  48.7 9.0 %collective-permute-start.17 = (bf16[128,1024]{1,0:T(8,128)(2,1)S(1)}, bf16[128,1024]{1,0:T(8,128)(2,1)S(1)}, u32[]{:S(2)}, u32[]{:S(2)}) collective-permute-start(bf16[128,1024]{1,0:T(8,128)(2,1)S(1)} %collective-permute-done.16.refs_1_), channel_id=1, source_target_pairs={{0,8},{8,16},{16,24},{24,28},{28,20},{20,12},{12,4},{4,0},{1,9},{9... | collective-permute-start | bytes 786440 | tf_op jit(solution)/shard_map/ppermute | solution.py:565
  49.4 10.9 %collective-permute-start.21 = (bf16[128,1024]{1,0:T(8,128)(2,1)S(1)}, bf16[128,1024]{1,0:T(8,128)(2,1)S(1)}, u32[]{:S(2)}, u32[]{:S(2)}) collective-permute-start(bf16[128,1024]{1,0:T(8,128)(2,1)S(1)} %collective-permute-done.20.refs_2_), channel_id=1, source_target_pairs={{8,0},{16,8},{24,16},{28,24},{20,28},{12,20},{4,12},{0,4},{9,1},{1... | collective-permute-start | bytes 786440 | tf_op jit(solution)/shard_map/ppermute | solution.py:566
  52.8 8.9 %collective-permute-start.13 = (bf16[2,128,512]{2,1,0:T(8,128)(2,1)S(1)}, bf16[2,128,512]{2,1,0:T(8,128)(2,1)S(1)}, u32[]{:S(2)}, u32[]{:S(2)}) collective-permute-start(bf16[2,128,512]{2,1,0:T(8,128)(2,1)S(1)} %shard_map.113.refs_0_), channel_id=1, source_target_pairs={{0,1},{1,0},{2,3},{3,2},{4,5},{5,4},{6,7},{7,6},{8,9},{9,8},{10,11... | collective-permute-start | bytes 786440 | tf_op jit(solution)/shard_map/ppermute | solution.py:339
  54.9 8.6 %collective-permute-start.15 = (bf16[2,128,512]{2,1,0:T(8,128)(2,1)S(1)}, bf16[2,128,512]{2,1,0:T(8,128)(2,1)S(1)}, u32[]{:S(2)}, u32[]{:S(2)}) collective-permute-start(bf16[2,128,512]{2,1,0:T(8,128)(2,1)S(1)} %collective-permute-done.14.refs_2_), channel_id=1, source_target_pairs={{0,1},{1,0},{2,3},{3,2},{4,5},{5,4},{6,7},{7,6},{8,9},{9,8},{10,11... | collective-permute-start | bytes 786440 | tf_op jit(solution)/shard_map/ppermute | solution.py:339
  55.1 9.2 %collective-permute-start.12 = (bf16[8,128,128]{2,1,0:T(8,128)(2,1)S(1)}, bf16[8,128,128]{2,1,0:T(8,128)(2,1)S(1)}, u32[]{:S(2)}, u32[]{:S(2)}) collective-permute-start(bf16[8,128,128]{2,1,0:T(8,128)(2,1)S(1)} %shard_map.115), channel_id=1, source_target_pairs={{0,4},{4,0},{8,12},{12,8},{16,20},{20,16},{24,28},{28,24},{1,5},{5... | collective-permute-start | bytes 786440 | tf_op jit(solution)/shard_map/ppermute | solution.py:44
  57.8 11.7 %collective-permute-start.18 = (bf16[128,1024]{1,0:T(8,128)(2,1)S(1)}, bf16[128,1024]{1,0:T(8,128)(2,1)S(1)}, u32[]{:S(2)}, u32[]{:S(2)}) collective-permute-start(bf16[128,1024]{1,0:T(8,128)(2,1)S(1)} %collective-permute-done.17.refs_3_), channel_id=1, source_target_pairs={{0,8},{8,16},{16,24},{24,28},{28,20},{20,12},{12,4},{4,0},{1,9},{9... | collective-permute-start | bytes 786440 | tf_op jit(solution)/shard_map/ppermute | solution.py:565
  60.3 9.3 %collective-permute-start.22 = (bf16[128,1024]{1,0:T(8,128)(2,1)S(1)}, bf16[128,1024]{1,0:T(8,128)(2,1)S(1)}, u32[]{:S(2)}, u32[]{:S(2)}) collective-permute-start(bf16[128,1024]{1,0:T(8,128)(2,1)S(1)} %collective-permute-done.21.refs_4_), channel_id=1, source_target_pairs={{8,0},{16,8},{24,16},{28,24},{20,28},{12,20},{4,12},{0,4},{9,1},{1... | collective-permute-start | bytes 786440 | tf_op jit(solution)/shard_map/ppermute | solution.py:566
  61.8 9.9 %collective-permute-start.10 = (bf16[1,128,1024]{2,1,0:T(8,128)(2,1)S(1)}, bf16[1,128,1024]{2,1,0:T(8,128)(2,1)S(1)}, u32[]{:S(2)}, u32[]{:S(2)}) collective-permute-start(bf16[1,128,1024]{2,1,0:T(8,128)(2,1)S(1)} %slice.34), channel_id=1, source_target_pairs={{0,2},{1,3},{2,0},{3,1},{4,6},{5,7},{6,4},{7,5},{8,10},{9,11},{10,... | collective-permute-start | bytes 786440 | tf_op jit(solution)/shard_map/ppermute | solution.py:339
  69.5 5.2 %collective-permute-start.19 = (bf16[64,1024]{1,0:T(8,128)(2,1)S(1)}, bf16[64,1024]{1,0:T(8,128)(2,1)S(1)}, u32[]{:S(2)}, u32[]{:S(2)}) collective-permute-start(bf16[64,1024]{1,0:T(8,128)(2,1)S(1)} %slice.26), channel_id=1, source_target_pairs={{0,8},{8,16},{16,24},{24,28},{28,20},{20,12},{12,4},{4,0},{1,9},{9... | collective-permute-start | bytes 393224 | tf_op jit(solution)/shard_map/ppermute | solution.py:575
  69.6 5.2 %collective-permute-start.23 = (bf16[64,1024]{1,0:T(8,128)(2,1)S(1)}, bf16[64,1024]{1,0:T(8,128)(2,1)S(1)}, u32[]{:S(2)}, u32[]{:S(2)}) collective-permute-start(bf16[64,1024]{1,0:T(8,128)(2,1)S(1)} %slice.27), channel_id=1, source_target_pairs={{8,0},{16,8},{24,16},{28,24},{20,28},{12,20},{4,12},{0,4},{9,1},{1... | collective-permute-start | bytes 393224 | tf_op jit(solution)/shard_map/ppermute | solution.py:576

commit v14 on v11

--- a/solution.py
+++ b/solution.py
@@ -50,15 +50,20 @@
 
 def state_kernel(k_hbm, v_hbm, grad_hbm, *refs):
     s_ref, kh_ref, vh_ref, grad_ref, low_ref, k_ref, v_ref, sems = refs
-    copies = [
-        pltpu.make_async_copy(k_hbm, k_ref, sems.at[0]),
-        pltpu.make_async_copy(v_hbm, v_ref, sems.at[1]),
-        pltpu.make_async_copy(grad_hbm, grad_ref, sems.at[2]),
-        pltpu.make_async_copy(grad_hbm.at[pl.ds(0, low_ref.shape[0])], low_ref, sems.at[3]),
+    pieces = (sems.shape[0] - 2) // 2
+    share = k_ref.shape[0] // pieces
+    copies = []
+    for i in range(pieces):
+        at = pl.ds(i * share, share)
+        copies.append(pltpu.make_async_copy(k_hbm.at[at], k_ref.at[at], sems.at[2 + 2 * i]))
+        copies.append(pltpu.make_async_copy(v_hbm.at[at], v_ref.at[at], sems.at[3 + 2 * i]))
+    later = [
+        pltpu.make_async_copy(grad_hbm, grad_ref, sems.at[0]),
+        pltpu.make_async_copy(grad_hbm.at[pl.ds(0, low_ref.shape[0])], low_ref, sems.at[1]),
     ]
+    for copy in copies + later:
+        copy.start()
     for copy in copies:
-        copy.start()
-    for copy in copies[:2]:
         copy.wait()
     for h in range(k_ref.shape[1]):
         k = k_ref[:, h, :].astype(BF)
@@ -66,8 +71,8 @@
         kh_ref[h] = k
         vh_ref[h] = v
         s_ref[h] = mm(k, v, TN).astype(BF)
-    copies[2].wait()
-    copies[3].wait()
+    for copy in later:
+        copy.wait()
 
 
 def weight_of(lam_ref, h, rows):
@@ -329,7 +334,7 @@
         scratch_shapes=[
             pltpu.VMEM(keys.shape, F32),
             pltpu.VMEM(keys.shape, F32),
-            pltpu.SemaphoreType.DMA((4,)),
+            pltpu.SemaphoreType.DMA((10,)),
         ],
         compiler_params=PARAMS,
         cost_estimate=cost(flops_head, 7 * moved_head),

time: 76.5 us -> 76.6 us (level)
  no operation moved by 1% of the time
where the time goes in v14:
time: 76.6 us; the launch traced here: 76.5 us
  starting transfers between devices  31 us (40%)
  waiting for transfers between devices  24 us (31%)
  Pallas kernels  19.6 us (26%)
  other arithmetic  0.95 us (1%)
  between operations  0.87 us (1%)
    ppermute x5, waiting for transfers between devices, across(): return lax.ppermute(block, axis, route)  11.3 us
    ppermute x5, starting transfers between devices, across(): return lax.ppermute(block, axis, route)  8.19 us
    ppermute x3, waiting for transfers between devices, body(): ahead = lax.ppermute(ahead, 'seq', forward)  7.12 us
    ppermute x8, starting transfers between devices, to_group(): return lax.ppermute(block, 'head', [(at, at ^ i) for at in range(heads)])  6.71 us
    ppermute x3, starting transfers between devices, body(): behind = lax.ppermute(behind, 'seq', backward)  4.63 us
    ppermute x1, starting transfers between devices, body(): lax.ppermute(grad_blocks[far][half:], axes, turn_route(far))  3.92 us
    pallas_call x1, Pallas kernels, body(): pl.pallas_call(local_kernel, out_shape=(pltpu.VMEM((heads_dev, rows, rows...  3.66 us
    ppermute x3, starting transfers between devices, body(): ahead = lax.ppermute(ahead, 'seq', forward)  3.2 us
  transfers between devices with their start and end apart: 24, of which 10 were waited for; matrix products, arithmetic and copies ran while one was open for 1% of the time, Pallas kernels for 19%

profile of v14, /device:TPU:0, one launch (start us, length us, event | category | flops | bytes accessed | tf_op | source)
XLA Modules:
  0.0 76.5 jit_solution(6510911276958213880)
XLA Ops:
  0.6 2.6 %shard_map.101 = (bf16[8,128,128]{2,1,0:T(8,128)(2,1)S(1)}, bf16[8,128,128]{2,1,0:T(8,128)(2,1)S(1)}, bf16[8,128,128]{2,1,0:T(8,128)(2,1)S(1)}, bf16[128,1024]{1,0:T(8,128)(2,1)S(1)}, bf16[64,1024]{1,0:T(8,128)(2,1)S(1)}) custom-call(f32[128,8,128]{2,1,0:T(8,128)} %k_hbm.1, f32[128,8,128]{2,1,0:T(8,128)} %v_hbm.1, bf16[128,1024]{1,0:T(8,128)(2,1)} %grad_hbm.1), custom_call_target="tpu_custom_call" | custom-call | flops 33554432 | bytes 1835008 | tf_op jit(solution)/shard_map/pallas_call | solution.py:329
  3.2 3.0 %collective-permute-start.3 = (bf16[128,1024]{1,0:T(8,128)(2,1)S(1)}, bf16[128,1024]{1,0:T(8,128)(2,1)S(1)}, u32[]{:S(2)}, u32[]{:S(2)}) collective-permute-start(bf16[128,1024]{1,0:T(8,128)(2,1)S(1)} %get-tuple-element.32.refs_0_), channel_id=1, source_target_pairs={{0,2},{1,3},{2,0},{3,1},{4,6},{5,7},{6,4},{7,5},{8,10},{9,11},{10,... | collective-permute-start | bytes 786440 | tf_op jit(solution)/shard_map/ppermute | solution.py:344
  6.2 1.5 %collective-permute-start = (bf16[8,128,128]{2,1,0:T(8,128)(2,1)S(1)}, bf16[8,128,128]{2,1,0:T(8,128)(2,1)S(1)}, u32[]{:S(2)}, u32[]{:S(2)}) collective-permute-start(bf16[8,128,128]{2,1,0:T(8,128)(2,1)S(1)} %get-tuple-element.31.running_ref), channel_id=1, source_target_pairs={{0,4},{4,0},{8,12},{12,8},{16,20},{20,16},{24,28},{28,24},{1,5},{5... | collective-permute-start | bytes 786440 | tf_op jit(solution)/shard_map/ppermute | solution.py:44
  7.8 0.0 collective-permute-start.2
  7.8 3.7 %shard_map.102 = (bf16[8,128,128]{2,1,0:T(8,128)(2,1)S(1)}, f32[8,128,128]{2,1,0:T(8,128)S(1)}, bf16[8,128,128]{2,1,0:T(8,128)(2,1)S(1)}, bf16[3,8,128,128]{3,2,...) custom-call(f32[128,8,128]{2,1,0:T(8,128)} %q_hbm.1, ...), custom_call_target="tpu_custom_call" | custom-call | flops 67108864 | bytes 3145728 | tf_op jit(solution)/shard_map/pallas_call | solution.py:353
  11.4 1.1 %collective-permute-done.3.block_ref.refs_2_ = bf16[128,1024]{1,0:T(8,128)(2,1)S(1)} collective-permute-done((bf16[128,1024]{1,0:T(8,128)(2,1)S(1)}, bf16[128,1024]{1,0:T(8,128)(2,1)S(1)}, u32[]{:S(2)}, u32[]{:S(2)}) %collective-permute-start.3) | collective-permute-done | bytes 262176 | tf_op jit(solution)/shard_map/ppermute | solution.py:344
  12.6 0.1 collective-permute-start.4
  12.6 1.4 %collective-permute-done.arrived_ref.refs_0_ = bf16[8,128,128]{2,1,0:T(8,128)(2,1)S(1)} collective-permute-done((bf16[8,128,128]{2,1,0:T(8,128)(2,1)S(1)}, bf16[8,128,128]{2,1,0:T(8,128)(2,1)S(1)}, u32[]{:S(2)}, u32[]{:S(2)}) %collective-permute-start) | collective-permute-done | bytes 262176 | tf_op jit(solution)/shard_map/ppermute | solution.py:44
  14.0 0.1 shard_map.103.refs_6_.running_ref
  14.1 1.6 %collective-permute-start.1 = (bf16[8,128,128]{2,1,0:T(8,128)(2,1)S(1)}, bf16[8,128,128]{2,1,0:T(8,128)(2,1)S(1)}, u32[]{:S(2)}, u32[]{:S(2)}) collective-permute-start(bf16[8,128,128]{2,1,0:T(8,128)(2,1)S(1)} %shard_map.103.refs_6_.running_ref), channel_id=1, source_target_pairs={{0,8},{8,0},{4,12},{12,4},{16,24},{24,16},{20,28},{28,20},{1,9},{9... | collective-permute-start | bytes 786440 | tf_op jit(solution)/shard_map/ppermute | solution.py:44
  15.7 0.7 collective-permute-start.6
  16.4 3.9 %collective-permute-start.7 = (bf16[64,1024]{1,0:T(8,128)(2,1)S(1)}, bf16[64,1024]{1,0:T(8,128)(2,1)S(1)}, u32[]{:S(2)}, u32[]{:S(2)}) collective-permute-start(bf16[64,1024]{1,0:T(8,128)(2,1)S(1)} %slice.23), channel_id=1, source_target_pairs={{2,0},{3,10},{0,18},{1,24},{6,4},{7,14},{4,22},{5,28},{10,2},{11,8... | collective-permute-start | bytes 393224 | tf_op jit(solution)/shard_map/ppermute | solution.py:406
  20.3 0.0 collective-permute-done.2.refs_1_
  20.3 0.0 collective-permute-done.4.refs_3_
  20.3 2.8 %shard_map.105 = (bf16[1024,128]{1,0:T(8,128)(2,1)S(1)}, bf16[8,128,128]{2,1,0:T(8,128)(2,1)S(1)}, bf16[8,128,128]{2,1,0:T(8,128)(2,1)S(1)}, bf16[8,128,128]{2,1,0:T(8,128)(2,1)S(1)}) custom-call(bf16[128,1024]{1,0:T(8,128)(2,1)S(1)} %get-tuple-element.32.refs_0_, bf16[128,1024]{1,0:T(8,128)(2,1)S(1)} %collective-permute-done.2.refs_1_, ...), custom_call_target="tpu_custom_call" | custom-call | flops 1073741824 | bytes 8388608 | tf_op jit(solution)/shard_map/pallas_call | solution.py:423
  23.1 0.0 collective-permute-done.1.arrived_ref.refs_1_
  23.2 0.1 shard_map.106.after_ref
  23.2 3.4 %collective-permute-start.5 = (bf16[8,128,128]{2,1,0:T(8,128)(2,1)S(1)}, bf16[8,128,128]{2,1,0:T(8,128)(2,1)S(1)}, u32[]{:S(2)}, u32[]{:S(2)}) collective-permute-start(bf16[8,128,128]{2,1,0:T(8,128)(2,1)S(1)} %shard_map.106.after_ref), channel_id=1, source_target_pairs={{0,16},{16,0},{4,20},{20,4},{8,24},{24,8},{12,28},{28,12},{1,17},{... | collective-permute-start | bytes 786440 | tf_op jit(solution)/shard_map/ppermute | solution.py:44
  26.6 0.0 collective-permute-done.6.low_ref
  26.6 0.0 collective-permute-done.7.high_ref
  26.7 1.6 %collective-permute-start.8 = (bf16[128,512]{1,0:T(8,128)(2,1)S(1)}, bf16[128,512]{1,0:T(8,128)(2,1)S(1)}, u32[]{:S(2)}, u32[]{:S(2)}) collective-permute-start(bf16[128,512]{1,0:T(8,128)(2,1)S(1)} %get-tuple-element.41.refs_4_), channel_id=1, source_target_pairs={{0,4},{4,0},{8,12},{12,8},{16,20},{20,16},{24,28},{28,24},{1,5},{5... | collective-permute-start | bytes 393224 | tf_op jit(solution)/shard_map/ppermute | solution.py:457
  28.3 1.3 %shard_map.107 = (f32[8,128,128]{2,1,0:T(8,128)S(1)}, f32[8,128,128]{2,1,0:T(8,128)S(1)}, f32[8,128,128]{2,1,0:T(8,128)S(1)}) custom-call(bf16[1024,128]{1,0:T(8,128)(2,1)S(1)} %get-tuple-element.35.gt_ref, bf16[8,128,128]{2,1,0:T(8,128)(2,1)S(1)} %get-tuple-element.36.qh_ref, bf16[8,128,128]{2,1,0:T(8,128)(2,1)S(1)} %get-tuple-element.27.kh_ref, ...), custom_call_target="tpu_custom_call" | custom-call | flops 201326592 | bytes 3670016 | tf_op jit(solution)/shard_map/pallas_call | solution.py:479
  29.6 2.8 %collective-permute-done.8.refs_1_ = bf16[128,512]{1,0:T(8,128)(2,1)S(1)} collective-permute-done((bf16[128,512]{1,0:T(8,128)(2,1)S(1)}, bf16[128,512]{1,0:T(8,128)(2,1)S(1)}, u32[]{:S(2)}, u32[]{:S(2)}) %collective-permute-start.8) | collective-permute-done | bytes 131104 | tf_op jit(solution)/shard_map/ppermute | solution.py:457
  32.4 6.6 %collective-permute-done.5.refs_2_.refs_0_.state_ref = bf16[8,128,128]{2,1,0:T(8,128)(2,1)S(1)} collective-permute-done((bf16[8,128,128]{2,1,0:T(8,128)(2,1)S(1)}, bf16[8,128,128]{2,1,0:T(8,128)(2,1)S(1)}, u32[]{:S(2)}, u32[]{:S(2)}) %collective-permute-start.5) | collective-permute-done | bytes 262176 | tf_op jit(solution)/shard_map/ppermute | solution.py:44
  39.0 0.4 shard_map.109.after_ref.att_ref.refs_0_
  39.4 0.7 shard_map.113
  40.1 0.1 collective-permute-start.9
  40.2 0.1 collective-permute-start.16
  40.3 2.0 %collective-permute-start.20 = (bf16[128,1024]{1,0:T(8,128)(2,1)S(1)}, bf16[128,1024]{1,0:T(8,128)(2,1)S(1)}, u32[]{:S(2)}, u32[]{:S(2)}) collective-permute-start(bf16[128,1024]{1,0:T(8,128)(2,1)S(1)} %shard_map.109.after_ref.att_ref.refs_0_), channel_id=1, source_target_pairs={{8,0},{16,8},{24,16},{28,24},{20,28},{12,20},{4,12},{0,4},{9,1},{1... | collective-permute-start | bytes 786440 | tf_op jit(solution)/shard_map/ppermute | solution.py:571
  42.2 1.7 %collective-permute-start.14 = (bf16[2,128,512]{2,1,0:T(8,128)(2,1)S(1)}, bf16[2,128,512]{2,1,0:T(8,128)(2,1)S(1)}, u32[]{:S(2)}, u32[]{:S(2)}) collective-permute-start(bf16[2,128,512]{2,1,0:T(8,128)(2,1)S(1)} %shard_map.112.after_ref.refs_0_), channel_id=1, source_target_pairs={{0,2},{1,3},{2,0},{3,1},{4,6},{5,7},{6,4},{7,5},{8,10},{9,11},{10,... | collective-permute-start | bytes 786440 | tf_op jit(solution)/shard_map/ppermute | solution.py:344
  44.0 0.1 shard_map.110.after_ref
  44.1 0.2 collective-permute-start.11
  44.2 4.7 %collective-permute-done.16.refs_1_ = bf16[128,1024]{1,0:T(8,128)(2,1)S(1)} collective-permute-done((bf16[128,1024]{1,0:T(8,128)(2,1)S(1)}, bf16[128,1024]{1,0:T(8,128)(2,1)S(1)}, u32[]{:S(2)}, u32[]{:S(2)}) %collective-permute-start.16) | collective-permute-done | bytes 262176 | tf_op jit(solution)/shard_map/ppermute | solution.py:570
  48.9 0.6 collective-permute-start.17
  49.5 0.0 collective-permute-done.20.refs_2_
  49.5 1.4 %collective-permute-start.21 = (bf16[128,1024]{1,0:T(8,128)(2,1)S(1)}, bf16[128,1024]{1,0:T(8,128)(2,1)S(1)}, u32[]{:S(2)}, u32[]{:S(2)}) collective-permute-start(bf16[128,1024]{1,0:T(8,128)(2,1)S(1)} %collective-permute-done.20.refs_2_), channel_id=1, source_target_pairs={{8,0},{16,8},{24,16},{28,24},{20,28},{12,20},{4,12},{0,4},{9,1},{1... | collective-permute-start | bytes 786440 | tf_op jit(solution)/shard_map/ppermute | solution.py:571
  50.9 0.7 shard_map.111
  51.6 0.0 collective-permute-done.14.refs_2_
  51.6 0.1 collective-permute-start.13
  51.7 3.3 %collective-permute-done.11.refs_1_ = bf16[8,128,128]{2,1,0:T(8,128)(2,1)S(1)} collective-permute-done((bf16[8,128,128]{2,1,0:T(8,128)(2,1)S(1)}, bf16[8,128,128]{2,1,0:T(8,128)(2,1)S(1)}, u32[]{:S(2)}, u32[]{:S(2)}) %collective-permute-start.11) | collective-permute-done | bytes 262176 | tf_op jit(solution)/shard_map/ppermute | solution.py:44
  55.0 0.0 collective-permute-start.15
  55.0 0.1 shard_map.115
  55.2 0.0 collective-permute-done.9
  55.2 1.5 %collective-permute-start.12 = (bf16[8,128,128]{2,1,0:T(8,128)(2,1)S(1)}, bf16[8,128,128]{2,1,0:T(8,128)(2,1)S(1)}, u32[]{:S(2)}, u32[]{:S(2)}) collective-permute-start(bf16[8,128,128]{2,1,0:T(8,128)(2,1)S(1)} %shard_map.115), channel_id=1, source_target_pairs={{0,4},{4,0},{8,12},{12,8},{16,20},{20,16},{24,28},{28,24},{1,5},{5... | collective-permute-start | bytes 786440 | tf_op jit(solution)/shard_map/ppermute | solution.py:44
  56.7 1.2 %collective-permute-done.17.refs_3_ = bf16[128,1024]{1,0:T(8,128)(2,1)S(1)} collective-permute-done((bf16[128,1024]{1,0:T(8,128)(2,1)S(1)}, bf16[128,1024]{1,0:T(8,128)(2,1)S(1)}, u32[]{:S(2)}, u32[]{:S(2)}) %collective-permute-start.17) | collective-permute-done | bytes 262176 | tf_op jit(solution)/shard_map/ppermute | solution.py:570
  57.9 2.5 %collective-permute-start.18 = (bf16[128,1024]{1,0:T(8,128)(2,1)S(1)}, bf16[128,1024]{1,0:T(8,128)(2,1)S(1)}, u32[]{:S(2)}, u32[]{:S(2)}) collective-permute-start(bf16[128,1024]{1,0:T(8,128)(2,1)S(1)} %collective-permute-done.17.refs_3_), channel_id=1, source_target_pairs={{0,8},{8,16},{16,24},{24,28},{28,20},{20,12},{12,4},{4,0},{1,9},{9... | collective-permute-start | bytes 786440 | tf_op jit(solution)/shard_map/ppermute | solution.py:570
  60.4 1.2 %collective-permute-start.22 = (bf16[128,1024]{1,0:T(8,128)(2,1)S(1)}, bf16[128,1024]{1,0:T(8,128)(2,1)S(1)}, u32[]{:S(2)}, u32[]{:S(2)}) collective-permute-start(bf16[128,1024]{1,0:T(8,128)(2,1)S(1)} %collective-permute-done.21.refs_4_), channel_id=1, source_target_pairs={{8,0},{16,8},{24,16},{28,24},{20,28},{12,20},{4,12},{0,4},{9,1},{1... | collective-permute-start | bytes 786440 | tf_op jit(solution)/shard_map/ppermute | solution.py:571
  61.6 0.2 convert_add_fusion
  61.9 0.0 collective-permute-done.13.refs_1_
  61.9 1.8 %collective-permute-start.10 = (bf16[1,128,1024]{2,1,0:T(8,128)(2,1)S(1)}, bf16[1,128,1024]{2,1,0:T(8,128)(2,1)S(1)}, u32[]{:S(2)}, u32[]{:S(2)}) collective-permute-start(bf16[1,128,1024]{2,1,0:T(8,128)(2,1)S(1)} %slice.34), channel_id=1, source_target_pairs={{0,2},{1,3},{2,0},{3,1},{4,6},{5,7},{6,4},{7,5},{8,10},{9,11},{10,... | collective-permute-start | bytes 786440 | tf_op jit(solution)/shard_map/ppermute | solution.py:344
  63.7 1.3 %shard_map.114 = f32[128,8,128]{2,1,0:T(8,128)} custom-call(bf16[1024,128]{1,0:T(8,128)(2,1)S(1)} %get-tuple-element.35.gt_ref, f32[5,8,128]{2,1,0:T(8,128)S(1)} %get-tuple-element.38.lam_ref, f32[8,128,128]{2,1,0:T(8,128)S(1)} %get-tuple-element.44.dql_ref, bf16[8,128,128]{2,1,0:T(8,128)(2,1)S(1)} %collective-permute-done.5.refs_2_.refs_0_.state_ref, ...), custom_call_target="tpu_custom_call" | custom-call | flops 33554432 | bytes 1572864 | tf_op jit(solution)/shard_map/pallas_call | solution.py:511
  65.0 0.0 collective-permute-done.15.refs_3_
  65.0 0.1 shard_map.117.cols_ref
  65.1 0.0 collective-permute-done.12.refs_2_
  65.1 1.7 %shard_map.116 = (f32[128,8,128]{2,1,0:T(8,128)}, f32[128,8,128]{2,1,0:T(8,128)}) custom-call(bf16[8,128,128]{2,1,0:T(8,128)(2,1)S(1)} %get-tuple-element.27.kh_ref, bf16[8,128,128]{2,1,0:T(8,128)(2,1)S(1)} %get-tuple-element.28.vh_ref, f32[8,128,128]{2,1,0:T(8,128)S(1)} %get-tuple-element.39.refs_3_.dkl_ref, f32[8,128,128]{2,1,0:T(8,128)S(1)} %get-tuple-element.45.dvl_ref, ...), custom_call_target="tpu_custom_call" | custom-call | flops 67108864 | bytes 2883584 | tf_op jit(solution)/shard_map/pallas_call | solution.py:540
  66.8 1.5 %shard_map.118.refs_2_ = f32[1024,512]{1,0:T(8,128)S(1)} custom-call(bf16[8,128,512]{2,1,0:T(8,128)(2,1)S(1)} %shard_map.117.cols_ref, f32[128,8,128]{2,1,0:T(8,128)} %get-tuple-element.24.after_ref, bf16[128,1024]{1,0:T(8,128)(2,1)S(1)} %shard_map.109.after_ref.att_ref.refs_0_, bf16[128,1024]{1,0:T(8,128)(2,1)S(1)} %collective-permute-done.16.refs_1_, ...), custom_call_target="tpu_custom_call" | custom-call | flops 671088640 | bytes 2097152 | tf_op jit(solution)/shard_map/pallas_call | solution.py:555
  68.4 1.2 %collective-permute-done.18.refs_0_ = bf16[128,1024]{1,0:T(8,128)(2,1)S(1)} collective-permute-done((bf16[128,1024]{1,0:T(8,128)(2,1)S(1)}, bf16[128,1024]{1,0:T(8,128)(2,1)S(1)}, u32[]{:S(2)}, u32[]{:S(2)}) %collective-permute-start.18) | collective-permute-done | bytes 262176 | tf_op jit(solution)/shard_map/ppermute | solution.py:570
  69.6 0.1 collective-permute-start.19
  69.7 2.1 %collective-permute-start.23 = (bf16[64,1024]{1,0:T(8,128)(2,1)S(1)}, bf16[64,1024]{1,0:T(8,128)(2,1)S(1)}, u32[]{:S(2)}, u32[]{:S(2)}) collective-permute-start(bf16[64,1024]{1,0:T(8,128)(2,1)S(1)} %slice.27), channel_id=1, source_target_pairs={{8,0},{16,8},{24,16},{28,24},{20,28},{12,20},{4,12},{0,4},{9,1},{1... | collective-permute-start | bytes 393224 | tf_op jit(solution)/shard_map/ppermute | solution.py:581
  71.7 0.8 fusion.1
  72.5 0.7 shard_map.119.total_ref
  73.2 1.5 %collective-permute-done.19.low_ref = bf16[64,1024]{1,0:T(8,128)(2,1)S(1)} collective-permute-done((bf16[64,1024]{1,0:T(8,128)(2,1)S(1)}, bf16[64,1024]{1,0:T(8,128)(2,1)S(1)}, u32[]{:S(2)}, u32[]{:S(2)}) %collective-permute-start.19) | collective-permute-done | bytes 131104 | tf_op jit(solution)/shard_map/ppermute | solution.py:580
  74.8 0.1 collective-permute-done.23.high_ref
  74.9 1.6 %shard_map.120 = f32[1024,512]{1,0:T(8,128)} custom-call(bf16[8,128,512]{2,1,0:T(8,128)(2,1)S(1)} %shard_map.117.cols_ref, bf16[64,1024]{1,0:T(8,128)(2,1)S(1)} %collective-permute-done.19.low_ref, bf16[64,1024]{1,0:T(8,128)(2,1)S(1)} %collective-permute-done.23.high_ref, f32[1024,512]{1,0:T(8,128)S(1)} %shard_map.119.total_ref, ...), custom_call_target="tpu_custom_call" | custom-call | flops 134217728 | bytes 4194304 | tf_op jit(solution)/shard_map/pallas_call | solution.py:583
  (10 shorter events, 0.1 us)
Async XLA Ops:
  3.2 9.3 %collective-permute-start.3 = (bf16[128,1024]{1,0:T(8,128)(2,1)S(1)}, bf16[128,1024]{1,0:T(8,128)(2,1)S(1)}, u32[]{:S(2)}, u32[]{:S(2)}) collective-permute-start(bf16[128,1024]{1,0:T(8,128)(2,1)S(1)} %get-tuple-element.32.refs_0_), channel_id=1, source_target_pairs={{0,2},{1,3},{2,0},{3,1},{4,6},{5,7},{6,4},{7,5},{8,10},{9,11},{10,... | collective-permute-start | bytes 786440 | tf_op jit(solution)/shard_map/ppermute | solution.py:344
  6.2 7.8 %collective-permute-start = (bf16[8,128,128]{2,1,0:T(8,128)(2,1)S(1)}, bf16[8,128,128]{2,1,0:T(8,128)(2,1)S(1)}, u32[]{:S(2)}, u32[]{:S(2)}) collective-permute-start(bf16[8,128,128]{2,1,0:T(8,128)(2,1)S(1)} %get-tuple-element.31.running_ref), channel_id=1, source_target_pairs={{0,4},{4,0},{8,12},{12,8},{16,20},{20,16},{24,28},{28,24},{1,5},{5... | collective-permute-start | bytes 786440 | tf_op jit(solution)/shard_map/ppermute | solution.py:44
  7.8 12.6 %collective-permute-start.2 = (bf16[128,1024]{1,0:T(8,128)(2,1)S(1)}, bf16[128,1024]{1,0:T(8,128)(2,1)S(1)}, u32[]{:S(2)}, u32[]{:S(2)}) collective-permute-start(bf16[128,1024]{1,0:T(8,128)(2,1)S(1)} %get-tuple-element.32.refs_0_), channel_id=1, source_target_pairs={{0,1},{1,0},{2,3},{3,2},{4,5},{5,4},{6,7},{7,6},{8,9},{9,8},{10,11... | collective-permute-start | bytes 786440 | tf_op jit(solution)/shard_map/ppermute | solution.py:344
  12.6 7.8 %collective-permute-start.4 = (bf16[128,1024]{1,0:T(8,128)(2,1)S(1)}, bf16[128,1024]{1,0:T(8,128)(2,1)S(1)}, u32[]{:S(2)}, u32[]{:S(2)}) collective-permute-start(bf16[128,1024]{1,0:T(8,128)(2,1)S(1)} %shard_map.104), channel_id=1, source_target_pairs={{0,1},{1,0},{2,3},{3,2},{4,5},{5,4},{6,7},{7,6},{8,9},{9,8},{10,11... | collective-permute-start | bytes 786440 | tf_op jit(solution)/shard_map/ppermute | solution.py:344
  14.1 9.1 %collective-permute-start.1 = (bf16[8,128,128]{2,1,0:T(8,128)(2,1)S(1)}, bf16[8,128,128]{2,1,0:T(8,128)(2,1)S(1)}, u32[]{:S(2)}, u32[]{:S(2)}) collective-permute-start(bf16[8,128,128]{2,1,0:T(8,128)(2,1)S(1)} %shard_map.103.refs_6_.running_ref), channel_id=1, source_target_pairs={{0,8},{8,0},{4,12},{12,4},{16,24},{24,16},{20,28},{28,20},{1,9},{9... | collective-permute-start | bytes 786440 | tf_op jit(solution)/shard_map/ppermute | solution.py:44
  15.7 10.9 %collective-permute-start.6 = (bf16[64,1024]{1,0:T(8,128)(2,1)S(1)}, bf16[64,1024]{1,0:T(8,128)(2,1)S(1)}, u32[]{:S(2)}, u32[]{:S(2)}) collective-permute-start(bf16[64,1024]{1,0:T(8,128)(2,1)S(1)} %get-tuple-element.40), channel_id=1, source_target_pairs={{0,0},{1,10},{2,18},{3,24},{4,4},{5,14},{6,22},{7,28},{8,2},{9,8},... | collective-permute-start | bytes 393224 | tf_op jit(solution)/shard_map/ppermute | solution.py:405
  16.4 10.3 %collective-permute-start.7 = (bf16[64,1024]{1,0:T(8,128)(2,1)S(1)}, bf16[64,1024]{1,0:T(8,128)(2,1)S(1)}, u32[]{:S(2)}, u32[]{:S(2)}) collective-permute-start(bf16[64,1024]{1,0:T(8,128)(2,1)S(1)} %slice.23), channel_id=1, source_target_pairs={{2,0},{3,10},{0,18},{1,24},{6,4},{7,14},{4,22},{5,28},{10,2},{11,8... | collective-permute-start | bytes 393224 | tf_op jit(solution)/shard_map/ppermute | solution.py:406
  23.2 15.7 %collective-permute-start.5 = (bf16[8,128,128]{2,1,0:T(8,128)(2,1)S(1)}, bf16[8,128,128]{2,1,0:T(8,128)(2,1)S(1)}, u32[]{:S(2)}, u32[]{:S(2)}) collective-permute-start(bf16[8,128,128]{2,1,0:T(8,128)(2,1)S(1)} %shard_map.106.after_ref), channel_id=1, source_target_pairs={{0,16},{16,0},{4,20},{20,4},{8,24},{24,8},{12,28},{28,12},{1,17},{... | collective-permute-start | bytes 786440 | tf_op jit(solution)/shard_map/ppermute | solution.py:44
  26.7 5.7 %collective-permute-start.8 = (bf16[128,512]{1,0:T(8,128)(2,1)S(1)}, bf16[128,512]{1,0:T(8,128)(2,1)S(1)}, u32[]{:S(2)}, u32[]{:S(2)}) collective-permute-start(bf16[128,512]{1,0:T(8,128)(2,1)S(1)} %get-tuple-element.41.refs_4_), channel_id=1, source_target_pairs={{0,4},{4,0},{8,12},{12,8},{16,20},{20,16},{24,28},{28,24},{1,5},{5... | collective-permute-start | bytes 393224 | tf_op jit(solution)/shard_map/ppermute | solution.py:457
  40.1 15.1 %collective-permute-start.9 = (bf16[2,128,1024]{2,1,0:T(8,128)(2,1)S(1)}, bf16[2,128,1024]{2,1,0:T(8,128)(2,1)S(1)}, u32[]{:S(2)}, u32[]{:S(2)}) collective-permute-start(bf16[2,128,1024]{2,1,0:T(8,128)(2,1)S(1)} %shard_map.113), channel_id=1, source_target_pairs={{0,1},{1,0},{2,3},{3,2},{4,5},{5,4},{6,7},{7,6},{8,9},{9,8},{10,11... | collective-permute-start | bytes 1572872 | tf_op jit(solution)/shard_map/ppermute | solution.py:344
  40.2 8.7 %collective-permute-start.16 = (bf16[128,1024]{1,0:T(8,128)(2,1)S(1)}, bf16[128,1024]{1,0:T(8,128)(2,1)S(1)}, u32[]{:S(2)}, u32[]{:S(2)}) collective-permute-start(bf16[128,1024]{1,0:T(8,128)(2,1)S(1)} %shard_map.109.after_ref.att_ref.refs_0_), channel_id=1, source_target_pairs={{0,8},{8,16},{16,24},{24,28},{28,20},{20,12},{12,4},{4,0},{1,9},{9... | collective-permute-start | bytes 786440 | tf_op jit(solution)/shard_map/ppermute | solution.py:570
  40.3 9.2 %collective-permute-start.20 = (bf16[128,1024]{1,0:T(8,128)(2,1)S(1)}, bf16[128,1024]{1,0:T(8,128)(2,1)S(1)}, u32[]{:S(2)}, u32[]{:S(2)}) collective-permute-start(bf16[128,1024]{1,0:T(8,128)(2,1)S(1)} %shard_map.109.after_ref.att_ref.refs_0_), channel_id=1, source_target_pairs={{8,0},{16,8},{24,16},{28,24},{20,28},{12,20},{4,12},{0,4},{9,1},{1... | collective-permute-start | bytes 786440 | tf_op jit(solution)/shard_map/ppermute | solution.py:571
  42.2 9.4 %collective-permute-start.14 = (bf16[2,128,512]{2,1,0:T(8,128)(2,1)S(1)}, bf16[2,128,512]{2,1,0:T(8,128)(2,1)S(1)}, u32[]{:S(2)}, u32[]{:S(2)}) collective-permute-start(bf16[2,128,512]{2,1,0:T(8,128)(2,1)S(1)} %shard_map.112.after_ref.refs_0_), channel_id=1, source_target_pairs={{0,2},{1,3},{2,0},{3,1},{4,6},{5,7},{6,4},{7,5},{8,10},{9,11},{10,... | collective-permute-start | bytes 786440 | tf_op jit(solution)/shard_map/ppermute | solution.py:344
  44.1 11.0 %collective-permute-start.11 = (bf16[8,128,128]{2,1,0:T(8,128)(2,1)S(1)}, bf16[8,128,128]{2,1,0:T(8,128)(2,1)S(1)}, u32[]{:S(2)}, u32[]{:S(2)}) collective-permute-start(bf16[8,128,128]{2,1,0:T(8,128)(2,1)S(1)} %shard_map.110.after_ref), channel_id=1, source_target_pairs={{0,8},{8,0},{4,12},{12,4},{16,24},{24,16},{20,28},{28,20},{1,9},{9... | collective-permute-start | bytes 786440 | tf_op jit(solution)/shard_map/ppermute | solution.py:44
  48.9 9.0 %collective-permute-start.17 = (bf16[128,1024]{1,0:T(8,128)(2,1)S(1)}, bf16[128,1024]{1,0:T(8,128)(2,1)S(1)}, u32[]{:S(2)}, u32[]{:S(2)}) collective-permute-start(bf16[128,1024]{1,0:T(8,128)(2,1)S(1)} %collective-permute-done.16.refs_1_), channel_id=1, source_target_pairs={{0,8},{8,16},{16,24},{24,28},{28,20},{20,12},{12,4},{4,0},{1,9},{9... | collective-permute-start | bytes 786440 | tf_op jit(solution)/shard_map/ppermute | solution.py:570
  49.5 10.9 %collective-permute-start.21 = (bf16[128,1024]{1,0:T(8,128)(2,1)S(1)}, bf16[128,1024]{1,0:T(8,128)(2,1)S(1)}, u32[]{:S(2)}, u32[]{:S(2)}) collective-permute-start(bf16[128,1024]{1,0:T(8,128)(2,1)S(1)} %collective-permute-done.20.refs_2_), channel_id=1, source_target_pairs={{8,0},{16,8},{24,16},{28,24},{20,28},{12,20},{4,12},{0,4},{9,1},{1... | collective-permute-start | bytes 786440 | tf_op jit(solution)/shard_map/ppermute | solution.py:571
  51.6 10.2 %collective-permute-start.13 = (bf16[2,128,512]{2,1,0:T(8,128)(2,1)S(1)}, bf16[2,128,512]{2,1,0:T(8,128)(2,1)S(1)}, u32[]{:S(2)}, u32[]{:S(2)}) collective-permute-start(bf16[2,128,512]{2,1,0:T(8,128)(2,1)S(1)} %shard_map.112.after_ref.refs_0_), channel_id=1, source_target_pairs={{0,1},{1,0},{2,3},{3,2},{4,5},{5,4},{6,7},{7,6},{8,9},{9,8},{10,11... | collective-permute-start | bytes 786440 | tf_op jit(solution)/shard_map/ppermute | solution.py:344
  55.0 9.9 %collective-permute-start.15 = (bf16[2,128,512]{2,1,0:T(8,128)(2,1)S(1)}, bf16[2,128,512]{2,1,0:T(8,128)(2,1)S(1)}, u32[]{:S(2)}, u32[]{:S(2)}) collective-permute-start(bf16[2,128,512]{2,1,0:T(8,128)(2,1)S(1)} %collective-permute-done.14.refs_2_), channel_id=1, source_target_pairs={{0,1},{1,0},{2,3},{3,2},{4,5},{5,4},{6,7},{7,6},{8,9},{9,8},{10,11... | collective-permute-start | bytes 786440 | tf_op jit(solution)/shard_map/ppermute | solution.py:344
  55.2 9.9 %collective-permute-start.12 = (bf16[8,128,128]{2,1,0:T(8,128)(2,1)S(1)}, bf16[8,128,128]{2,1,0:T(8,128)(2,1)S(1)}, u32[]{:S(2)}, u32[]{:S(2)}) collective-permute-start(bf16[8,128,128]{2,1,0:T(8,128)(2,1)S(1)} %shard_map.115), channel_id=1, source_target_pairs={{0,4},{4,0},{8,12},{12,8},{16,20},{20,16},{24,28},{28,24},{1,5},{5... | collective-permute-start | bytes 786440 | tf_op jit(solution)/shard_map/ppermute | solution.py:44
  57.9 11.7 %collective-permute-start.18 = (bf16[128,1024]{1,0:T(8,128)(2,1)S(1)}, bf16[128,1024]{1,0:T(8,128)(2,1)S(1)}, u32[]{:S(2)}, u32[]{:S(2)}) collective-permute-start(bf16[128,1024]{1,0:T(8,128)(2,1)S(1)} %collective-permute-done.17.refs_3_), channel_id=1, source_target_pairs={{0,8},{8,16},{16,24},{24,28},{28,20},{20,12},{12,4},{4,0},{1,9},{9... | collective-permute-start | bytes 786440 | tf_op jit(solution)/shard_map/ppermute | solution.py:570
  60.4 9.3 %collective-permute-start.22 = (bf16[128,1024]{1,0:T(8,128)(2,1)S(1)}, bf16[128,1024]{1,0:T(8,128)(2,1)S(1)}, u32[]{:S(2)}, u32[]{:S(2)}) collective-permute-start(bf16[128,1024]{1,0:T(8,128)(2,1)S(1)} %collective-permute-done.21.refs_4_), channel_id=1, source_target_pairs={{8,0},{16,8},{24,16},{28,24},{20,28},{12,20},{4,12},{0,4},{9,1},{1... | collective-permute-start | bytes 786440 | tf_op jit(solution)/shard_map/ppermute | solution.py:571
  61.9 9.9 %collective-permute-start.10 = (bf16[1,128,1024]{2,1,0:T(8,128)(2,1)S(1)}, bf16[1,128,1024]{2,1,0:T(8,128)(2,1)S(1)}, u32[]{:S(2)}, u32[]{:S(2)}) collective-permute-start(bf16[1,128,1024]{2,1,0:T(8,128)(2,1)S(1)} %slice.34), channel_id=1, source_target_pairs={{0,2},{1,3},{2,0},{3,1},{4,6},{5,7},{6,4},{7,5},{8,10},{9,11},{10,... | collective-permute-start | bytes 786440 | tf_op jit(solution)/shard_map/ppermute | solution.py:344
  69.6 5.2 %collective-permute-start.19 = (bf16[64,1024]{1,0:T(8,128)(2,1)S(1)}, bf16[64,1024]{1,0:T(8,128)(2,1)S(1)}, u32[]{:S(2)}, u32[]{:S(2)}) collective-permute-start(bf16[64,1024]{1,0:T(8,128)(2,1)S(1)} %slice.26), channel_id=1, source_target_pairs={{0,8},{8,16},{16,24},{24,28},{28,20},{20,12},{12,4},{4,0},{1,9},{9... | collective-permute-start | bytes 393224 | tf_op jit(solution)/shard_map/ppermute | solution.py:580
  69.7 5.2 %collective-permute-start.23 = (bf16[64,1024]{1,0:T(8,128)(2,1)S(1)}, bf16[64,1024]{1,0:T(8,128)(2,1)S(1)}, u32[]{:S(2)}, u32[]{:S(2)}) collective-permute-start(bf16[64,1024]{1,0:T(8,128)(2,1)S(1)} %slice.27), channel_id=1, source_target_pairs={{8,0},{16,8},{24,16},{28,24},{20,28},{12,20},{4,12},{0,4},{9,1},{1... | collective-permute-start | bytes 393224 | tf_op jit(solution)/shard_map/ppermute | solution.py:581

commit v15 on v11

--- a/solution.py
+++ b/solution.py
@@ -483,11 +483,11 @@
     attended = pl.pallas_call(
         functools.partial(attended_kernel, seq_bits),
         out_shape=like((rows, width), BF),
-        in_specs=[VMEM] * (2 + seq_bits) + [ANY] * 2,
+        in_specs=[VMEM] * (2 + seq_bits) + [ANY],
         out_specs=VMEM,
         compiler_params=PARAMS,
         cost_estimate=cost(seq_bits * flops_head, 8 * moved_head),
-    )(att_local, qw, *partner_states, key_local, own_chunks[-1])
+    )(att_local, qw, *partner_states, key_local)
 
     first_pending = attended
     for digit in reversed(range(top)):

time: 76.5 us -> 76.5 us (level)
  no operation moved by 1% of the time
where the time goes in v15:
time: 76.5 us; the launch traced here: 76.4 us
  starting transfers between devices  31 us (41%)
  waiting for transfers between devices  24 us (31%)
  Pallas kernels  19.5 us (25%)
  other arithmetic  0.95 us (1%)
  between operations  0.87 us (1%)
    ppermute x5, waiting for transfers between devices, across(): return lax.ppermute(block, axis, route)  11.3 us
    ppermute x5, starting transfers between devices, across(): return lax.ppermute(block, axis, route)  8.21 us
    ppermute x3, waiting for transfers between devices, body(): ahead = lax.ppermute(ahead, 'seq', forward)  7.14 us
    ppermute x8, starting transfers between devices, to_group(): return lax.ppermute(block, 'head', [(at, at ^ i) for at in range(heads)])  6.7 us
    ppermute x3, starting transfers between devices, body(): behind = lax.ppermute(behind, 'seq', backward)  4.65 us
    ppermute x1, starting transfers between devices, body(): lax.ppermute(grad_blocks[far][half:], axes, turn_route(far))  3.92 us
    pallas_call x1, Pallas kernels, body(): pl.pallas_call(local_kernel, out_shape=(pltpu.VMEM((heads_dev, rows, rows...  3.66 us
    ppermute x3, starting transfers between devices, body(): ahead = lax.ppermute(ahead, 'seq', forward)  3.18 us
  transfers between devices with their start and end apart: 24, of which 10 were waited for; matrix products, arithmetic and copies ran while one was open for 1% of the time, Pallas kernels for 19%

profile of v15, /device:TPU:0, one launch (start us, length us, event | category | flops | bytes accessed | tf_op | source)
XLA Modules:
  0.0 76.4 jit_solution(1779135920675469377)
XLA Ops:
  0.6 2.5 %shard_map.101 = (bf16[8,128,128]{2,1,0:T(8,128)(2,1)S(1)}, bf16[8,128,128]{2,1,0:T(8,128)(2,1)S(1)}, bf16[8,128,128]{2,1,0:T(8,128)(2,1)S(1)}, bf16[128,1024]{1,0:T(8,128)(2,1)S(1)}, bf16[64,1024]{1,0:T(8,128)(2,1)S(1)}) custom-call(f32[128,8,128]{2,1,0:T(8,128)} %k_hbm.1, f32[128,8,128]{2,1,0:T(8,128)} %v_hbm.1, bf16[128,1024]{1,0:T(8,128)(2,1)} %grad_hbm.1), custom_call_target="tpu_custom_call" | custom-call | flops 33554432 | bytes 1835008 | tf_op jit(solution)/shard_map/pallas_call | solution.py:324
  3.1 3.0 %collective-permute-start.3 = (bf16[128,1024]{1,0:T(8,128)(2,1)S(1)}, bf16[128,1024]{1,0:T(8,128)(2,1)S(1)}, u32[]{:S(2)}, u32[]{:S(2)}) collective-permute-start(bf16[128,1024]{1,0:T(8,128)(2,1)S(1)} %get-tuple-element.32.refs_0_), channel_id=1, source_target_pairs={{0,2},{1,3},{2,0},{3,1},{4,6},{5,7},{6,4},{7,5},{8,10},{9,11},{10,... | collective-permute-start | bytes 786440 | tf_op jit(solution)/shard_map/ppermute | solution.py:339
  6.1 1.5 %collective-permute-start = (bf16[8,128,128]{2,1,0:T(8,128)(2,1)S(1)}, bf16[8,128,128]{2,1,0:T(8,128)(2,1)S(1)}, u32[]{:S(2)}, u32[]{:S(2)}) collective-permute-start(bf16[8,128,128]{2,1,0:T(8,128)(2,1)S(1)} %get-tuple-element.31.running_ref), channel_id=1, source_target_pairs={{0,4},{4,0},{8,12},{12,8},{16,20},{20,16},{24,28},{28,24},{1,5},{5... | collective-permute-start | bytes 786440 | tf_op jit(solution)/shard_map/ppermute | solution.py:44
  7.6 0.0 collective-permute-start.2
  7.6 3.7 %shard_map.102 = (bf16[8,128,128]{2,1,0:T(8,128)(2,1)S(1)}, f32[8,128,128]{2,1,0:T(8,128)S(1)}, bf16[8,128,128]{2,1,0:T(8,128)(2,1)S(1)}, bf16[3,8,128,128]{3,2,...) custom-call(f32[128,8,128]{2,1,0:T(8,128)} %q_hbm.1, ...), custom_call_target="tpu_custom_call" | custom-call | flops 67108864 | bytes 3145728 | tf_op jit(solution)/shard_map/pallas_call | solution.py:348
  11.3 1.1 %collective-permute-done.3.block_ref.refs_2_ = bf16[128,1024]{1,0:T(8,128)(2,1)S(1)} collective-permute-done((bf16[128,1024]{1,0:T(8,128)(2,1)S(1)}, bf16[128,1024]{1,0:T(8,128)(2,1)S(1)}, u32[]{:S(2)}, u32[]{:S(2)}) %collective-permute-start.3) | collective-permute-done | bytes 262176 | tf_op jit(solution)/shard_map/ppermute | solution.py:339
  12.4 0.1 collective-permute-start.4
  12.5 1.4 %collective-permute-done.arrived_ref.refs_0_ = bf16[8,128,128]{2,1,0:T(8,128)(2,1)S(1)} collective-permute-done((bf16[8,128,128]{2,1,0:T(8,128)(2,1)S(1)}, bf16[8,128,128]{2,1,0:T(8,128)(2,1)S(1)}, u32[]{:S(2)}, u32[]{:S(2)}) %collective-permute-start) | collective-permute-done | bytes 262176 | tf_op jit(solution)/shard_map/ppermute | solution.py:44
  13.9 0.1 shard_map.103.refs_6_.running_ref
  13.9 1.6 %collective-permute-start.1 = (bf16[8,128,128]{2,1,0:T(8,128)(2,1)S(1)}, bf16[8,128,128]{2,1,0:T(8,128)(2,1)S(1)}, u32[]{:S(2)}, u32[]{:S(2)}) collective-permute-start(bf16[8,128,128]{2,1,0:T(8,128)(2,1)S(1)} %shard_map.103.refs_6_.running_ref), channel_id=1, source_target_pairs={{0,8},{8,0},{4,12},{12,4},{16,24},{24,16},{20,28},{28,20},{1,9},{9... | collective-permute-start | bytes 786440 | tf_op jit(solution)/shard_map/ppermute | solution.py:44
  15.6 0.7 collective-permute-start.6
  16.3 3.9 %collective-permute-start.7 = (bf16[64,1024]{1,0:T(8,128)(2,1)S(1)}, bf16[64,1024]{1,0:T(8,128)(2,1)S(1)}, u32[]{:S(2)}, u32[]{:S(2)}) collective-permute-start(bf16[64,1024]{1,0:T(8,128)(2,1)S(1)} %slice.23), channel_id=1, source_target_pairs={{2,0},{3,10},{0,18},{1,24},{6,4},{7,14},{4,22},{5,28},{10,2},{11,8... | collective-permute-start | bytes 393224 | tf_op jit(solution)/shard_map/ppermute | solution.py:401
  20.2 0.0 collective-permute-done.2.refs_1_
  20.2 0.0 collective-permute-done.4.refs_3_
  20.2 2.8 %shard_map.105 = (bf16[1024,128]{1,0:T(8,128)(2,1)S(1)}, bf16[8,128,128]{2,1,0:T(8,128)(2,1)S(1)}, bf16[8,128,128]{2,1,0:T(8,128)(2,1)S(1)}, bf16[8,128,128]{2,1,0:T(8,128)(2,1)S(1)}) custom-call(bf16[128,1024]{1,0:T(8,128)(2,1)S(1)} %get-tuple-element.32.refs_0_, bf16[128,1024]{1,0:T(8,128)(2,1)S(1)} %collective-permute-done.2.refs_1_, ...), custom_call_target="tpu_custom_call" | custom-call | flops 1073741824 | bytes 8388608 | tf_op jit(solution)/shard_map/pallas_call | solution.py:418
  23.0 0.0 collective-permute-done.1.arrived_ref.refs_1_
  23.0 0.1 shard_map.106.after_ref
  23.1 3.4 %collective-permute-start.5 = (bf16[8,128,128]{2,1,0:T(8,128)(2,1)S(1)}, bf16[8,128,128]{2,1,0:T(8,128)(2,1)S(1)}, u32[]{:S(2)}, u32[]{:S(2)}) collective-permute-start(bf16[8,128,128]{2,1,0:T(8,128)(2,1)S(1)} %shard_map.106.after_ref), channel_id=1, source_target_pairs={{0,16},{16,0},{4,20},{20,4},{8,24},{24,8},{12,28},{28,12},{1,17},{... | collective-permute-start | bytes 786440 | tf_op jit(solution)/shard_map/ppermute | solution.py:44
  26.5 0.0 collective-permute-done.6.low_ref
  26.5 0.0 collective-permute-done.7.high_ref
  26.6 1.6 %collective-permute-start.8 = (bf16[128,512]{1,0:T(8,128)(2,1)S(1)}, bf16[128,512]{1,0:T(8,128)(2,1)S(1)}, u32[]{:S(2)}, u32[]{:S(2)}) collective-permute-start(bf16[128,512]{1,0:T(8,128)(2,1)S(1)} %get-tuple-element.43), channel_id=1, source_target_pairs={{0,4},{4,0},{8,12},{12,8},{16,20},{20,16},{24,28},{28,24},{1,5},{5... | collective-permute-start | bytes 393224 | tf_op jit(solution)/shard_map/ppermute | solution.py:452
  28.2 1.3 %shard_map.107 = (f32[8,128,128]{2,1,0:T(8,128)S(1)}, f32[8,128,128]{2,1,0:T(8,128)S(1)}, f32[8,128,128]{2,1,0:T(8,128)S(1)}) custom-call(bf16[1024,128]{1,0:T(8,128)(2,1)S(1)} %get-tuple-element.35.gt_ref, bf16[8,128,128]{2,1,0:T(8,128)(2,1)S(1)} %get-tuple-element.36.qh_ref, bf16[8,128,128]{2,1,0:T(8,128)(2,1)S(1)} %get-tuple-element.27.kh_ref, ...), custom_call_target="tpu_custom_call" | custom-call | flops 201326592 | bytes 3670016 | tf_op jit(solution)/shard_map/pallas_call | solution.py:474
  29.5 2.8 %collective-permute-done.8.refs_1_ = bf16[128,512]{1,0:T(8,128)(2,1)S(1)} collective-permute-done((bf16[128,512]{1,0:T(8,128)(2,1)S(1)}, bf16[128,512]{1,0:T(8,128)(2,1)S(1)}, u32[]{:S(2)}, u32[]{:S(2)}) %collective-permute-start.8) | collective-permute-done | bytes 131104 | tf_op jit(solution)/shard_map/ppermute | solution.py:452
  32.3 6.6 %collective-permute-done.5.refs_2_.refs_0_.state_ref = bf16[8,128,128]{2,1,0:T(8,128)(2,1)S(1)} collective-permute-done((bf16[8,128,128]{2,1,0:T(8,128)(2,1)S(1)}, bf16[8,128,128]{2,1,0:T(8,128)(2,1)S(1)}, u32[]{:S(2)}, u32[]{:S(2)}) %collective-permute-start.5) | collective-permute-done | bytes 262176 | tf_op jit(solution)/shard_map/ppermute | solution.py:44
  38.9 0.4 shard_map.108.after_ref.att_ref.refs_0_
  39.2 0.7 shard_map.113
  40.0 0.1 collective-permute-start.9
  40.0 0.1 collective-permute-start.16
  40.2 2.0 %collective-permute-start.20 = (bf16[128,1024]{1,0:T(8,128)(2,1)S(1)}, bf16[128,1024]{1,0:T(8,128)(2,1)S(1)}, u32[]{:S(2)}, u32[]{:S(2)}) collective-permute-start(bf16[128,1024]{1,0:T(8,128)(2,1)S(1)} %shard_map.108.after_ref.att_ref.refs_0_), channel_id=1, source_target_pairs={{8,0},{16,8},{24,16},{28,24},{20,28},{12,20},{4,12},{0,4},{9,1},{1... | collective-permute-start | bytes 786440 | tf_op jit(solution)/shard_map/ppermute | solution.py:566
  42.1 1.7 %collective-permute-start.14 = (bf16[2,128,512]{2,1,0:T(8,128)(2,1)S(1)}, bf16[2,128,512]{2,1,0:T(8,128)(2,1)S(1)}, u32[]{:S(2)}, u32[]{:S(2)}) collective-permute-start(bf16[2,128,512]{2,1,0:T(8,128)(2,1)S(1)} %shard_map.112.after_ref.refs_0_), channel_id=1, source_target_pairs={{0,2},{1,3},{2,0},{3,1},{4,6},{5,7},{6,4},{7,5},{8,10},{9,11},{10,... | collective-permute-start | bytes 786440 | tf_op jit(solution)/shard_map/ppermute | solution.py:339
  43.8 0.1 shard_map.109.after_ref
  43.9 0.2 collective-permute-start.11
  44.1 4.7 %collective-permute-done.16.refs_1_ = bf16[128,1024]{1,0:T(8,128)(2,1)S(1)} collective-permute-done((bf16[128,1024]{1,0:T(8,128)(2,1)S(1)}, bf16[128,1024]{1,0:T(8,128)(2,1)S(1)}, u32[]{:S(2)}, u32[]{:S(2)}) %collective-permute-start.16) | collective-permute-done | bytes 262176 | tf_op jit(solution)/shard_map/ppermute | solution.py:565
  48.8 0.6 collective-permute-start.17
  49.3 0.0 collective-permute-done.20.refs_2_
  49.3 1.4 %collective-permute-start.21 = (bf16[128,1024]{1,0:T(8,128)(2,1)S(1)}, bf16[128,1024]{1,0:T(8,128)(2,1)S(1)}, u32[]{:S(2)}, u32[]{:S(2)}) collective-permute-start(bf16[128,1024]{1,0:T(8,128)(2,1)S(1)} %collective-permute-done.20.refs_2_), channel_id=1, source_target_pairs={{8,0},{16,8},{24,16},{28,24},{20,28},{12,20},{4,12},{0,4},{9,1},{1... | collective-permute-start | bytes 786440 | tf_op jit(solution)/shard_map/ppermute | solution.py:566
  50.8 0.7 shard_map.110
  51.5 0.0 collective-permute-done.14.refs_2_
  51.5 0.1 collective-permute-start.13
  51.6 3.3 %collective-permute-done.11.refs_1_ = bf16[8,128,128]{2,1,0:T(8,128)(2,1)S(1)} collective-permute-done((bf16[8,128,128]{2,1,0:T(8,128)(2,1)S(1)}, bf16[8,128,128]{2,1,0:T(8,128)(2,1)S(1)}, u32[]{:S(2)}, u32[]{:S(2)}) %collective-permute-start.11) | collective-permute-done | bytes 262176 | tf_op jit(solution)/shard_map/ppermute | solution.py:44
  54.9 0.0 collective-permute-start.15
  54.9 0.1 shard_map.115
  55.1 0.0 collective-permute-done.9
  55.1 1.5 %collective-permute-start.12 = (bf16[8,128,128]{2,1,0:T(8,128)(2,1)S(1)}, bf16[8,128,128]{2,1,0:T(8,128)(2,1)S(1)}, u32[]{:S(2)}, u32[]{:S(2)}) collective-permute-start(bf16[8,128,128]{2,1,0:T(8,128)(2,1)S(1)} %shard_map.115), channel_id=1, source_target_pairs={{0,4},{4,0},{8,12},{12,8},{16,20},{20,16},{24,28},{28,24},{1,5},{5... | collective-permute-start | bytes 786440 | tf_op jit(solution)/shard_map/ppermute | solution.py:44
  56.6 1.2 %collective-permute-done.17.refs_3_ = bf16[128,1024]{1,0:T(8,128)(2,1)S(1)} collective-permute-done((bf16[128,1024]{1,0:T(8,128)(2,1)S(1)}, bf16[128,1024]{1,0:T(8,128)(2,1)S(1)}, u32[]{:S(2)}, u32[]{:S(2)}) %collective-permute-start.17) | collective-permute-done | bytes 262176 | tf_op jit(solution)/shard_map/ppermute | solution.py:565
  57.8 2.5 %collective-permute-start.18 = (bf16[128,1024]{1,0:T(8,128)(2,1)S(1)}, bf16[128,1024]{1,0:T(8,128)(2,1)S(1)}, u32[]{:S(2)}, u32[]{:S(2)}) collective-permute-start(bf16[128,1024]{1,0:T(8,128)(2,1)S(1)} %collective-permute-done.17.refs_3_), channel_id=1, source_target_pairs={{0,8},{8,16},{16,24},{24,28},{28,20},{20,12},{12,4},{4,0},{1,9},{9... | collective-permute-start | bytes 786440 | tf_op jit(solution)/shard_map/ppermute | solution.py:565
  60.3 1.2 %collective-permute-start.22 = (bf16[128,1024]{1,0:T(8,128)(2,1)S(1)}, bf16[128,1024]{1,0:T(8,128)(2,1)S(1)}, u32[]{:S(2)}, u32[]{:S(2)}) collective-permute-start(bf16[128,1024]{1,0:T(8,128)(2,1)S(1)} %collective-permute-done.21.refs_4_), channel_id=1, source_target_pairs={{8,0},{16,8},{24,16},{28,24},{20,28},{12,20},{4,12},{0,4},{9,1},{1... | collective-permute-start | bytes 786440 | tf_op jit(solution)/shard_map/ppermute | solution.py:566
  61.5 0.2 convert_add_fusion
  61.8 0.0 collective-permute-done.13.refs_1_
  61.8 1.8 %collective-permute-start.10 = (bf16[1,128,1024]{2,1,0:T(8,128)(2,1)S(1)}, bf16[1,128,1024]{2,1,0:T(8,128)(2,1)S(1)}, u32[]{:S(2)}, u32[]{:S(2)}) collective-permute-start(bf16[1,128,1024]{2,1,0:T(8,128)(2,1)S(1)} %slice.34), channel_id=1, source_target_pairs={{0,2},{1,3},{2,0},{3,1},{4,6},{5,7},{6,4},{7,5},{8,10},{9,11},{10,... | collective-permute-start | bytes 786440 | tf_op jit(solution)/shard_map/ppermute | solution.py:339
  63.5 1.3 %shard_map.114 = f32[128,8,128]{2,1,0:T(8,128)} custom-call(bf16[1024,128]{1,0:T(8,128)(2,1)S(1)} %get-tuple-element.35.gt_ref, f32[5,8,128]{2,1,0:T(8,128)S(1)} %get-tuple-element.38.lam_ref, f32[8,128,128]{2,1,0:T(8,128)S(1)} %get-tuple-element.44.dql_ref, bf16[8,128,128]{2,1,0:T(8,128)(2,1)S(1)} %collective-permute-done.5.refs_2_.refs_0_.state_ref, ...), custom_call_target="tpu_custom_call" | custom-call | flops 33554432 | bytes 1572864 | tf_op jit(solution)/shard_map/pallas_call | solution.py:506
  64.9 0.1 shard_map.117.cols_ref
  65.0 0.0 collective-permute-done.12.refs_2_
  65.0 1.7 %shard_map.116 = (f32[128,8,128]{2,1,0:T(8,128)}, f32[128,8,128]{2,1,0:T(8,128)}) custom-call(bf16[8,128,128]{2,1,0:T(8,128)(2,1)S(1)} %get-tuple-element.27.kh_ref, bf16[8,128,128]{2,1,0:T(8,128)(2,1)S(1)} %get-tuple-element.28.vh_ref, f32[8,128,128]{2,1,0:T(8,128)S(1)} %get-tuple-element.39.refs_3_.dkl_ref, f32[8,128,128]{2,1,0:T(8,128)S(1)} %get-tuple-element.45.dvl_ref, ...), custom_call_target="tpu_custom_call" | custom-call | flops 67108864 | bytes 2883584 | tf_op jit(solution)/shard_map/pallas_call | solution.py:535
  66.7 1.5 %shard_map.118.refs_2_ = f32[1024,512]{1,0:T(8,128)S(1)} custom-call(bf16[8,128,512]{2,1,0:T(8,128)(2,1)S(1)} %shard_map.117.cols_ref, f32[128,8,128]{2,1,0:T(8,128)} %get-tuple-element.24.after_ref, bf16[128,1024]{1,0:T(8,128)(2,1)S(1)} %shard_map.108.after_ref.att_ref.refs_0_, bf16[128,1024]{1,0:T(8,128)(2,1)S(1)} %collective-permute-done.16.refs_1_, ...), custom_call_target="tpu_custom_call" | custom-call | flops 671088640 | bytes 2097152 | tf_op jit(solution)/shard_map/pallas_call | solution.py:550
  68.2 1.2 %collective-permute-done.18.refs_0_ = bf16[128,1024]{1,0:T(8,128)(2,1)S(1)} collective-permute-done((bf16[128,1024]{1,0:T(8,128)(2,1)S(1)}, bf16[128,1024]{1,0:T(8,128)(2,1)S(1)}, u32[]{:S(2)}, u32[]{:S(2)}) %collective-permute-start.18) | collective-permute-done | bytes 262176 | tf_op jit(solution)/shard_map/ppermute | solution.py:565
  69.5 0.1 collective-permute-start.19
  69.6 2.1 %collective-permute-start.23 = (bf16[64,1024]{1,0:T(8,128)(2,1)S(1)}, bf16[64,1024]{1,0:T(8,128)(2,1)S(1)}, u32[]{:S(2)}, u32[]{:S(2)}) collective-permute-start(bf16[64,1024]{1,0:T(8,128)(2,1)S(1)} %slice.27), channel_id=1, source_target_pairs={{8,0},{16,8},{24,16},{28,24},{20,28},{12,20},{4,12},{0,4},{9,1},{1... | collective-permute-start | bytes 393224 | tf_op jit(solution)/shard_map/ppermute | solution.py:576
  71.6 0.0 collective-permute-done.10
  71.6 0.8 fusion.1
  72.4 0.7 shard_map.119.total_ref
  73.1 1.5 %collective-permute-done.19.low_ref = bf16[64,1024]{1,0:T(8,128)(2,1)S(1)} collective-permute-done((bf16[64,1024]{1,0:T(8,128)(2,1)S(1)}, bf16[64,1024]{1,0:T(8,128)(2,1)S(1)}, u32[]{:S(2)}, u32[]{:S(2)}) %collective-permute-start.19) | collective-permute-done | bytes 131104 | tf_op jit(solution)/shard_map/ppermute | solution.py:575
  74.7 0.1 collective-permute-done.23.high_ref
  74.8 1.6 %shard_map.120 = f32[1024,512]{1,0:T(8,128)} custom-call(bf16[8,128,512]{2,1,0:T(8,128)(2,1)S(1)} %shard_map.117.cols_ref, bf16[64,1024]{1,0:T(8,128)(2,1)S(1)} %collective-permute-done.19.low_ref, bf16[64,1024]{1,0:T(8,128)(2,1)S(1)} %collective-permute-done.23.high_ref, f32[1024,512]{1,0:T(8,128)S(1)} %shard_map.119.total_ref, ...), custom_call_target="tpu_custom_call" | custom-call | flops 134217728 | bytes 4194304 | tf_op jit(solution)/shard_map/pallas_call | solution.py:578
  (10 shorter events, 0.1 us)
Async XLA Ops:
  3.1 9.3 %collective-permute-start.3 = (bf16[128,1024]{1,0:T(8,128)(2,1)S(1)}, bf16[128,1024]{1,0:T(8,128)(2,1)S(1)}, u32[]{:S(2)}, u32[]{:S(2)}) collective-permute-start(bf16[128,1024]{1,0:T(8,128)(2,1)S(1)} %get-tuple-element.32.refs_0_), channel_id=1, source_target_pairs={{0,2},{1,3},{2,0},{3,1},{4,6},{5,7},{6,4},{7,5},{8,10},{9,11},{10,... | collective-permute-start | bytes 786440 | tf_op jit(solution)/shard_map/ppermute | solution.py:339
  6.1 7.8 %collective-permute-start = (bf16[8,128,128]{2,1,0:T(8,128)(2,1)S(1)}, bf16[8,128,128]{2,1,0:T(8,128)(2,1)S(1)}, u32[]{:S(2)}, u32[]{:S(2)}) collective-permute-start(bf16[8,128,128]{2,1,0:T(8,128)(2,1)S(1)} %get-tuple-element.31.running_ref), channel_id=1, source_target_pairs={{0,4},{4,0},{8,12},{12,8},{16,20},{20,16},{24,28},{28,24},{1,5},{5... | collective-permute-start | bytes 786440 | tf_op jit(solution)/shard_map/ppermute | solution.py:44
  7.6 12.6 %collective-permute-start.2 = (bf16[128,1024]{1,0:T(8,128)(2,1)S(1)}, bf16[128,1024]{1,0:T(8,128)(2,1)S(1)}, u32[]{:S(2)}, u32[]{:S(2)}) collective-permute-start(bf16[128,1024]{1,0:T(8,128)(2,1)S(1)} %get-tuple-element.32.refs_0_), channel_id=1, source_target_pairs={{0,1},{1,0},{2,3},{3,2},{4,5},{5,4},{6,7},{7,6},{8,9},{9,8},{10,11... | collective-permute-start | bytes 786440 | tf_op jit(solution)/shard_map/ppermute | solution.py:339
  12.4 7.8 %collective-permute-start.4 = (bf16[128,1024]{1,0:T(8,128)(2,1)S(1)}, bf16[128,1024]{1,0:T(8,128)(2,1)S(1)}, u32[]{:S(2)}, u32[]{:S(2)}) collective-permute-start(bf16[128,1024]{1,0:T(8,128)(2,1)S(1)} %shard_map.104), channel_id=1, source_target_pairs={{0,1},{1,0},{2,3},{3,2},{4,5},{5,4},{6,7},{7,6},{8,9},{9,8},{10,11... | collective-permute-start | bytes 786440 | tf_op jit(solution)/shard_map/ppermute | solution.py:339
  13.9 9.1 %collective-permute-start.1 = (bf16[8,128,128]{2,1,0:T(8,128)(2,1)S(1)}, bf16[8,128,128]{2,1,0:T(8,128)(2,1)S(1)}, u32[]{:S(2)}, u32[]{:S(2)}) collective-permute-start(bf16[8,128,128]{2,1,0:T(8,128)(2,1)S(1)} %shard_map.103.refs_6_.running_ref), channel_id=1, source_target_pairs={{0,8},{8,0},{4,12},{12,4},{16,24},{24,16},{20,28},{28,20},{1,9},{9... | collective-permute-start | bytes 786440 | tf_op jit(solution)/shard_map/ppermute | solution.py:44
  15.6 11.0 %collective-permute-start.6 = (bf16[64,1024]{1,0:T(8,128)(2,1)S(1)}, bf16[64,1024]{1,0:T(8,128)(2,1)S(1)}, u32[]{:S(2)}, u32[]{:S(2)}) collective-permute-start(bf16[64,1024]{1,0:T(8,128)(2,1)S(1)} %get-tuple-element.41), channel_id=1, source_target_pairs={{0,0},{1,10},{2,18},{3,24},{4,4},{5,14},{6,22},{7,28},{8,2},{9,8},... | collective-permute-start | bytes 393224 | tf_op jit(solution)/shard_map/ppermute | solution.py:400
  16.3 10.3 %collective-permute-start.7 = (bf16[64,1024]{1,0:T(8,128)(2,1)S(1)}, bf16[64,1024]{1,0:T(8,128)(2,1)S(1)}, u32[]{:S(2)}, u32[]{:S(2)}) collective-permute-start(bf16[64,1024]{1,0:T(8,128)(2,1)S(1)} %slice.23), channel_id=1, source_target_pairs={{2,0},{3,10},{0,18},{1,24},{6,4},{7,14},{4,22},{5,28},{10,2},{11,8... | collective-permute-start | bytes 393224 | tf_op jit(solution)/shard_map/ppermute | solution.py:401
  23.1 15.7 %collective-permute-start.5 = (bf16[8,128,128]{2,1,0:T(8,128)(2,1)S(1)}, bf16[8,128,128]{2,1,0:T(8,128)(2,1)S(1)}, u32[]{:S(2)}, u32[]{:S(2)}) collective-permute-start(bf16[8,128,128]{2,1,0:T(8,128)(2,1)S(1)} %shard_map.106.after_ref), channel_id=1, source_target_pairs={{0,16},{16,0},{4,20},{20,4},{8,24},{24,8},{12,28},{28,12},{1,17},{... | collective-permute-start | bytes 786440 | tf_op jit(solution)/shard_map/ppermute | solution.py:44
  26.6 5.7 %collective-permute-start.8 = (bf16[128,512]{1,0:T(8,128)(2,1)S(1)}, bf16[128,512]{1,0:T(8,128)(2,1)S(1)}, u32[]{:S(2)}, u32[]{:S(2)}) collective-permute-start(bf16[128,512]{1,0:T(8,128)(2,1)S(1)} %get-tuple-element.43), channel_id=1, source_target_pairs={{0,4},{4,0},{8,12},{12,8},{16,20},{20,16},{24,28},{28,24},{1,5},{5... | collective-permute-start | bytes 393224 | tf_op jit(solution)/shard_map/ppermute | solution.py:452
  40.0 15.1 %collective-permute-start.9 = (bf16[2,128,1024]{2,1,0:T(8,128)(2,1)S(1)}, bf16[2,128,1024]{2,1,0:T(8,128)(2,1)S(1)}, u32[]{:S(2)}, u32[]{:S(2)}) collective-permute-start(bf16[2,128,1024]{2,1,0:T(8,128)(2,1)S(1)} %shard_map.113), channel_id=1, source_target_pairs={{0,1},{1,0},{2,3},{3,2},{4,5},{5,4},{6,7},{7,6},{8,9},{9,8},{10,11... | collective-permute-start | bytes 1572872 | tf_op jit(solution)/shard_map/ppermute | solution.py:339
  40.0 8.7 %collective-permute-start.16 = (bf16[128,1024]{1,0:T(8,128)(2,1)S(1)}, bf16[128,1024]{1,0:T(8,128)(2,1)S(1)}, u32[]{:S(2)}, u32[]{:S(2)}) collective-permute-start(bf16[128,1024]{1,0:T(8,128)(2,1)S(1)} %shard_map.108.after_ref.att_ref.refs_0_), channel_id=1, source_target_pairs={{0,8},{8,16},{16,24},{24,28},{28,20},{20,12},{12,4},{4,0},{1,9},{9... | collective-permute-start | bytes 786440 | tf_op jit(solution)/shard_map/ppermute | solution.py:565
  40.2 9.2 %collective-permute-start.20 = (bf16[128,1024]{1,0:T(8,128)(2,1)S(1)}, bf16[128,1024]{1,0:T(8,128)(2,1)S(1)}, u32[]{:S(2)}, u32[]{:S(2)}) collective-permute-start(bf16[128,1024]{1,0:T(8,128)(2,1)S(1)} %shard_map.108.after_ref.att_ref.refs_0_), channel_id=1, source_target_pairs={{8,0},{16,8},{24,16},{28,24},{20,28},{12,20},{4,12},{0,4},{9,1},{1... | collective-permute-start | bytes 786440 | tf_op jit(solution)/shard_map/ppermute | solution.py:566
  42.1 9.4 %collective-permute-start.14 = (bf16[2,128,512]{2,1,0:T(8,128)(2,1)S(1)}, bf16[2,128,512]{2,1,0:T(8,128)(2,1)S(1)}, u32[]{:S(2)}, u32[]{:S(2)}) collective-permute-start(bf16[2,128,512]{2,1,0:T(8,128)(2,1)S(1)} %shard_map.112.after_ref.refs_0_), channel_id=1, source_target_pairs={{0,2},{1,3},{2,0},{3,1},{4,6},{5,7},{6,4},{7,5},{8,10},{9,11},{10,... | collective-permute-start | bytes 786440 | tf_op jit(solution)/shard_map/ppermute | solution.py:339
  43.9 11.0 %collective-permute-start.11 = (bf16[8,128,128]{2,1,0:T(8,128)(2,1)S(1)}, bf16[8,128,128]{2,1,0:T(8,128)(2,1)S(1)}, u32[]{:S(2)}, u32[]{:S(2)}) collective-permute-start(bf16[8,128,128]{2,1,0:T(8,128)(2,1)S(1)} %shard_map.109.after_ref), channel_id=1, source_target_pairs={{0,8},{8,0},{4,12},{12,4},{16,24},{24,16},{20,28},{28,20},{1,9},{9... | collective-permute-start | bytes 786440 | tf_op jit(solution)/shard_map/ppermute | solution.py:44
  48.8 9.0 %collective-permute-start.17 = (bf16[128,1024]{1,0:T(8,128)(2,1)S(1)}, bf16[128,1024]{1,0:T(8,128)(2,1)S(1)}, u32[]{:S(2)}, u32[]{:S(2)}) collective-permute-start(bf16[128,1024]{1,0:T(8,128)(2,1)S(1)} %collective-permute-done.16.refs_1_), channel_id=1, source_target_pairs={{0,8},{8,16},{16,24},{24,28},{28,20},{20,12},{12,4},{4,0},{1,9},{9... | collective-permute-start | bytes 786440 | tf_op jit(solution)/shard_map/ppermute | solution.py:565
  49.3 10.9 %collective-permute-start.21 = (bf16[128,1024]{1,0:T(8,128)(2,1)S(1)}, bf16[128,1024]{1,0:T(8,128)(2,1)S(1)}, u32[]{:S(2)}, u32[]{:S(2)}) collective-permute-start(bf16[128,1024]{1,0:T(8,128)(2,1)S(1)} %collective-permute-done.20.refs_2_), channel_id=1, source_target_pairs={{8,0},{16,8},{24,16},{28,24},{20,28},{12,20},{4,12},{0,4},{9,1},{1... | collective-permute-start | bytes 786440 | tf_op jit(solution)/shard_map/ppermute | solution.py:566
  51.5 10.2 %collective-permute-start.13 = (bf16[2,128,512]{2,1,0:T(8,128)(2,1)S(1)}, bf16[2,128,512]{2,1,0:T(8,128)(2,1)S(1)}, u32[]{:S(2)}, u32[]{:S(2)}) collective-permute-start(bf16[2,128,512]{2,1,0:T(8,128)(2,1)S(1)} %shard_map.112.after_ref.refs_0_), channel_id=1, source_target_pairs={{0,1},{1,0},{2,3},{3,2},{4,5},{5,4},{6,7},{7,6},{8,9},{9,8},{10,11... | collective-permute-start | bytes 786440 | tf_op jit(solution)/shard_map/ppermute | solution.py:339
  54.9 9.9 %collective-permute-start.15 = (bf16[2,128,512]{2,1,0:T(8,128)(2,1)S(1)}, bf16[2,128,512]{2,1,0:T(8,128)(2,1)S(1)}, u32[]{:S(2)}, u32[]{:S(2)}) collective-permute-start(bf16[2,128,512]{2,1,0:T(8,128)(2,1)S(1)} %collective-permute-done.14.refs_2_), channel_id=1, source_target_pairs={{0,1},{1,0},{2,3},{3,2},{4,5},{5,4},{6,7},{7,6},{8,9},{9,8},{10,11... | collective-permute-start | bytes 786440 | tf_op jit(solution)/shard_map/ppermute | solution.py:339
  55.1 9.9 %collective-permute-start.12 = (bf16[8,128,128]{2,1,0:T(8,128)(2,1)S(1)}, bf16[8,128,128]{2,1,0:T(8,128)(2,1)S(1)}, u32[]{:S(2)}, u32[]{:S(2)}) collective-permute-start(bf16[8,128,128]{2,1,0:T(8,128)(2,1)S(1)} %shard_map.115), channel_id=1, source_target_pairs={{0,4},{4,0},{8,12},{12,8},{16,20},{20,16},{24,28},{28,24},{1,5},{5... | collective-permute-start | bytes 786440 | tf_op jit(solution)/shard_map/ppermute | solution.py:44
  57.8 11.7 %collective-permute-start.18 = (bf16[128,1024]{1,0:T(8,128)(2,1)S(1)}, bf16[128,1024]{1,0:T(8,128)(2,1)S(1)}, u32[]{:S(2)}, u32[]{:S(2)}) collective-permute-start(bf16[128,1024]{1,0:T(8,128)(2,1)S(1)} %collective-permute-done.17.refs_3_), channel_id=1, source_target_pairs={{0,8},{8,16},{16,24},{24,28},{28,20},{20,12},{12,4},{4,0},{1,9},{9... | collective-permute-start | bytes 786440 | tf_op jit(solution)/shard_map/ppermute | solution.py:565
  60.3 9.3 %collective-permute-start.22 = (bf16[128,1024]{1,0:T(8,128)(2,1)S(1)}, bf16[128,1024]{1,0:T(8,128)(2,1)S(1)}, u32[]{:S(2)}, u32[]{:S(2)}) collective-permute-start(bf16[128,1024]{1,0:T(8,128)(2,1)S(1)} %collective-permute-done.21.refs_4_), channel_id=1, source_target_pairs={{8,0},{16,8},{24,16},{28,24},{20,28},{12,20},{4,12},{0,4},{9,1},{1... | collective-permute-start | bytes 786440 | tf_op jit(solution)/shard_map/ppermute | solution.py:566
  61.8 9.9 %collective-permute-start.10 = (bf16[1,128,1024]{2,1,0:T(8,128)(2,1)S(1)}, bf16[1,128,1024]{2,1,0:T(8,128)(2,1)S(1)}, u32[]{:S(2)}, u32[]{:S(2)}) collective-permute-start(bf16[1,128,1024]{2,1,0:T(8,128)(2,1)S(1)} %slice.34), channel_id=1, source_target_pairs={{0,2},{1,3},{2,0},{3,1},{4,6},{5,7},{6,4},{7,5},{8,10},{9,11},{10,... | collective-permute-start | bytes 786440 | tf_op jit(solution)/shard_map/ppermute | solution.py:339
  69.5 5.2 %collective-permute-start.19 = (bf16[64,1024]{1,0:T(8,128)(2,1)S(1)}, bf16[64,1024]{1,0:T(8,128)(2,1)S(1)}, u32[]{:S(2)}, u32[]{:S(2)}) collective-permute-start(bf16[64,1024]{1,0:T(8,128)(2,1)S(1)} %slice.26), channel_id=1, source_target_pairs={{0,8},{8,16},{16,24},{24,28},{28,20},{20,12},{12,4},{4,0},{1,9},{9... | collective-permute-start | bytes 393224 | tf_op jit(solution)/shard_map/ppermute | solution.py:575
  69.6 5.2 %collective-permute-start.23 = (bf16[64,1024]{1,0:T(8,128)(2,1)S(1)}, bf16[64,1024]{1,0:T(8,128)(2,1)S(1)}, u32[]{:S(2)}, u32[]{:S(2)}) collective-permute-start(bf16[64,1024]{1,0:T(8,128)(2,1)S(1)} %slice.27), channel_id=1, source_target_pairs={{8,0},{16,8},{24,16},{28,24},{20,28},{12,20},{4,12},{0,4},{9,1},{1... | collective-permute-start | bytes 393224 | tf_op jit(solution)/shard_map/ppermute | solution.py:576
